TPU v7x, 32 devices: a whole 2x2x4 slice. The times are simulated.
32 devices in a mesh: dp: 16 (over z, x, core), tensor: 2 (over y).
Axes of the slice: x: 2, y: 2, z: 4, core: 2. Of those that a mesh axis runs over, the one named last changes fastest.
Arguments:
- hidden_in: bfloat16 [16384, 1536], P(('dp', 'tensor')), may hold values from -6 to 6
- cotangent: bfloat16 [16384, 1536], P(('dp', 'tensor')), may hold values from -6 to 6
- lengths: int32 [16], P('dp'), may hold values from 640 to 1024, as said below
- gate_value_weight: bfloat16 [2, 2, 1536, 3072], P(None, None, 'dp', 'tensor'), may hold values from -0.15625 to 0.15625
- state_weight: bfloat16 [2, 1536, 256], P(None, 'dp'), may hold values from -0.15625 to 0.15625
- step_weight: bfloat16 [2, 1536, 48], P(None, 'dp', 'tensor'), may hold values from -0.15625 to 0.15625
- out_weight: bfloat16 [2, 3072, 1536], P(None, 'tensor', 'dp'), may hold values from -0.109375 to 0.109375
- pre_gain: float32 [2, 1536], replicated, may hold values from 0.5 to 1.5
- conv_taps: float32 [2, 5, 3328], replicated, may hold values from -3 to 3
- decay_log: float32 [2, 48], replicated, may hold values from 0 to 2.77
- step_bias: float32 [2, 48], replicated, may hold values from -6 to -2
- skip_gain: float32 [2, 48], replicated, may hold values from 0.5 to 1.5
- norm_gain: float32 [2, 3072], replicated, may hold values from 0.5 to 1.5
Outputs:
- out_hidden: float32 [16384, 1536], P(('dp', 'tensor'))
- grad_hidden: float32 [16384, 1536], P(('dp', 'tensor'))
- grad_gate_value: float32 [2, 2, 1536, 3072], P(None, None, 'dp', 'tensor')
- grad_state: float32 [2, 1536, 256], P(None, 'dp')
- grad_step: float32 [2, 1536, 48], P(None, 'dp', 'tensor')
- grad_out: float32 [2, 3072, 1536], P(None, 'tensor', 'dp')
- grad_pre_gain: float32 [2, 1536], replicated
- grad_conv_taps: float32 [2, 5, 3328], replicated
- grad_decay_log: float32 [2, 48], replicated
- grad_step_bias: float32 [2, 48], replicated
- grad_skip_gain: float32 [2, 48], replicated
- grad_norm_gain: float32 [2, 3072], replicated
Inputs may be any that keep to these rules, and one draw needn't show every extreme that they name: A sequence's valid positions are its first lengths positions; in every draw some sequence has all 1024 positions valid and some has exactly 640.
All inputs are finite; a program needn't handle non-finite values.
Results may differ from a plain program's by a relative error of at most 0.02.
Values may be sent and summed in bfloat16 or wider, within the bound.
A program may use at most 448 MiB of HBM per device.

v0:
```python
import jax
import jax.numpy as jnp
from jax import lax
from jax.sharding import PartitionSpec as P

DI = 3072
HEAD = 64
N = 128
KCONV = 4
BLOCK = 256
LAYERS = 2
SEQ = 1024
H = 48


EPSILON = 1e-05


def exact_dot(left, right):
    return jnp.dot(left, right, precision=lax.Precision.HIGHEST, preferred_element_type=jnp.float32)


def exact_einsum(pattern, *operands):
    return jnp.einsum(pattern, *operands, precision=lax.Precision.HIGHEST)


def dot_first(left, right):
    return lax.dot_general(
        left, right, (((0,), (0,)), ((), ())), preferred_element_type=jnp.float32
    )


def dot_last(left, right):
    return lax.dot_general(
        left, right, (((1,), (1,)), ((), ())), preferred_element_type=jnp.float32
    )


def scan_state(value_heads, step_size, decay_rate, input_rows, output_rows):
    block_count = value_heads.shape[0] // BLOCK
    causal_mask = (jnp.arange(BLOCK)[:, None] >= jnp.arange(BLOCK)[None, :])[:, :, None]

    def one_block(carry_state, pieces):
        value_block, step_block, input_block, output_block = pieces
        log_decay = step_block * decay_rate[None, :]
        running = jnp.cumsum(log_decay, axis=0)
        between = running[:, None, :] - running[None, :, :]
        decay_table = jnp.where(causal_mask, jnp.exp(jnp.where(causal_mask, between, 0.0)), 0.0)
        scores = exact_dot(output_block, input_block.T)
        weights = scores[:, :, None] * decay_table * step_block[None, :, :]
        within_block = exact_einsum("tsh,shp->thp", weights, value_block)
        from_state = (
            exact_einsum("tn,hpn->thp", output_block, carry_state) * jnp.exp(running)[:, :, None]
        )
        tail_weight = jnp.exp(running[-1][None, :] - running) * step_block
        state_next = carry_state * jnp.exp(running[-1])[:, None, None] + exact_einsum(
            "sh,shp,sn->hpn", tail_weight, value_block, input_block
        )
        return (state_next, within_block + from_state)

    def blockwise(values):
        return values.reshape((block_count, BLOCK) + values.shape[1:])

    start_state = jnp.zeros(
        (value_heads.shape[1], value_heads.shape[2], input_rows.shape[1]), jnp.float32
    )
    final_state, outputs = lax.scan(
        jax.checkpoint(one_block),
        start_state,
        (
            blockwise(value_heads),
            blockwise(step_size),
            blockwise(input_rows),
            blockwise(output_rows),
        ),
    )
    return outputs.reshape(value_heads.shape)


def convolve(values, tap_rows):
    seq_length = values.shape[0]
    padded = jnp.pad(values, ((KCONV - 1, 0), (0, 0)))
    summed = jnp.broadcast_to(tap_rows[KCONV][None, :], values.shape)
    for offset in range(KCONV):
        summed = summed + tap_rows[offset][None, :] * padded[offset : offset + seq_length]
    return jax.nn.silu(summed)


def filter_piece(values, tap_rows):
    return jax.vmap(convolve, (0, None))(values, tap_rows)


def state_piece(value_conv, state_conv, step_in, decay_local, bias_local, skip_local):
    heads_local = step_in.shape[2]
    value_heads = value_conv.reshape(value_conv.shape[0], value_conv.shape[1], heads_local, HEAD)
    step_size = jax.nn.softplus(step_in + bias_local)
    decay_rate = -jnp.exp(decay_local)
    scanned = jax.vmap(scan_state, (0, 0, None, 0, 0))(
        value_heads, step_size, decay_rate, state_conv[:, :, :N], state_conv[:, :, N:]
    )
    scanned = scanned + skip_local[:, None] * value_heads
    return scanned.reshape(value_conv.shape)


def per_device(
    hidden_in,
    cotangent,
    lengths,
    gate_value_weight,
    state_weight,
    step_weight,
    out_weight,
    pre_gain,
    conv_taps,
    decay_log,
    step_bias,
    skip_gain,
    norm_gain,
):
    tensor_index = lax.axis_index("tensor")
    local_rows = hidden_in.shape[0]
    width_local = gate_value_weight.shape[3]
    heads_local = step_weight.shape[2]
    seq_count = lengths.shape[0]
    row_start = tensor_index * local_rows
    global_rows = row_start + jnp.arange(local_rows)
    seq_of_row = global_rows // SEQ
    position = global_rows % SEQ
    row_length = jnp.sum(
        jnp.where(seq_of_row[:, None] == jnp.arange(seq_count)[None, :], lengths[None, :], 0),
        axis=1,
    )
    keep_rows = (position < row_length).astype(jnp.float32)[:, None]

    def to_seqs(values):
        return values.reshape(seq_count, SEQ, values.shape[-1])

    def head_slice(table, layer_index):
        return lax.dynamic_slice_in_dim(table[layer_index], tensor_index * heads_local, heads_local)

    hidden = hidden_in.astype(jnp.float32)
    saved_layers = []
    for layer_index in range(LAYERS):
        weights = (
            lax.all_gather(gate_value_weight[layer_index], "dp", axis=1, tiled=True),
            lax.all_gather(state_weight[layer_index], "dp", axis=0, tiled=True),
            lax.all_gather(step_weight[layer_index], "dp", axis=0, tiled=True),
            lax.all_gather(out_weight[layer_index], "dp", axis=1, tiled=True),
        )
        gate_value_full, state_full, step_full, out_full = weights
        inv_rows = lax.rsqrt(jnp.mean(hidden * hidden, axis=-1, keepdims=True) + EPSILON)
        normed = (hidden * inv_rows * pre_gain[layer_index]).astype(jnp.bfloat16)
        normed_all = lax.all_gather(normed, "tensor", axis=0, tiled=True)
        projected = jnp.einsum(
            "fd,kdc->kfc", normed_all, gate_value_full, preferred_element_type=jnp.float32
        )
        state_in = jnp.dot(normed_all, state_full, preferred_element_type=jnp.float32)
        step_in = jnp.dot(normed_all, step_full, preferred_element_type=jnp.float32)
        layer_taps = conv_taps[layer_index]
        taps_value = lax.dynamic_slice_in_dim(
            layer_taps, tensor_index * width_local, width_local, 1
        )
        taps_state = layer_taps[:, DI:]
        value_conv, pull_value = jax.vjp(filter_piece, to_seqs(projected[1]), taps_value)
        state_conv, pull_state = jax.vjp(filter_piece, to_seqs(state_in), taps_state)
        scanned, pull_scan = jax.vjp(
            state_piece,
            value_conv,
            state_conv,
            to_seqs(step_in),
            head_slice(decay_log, layer_index),
            head_slice(step_bias, layer_index),
            head_slice(skip_gain, layer_index),
        )
        scanned = scanned.reshape(-1, width_local)
        gate_in = projected[0]
        gated_rows = scanned * jax.nn.silu(gate_in)
        square_sum = lax.psum(jnp.sum(gated_rows * gated_rows, axis=-1), "tensor")
        inv_gate = lax.rsqrt(square_sum / DI + EPSILON)[:, None]
        gain_local = lax.dynamic_slice_in_dim(
            norm_gain[layer_index], tensor_index * width_local, width_local
        )
        gate_norm = (gated_rows * inv_gate * gain_local).astype(jnp.bfloat16)
        mixed_rows = lax.psum_scatter(
            jnp.dot(gate_norm, out_full, preferred_element_type=jnp.float32),
            "tensor",
            scatter_dimension=0,
            tiled=True,
        )
        saved_layers.append(
            (
                hidden,
                inv_rows,
                normed_all,
                gate_in,
                scanned,
                gated_rows,
                inv_gate,
                gain_local,
                gate_norm,
                pull_value,
                pull_state,
                pull_scan,
                weights,
            )
        )
        hidden = keep_rows * (hidden + mixed_rows)
    out_hidden = hidden
    grad_flow = cotangent.astype(jnp.float32)
    grads_gate_value, grads_state, grads_step, grads_out = ([], [], [], [])
    grads_pre, grads_taps, grads_decay, grads_bias, grads_skip, grads_gain = (
        [],
        [],
        [],
        [],
        [],
        [],
    )
    for layer_index in reversed(range(LAYERS)):
        (
            hidden,
            inv_rows,
            normed_all,
            gate_in,
            scanned,
            gated_rows,
            inv_gate,
            gain_local,
            gate_norm,
            pull_value,
            pull_state,
            pull_scan,
            weights,
        ) = saved_layers[layer_index]
        gate_value_full, state_full, step_full, out_full = weights
        grad_mix = keep_rows * grad_flow
        mix_all = lax.all_gather(grad_mix.astype(jnp.bfloat16), "tensor", axis=0, tiled=True)
        grad_gate_norm = dot_last(mix_all, out_full)
        grad_out_weight = dot_first(gate_norm, mix_all)
        grad_gain_local = jnp.sum(grad_gate_norm * gated_rows * inv_gate, axis=0)
        scaled = grad_gate_norm * gain_local
        cross_sum = lax.psum(jnp.sum(gated_rows * scaled, axis=-1), "tensor")
        grad_gated = (
            inv_gate * scaled
            - gated_rows * (inv_gate * inv_gate * inv_gate) * cross_sum[:, None] / DI
        )
        sigmoid_gate = jax.nn.sigmoid(gate_in)
        grad_scanned = grad_gated * gate_in * sigmoid_gate
        grad_gate_in = grad_gated * scanned * sigmoid_gate * (1.0 + gate_in * (1.0 - sigmoid_gate))
        grad_value_conv, grad_state_conv, grad_step_in, grad_decay, grad_bias, grad_skip = (
            pull_scan(to_seqs(grad_scanned))
        )
        grad_state_sum = lax.psum(grad_state_conv.astype(jnp.bfloat16), "tensor").astype(
            jnp.float32
        )
        grad_value_in, grad_taps_value = pull_value(grad_value_conv)
        grad_state_in = pull_state(grad_state_sum)[0]
        grad_taps_state = pull_state(grad_state_conv)[1]
        low_gate_value = jnp.stack([grad_gate_in, grad_value_in.reshape(-1, width_local)]).astype(
            jnp.bfloat16
        )
        low_state = grad_state_in.reshape(-1, 2 * N).astype(jnp.bfloat16)
        low_step = grad_step_in.reshape(-1, heads_local).astype(jnp.bfloat16)
        grad_gate_value_weight = jnp.einsum(
            "fd,kfc->kdc", normed_all, low_gate_value, preferred_element_type=jnp.float32
        )
        grad_state_weight = dot_first(normed_all, low_state)
        grad_step_weight = dot_first(normed_all, low_step)
        partial_sum = jnp.einsum(
            "kfc,kdc->fd", low_gate_value, gate_value_full, preferred_element_type=jnp.float32
        )
        grad_normed = lax.psum_scatter(
            (partial_sum + dot_last(low_step, step_full)).astype(jnp.bfloat16),
            "tensor",
            scatter_dimension=0,
            tiled=True,
        ).astype(jnp.float32)
        own_state = lax.dynamic_slice_in_dim(low_state, row_start, local_rows, 0)
        grad_normed = grad_normed + dot_last(own_state, state_full)
        unit_rows = hidden * inv_rows
        grads_pre.append(jnp.sum(grad_normed * unit_rows, axis=0))
        grad_unit = grad_normed * pre_gain[layer_index]
        grad_flow = grad_mix + inv_rows * (
            grad_unit - unit_rows * jnp.mean(grad_unit * unit_rows, axis=-1, keepdims=True)
        )
        scattered = (
            lax.psum_scatter(
                grad_gate_value_weight.astype(jnp.bfloat16), "dp", scatter_dimension=1, tiled=True
            ).astype(jnp.float32),
            lax.psum_scatter(
                grad_state_weight.astype(jnp.bfloat16), "dp", scatter_dimension=0, tiled=True
            ).astype(jnp.float32),
            lax.psum_scatter(
                grad_step_weight.astype(jnp.bfloat16), "dp", scatter_dimension=0, tiled=True
            ).astype(jnp.float32),
            lax.psum_scatter(
                grad_out_weight.astype(jnp.bfloat16), "dp", scatter_dimension=1, tiled=True
            ).astype(jnp.float32),
        )
        grads_gate_value.append(scattered[0])
        grads_state.append(scattered[1])
        grads_step.append(scattered[2])
        grads_out.append(scattered[3])
        taps_full = jnp.zeros((KCONV + 1, DI + 2 * N), jnp.float32)
        taps_full = lax.dynamic_update_slice(
            taps_full, grad_taps_value, (0, tensor_index * width_local)
        )
        taps_full = lax.dynamic_update_slice(taps_full, grad_taps_state, (0, DI))
        grads_taps.append(taps_full)
        head_start = tensor_index * heads_local
        grads_decay.append(
            lax.dynamic_update_slice(jnp.zeros((H,), jnp.float32), grad_decay, (head_start,))
        )
        grads_bias.append(
            lax.dynamic_update_slice(jnp.zeros((H,), jnp.float32), grad_bias, (head_start,))
        )
        grads_skip.append(
            lax.dynamic_update_slice(jnp.zeros((H,), jnp.float32), grad_skip, (head_start,))
        )
        grads_gain.append(
            lax.dynamic_update_slice(
                jnp.zeros((DI,), jnp.float32), grad_gain_local, (tensor_index * width_local,)
            )
        )
    small_sums = lax.psum(
        (
            jnp.stack(grads_pre[::-1]),
            jnp.stack(grads_taps[::-1]),
            jnp.stack(grads_decay[::-1]),
            jnp.stack(grads_bias[::-1]),
            jnp.stack(grads_skip[::-1]),
            jnp.stack(grads_gain[::-1]),
        ),
        ("dp", "tensor"),
    )
    return (
        out_hidden,
        grad_flow,
        jnp.stack(grads_gate_value[::-1]),
        jnp.stack(grads_state[::-1]),
        jnp.stack(grads_step[::-1]),
        jnp.stack(grads_out[::-1]),
        small_sums[0],
        small_sums[1],
        small_sums[2],
        small_sums[3],
        small_sums[4],
        small_sums[5],
    )


def solution(mesh):
    in_specs = (
        P(("dp", "tensor"), None),
        P(("dp", "tensor"), None),
        P("dp"),
        P(None, None, "dp", "tensor"),
        P(None, "dp", None),
        P(None, "dp", "tensor"),
        P(None, "tensor", "dp"),
        P(),
        P(),
        P(),
        P(),
        P(),
        P(),
    )
    out_specs = (
        P(("dp", "tensor"), None),
        P(("dp", "tensor"), None),
        P(None, None, "dp", "tensor"),
        P(None, "dp", None),
        P(None, "dp", "tensor"),
        P(None, "tensor", "dp"),
        P(),
        P(),
        P(),
        P(),
        P(),
        P(),
    )
    return jax.shard_map(
        per_device, mesh=mesh, in_specs=in_specs, out_specs=out_specs, check_vma=False
    )
```

profile of v0, /device:TPU:0, one launch (start us, length us, event | category | flops | bytes accessed | tf_op | source)
XLA Modules:
  0.0 2567.4 jit_solution(5405733779004939801)
XLA Ops:
  15.4 25.4 all-gather.2
  41.1 19.6 all-gather
  70.3 74.9 %all-gather.25.cloned.1.call-done = bf16[1,2,1536,1536]{3,2,1,0:T(8,128)(2,1)} async-done(((bf16[1,2,96,1536]{3,2,1,0:T(8,128)(2,1)}), bf16[1,2,1536,1536]{3,2,1,0:T(8,128)(2,1)}) %all-gather.25.cloned.1.call-update) | async-done | bytes 9437200 | tf_op jit(solution)/shard_map/all_gather | solution.py:145
  214.2 95.0 %while.88 = (s32[]{:T(128)}, f32[1,24,64,128]{3,2,1,0:T(8,128)S(1)}, f32[4,1,256,24,64]{2,4,3,1,0:T(8,128)}, f32[4,1,24,64,128]{4,3,2,1,0:T(8,128)}, f32[4,1,256...) while((s32[]{:T(128)}, ...), condition=%wide.region_4.6_spmd.clone.clone, body=%wide.region_1.5_spmd.clone.clone.sunk | while | flops 2527414272 | bytes 13679193 | solution.py:67
  382.7 73.9 %reduce-scatter.15.cloned.1.call-done = f32[512,1536]{1,0:T(8,128)} async-done(((f32[1024,1536]{1,0:T(8,128)}), f32[512,1536]{1,0:T(8,128)}) %reduce-scatter.15.cloned.1.call-update) | async-done | bytes 3145744 | tf_op jit(solution)/shard_map/reduce_scatter | solution.py:184
  464.7 28.2 %all-gather.4 = bf16[1,1536,24]{2,0,1:T(2,128)(2,1)S(1)} all-gather(bf16[1,96,24]{2,0,1:T(2,128)(2,1)S(1)} %copy.555), channel_id=6, replica_groups=mesh['dp'=16,'tensor'=2] {'dp'}, dimensions={1}, use_global_device_ids=true | all-gather | bytes 78336 | tf_op jit(solution)/shard_map/all_gather | solution.py:147
  494.5 22.4 all-gather.6
  517.1 29.8 %all-gather.29.cloned.1.call-done = bf16[1,2,1536,1536]{3,2,1,0:T(8,128)(2,1)} async-done(((bf16[1,2,96,1536]{3,2,1,0:T(8,128)(2,1)}), bf16[1,2,1536,1536]{3,2,1,0:T(8,128)(2,1)}) %all-gather.29.cloned.1.call-update) | async-done | bytes 9437200 | tf_op jit(solution)/shard_map/all_gather | solution.py:145
  546.9 46.7 %all-gather.19.cloned.1.call-done = bf16[1024,1536]{1,0:T(8,128)(2,1)} async-done(((bf16[512,1536]{1,0:T(8,128)(2,1)}), bf16[1024,1536]{1,0:T(8,128)(2,1)}) %all-gather.19.cloned.1.call-update) | async-done | bytes 3145744 | tf_op jit(solution)/shard_map/all_gather | solution.py:153
  668.4 83.5 %while.89 = (s32[]{:T(128)}, f32[1,24,64,128]{3,2,1,0:T(8,128)S(1)}, f32[4,1,256,24,64]{2,4,3,1,0:T(8,128)}, f32[4,1,24,64,128]{4,3,2,1,0:T(8,128)}, f32[4,1,256...) while((s32[]{:T(128)}, ...), condition=%wide.region_12.14_spmd.clone.clone, body=%wide.region_9.13_spmd.clone.clone.sunk | while | flops 2527414272 | bytes 13679193 | solution.py:67
  868.3 222.5 %while.86 = (s32[]{:T(128)}, f32[24]{0:T(128)}, f32[1,24,64,128]{3,2,1,0:T(8,128)}, f32[4,1,256,24,64]{2,4,3,1,0:T(8,128)}, f32[4,1,256,24]{2,0,3,1:T(4,128)}, /...) while((s32[]{:T(128)}, f32[24]{0:T(128)}, ...), condition=%wide.region_31.33_spmd.clone, body=%wide.region_18.32_spmd.clone.sunk | while | flops 5775548416 | bytes 40402288 | solution.py:67
  1182.2 32.0 %reduce-scatter.19.cloned.1.call-done = bf16[512,1536]{1,0:T(8,128)(2,1)} async-done(((bf16[1024,1536]{1,0:T(8,128)(2,1)}), bf16[512,1536]{1,0:T(8,128)(2,1)}) %reduce-scatter.19.cloned.1.call-update) | async-done | bytes 1572880 | tf_op jit(solution)/shard_map/reduce_scatter | solution.py:272
  1219.2 74.4 %reduce-scatter.17.cloned.1.call-done = f32[512,1536]{1,0:T(8,128)} async-done(((f32[1024,1536]{1,0:T(8,128)}), f32[512,1536]{1,0:T(8,128)}) %reduce-scatter.17.cloned.1.call-update) | async-done | bytes 3145744 | tf_op jit(solution)/shard_map/reduce_scatter | solution.py:184
  1299.8 45.0 %all-gather.23.cloned.1.call-done = bf16[1024,1536]{1,0:T(8,128)(2,1)} async-done(((bf16[512,1536]{1,0:T(8,128)(2,1)}), bf16[1024,1536]{1,0:T(8,128)(2,1)}) %all-gather.23.cloned.1.call-update) | async-done | bytes 3145744 | tf_op jit(solution)/shard_map/all_gather | solution.py:237
  1404.1 222.7 %while.87 = (s32[]{:T(128)}, f32[24]{0:T(128)}, f32[1,24,64,128]{3,2,1,0:T(8,128)}, f32[4,1,256,24,64]{2,4,3,1,0:T(8,128)}, f32[4,1,256,24]{2,0,3,1:T(4,128)}, /...) while((s32[]{:T(128)}, f32[24]{0:T(128)}, ...), condition=%wide.region_50.52_spmd.clone, body=%wide.region_37.51_spmd.clone.sunk | while | flops 5775548416 | bytes 40402288 | solution.py:67
  1749.9 24.0 copy.505
  1789.0 24.0 copy.503
  1835.5 59.6 %reduce-scatter.23.cloned.1.call-done = bf16[96,256]{1,0:T(8,128)(2,1)} async-done(((bf16[1536,256]{1,0:T(8,128)(2,1)}), bf16[96,256]{1,0:T(8,128)(2,1)}) %reduce-scatter.23.cloned.1.call-update) | async-done | bytes 49168 | tf_op jit(solution)/shard_map/reduce_scatter | solution.py:290
  1896.5 43.1 %reduce-scatter.21.cloned.1.call-done = bf16[512,1536]{1,0:T(8,128)(2,1)} async-done(((bf16[1024,1536]{1,0:T(8,128)(2,1)}), bf16[512,1536]{1,0:T(8,128)(2,1)}) %reduce-scatter.21.cloned.1.call-update) | async-done | bytes 1572880 | tf_op jit(solution)/shard_map/reduce_scatter | solution.py:272
  1945.8 41.5 %all-reduce.50 = (f32[2,1536]{1,0:T(2,128)}, f32[2,48]{1,0:T(2,128)}, f32[2,48]{1,0:T(2,128)}, f32[2,48]{1,0:T(2,128)}, f32[2,3072]{1,0:T(2,128)}) all-reduce(f32[2,1536]{1,0:T(2,128)S(1)} %pad_maximum_fusion.8, f32[2,48]{1,0:T(2,128)S(1)} %pad_maximum_fusion.9, ...), channel_id=1, replica_groups=mesh['dp'=16,'tensor'=2] {'dp','tensor'}, use_global_device_ids=true, to_apply=%region_64.66 | all-reduce | flops 9504 | bytes 76032 | tf_op jit(solution)/shard_map/psum | solution.py:325
  1987.3 32.4 %reduce-scatter.29.cloned.1.call-done = bf16[1536,96]{0,1:T(8,128)(2,1)} async-done(((bf16[1536,1536]{0,1:T(8,128)(2,1)}), bf16[1536,96]{0,1:T(8,128)(2,1)}) %reduce-scatter.29.cloned.1.call-update) | async-done | bytes 294928 | tf_op jit(solution)/shard_map/reduce_scatter | solution.py:296
  2019.7 78.8 %reduce-scatter.27.cloned.1.call-done = bf16[1536,96]{0,1:T(8,128)(2,1)} async-done(((bf16[1536,1536]{0,1:T(8,128)(2,1)}), bf16[1536,96]{0,1:T(8,128)(2,1)}) %reduce-scatter.27.cloned.1.call-update) | async-done | bytes 294928 | tf_op jit(solution)/shard_map/reduce_scatter | solution.py:296
  2100.6 330.9 %all-reduce.63.cloned.1.call-done = (bf16[2,1536,1536]{2,0,1:T(2,128)(2,1)}, bf16[2,1536,1536]{2,0,1:T(2,128)(2,1)}) async-done(((bf16[2,1536,1536]{2,0,1:T(2,128)(2,1)}, bf16[2,1536,1536]{2,0,1:T(2,128)(2,1)}), (bf16[2,1536,1536]{2,0,1:T(2,128)(2,1)}, bf16[2,1536,1536]{2,0,1:T(2,128)(2,1)})) %all-reduce.63.cloned.1.call-update) | async-done | bytes 18874384
  2437.9 121.0 %all-reduce.61.cloned.1.call-done = f32[2,5,3328]{2,0,1:T(2,128)} async-done(((f32[2,5,3328]{2,0,1:T(2,128)}), f32[2,5,3328]{2,0,1:T(2,128)}) %all-reduce.61.cloned.1.call-update) | async-done | bytes 133136 | tf_op jit(solution)/shard_map/psum | solution.py:325
  (1165 shorter events, 1306.6 us)
Async XLA Ops:
  7.2 55.1 %all-gather.17.cloned.1.call-start = ((), (), s32[]{:S(2)}) async-start(), calls=%async_computation.10 | async-start | bytes 4718592 | tf_op jit(solution)/shard_map/all_gather | solution.py:153
  8.2 452.5 %copy-start.40 = (f32[1536]{0:T(1024)}, f32[1536]{0:T(1024)S(1)}, u32[]{:S(2)}) copy-start(f32[1536]{0:T(1024)S(1)} %get-tuple-element.1544) | copy-start | bytes 18436
  13.1 132.1 %all-gather.25.cloned.1.call-start = ((), (), s32[]{:S(2)}) async-start(), calls=%async_computation.25 | async-start | bytes 10027008 | tf_op jit(solution)/shard_map/all_gather | solution.py:145
  14.2 356.2 %all-gather.27.cloned.1.call-start = ((), (), s32[]{:S(2)}) async-start(), calls=%async_computation.26 | async-start | bytes 5013504 | tf_op jit(solution)/shard_map/all_gather | solution.py:148
  15.2 441.4 %reduce-scatter.15.cloned.1.call-start = ((), (), s32[]{:S(2)}) async-start(), calls=%async_computation.11 | async-start | bytes 9437184 | tf_op jit(solution)/shard_map/reduce_scatter | solution.py:184
  61.2 432.7 %copy-start.117 = (f32[1,48]{1,0:T(1,128)}, f32[1,48]{1,0:T(1,128)S(1)}, u32[]{:S(2)}) copy-start(f32[1,48]{1,0:T(1,128)S(1)} %get-tuple-element.1775) | copy-start | bytes 580
  381.1 165.8 %all-gather.29.cloned.1.call-start = ((), (), s32[]{:S(2)}) async-start(), calls=%async_computation.27 | async-start | bytes 10027008 | tf_op jit(solution)/shard_map/all_gather | solution.py:145
  381.6 211.9 %all-gather.19.cloned.1.call-start = ((), (), s32[]{:S(2)}) async-start(), calls=%async_computation.12 | async-start | bytes 4718592 | tf_op jit(solution)/shard_map/all_gather | solution.py:153
  463.8 339.2 %all-gather.31.cloned.1.call-start = ((), (), s32[]{:S(2)}) async-start(), calls=%async_computation.28 | async-start | bytes 5013504 | tf_op jit(solution)/shard_map/all_gather | solution.py:148
  464.5 338.4 %all-gather.21.cloned.1.call-start = ((), (), s32[]{:S(2)}) async-start(), calls=%async_computation.14 | async-start | bytes 4718592 | tf_op jit(solution)/shard_map/all_gather | solution.py:237
  517.0 661.4 %all-reduce.57.cloned.1.call-start = ((), (), s32[]{:S(2)}) async-start(), calls=%async_computation.16 | async-start | bytes 1048576 | tf_op jit(solution)/shard_map/psum | solution.py:253
  1139.8 74.3 %reduce-scatter.19.cloned.1.call-start = ((), (), s32[]{:S(2)}) async-start(), calls=%async_computation.15 | async-start | bytes 4718592 | tf_op jit(solution)/shard_map/reduce_scatter | solution.py:272
  1167.3 126.4 %reduce-scatter.17.cloned.1.call-start = ((), (), s32[]{:S(2)}) async-start(), calls=%async_computation.13 | async-start | bytes 9437184 | tf_op jit(solution)/shard_map/reduce_scatter | solution.py:184
  1178.1 166.7 %all-gather.23.cloned.1.call-start = ((), (), s32[]{:S(2)}) async-start(), calls=%async_computation.17 | async-start | bytes 4718592 | tf_op jit(solution)/shard_map/all_gather | solution.py:237
  1299.7 390.1 %all-reduce.59.cloned.1.call-start = ((), (), s32[]{:S(2)}) async-start(), calls=%async_computation.19 | async-start | bytes 1048576 | tf_op jit(solution)/shard_map/psum | solution.py:253
  1630.0 189.8 %reduce-scatter.33.cloned.1.call-start = ((), (), s32[]{:S(2)}) async-start(), calls=%async_computation.30 | async-start | bytes 417792
  1633.4 197.9 %reduce-scatter.31.cloned.1.call-start = ((), (), s32[]{:S(2)}) async-start(), calls=%async_computation.29 | async-start | bytes 417792
  1635.8 199.7 %reduce-scatter.25.cloned.1.call-start = ((), (), s32[]{:S(2)}) async-start(), calls=%async_computation.21 | async-start | bytes 835584 | tf_op jit(solution)/shard_map/reduce_scatter | solution.py:290
  1639.8 255.2 %reduce-scatter.23.cloned.1.call-start = ((), (), s32[]{:S(2)}) async-start(), calls=%async_computation.20 | async-start | bytes 835584 | tf_op jit(solution)/shard_map/reduce_scatter | solution.py:290
  1694.9 244.7 %reduce-scatter.21.cloned.1.call-start = ((), (), s32[]{:S(2)}) async-start(), calls=%async_computation.18 | async-start | bytes 4718592 | tf_op jit(solution)/shard_map/reduce_scatter | solution.py:272
  1712.4 307.3 %reduce-scatter.29.cloned.1.call-start = ((), (), s32[]{:S(2)}) async-start(), calls=%async_computation.23 | async-start | bytes 5013504 | tf_op jit(solution)/shard_map/reduce_scatter | solution.py:296
  1723.1 375.4 %reduce-scatter.27.cloned.1.call-start = ((), (), s32[]{:S(2)}) async-start(), calls=%async_computation.22 | async-start | bytes 5013504 | tf_op jit(solution)/shard_map/reduce_scatter | solution.py:296
  1733.9 697.6 %all-reduce.63.cloned.1.call-start = ((), (), s32[]{:S(2)}) async-start(), calls=%async_computation.31 | async-start | bytes 37748736
  1813.2 745.7 %all-reduce.61.cloned.1.call-start = ((), (), s32[]{:S(2)}) async-start(), calls=%async_computation.24 | async-start | bytes 266240 | tf_op jit(solution)/shard_map/psum | solution.py:325
  (168 other events, 5940.3 us)
Sparse Core Ops, SparseCore 0:
  13.2 47.6 all-gather.16
  63.7 81.4 all-gather.24
  148.1 51.5 all-gather.26
  381.2 75.3 reduce-scatter.14
  458.9 87.8 all-gather.28
  548.3 45.2 all-gather.18
  596.1 53.3 all-gather.30
  651.7 43.4 all-gather.20
  1139.9 28.6 all-reduce.56
  1170.7 43.3 reduce-scatter.18
  1216.5 77.0 reduce-scatter.16
  1299.8 44.9 all-gather.22
  1630.1 28.5 all-reduce.58
  1662.5 55.5 reduce-scatter.32
  1721.5 54.5 reduce-scatter.30
  1779.9 55.5 reduce-scatter.24
  1839.5 55.5 reduce-scatter.22
  1897.2 42.3 reduce-scatter.20
  1943.5 76.1 reduce-scatter.28
  2023.9 74.5 reduce-scatter.26
  2102.6 328.9 all-reduce.62
  2438.6 120.2 all-reduce.60
where the time goes:
time: 2590 us; the launch traced here: 2570 us
  waiting for transfers between devices  1050 us (41%)
  matrix products  615 us (24%)
  local copies, waits for them, and re-layouts  428 us (17%)
  other arithmetic  287 us (11%)
  blocking collectives  157 us (6%)
    dot_general x80, matrix products, exact_einsum(): return jnp.einsum(pattern, *operands, precision=lax.Precision.HIGHEST)  392 us
    unnamed x25, waiting for transfers between devices  332 us
    reduce_scatter x2, waiting for transfers between devices, per_device(): lax.psum_scatter(jnp.dot(gate_norm, out_full, preferred_element_type=jnp....  148 us
    psum x1, waiting for transfers between devices, per_device(): lax.psum((jnp.stack(grads_pre[::-1]), jnp.stack(grads_taps[::-1]), jnp.st...  121 us
    reduce_scatter x2, waiting for transfers between devices, per_device(): lax.psum_scatter(grad_out_weight.astype(jnp.bfloat16), 'dp', scatter_dime...  111 us
    all_gather x2, waiting for transfers between devices, per_device(): lax.all_gather(gate_value_weight[layer_index], 'dp', axis=1, tiled=True)  105 us
    reduce_scatter x2, waiting for transfers between devices, per_device(): lax.psum_scatter((partial_sum + dot_last(low_step, step_full)).astype(jnp...  75.1 us
    reduce_scatter x2, waiting for transfers between devices, per_device(): lax.psum_scatter(grad_state_weight.astype(jnp.bfloat16), 'dp', scatter_di...  61.6 us
  transfers between devices with their start and end apart: 22, of which 14 were waited for; matrix products, arithmetic and copies ran while one was open for 27% of the time, Pallas kernels for 0%

commit v1 on v0

v1 whole, which is shorter than its diff:
```python
import functools
import jax
import jax.numpy as jnp
from jax import lax
from jax.experimental import pallas as pl
from jax.experimental.pallas import tpu as pltpu
from jax.sharding import PartitionSpec as P

HEAD = 64
N = 128
KCONV = 4
PAIR = 2 * HEAD
SIDE = 2 * N + 128
F32 = jnp.float32
BF16 = jnp.bfloat16


def dot_nn(a, b):
    return lax.dot_general(a, b, (((1,), (0,)), ((), ())), preferred_element_type=F32)


def dot_nt(a, b):
    return lax.dot_general(a, b, (((1,), (1,)), ((), ())), preferred_element_type=F32)


def dot_tn(a, b):
    return lax.dot_general(a, b, (((0,), (0,)), ((), ())), preferred_element_type=F32)


def exact_nn(a, b):
    return lax.dot_general(
        a, b, (((1,), (0,)), ((), ())), precision=lax.Precision.HIGHEST, preferred_element_type=F32
    )


def softplus(a):
    return jnp.maximum(a, 0.0) + jnp.log1p(jnp.exp(-jnp.abs(a)))


def sigmoid(a):
    return 1.0 / (1.0 + jnp.exp(-a))


def iota(shape, dim):
    return lax.broadcasted_iota(jnp.int32, shape, dim)


def stacked(values, low_half):
    zero = jnp.zeros_like(values)
    return jnp.concatenate([jnp.where(low_half, values, zero), jnp.where(low_half, zero, values)], 0)


def block_prep(side, headp_ref, q):
    step = softplus(side + headp_ref[0:1, :])
    lower = (iota((q, q), 0) >= iota((q, q), 1)).astype(F32)
    running = exact_nn(lower, step * headp_ref[1:2, :])
    return step, running


def forward_kernel(
    gate_ref, value_ref, normed_ref, side_weight_ref, chan_ref, state_taps_ref, headp_ref,
    gnl_ref, scanned_ref, pre_ref, side_ref, states_ref, square_ref,
    state, vbuf, sbuf, step_s, run_s, runt_s, cb_s, bmat, bmat_t, cmat,
):
    q, width = gate_ref.shape
    step_index = pl.program_id(0)

    @pl.when(step_index == 0)
    def _():
        state[...] = jnp.zeros_like(state)
        vbuf[0:8, :] = jnp.zeros((8, width), F32)
        sbuf[0:8, :] = jnp.zeros((8, 2 * N), F32)

    @pl.when(step_index > 0)
    def _():
        vbuf[0:8, :] = vbuf[q : q + 8, :]
        sbuf[0:8, :] = sbuf[q : q + 8, :]

    side = dot_nn(normed_ref[...], side_weight_ref[...])
    side_ref[:, 0:SIDE] = side
    sbuf[8 : q + 8, :] = side[:, 0 : 2 * N]
    pre_state = state_taps_ref[4:5, :] + state_taps_ref[3:4, :] * sbuf[8 : q + 8, :]
    for k in range(KCONV - 1):
        pre_state = pre_state + state_taps_ref[k : k + 1, :] * sbuf[5 + k : 5 + k + q, :]
    side_ref[:, SIDE : SIDE + 2 * N] = pre_state
    conv_state = (pre_state * sigmoid(pre_state)).astype(BF16)
    bmat[...] = conv_state[:, 0:N]
    cmat[...] = conv_state[:, N : 2 * N]
    bmat_t[...] = conv_state[:, 0:N].T
    cb_s[...] = dot_nt(conv_state[:, N : 2 * N], conv_state[:, 0:N])
    step, running = block_prep(side[:, 2 * N :], headp_ref, q)
    step_s[...] = step
    run_s[...] = running
    runt_s[...] = running.T
    square_ref[...] = jnp.zeros_like(square_ref)
    causal = iota((q, q), 0) >= iota((q, q), 1)
    low_half = iota((1, PAIR), 1) < HEAD

    def one_pair(p, _):
        lanes = pl.ds(pl.multiple_of(p * PAIR, PAIR), PAIR)
        vbuf[8 : q + 8, lanes] = value_ref[:, lanes].astype(F32)
        pre = chan_ref[4:5, lanes] + chan_ref[3:4, lanes] * vbuf[8 : q + 8, lanes]
        for k in range(KCONV - 1):
            pre = pre + chan_ref[k : k + 1, lanes] * vbuf[5 + k : 5 + k + q, lanes]
        pre_ref[:, lanes] = pre.astype(BF16)
        x = pre * sigmoid(pre)
        turn = lax.rem(128 - 2 * p, 128)
        run_two = pltpu.roll(run_s[...], turn, 1)
        step_two = pltpu.roll(step_s[...], turn, 1)
        run_a, run_b = run_two[:, 0:1], run_two[:, 1:2]
        run_pair = jnp.where(low_half, run_a, run_b)
        u = x * jnp.where(low_half, step_two[:, 0:1], step_two[:, 1:2])
        cb = cb_s[...]
        table_a = jnp.where(causal, jnp.exp(run_a - runt_s[pl.ds(2 * p, 1), :]), 0.0)
        table_b = jnp.where(causal, jnp.exp(run_b - runt_s[pl.ds(2 * p + 1, 1), :]), 0.0)
        mixing = jnp.concatenate([(table_a * cb).astype(BF16), (table_b * cb).astype(BF16)], 1)
        within = dot_nn(mixing, stacked(u.astype(BF16), low_half))
        start = state[:, lanes]
        start_low = start.astype(BF16)
        states_ref[0, :, lanes] = start_low
        y = within + dot_nn(cmat[...], start_low) * jnp.exp(run_pair)
        last = run_pair[q - 1 : q, :]
        tail = (u * jnp.exp(last - run_pair)).astype(BF16)
        state[:, lanes] = start * jnp.exp(last) + dot_nn(bmat_t[...], tail)
        scanned = y + chan_ref[5:6, lanes] * x
        scanned_ref[:, lanes] = scanned.astype(BF16)
        gate = gate_ref[:, lanes].astype(F32)
        gated = scanned * (gate * sigmoid(gate))
        gnl_ref[:, lanes] = (gated * chan_ref[6:7, lanes]).astype(BF16)
        square_ref[...] += gated * gated
        return 0

    lax.fori_loop(0, width // PAIR, one_pair, 0)


def backward_kernel(
    channels, gate_ref, value_ref, pre_ref, scanned_ref, dgn_ref, side_ref, states_ref, rows_ref,
    chan_ref, state_taps_ref, headp_ref,
    low_ref, dchan_ref, dstate_ref, dhead_ref,
    lam, gbuf, gsbuf, step_s, run_s, runt_s, cbt_s, bmat, cmat, cmat_t,
    dcbt, db, dc, col_s, rowt_s, xdu_s, e_s, g_s, klan, spread,
):
    q, width = gate_ref.shape
    step_index = pl.program_id(0)

    @pl.when(step_index == 0)
    def _():
        lam[...] = jnp.zeros_like(lam)
        gbuf[q : q + 8, :] = jnp.zeros((8, width), F32)
        gsbuf[q : q + 8, :] = jnp.zeros((8, 2 * N), F32)
        dchan_ref[...] = jnp.zeros_like(dchan_ref)
        dstate_ref[...] = jnp.zeros_like(dstate_ref)
        dhead_ref[...] = jnp.zeros_like(dhead_ref)
        rowt_s[...] = jnp.zeros_like(rowt_s)
        spread[...] = ((iota((width, 128), 0) // HEAD) == iota((width, 128), 1)).astype(BF16)

    @pl.when(step_index > 0)
    def _():
        gbuf[q : q + 8, :] = gbuf[0:8, :]
        gsbuf[q : q + 8, :] = gsbuf[0:8, :]

    pre_state = side_ref[:, SIDE : SIDE + 2 * N]
    sig_state = sigmoid(pre_state)
    conv_state = (pre_state * sig_state).astype(BF16)
    bmat[...] = conv_state[:, 0:N]
    cmat[...] = conv_state[:, N : 2 * N]
    cmat_t[...] = conv_state[:, N : 2 * N].T
    cbt_s[...] = dot_nt(conv_state[:, 0:N], conv_state[:, N : 2 * N])
    step, running = block_prep(side_ref[:, 2 * N : SIDE], headp_ref, q)
    step_s[...] = step
    run_s[...] = running
    runt_s[...] = running.T
    dcbt[...] = jnp.zeros_like(dcbt)
    db[...] = jnp.zeros_like(db)
    dc[...] = jnp.zeros_like(dc)
    col_s[...] = jnp.zeros_like(col_s)
    causal_t = iota((q, q), 1) >= iota((q, q), 0)
    low_half = iota((1, PAIR), 1) < HEAD
    head_lane = iota((1, 128), 1)

    def one_pair(p, _):
        lanes = pl.ds(pl.multiple_of(p * PAIR, PAIR), PAIR)
        inv = rows_ref[:, 0:1]
        pull = rows_ref[:, 1:2]
        gain = chan_ref[6:7, lanes]
        skip = chan_ref[5:6, lanes]
        gate = gate_ref[:, lanes].astype(F32)
        sig_gate = sigmoid(gate)
        silu_gate = gate * sig_gate
        scanned = scanned_ref[:, lanes].astype(F32)
        gated = scanned * silu_gate
        dgn = dgn_ref[:, lanes].astype(F32) * inv
        dgated = dgn * gain - gated * pull
        dchan_ref[6:7, lanes] += jnp.sum(dgn * gated, 0, keepdims=True)
        dy = dgated * silu_gate
        low_ref[:, lanes] = (
            dgated * scanned * (sig_gate + silu_gate * (1.0 - sig_gate))
        ).astype(BF16)
        pre = pre_ref[:, lanes].astype(F32)
        sig_pre = sigmoid(pre)
        x = pre * sig_pre
        dchan_ref[5:6, lanes] += jnp.sum(x * dy, 0, keepdims=True)
        turn = lax.rem(128 - 2 * p, 128)
        run_two = pltpu.roll(run_s[...], turn, 1)
        step_two = pltpu.roll(step_s[...], turn, 1)
        run_a, run_b = run_two[:, 0:1], run_two[:, 1:2]
        run_pair = jnp.where(low_half, run_a, run_b)
        step_pair = jnp.where(low_half, step_two[:, 0:1], step_two[:, 1:2])
        u = x * step_pair
        u_low = u.astype(BF16)
        dy_stack = stacked(dy.astype(BF16), low_half)
        products = dot_nt(u_low, dy_stack)
        cbt = cbt_s[...]
        table_a = jnp.where(causal_t, jnp.exp(runt_s[pl.ds(2 * p, 1), :] - run_a), 0.0)
        table_b = jnp.where(causal_t, jnp.exp(runt_s[pl.ds(2 * p + 1, 1), :] - run_b), 0.0)
        mix_a = table_a * cbt
        mix_b = table_b * cbt
        mixing = jnp.concatenate([mix_a.astype(BF16), mix_b.astype(BF16)], 1)
        prod_a = products[:, 0:q]
        prod_b = products[:, q : 2 * q]
        dcbt[...] += prod_a * table_a + prod_b * table_b
        flow_a = prod_a * mix_a
        flow_b = prod_b * mix_b
        rowt_s[pl.ds(2 * p, 1), :] = jnp.sum(flow_a, 0, keepdims=True)
        rowt_s[pl.ds(2 * p + 1, 1), :] = jnp.sum(flow_b, 0, keepdims=True)
        col_s[...] += jnp.where(
            head_lane == 2 * p, jnp.sum(flow_a, 1, keepdims=True), 0.0
        ) + jnp.where(head_lane == 2 * p + 1, jnp.sum(flow_b, 1, keepdims=True), 0.0)
        start_low = states_ref[0, :, lanes]
        lam_one = lam[:, lanes]
        lam_low = lam_one.astype(BF16)
        grow = jnp.exp(run_pair)
        last = run_pair[q - 1 : q, :]
        grow_last = jnp.exp(last)
        fade = jnp.exp(last - run_pair)
        from_state = dot_nn(cmat[...], start_low) * grow
        e_s[:, lanes] = (dy * from_state).astype(BF16)
        from_lam = dot_nn(bmat[...], lam_low) * fade
        g_s[:, lanes] = (u * from_lam).astype(BF16)
        du = dot_nn(mixing, dy_stack) + from_lam
        dy_grow = (dy * grow).astype(BF16)
        dc[...] += dot_nt(dy_grow, start_low)
        db[...] += dot_nt((u * fade).astype(BF16), lam_low)
        klan[:, lanes] = jnp.sum(lam_one * start_low.astype(F32), 0, keepdims=True) * grow_last
        lam[:, lanes] = lam_one * grow_last + dot_nn(cmat_t[...], dy_grow)
        xdu_s[:, lanes] = (x * du).astype(BF16)
        gp = (du * step_pair + skip * dy) * (sig_pre * (1.0 + pre * (1.0 - sig_pre)))
        gbuf[0:q, lanes] = gp
        value = value_ref[:, lanes].astype(F32)
        dv = chan_ref[3:4, lanes] * gp
        dchan_ref[3:4, lanes] += jnp.sum(value * gp, 0, keepdims=True)
        dchan_ref[4:5, lanes] += jnp.sum(gp, 0, keepdims=True)
        for k in range(KCONV - 1):
            later = gbuf[3 - k : 3 - k + q, lanes]
            dv = dv + chan_ref[k : k + 1, lanes] * later
            dchan_ref[k : k + 1, lanes] += jnp.sum(value * later, 0, keepdims=True)
        low_ref[:, pl.ds(pl.multiple_of(width + p * PAIR, PAIR), PAIR)] = dv.astype(BF16)
        return 0

    lax.fori_loop(0, width // PAIR, one_pair, 0)

    dcbt_low = dcbt[...].astype(BF16)
    dconv = jnp.concatenate(
        [db[...] + dot_nn(dcbt_low, cmat[...]), dc[...] + dot_tn(dcbt_low, bmat[...])], 1
    )
    gp_state = dconv * (sig_state * (1.0 + pre_state * (1.0 - sig_state)))
    gsbuf[0:q, :] = gp_state
    state_in = side_ref[:, 0 : 2 * N]
    dstate = state_taps_ref[3:4, :] * gp_state
    dstate_ref[3:4, :] += jnp.sum(state_in * gp_state, 0, keepdims=True)
    dstate_ref[4:5, :] += jnp.sum(gp_state, 0, keepdims=True)
    for k in range(KCONV - 1):
        later = gsbuf[3 - k : 3 - k + q, :]
        dstate = dstate + state_taps_ref[k : k + 1, :] * later
        dstate_ref[k : k + 1, :] += jnp.sum(state_in * later, 0, keepdims=True)
    low_ref[:, 2 * width : 2 * width + 2 * N] = dstate.astype(BF16)

    heads = spread[...]
    direct = dot_nn(xdu_s[...], heads)
    from_start = dot_nn(e_s[...], heads)
    to_end = dot_nn(g_s[...], heads)
    across = exact_nn(jnp.broadcast_to(klan[...], (8, width)), heads.astype(F32))[0:1, :]
    upper = (iota((q, q), 0) <= iota((q, q), 1)).astype(F32)
    strict = (iota((q, q), 0) > iota((q, q), 1)).astype(F32)
    dlog = (
        exact_nn(upper, rowt_s[...].T - col_s[...] + from_start) + exact_nn(strict, to_end) + across
    )
    rate = headp_ref[1:2, :]
    dstep = direct + rate * dlog
    dstep_in = dstep * sigmoid(side_ref[:, 2 * N : SIDE] + headp_ref[0:1, :])
    low_ref[:, 2 * width + 2 * N :] = dstep_in.astype(BF16)
    dhead_ref[0:1, :] += jnp.sum(step * dlog, 0, keepdims=True) * rate
    dhead_ref[1:2, :] += jnp.sum(dstep_in, 0, keepdims=True)


def forward_mixer(projected, normed, packed, chan, state_taps, headp, q, width):
    rows, depth = normed.shape
    blocks = rows // q
    wide = lambda column: pl.BlockSpec((q, width), lambda i: (i, column))
    fixed = lambda shape: pl.BlockSpec(shape, lambda i: (0,) * len(shape))
    return pl.pallas_call(
        forward_kernel,
        grid=(blocks,),
        in_specs=[
            wide(0), wide(1),
            pl.BlockSpec((q, depth), lambda i: (i, 0)),
            pl.BlockSpec((depth, SIDE), lambda i: (0, 2 * width // SIDE)),
            fixed((8, width)), fixed((8, 2 * N)), fixed((8, 128)),
        ],
        out_specs=[
            wide(0), wide(0), wide(0),
            pl.BlockSpec((q, SIDE + 2 * N), lambda i: (i, 0)),
            pl.BlockSpec((1, N, width), lambda i: (i, 0, 0)),
            pl.BlockSpec((q, 128), lambda i: (i, 0)),
        ],
        out_shape=[
            jax.ShapeDtypeStruct((rows, width), BF16),
            jax.ShapeDtypeStruct((rows, width), BF16),
            jax.ShapeDtypeStruct((rows, width), BF16),
            jax.ShapeDtypeStruct((rows, SIDE + 2 * N), F32),
            jax.ShapeDtypeStruct((blocks, N, width), BF16),
            jax.ShapeDtypeStruct((rows, 128), F32),
        ],
        scratch_shapes=[
            pltpu.VMEM((N, width), F32), pltpu.VMEM((q + 8, width), F32), pltpu.VMEM((q + 8, 2 * N), F32),
            pltpu.VMEM((q, 128), F32), pltpu.VMEM((q, 128), F32), pltpu.VMEM((128, q), F32),
            pltpu.VMEM((q, q), F32), pltpu.VMEM((q, N), BF16), pltpu.VMEM((N, q), BF16),
            pltpu.VMEM((q, N), BF16),
        ],
        compiler_params=pltpu.CompilerParams(vmem_limit_bytes=48 << 20),
        name="forward_mixer",
    )(projected, projected, normed, packed, chan, state_taps, headp)


def backward_mixer(projected, pre, scanned, dgn, side, states, rows_in, chan, state_taps, headp, q, width):
    rows = pre.shape[0]
    blocks = rows // q
    back = lambda i: blocks - 1 - i
    wide = lambda column: pl.BlockSpec((q, width), lambda i: (back(i), column))
    fixed = lambda shape: pl.BlockSpec(shape, lambda i: (0,) * len(shape))
    return pl.pallas_call(
        functools.partial(backward_kernel, 0),
        grid=(blocks,),
        in_specs=[
            wide(0), wide(1), wide(0), wide(0), wide(0),
            pl.BlockSpec((q, SIDE + 2 * N), lambda i: (back(i), 0)),
            pl.BlockSpec((1, N, width), lambda i: (back(i), 0, 0)),
            pl.BlockSpec((q, 128), lambda i: (back(i), 0)),
            fixed((8, width)), fixed((8, 2 * N)), fixed((8, 128)),
        ],
        out_specs=[
            pl.BlockSpec((q, 2 * width + SIDE), lambda i: (back(i), 0)),
            fixed((8, width)), fixed((8, 2 * N)), fixed((8, 128)),
        ],
        out_shape=[
            jax.ShapeDtypeStruct((rows, 2 * width + SIDE), BF16),
            jax.ShapeDtypeStruct((8, width), F32),
            jax.ShapeDtypeStruct((8, 2 * N), F32),
            jax.ShapeDtypeStruct((8, 128), F32),
        ],
        scratch_shapes=[
            pltpu.VMEM((N, width), F32), pltpu.VMEM((q + 8, width), F32), pltpu.VMEM((q + 8, 2 * N), F32),
            pltpu.VMEM((q, 128), F32), pltpu.VMEM((q, 128), F32), pltpu.VMEM((128, q), F32),
            pltpu.VMEM((q, q), F32), pltpu.VMEM((q, N), BF16), pltpu.VMEM((q, N), BF16), pltpu.VMEM((N, q), BF16),
            pltpu.VMEM((q, q), F32), pltpu.VMEM((q, N), F32), pltpu.VMEM((q, N), F32),
            pltpu.VMEM((q, 128), F32), pltpu.VMEM((128, q), F32),
            pltpu.VMEM((q, width), BF16), pltpu.VMEM((q, width), BF16), pltpu.VMEM((q, width), BF16),
            pltpu.VMEM((1, width), F32), pltpu.VMEM((width, 128), BF16),
        ],
        compiler_params=pltpu.CompilerParams(vmem_limit_bytes=48 << 20),
        name="backward_mixer",
    )(projected, projected, pre, scanned, dgn, side, states, rows_in, chan, state_taps, headp)


LAYERS = 2
EPSILON = 1e-05
BLOCK = 256


def gather_rows(values):
    return lax.all_gather(values, "tensor", axis=0, tiled=True)


def scatter_rows(values):
    return lax.psum_scatter(values, "tensor", scatter_dimension=0, tiled=True)


def per_device(
    inner,
    hidden_in,
    cotangent,
    lengths,
    gate_value_weight,
    state_weight,
    step_weight,
    out_weight,
    pre_gain,
    conv_taps,
    decay_log,
    step_bias,
    skip_gain,
    norm_gain,
):
    tensor_index = lax.axis_index("tensor")
    local_rows = hidden_in.shape[0]
    width = gate_value_weight.shape[3]
    heads = step_weight.shape[2]
    head_start = tensor_index * heads
    lane_start = tensor_index * width
    row_start = tensor_index * local_rows
    seq_rows = local_rows * lax.axis_size("tensor")
    q = min(BLOCK, seq_rows)
    position = row_start + jnp.arange(local_rows)
    keep_rows = (position < lengths[0]).astype(F32)[:, None]

    def own(values):
        return lax.dynamic_slice_in_dim(values, row_start, local_rows, 0)

    def part(table, start, size, axis=0):
        return lax.dynamic_slice_in_dim(table, start, size, axis)

    projections, outputs = [], []
    for layer in range(LAYERS):
        shard = jnp.concatenate(
            [
                gate_value_weight[layer, 0],
                gate_value_weight[layer, 1],
                state_weight[layer],
                jnp.pad(step_weight[layer], ((0, 0), (0, 128 - heads))),
            ],
            axis=1,
        )
        projections.append(lax.all_gather(shard, "dp", axis=0, tiled=True))
        outputs.append(lax.all_gather(out_weight[layer].T, "dp", axis=0, tiled=True))

    tables = []
    for layer in range(LAYERS):
        taps = conv_taps[layer]
        chan = jnp.concatenate(
            [
                part(taps, lane_start, width, 1),
                jnp.repeat(part(skip_gain[layer], head_start, heads), HEAD)[None],
                part(norm_gain[layer], lane_start, width)[None],
                jnp.zeros((1, width), F32),
            ],
            axis=0,
        )
        state_taps = jnp.pad(taps[:, inner:], ((0, 8 - taps.shape[0]), (0, 0)))
        headp = jnp.pad(
            jnp.stack(
                [
                    part(step_bias[layer], head_start, heads),
                    -jnp.exp(part(decay_log[layer], head_start, heads)),
                ]
            ),
            ((0, 6), (0, 128 - heads)),
        )
        tables.append((chan, state_taps, headp))

    hidden = hidden_in.astype(F32)
    saved = []
    for layer in range(LAYERS):
        chan, state_taps, headp = tables[layer]
        inv_rows = lax.rsqrt(jnp.mean(hidden * hidden, axis=-1, keepdims=True) + EPSILON)
        normed = (hidden * inv_rows * pre_gain[layer]).astype(BF16)
        normed_all = gather_rows(normed)
        projected = dot_nn(normed_all, projections[layer][:, : 2 * width]).astype(BF16)
        gnl, scanned, pre, side, states, squares = forward_mixer(
            projected, normed_all, projections[layer], chan, state_taps, headp, q, width
        )
        square_sum = lax.psum(jnp.sum(squares, axis=-1), "tensor")
        inv_gate = lax.rsqrt(square_sum / inner + EPSILON)[:, None]
        mixed_raw = scatter_rows(dot_nt(gnl, outputs[layer]).astype(BF16)).astype(F32)
        saved.append(
            (hidden, inv_rows, normed_all, projected, gnl, scanned, pre, side, states, inv_gate, mixed_raw)
        )
        hidden = keep_rows * (hidden + mixed_raw * own(inv_gate))
    out_hidden = hidden

    grad_flow = cotangent.astype(F32)
    grads_projection, grads_output, small = [], [], []
    for layer in reversed(range(LAYERS)):
        chan, state_taps, headp = tables[layer]
        (hidden, inv_rows, normed_all, projected, gnl, scanned, pre, side, states, inv_gate, mixed_raw) = saved[layer]
        grad_mix = keep_rows * grad_flow
        mix_low = grad_mix.astype(BF16)
        mix_all = gather_rows(mix_low)
        cross = gather_rows(jnp.sum(mix_low.astype(F32) * mixed_raw, axis=-1, keepdims=True))
        rows_in = jnp.pad(
            jnp.concatenate([inv_gate, inv_gate * inv_gate * inv_gate * cross / inner], 1), ((0, 0), (0, 126))
        )
        dgn = dot_nn(mix_all, outputs[layer]).astype(BF16)
        scaled_mix = (mix_all.astype(F32) * inv_gate).astype(BF16)
        grad_output = dot_tn(scaled_mix, gnl).astype(BF16)
        grads_output.append(
            lax.psum_scatter(grad_output, "dp", scatter_dimension=0, tiled=True).astype(F32)
        )
        low, dchan, dstate, dhead = backward_mixer(
            projected, pre, scanned, dgn, side, states, rows_in, chan, state_taps, headp, q, width
        )
        grad_normed = scatter_rows(dot_nt(low, projections[layer]).astype(BF16)).astype(F32)
        grad_projection = dot_tn(normed_all, low).astype(BF16)
        grads_projection.append(
            lax.psum_scatter(grad_projection, "dp", scatter_dimension=0, tiled=True).astype(F32)
        )
        unit_rows = hidden * inv_rows
        grad_pre = jnp.sum(grad_normed * unit_rows, axis=0)
        grad_unit = grad_normed * pre_gain[layer]
        grad_flow = grad_mix + inv_rows * (
            grad_unit - unit_rows * jnp.mean(grad_unit * unit_rows, axis=-1, keepdims=True)
        )
        small.append((grad_pre, dchan, dstate, dhead))

    count = KCONV + 1
    pieces = []
    for layer in range(LAYERS):
        grad_pre, dchan, dstate, dhead = small[LAYERS - 1 - layer]

        def placed(values, total, start):
            full = jnp.zeros(values.shape[:-1] + (total,), F32)
            return lax.dynamic_update_slice_in_dim(full, values, start, values.ndim - 1)

        lanes = placed(dchan, inner, lane_start)
        skips = dchan[5].reshape(heads, HEAD).sum(axis=1)
        per_head = placed(
            jnp.stack([dhead[0, :heads], dhead[1, :heads], skips]),
            lax.axis_size("tensor") * heads,
            head_start,
        )
        pieces += [
            grad_pre,
            lanes[:count].reshape(-1),
            lanes[6],
            dstate[:count].reshape(-1),
            per_head.reshape(-1),
        ]
    flat = jnp.concatenate(pieces)
    flat = jnp.pad(flat, (0, -flat.shape[0] % 1024)).reshape(-1, 128)
    flat = lax.psum(flat, ("dp", "tensor")).reshape(-1)
    cut = [0]

    def take(*shape):
        size = 1
        for extent in shape:
            size *= extent
        cut[0] += size
        return flat[cut[0] - size : cut[0]].reshape(shape)

    all_heads = lax.axis_size("tensor") * heads
    sums = []
    for layer in range(LAYERS):
        g_pre, g_lanes, g_gain = take(hidden.shape[1]), take(count, inner), take(inner)
        g_state, g_heads = take(count, 2 * N), take(3, all_heads)
        sums.append((g_pre, jnp.concatenate([g_lanes, g_state], 1), g_heads[0], g_heads[1], g_heads[2], g_gain))
    proj = jnp.stack(grads_projection[::-1])
    grad_state = lax.psum(proj[:, :, 2 * width : 2 * width + 2 * N], "tensor")
    return (
        out_hidden,
        grad_flow,
        jnp.stack([proj[:, :, :width], proj[:, :, width : 2 * width]], 1),
        grad_state,
        proj[:, :, 2 * width + 2 * N : 2 * width + 2 * N + heads],
        jnp.stack(grads_output[::-1]).transpose(0, 2, 1),
    ) + tuple(jnp.stack([layer_sums[i] for layer_sums in sums]) for i in range(6))


def solution(mesh):
    def whole(*arrays):
        inner = arrays[3].shape[3]
        return jax.shard_map(
            functools.partial(per_device, inner),
            mesh=mesh,
            in_specs=(
                P(("dp", "tensor"), None),
                P(("dp", "tensor"), None),
                P("dp"),
                P(None, None, "dp", "tensor"),
                P(None, "dp", None),
                P(None, "dp", "tensor"),
                P(None, "tensor", "dp"),
                P(),
                P(),
                P(),
                P(),
                P(),
                P(),
            ),
            out_specs=(
                P(("dp", "tensor"), None),
                P(("dp", "tensor"), None),
                P(None, None, "dp", "tensor"),
                P(None, "dp", None),
                P(None, "dp", "tensor"),
                P(None, "tensor", "dp"),
                P(),
                P(),
                P(),
                P(),
                P(),
                P(),
            ),
            check_vma=False,
        )(*arrays)

    return whole
```

time: 2590 us -> 1440 us (0.56)
  matrix products: 615 us -> 154 us
  local copies, waits for them, and re-layouts: 428 us -> 32.2 us
  other arithmetic: 287 us -> 43.4 us
  Pallas kernels: 0 us -> 188 us
  blocking collectives: 157 us -> 19.2 us
  waiting for transfers between devices: 1050 us -> 976 us
    dot_general x136 -> x12, matrix products: 615 us -> 154 us  [the longest x4 55 us: dot_tn(): lax.dot_general(a, b, (((0,), (0,)), ((), ())), preferred_element_type=F32)]
    unnamed x25 -> x18, waiting for transfers between devices: 332 us -> 0.97 us
    pallas_call x0 -> x4, Pallas kernels: none -> 188 us  [the longest x2 117 us: backward_mixer(): pl.pallas_call(functools.partial(backward_kernel, 0), grid=(blocks,), in_...]
    reduce_scatter x8, waiting for transfers between devices: 396 us -> 555 us  [the longest x2 245 us: per_device(): lax.psum_scatter(grad_projection, 'dp', scatter_dimension=0, tiled=True)]
    all_gather x8, waiting for transfers between devices: 196 us -> 339 us  [the longest x2 176 us: per_device(): projections.append(lax.all_gather(shard, 'dp', axis=0, tiled=True))]
    all_gather x4 -> x2, blocking collectives: 95.7 us -> 9.24 us  [gather_rows(): return lax.all_gather(values, 'tensor', axis=0, tiled=True)]
    transpose x10 -> x1, local copies, waits for them, and re-layouts: 84.7 us -> 0.88 us  [per_device(): out_weight[layer]]
    reduce_sum x20 -> x8, other arithmetic: 96.8 us -> 15.2 us  [the longest x2 7.92 us: per_device(): jnp.sum(mix_low.astype(F32) * mixed_raw, axis=-1, keepdims=True)]
  transfers between devices with their start and end apart: 22 -> 18, of which waited for: 14 -> 18; matrix products, arithmetic and copies ran while one was open for 27% -> 9% of each run, Pallas kernels for 0% -> 5%
where the time goes in v1:
time: 1440 us; the launch traced here: 1430 us
  waiting for transfers between devices  976 us (68%)
  Pallas kernels  188 us (13%)
  matrix products  154 us (11%)
  other arithmetic  43.4 us (3%)
  local copies, waits for them, and re-layouts  32.2 us (2%)
  blocking collectives  19.2 us (1%)
  between operations  15.9 us (1%)
    reduce_scatter x2, waiting for transfers between devices, per_device(): lax.psum_scatter(grad_projection, 'dp', scatter_dimension=0, tiled=True)  245 us
    all_gather x2, waiting for transfers between devices, per_device(): projections.append(lax.all_gather(shard, 'dp', axis=0, tiled=True))  176 us
    reduce_scatter x4, waiting for transfers between devices, scatter_rows(): return lax.psum_scatter(values, 'tensor', scatter_dimension=0, tiled=True)  161 us
    all_gather x4, waiting for transfers between devices, gather_rows(): return lax.all_gather(values, 'tensor', axis=0, tiled=True)  158 us
    reduce_scatter x2, waiting for transfers between devices, per_device(): lax.psum_scatter(grad_output, 'dp', scatter_dimension=0, tiled=True)  149 us
    pallas_call x2, Pallas kernels, backward_mixer(): pl.pallas_call(functools.partial(backward_kernel, 0), grid=(blocks,), in_...  117 us
    pallas_call x2, Pallas kernels, forward_mixer(): pl.pallas_call(forward_kernel, grid=(blocks,), in_specs=[wide(0), wide(1)...  70.4 us
    psum x1, waiting for transfers between devices, per_device(): flat = lax.psum(flat, ('dp', 'tensor')).reshape(-1)  61.1 us
  transfers between devices with their start and end apart: 18, of which 18 were waited for; matrix products, arithmetic and copies ran while one was open for 9% of the time, Pallas kernels for 5%

profile of v1, /device:TPU:0, one launch (start us, length us, event | category | flops | bytes accessed | tf_op | source)
XLA Modules:
  0.0 1430.6 jit_solution(12244995504951183121)
XLA Ops:
  20.4 41.5 %all-gather.13.cloned.1.call-done.normed_ref = bf16[1024,1536]{1,0:T(8,128)(2,1)} async-done(((bf16[512,1536]{1,0:T(8,128)(2,1)}), bf16[1024,1536]{1,0:T(8,128)(2,1)}) %all-gather.13.cloned.1.call-update) | async-done | bytes 3145744 | tf_op jit(solution)/shard_map/all_gather | solution.py:381
  62.0 91.6 %all-gather.15.cloned.1.call-done.side_weight_ref = bf16[1536,3456]{1,0:T(8,128)(2,1)} async-done(((bf16[96,3456]{1,0:T(8,128)(2,1)}), bf16[1536,3456]{1,0:T(8,128)(2,1)}) %all-gather.15.cloned.1.call-update) | async-done | bytes 10616848 | tf_op jit(solution)/shard_map/all_gather | solution.py:433
  168.7 35.3 %forward_mixer.2 = (bf16[1024,1536]{1,0:T(8,128)(2,1)}, bf16[1024,1536]{1,0:T(8,128)(2,1)}, bf16[1024,1536]{1,0:T(8,128)(2,1)}, f32[1024,640]{1,0:T(8,128)S(1)},...) custom-call(bf16[1024,3072]{1,0:T(8,128)(2,1)} %fusion.4.gate_ref.value_ref, ...), custom_call_target="tpu_custom_call" | custom-call | tf_op jit(solution)/shard_map/forward_mixer/pallas_call | solution.py:301
  226.0 32.8 %reduce-scatter.9.cloned.1.call-done = bf16[512,1536]{1,0:T(8,128)(2,1)} async-done(((bf16[1024,1536]{1,0:T(8,128)(2,1)}), bf16[512,1536]{1,0:T(8,128)(2,1)}) %reduce-scatter.9.cloned.1.call-update) | async-done | bytes 1572880 | tf_op jit(solution)/shard_map/reduce_scatter | solution.py:385
  265.6 84.8 %all-gather.21.cloned.1.call-done.side_weight_ref = bf16[1536,3456]{1,0:T(8,128)(2,1)} async-done(((bf16[96,3456]{1,0:T(8,128)(2,1)}), bf16[1536,3456]{1,0:T(8,128)(2,1)}) %all-gather.21.cloned.1.call-update) | async-done | bytes 10616848 | tf_op jit(solution)/shard_map/all_gather | solution.py:433
  350.4 45.2 %all-gather.19.cloned.1.call-done.normed_ref = bf16[1024,1536]{1,0:T(8,128)(2,1)} async-done(((bf16[512,1536]{1,0:T(8,128)(2,1)}), bf16[1024,1536]{1,0:T(8,128)(2,1)}) %all-gather.19.cloned.1.call-update) | async-done | bytes 3145744 | tf_op jit(solution)/shard_map/all_gather | solution.py:381
  395.6 15.2 %fusion.7.gate_ref.value_ref = bf16[1024,3072]{1,0:T(8,128)(2,1)} fusion(bf16[1024,1536]{1,0:T(8,128)(2,1)} %all-gather.19.cloned.1.call-done.normed_ref, bf16[1536,3456]{1,0:T(8,128)(2,1)} %all-gather.21.cloned.1.call-done.side_weight_ref), kind=kOutput, calls=%fused_computation.11 | convolution fusion | flops 9666822144 | bytes 18874368 | tf_op jit(solution)/shard_map/dot_general | solution.py:19
  410.8 35.1 %forward_mixer.3 = (bf16[1024,1536]{1,0:T(8,128)(2,1)}, bf16[1024,1536]{1,0:T(8,128)(2,1)}, bf16[1024,1536]{1,0:T(8,128)(2,1)}, f32[1024,640]{1,0:T(8,128)S(1)},...) custom-call(bf16[1024,3072]{1,0:T(8,128)(2,1)} %fusion.7.gate_ref.value_ref, ...), custom_call_target="tpu_custom_call" | custom-call | tf_op jit(solution)/shard_map/forward_mixer/pallas_call | solution.py:301
  460.7 42.0 %reduce-scatter.11.cloned.1.call-done = bf16[512,1536]{1,0:T(8,128)(2,1)} async-done(((bf16[1024,1536]{1,0:T(8,128)(2,1)}), bf16[512,1536]{1,0:T(8,128)(2,1)}) %reduce-scatter.11.cloned.1.call-update) | async-done | bytes 1572880 | tf_op jit(solution)/shard_map/reduce_scatter | solution.py:385
  518.5 33.0 %all-gather.25.cloned.1.call-done = bf16[1024,1536]{1,0:T(8,128)(2,1)} async-done(((bf16[512,1536]{1,0:T(8,128)(2,1)}), bf16[1024,1536]{1,0:T(8,128)(2,1)}) %all-gather.25.cloned.1.call-update) | async-done | bytes 3145744 | tf_op jit(solution)/shard_map/all_gather | solution.py:381
  560.8 58.6 %backward_mixer.2 = (bf16[1024,3456]{1,0:T(8,128)(2,1)}, f32[8,1536]{1,0:T(8,128)S(1)}, f32[8,256]{1,0:T(8,128)S(1)}, f32[8,128]{1,0:T(8,128)S(1)}) custom-call(bf16[1024,3072]{1,0:T(8,128)(2,1)} %fusion.7.gate_ref.value_ref, bf16[1024,3072]{1,0:T(8,128)(2,1)} %fusion.7.gate_ref.value_ref, bf16[1024,1536]{1,0:T(8,128)(2,1)} %get-tuple-element.36.pre_ref, ...), custom_call_target="tpu_custom_call" | custom-call | tf_op jit(solution)/shard_map/backward_mixer/pallas_call | solution.py:341
  619.4 17.1 %convolution_convert_fusion.5 = bf16[1024,1536]{1,0:T(8,128)(2,1)} fusion(bf16[1024,3456]{1,0:T(8,128)(2,1)} %get-tuple-element.40, bf16[1536,3456]{1,0:T(8,128)(2,1)} %all-gather.21.cloned.1.call-done.side_weight_ref), kind=kOutput, calls=%fused_computation.27 | convolution fusion | flops 10873208832 | bytes 20840448 | tf_op jit(solution)/shard_map/dot_general | solution.py:23
  636.6 43.5 %reduce-scatter.13.cloned.1.call-done = bf16[512,1536]{1,0:T(8,128)(2,1)} async-done(((bf16[1024,1536]{1,0:T(8,128)(2,1)}), bf16[512,1536]{1,0:T(8,128)(2,1)}) %reduce-scatter.13.cloned.1.call-update) | async-done | bytes 1572880 | tf_op jit(solution)/shard_map/reduce_scatter | solution.py:385
  695.3 38.3 %all-gather.27.cloned.1.call-done = bf16[1024,1536]{1,0:T(8,128)(2,1)} async-done(((bf16[512,1536]{1,0:T(8,128)(2,1)}), bf16[1024,1536]{1,0:T(8,128)(2,1)}) %all-gather.27.cloned.1.call-update) | async-done | bytes 3145744 | tf_op jit(solution)/shard_map/all_gather | solution.py:381
  743.0 58.7 %backward_mixer.3 = (bf16[1024,3456]{1,0:T(8,128)(2,1)}, f32[8,1536]{1,0:T(8,128)S(1)}, f32[8,256]{1,0:T(8,128)S(1)}, f32[8,128]{1,0:T(8,128)S(1)}) custom-call(bf16[1024,3072]{1,0:T(8,128)(2,1)} %fusion.4.gate_ref.value_ref, bf16[1024,3072]{1,0:T(8,128)(2,1)} %fusion.4.gate_ref.value_ref, bf16[1024,1536]{1,0:T(8,128)(2,1)} %get-tuple-element.41.pre_ref, ...), custom_call_target="tpu_custom_call" | custom-call | tf_op jit(solution)/shard_map/backward_mixer/pallas_call | solution.py:341
  817.6 42.3 %reduce-scatter.15.cloned.1.call-done = bf16[512,1536]{1,0:T(8,128)(2,1)} async-done(((bf16[1024,1536]{1,0:T(8,128)(2,1)}), bf16[512,1536]{1,0:T(8,128)(2,1)}) %reduce-scatter.15.cloned.1.call-update) | async-done | bytes 1572880 | tf_op jit(solution)/shard_map/reduce_scatter | solution.py:385
  883.0 17.8 %convolution_convert_fusion = bf16[1536,3456]{1,0:T(8,128)(2,1)} fusion(bf16[1024,1536]{1,0:T(8,128)(2,1)} %all-gather.19.cloned.1.call-done.normed_ref, bf16[1024,3456]{1,0:T(8,128)(2,1)} %get-tuple-element.40), kind=kOutput, calls=%fused_computation | convolution fusion | flops 10876944384 | bytes 20840448 | tf_op jit(solution)/shard_map/dot_general | solution.py:27
  901.2 17.8 %convolution_convert_fusion.1 = bf16[1536,3456]{1,0:T(8,128)(2,1)} fusion(bf16[1024,1536]{1,0:T(8,128)(2,1)} %all-gather.13.cloned.1.call-done.normed_ref, bf16[1024,3456]{1,0:T(8,128)(2,1)} %get-tuple-element.45), kind=kOutput, calls=%fused_computation.1 | convolution fusion | flops 10876944384 | bytes 20840448 | tf_op jit(solution)/shard_map/dot_general | solution.py:27
  926.8 61.1 %all-reduce.14.cloned.1.call-done = f32[336,128]{1,0:T(8,128)} async-done(((f32[336,128]{1,0:T(8,128)}), f32[336,128]{1,0:T(8,128)}) %all-reduce.14.cloned.1.call-update) | async-done | bytes 172048 | tf_op jit(solution)/shard_map/psum | solution.py:539
  998.9 70.4 %reduce-scatter.23.cloned.1.call-done = bf16[96,1536]{1,0:T(8,128)(2,1)} async-done(((bf16[1536,1536]{1,0:T(8,128)(2,1)}), bf16[96,1536]{1,0:T(8,128)(2,1)}) %reduce-scatter.23.cloned.1.call-update) | async-done | bytes 294928 | tf_op jit(solution)/shard_map/reduce_scatter | solution.py:496
  1069.2 78.8 %reduce-scatter.21.cloned.1.call-done = bf16[96,1536]{1,0:T(8,128)(2,1)} async-done(((bf16[1536,1536]{1,0:T(8,128)(2,1)}), bf16[96,1536]{1,0:T(8,128)(2,1)}) %reduce-scatter.21.cloned.1.call-update) | async-done | bytes 294928 | tf_op jit(solution)/shard_map/reduce_scatter | solution.py:496
  1150.2 121.1 %reduce-scatter.19.cloned.1.call-done = bf16[96,3456]{1,0:T(8,128)(2,1)} async-done(((bf16[1536,3456]{1,0:T(8,128)(2,1)}), bf16[96,3456]{1,0:T(8,128)(2,1)}) %reduce-scatter.19.cloned.1.call-update) | async-done | bytes 663568 | tf_op jit(solution)/shard_map/reduce_scatter | solution.py:504
  1271.3 123.9 %reduce-scatter.17.cloned.1.call-done = bf16[96,3456]{1,0:T(8,128)(2,1)} async-done(((bf16[1536,3456]{1,0:T(8,128)(2,1)}), bf16[96,3456]{1,0:T(8,128)(2,1)}) %reduce-scatter.17.cloned.1.call-update) | async-done | bytes 663568 | tf_op jit(solution)/shard_map/reduce_scatter | solution.py:504
  1401.5 20.2 %all-reduce.12.cloned.1.call-done = f32[2,96,256]{2,1,0:T(8,128)} async-done(((f32[2,96,256]{2,1,0:T(8,128)}), f32[2,96,256]{2,1,0:T(8,128)}) %all-reduce.12.cloned.1.call-update) | async-done | bytes 196624 | tf_op jit(solution)/shard_map/psum | solution.py:556
  (236 shorter events, 188.7 us)
Async XLA Ops:
  7.2 54.8 %all-gather.13.cloned.1.call-start = ((), (), s32[]{:S(2)}) async-start(), calls=%async_computation.8 | async-start | bytes 4718592 | tf_op jit(solution)/shard_map/all_gather | solution.py:381
  14.2 139.3 %all-gather.15.cloned.1.call-start = ((), (), s32[]{:S(2)}) async-start(), calls=%async_computation.9 | async-start | bytes 11280384 | tf_op jit(solution)/shard_map/all_gather | solution.py:433
  17.3 189.9 %all-gather.17.cloned.1.call-start = ((), (), s32[]{:S(2)}) async-start(), calls=%async_computation.10 | async-start | bytes 5013504 | tf_op jit(solution)/shard_map/all_gather | solution.py:434
  18.3 240.4 %reduce-scatter.9.cloned.1.call-start = ((), (), s32[]{:S(2)}) async-start(), calls=%async_computation.11 | async-start | bytes 4718592 | tf_op jit(solution)/shard_map/reduce_scatter | solution.py:385
  216.6 133.8 %all-gather.21.cloned.1.call-start = ((), (), s32[]{:S(2)}) async-start(), calls=%async_computation.13 | async-start | bytes 11280384 | tf_op jit(solution)/shard_map/all_gather | solution.py:433
  219.9 175.6 %all-gather.19.cloned.1.call-start = ((), (), s32[]{:S(2)}) async-start(), calls=%async_computation.12 | async-start | bytes 4718592 | tf_op jit(solution)/shard_map/all_gather | solution.py:381
  263.8 187.6 %all-gather.23.cloned.1.call-start = ((), (), s32[]{:S(2)}) async-start(), calls=%async_computation.14 | async-start | bytes 5013504 | tf_op jit(solution)/shard_map/all_gather | solution.py:434
  264.5 238.2 %reduce-scatter.11.cloned.1.call-start = ((), (), s32[]{:S(2)}) async-start(), calls=%async_computation.15 | async-start | bytes 4718592 | tf_op jit(solution)/shard_map/reduce_scatter | solution.py:385
  460.7 90.8 %all-gather.25.cloned.1.call-start = ((), (), s32[]{:S(2)}) async-start(), calls=%async_computation.16 | async-start | bytes 4718592 | tf_op jit(solution)/shard_map/all_gather | solution.py:381
  506.4 173.6 %reduce-scatter.13.cloned.1.call-start = ((), (), s32[]{:S(2)}) async-start(), calls=%async_computation.17 | async-start | bytes 4718592 | tf_op jit(solution)/shard_map/reduce_scatter | solution.py:385
  636.5 97.1 %all-gather.27.cloned.1.call-start = ((), (), s32[]{:S(2)}) async-start(), calls=%async_computation.18 | async-start | bytes 4718592 | tf_op jit(solution)/shard_map/all_gather | solution.py:381
  688.5 171.4 %reduce-scatter.15.cloned.1.call-start = ((), (), s32[]{:S(2)}) async-start(), calls=%async_computation.19 | async-start | bytes 4718592 | tf_op jit(solution)/shard_map/reduce_scatter | solution.py:385
  733.6 68.0 %slice-start = ((s8[10616832]{0:T(1024)(128)(4,1)}), s8[4194304]{0:T(1024)(128)(4,1)S(1)}, s32[]{:S(2)}) async-start(s8[10616832]{0:T(1024)(128)(4,1)} %bitcast.112), calls=%async_computation.26 | async-start | bytes 8388608
  733.6 68.0 %slice-start.1 = ((s8[10616832]{0:T(1024)(128)(4,1)}), s8[4194304]{0:T(1024)(128)(4,1)S(1)}, s32[]{:S(2)}) async-start(s8[10616832]{0:T(1024)(128)(4,1)} %bitcast.112), calls=%async_computation.27 | async-start | bytes 8388608
  743.0 58.7 %slice-start.2 = ((s8[10616832]{0:T(1024)(128)(4,1)}), s8[2228224]{0:T(1024)(128)(4,1)S(1)}, s32[]{:S(2)}) async-start(s8[10616832]{0:T(1024)(128)(4,1)} %bitcast.112), calls=%async_computation.28 | async-start | bytes 4456448
  816.4 43.5 %copy-start.19 = (f32[1536]{0:T(1024)S(1)}, f32[1536]{0:T(1024)}, u32[]{:S(2)}) copy-start(f32[1536]{0:T(1024)} %copy-done.18) | copy-start | bytes 18436
  816.4 43.5 %copy-start.22 = (f32[512]{0:T(512)S(1)}, f32[512]{0:T(512)}, u32[]{:S(2)}) copy-start(f32[512]{0:T(512)} %copy-done.21) | copy-start | bytes 6148
  816.4 171.5 %all-reduce.14.cloned.1.call-start = ((), (), s32[]{:S(2)}) async-start(), calls=%async_computation.25 | async-start | bytes 344064 | tf_op jit(solution)/shard_map/psum | solution.py:539
  863.2 206.0 %reduce-scatter.23.cloned.1.call-start = ((), (), s32[]{:S(2)}) async-start(), calls=%async_computation.24 | async-start | bytes 5013504 | tf_op jit(solution)/shard_map/reduce_scatter | solution.py:496
  873.2 274.8 %reduce-scatter.21.cloned.1.call-start = ((), (), s32[]{:S(2)}) async-start(), calls=%async_computation.23 | async-start | bytes 5013504 | tf_op jit(solution)/shard_map/reduce_scatter | solution.py:496
  883.0 388.3 %reduce-scatter.19.cloned.1.call-start = ((), (), s32[]{:S(2)}) async-start(), calls=%async_computation.21 | async-start | bytes 11280384 | tf_op jit(solution)/shard_map/reduce_scatter | solution.py:504
  900.9 494.3 %reduce-scatter.17.cloned.1.call-start = ((), (), s32[]{:S(2)}) async-start(), calls=%async_computation.20 | async-start | bytes 11280384 | tf_op jit(solution)/shard_map/reduce_scatter | solution.py:504
  919.0 502.7 %all-reduce.12.cloned.1.call-start = ((), (), s32[]{:S(2)}) async-start(), calls=%async_computation.22 | async-start | bytes 393216 | tf_op jit(solution)/shard_map/psum | solution.py:556
  1271.3 126.2 %copy-start.13 = (bf16[96,3456]{1,0:T(8,128)(2,1)S(1)}, bf16[96,3456]{1,0:T(8,128)(2,1)}, u32[]{:S(2)}) copy-start(bf16[96,3456]{1,0:T(8,128)(2,1)} %reduce-scatter.19.cloned.1.call-done) | copy-start | bytes 1990660
  (26 other events, 190.9 us)
Sparse Core Ops, SparseCore 0:
  14.3 47.6 all-gather.12
  64.8 88.6 all-gather.14
  155.8 51.3 all-gather.16
  216.7 41.9 reduce-scatter.8
  261.7 88.6 all-gather.20
  352.4 43.1 all-gather.18
  398.1 53.2 all-gather.22
  460.8 41.9 reduce-scatter.10
  506.5 44.9 all-gather.24
  636.6 43.3 reduce-scatter.12
  688.7 44.9 all-gather.26
  816.6 43.3 reduce-scatter.14
  866.1 121.8 all-reduce.13
  991.6 77.5 reduce-scatter.22
  1073.4 74.5 reduce-scatter.20
  1151.9 119.2 reduce-scatter.18
  1275.2 119.9 reduce-scatter.16
  1399.6 22.0 all-reduce.11

commit v2 on v1

--- a/solution.py
+++ b/solution.py
@@ -58,7 +58,7 @@
 
 
 def forward_kernel(
-    gate_ref, value_ref, normed_ref, side_weight_ref, chan_ref, state_taps_ref, headp_ref,
+    turn_ref, gate_ref, value_ref, normed_ref, side_weight_ref, chan_ref, state_taps_ref, headp_ref,
     gnl_ref, scanned_ref, pre_ref, side_ref, states_ref, square_ref,
     state, vbuf, sbuf, step_s, run_s, runt_s, cb_s, bmat, bmat_t, cmat,
 ):
@@ -134,7 +134,7 @@
 
 
 def backward_kernel(
-    channels, gate_ref, value_ref, pre_ref, scanned_ref, dgn_ref, side_ref, states_ref, rows_ref,
+    turn_ref, gate_ref, value_ref, pre_ref, scanned_ref, dgn_ref, side_ref, states_ref, rows_ref,
     chan_ref, state_taps_ref, headp_ref,
     low_ref, dchan_ref, dstate_ref, dhead_ref,
     lam, gbuf, gsbuf, step_s, run_s, runt_s, cbt_s, bmat, cmat, cmat_t,
@@ -293,26 +293,37 @@
     dhead_ref[1:2, :] += jnp.sum(dstep_in, 0, keepdims=True)
 
 
-def forward_mixer(projected, normed, packed, chan, state_taps, headp, q, width):
+def forward_mixer(turn, projected, normed, packed, chan, state_taps, headp, q, width):
     rows, depth = normed.shape
     blocks = rows // q
-    wide = lambda column: pl.BlockSpec((q, width), lambda i: (i, column))
-    fixed = lambda shape: pl.BlockSpec(shape, lambda i: (0,) * len(shape))
+    place = lambda i, turn: lax.rem(i + turn[0], blocks)
+    wide = lambda column: pl.BlockSpec((q, width), lambda i, turn: (place(i, turn), column))
+    fixed = lambda shape: pl.BlockSpec(shape, lambda i, turn: (0,) * len(shape))
     return pl.pallas_call(
         forward_kernel,
-        grid=(blocks,),
-        in_specs=[
-            wide(0), wide(1),
-            pl.BlockSpec((q, depth), lambda i: (i, 0)),
-            pl.BlockSpec((depth, SIDE), lambda i: (0, 2 * width // SIDE)),
-            fixed((8, width)), fixed((8, 2 * N)), fixed((8, 128)),
-        ],
-        out_specs=[
-            wide(0), wide(0), wide(0),
-            pl.BlockSpec((q, SIDE + 2 * N), lambda i: (i, 0)),
-            pl.BlockSpec((1, N, width), lambda i: (i, 0, 0)),
-            pl.BlockSpec((q, 128), lambda i: (i, 0)),
-        ],
+        grid_spec=pltpu.PrefetchScalarGridSpec(
+            num_scalar_prefetch=1,
+            grid=(blocks,),
+            in_specs=[
+                wide(0), wide(1),
+                pl.BlockSpec((q, depth), lambda i, turn: (place(i, turn), 0)),
+                pl.BlockSpec((depth, SIDE), lambda i, turn: (0, 2 * width // SIDE)),
+                fixed((8, width)), fixed((8, 2 * N)), fixed((8, 128)),
+            ],
+            out_specs=[
+                wide(0), wide(0), wide(0),
+                pl.BlockSpec((q, SIDE + 2 * N), lambda i, turn: (place(i, turn), 0)),
+                pl.BlockSpec((1, N, width), lambda i, turn: (i, 0, 0)),
+                pl.BlockSpec((q, 128), lambda i, turn: (place(i, turn), 0)),
+            ],
+            scratch_shapes=[
+                pltpu.VMEM((N, width), F32), pltpu.VMEM((q + 8, width), F32),
+                pltpu.VMEM((q + 8, 2 * N), F32),
+                pltpu.VMEM((q, 128), F32), pltpu.VMEM((q, 128), F32), pltpu.VMEM((128, q), F32),
+                pltpu.VMEM((q, q), F32), pltpu.VMEM((q, N), BF16), pltpu.VMEM((N, q), BF16),
+                pltpu.VMEM((q, N), BF16),
+            ],
+        ),
         out_shape=[
             jax.ShapeDtypeStruct((rows, width), BF16),
             jax.ShapeDtypeStruct((rows, width), BF16),
@@ -321,55 +332,59 @@
             jax.ShapeDtypeStruct((blocks, N, width), BF16),
             jax.ShapeDtypeStruct((rows, 128), F32),
         ],
-        scratch_shapes=[
-            pltpu.VMEM((N, width), F32), pltpu.VMEM((q + 8, width), F32), pltpu.VMEM((q + 8, 2 * N), F32),
-            pltpu.VMEM((q, 128), F32), pltpu.VMEM((q, 128), F32), pltpu.VMEM((128, q), F32),
-            pltpu.VMEM((q, q), F32), pltpu.VMEM((q, N), BF16), pltpu.VMEM((N, q), BF16),
-            pltpu.VMEM((q, N), BF16),
-        ],
         compiler_params=pltpu.CompilerParams(vmem_limit_bytes=48 << 20),
+        cost_estimate=pl.CostEstimate(flops=rows * width * 20000, bytes_accessed=rows * width * 20, transcendentals=0),
         name="forward_mixer",
-    )(projected, projected, normed, packed, chan, state_taps, headp)
-
-
-def backward_mixer(projected, pre, scanned, dgn, side, states, rows_in, chan, state_taps, headp, q, width):
+    )(turn, projected, projected, normed, packed, chan, state_taps, headp)
+
+
+def backward_mixer(
+    turn, projected, pre, scanned, dgn, side, states, rows_in, chan, state_taps, headp, q, width, interpret=False
+):
     rows = pre.shape[0]
     blocks = rows // q
     back = lambda i: blocks - 1 - i
-    wide = lambda column: pl.BlockSpec((q, width), lambda i: (back(i), column))
-    fixed = lambda shape: pl.BlockSpec(shape, lambda i: (0,) * len(shape))
+    place = lambda i, turn: lax.rem(back(i) + turn[0], blocks)
+    wide = lambda column: pl.BlockSpec((q, width), lambda i, turn: (place(i, turn), column))
+    fixed = lambda shape: pl.BlockSpec(shape, lambda i, turn: (0,) * len(shape))
     return pl.pallas_call(
-        functools.partial(backward_kernel, 0),
-        grid=(blocks,),
-        in_specs=[
-            wide(0), wide(1), wide(0), wide(0), wide(0),
-            pl.BlockSpec((q, SIDE + 2 * N), lambda i: (back(i), 0)),
-            pl.BlockSpec((1, N, width), lambda i: (back(i), 0, 0)),
-            pl.BlockSpec((q, 128), lambda i: (back(i), 0)),
-            fixed((8, width)), fixed((8, 2 * N)), fixed((8, 128)),
-        ],
-        out_specs=[
-            pl.BlockSpec((q, 2 * width + SIDE), lambda i: (back(i), 0)),
-            fixed((8, width)), fixed((8, 2 * N)), fixed((8, 128)),
-        ],
+        backward_kernel,
+        grid_spec=pltpu.PrefetchScalarGridSpec(
+            num_scalar_prefetch=1,
+            grid=(blocks,),
+            in_specs=[
+                wide(0), wide(1), wide(0), wide(0), wide(0),
+                pl.BlockSpec((q, SIDE + 2 * N), lambda i, turn: (place(i, turn), 0)),
+                pl.BlockSpec((1, N, width), lambda i, turn: (back(i), 0, 0)),
+                pl.BlockSpec((q, 128), lambda i, turn: (place(i, turn), 0)),
+                fixed((8, width)), fixed((8, 2 * N)), fixed((8, 128)),
+            ],
+            out_specs=[
+                pl.BlockSpec((q, 2 * width + SIDE), lambda i, turn: (place(i, turn), 0)),
+                fixed((8, width)), fixed((8, 2 * N)), fixed((8, 128)),
+            ],
+            scratch_shapes=[
+                pltpu.VMEM((N, width), F32), pltpu.VMEM((q + 8, width), F32),
+                pltpu.VMEM((q + 8, 2 * N), F32),
+                pltpu.VMEM((q, 128), F32), pltpu.VMEM((q, 128), F32), pltpu.VMEM((128, q), F32),
+                pltpu.VMEM((q, q), F32), pltpu.VMEM((q, N), BF16), pltpu.VMEM((q, N), BF16),
+                pltpu.VMEM((N, q), BF16),
+                pltpu.VMEM((q, q), F32), pltpu.VMEM((q, N), F32), pltpu.VMEM((q, N), F32),
+                pltpu.VMEM((q, 128), F32), pltpu.VMEM((128, q), F32),
+                pltpu.VMEM((q, width), BF16), pltpu.VMEM((q, width), BF16), pltpu.VMEM((q, width), BF16),
+                pltpu.VMEM((1, width), F32), pltpu.VMEM((width, 128), BF16),
+            ],
+        ),
         out_shape=[
             jax.ShapeDtypeStruct((rows, 2 * width + SIDE), BF16),
             jax.ShapeDtypeStruct((8, width), F32),
             jax.ShapeDtypeStruct((8, 2 * N), F32),
             jax.ShapeDtypeStruct((8, 128), F32),
         ],
-        scratch_shapes=[
-            pltpu.VMEM((N, width), F32), pltpu.VMEM((q + 8, width), F32), pltpu.VMEM((q + 8, 2 * N), F32),
-            pltpu.VMEM((q, 128), F32), pltpu.VMEM((q, 128), F32), pltpu.VMEM((128, q), F32),
-            pltpu.VMEM((q, q), F32), pltpu.VMEM((q, N), BF16), pltpu.VMEM((q, N), BF16), pltpu.VMEM((N, q), BF16),
-            pltpu.VMEM((q, q), F32), pltpu.VMEM((q, N), F32), pltpu.VMEM((q, N), F32),
-            pltpu.VMEM((q, 128), F32), pltpu.VMEM((128, q), F32),
-            pltpu.VMEM((q, width), BF16), pltpu.VMEM((q, width), BF16), pltpu.VMEM((q, width), BF16),
-            pltpu.VMEM((1, width), F32), pltpu.VMEM((width, 128), BF16),
-        ],
         compiler_params=pltpu.CompilerParams(vmem_limit_bytes=48 << 20),
+        cost_estimate=pl.CostEstimate(flops=rows * width * 35000, bytes_accessed=rows * width * 20, transcendentals=0),
         name="backward_mixer",
-    )(projected, projected, pre, scanned, dgn, side, states, rows_in, chan, state_taps, headp)
+    )(turn, projected, projected, pre, scanned, dgn, side, states, rows_in, chan, state_taps, headp)
 
 
 LAYERS = 2
@@ -377,12 +392,70 @@
 BLOCK = 256
 
 
-def gather_rows(values):
-    return lax.all_gather(values, "tensor", axis=0, tiled=True)
-
-
-def scatter_rows(values):
-    return lax.psum_scatter(values, "tensor", scatter_dimension=0, tiled=True)
+class Pair:
+    def __init__(self, rows):
+        self.rows = rows
+
+    def swap(self, values):
+        return lax.ppermute(values, "tensor", [(0, 1), (1, 0)])
+
+    def turn(self, q):
+        return lax.axis_index("tensor") * (self.rows // q)
+
+    def gather(self, values):
+        return jnp.concatenate([values, self.swap(values)], 0)
+
+    def own(self, values):
+        return values[: self.rows]
+
+    def total(self, values):
+        there = self.swap(values)
+        return values + jnp.concatenate([there[self.rows :], there[: self.rows]], 0)
+
+    def project(self, function, values):
+        sent = self.swap(function(values[self.rows :]).astype(BF16))
+        return function(values[: self.rows]) + sent.astype(F32)
+
+    def sum_all(self, values):
+        return values + self.swap(values)
+
+
+class Group:
+    def __init__(self, rows):
+        self.rows = rows
+        self.start = lax.axis_index("tensor") * rows
+
+    def turn(self, q):
+        return jnp.zeros((), jnp.int32)
+
+    def gather(self, values):
+        return lax.all_gather(values, "tensor", axis=0, tiled=True)
+
+    def own(self, values):
+        return lax.dynamic_slice_in_dim(values, self.start, self.rows, 0)
+
+    def total(self, values):
+        return lax.psum(values, "tensor")
+
+    def project(self, function, values):
+        return lax.psum_scatter(
+            function(values).astype(BF16), "tensor", scatter_dimension=0, tiled=True
+        ).astype(F32)
+
+    def sum_all(self, values):
+        return lax.psum(values, "tensor")
+
+
+def sum_everywhere(values):
+    size = lax.axis_size("dp")
+    if lax.axis_size("tensor") != 2 or size & (size - 1):
+        return lax.psum(values, ("dp", "tensor"))
+    values = values + lax.ppermute(values, "tensor", [(0, 1), (1, 0)])
+    bit = 1
+    while bit < size:
+        values = values + lax.ppermute(values, "dp", [(i, i ^ bit) for i in range(size)])
+        bit *= 2
+    return values
 
 
 def per_device(
@@ -402,19 +475,18 @@
     norm_gain,
 ):
     tensor_index = lax.axis_index("tensor")
-    local_rows = hidden_in.shape[0]
+    tensor_size = lax.axis_size("tensor")
+    local_rows, depth = hidden_in.shape
     width = gate_value_weight.shape[3]
     heads = step_weight.shape[2]
+    all_heads = heads * tensor_size
     head_start = tensor_index * heads
     lane_start = tensor_index * width
-    row_start = tensor_index * local_rows
-    seq_rows = local_rows * lax.axis_size("tensor")
-    q = min(BLOCK, seq_rows)
-    position = row_start + jnp.arange(local_rows)
+    q = min(BLOCK, local_rows * tensor_size)
+    group = (Pair if tensor_size == 2 and local_rows % q == 0 else Group)(local_rows)
+    turn = group.turn(q).astype(jnp.int32).reshape(1)
+    position = tensor_index * local_rows + jnp.arange(local_rows)
     keep_rows = (position < lengths[0]).astype(F32)[:, None]
-
-    def own(values):
-        return lax.dynamic_slice_in_dim(values, row_start, local_rows, 0)
 
     def part(table, start, size, axis=0):
         return lax.dynamic_slice_in_dim(table, start, size, axis)
@@ -457,64 +529,65 @@
         )
         tables.append((chan, state_taps, headp))
 
+    last_mix = keep_rows * cotangent.astype(F32)
+    last_mix_all = group.gather(last_mix.astype(BF16))
     hidden = hidden_in.astype(F32)
     saved = []
     for layer in range(LAYERS):
         chan, state_taps, headp = tables[layer]
         inv_rows = lax.rsqrt(jnp.mean(hidden * hidden, axis=-1, keepdims=True) + EPSILON)
         normed = (hidden * inv_rows * pre_gain[layer]).astype(BF16)
-        normed_all = gather_rows(normed)
+        normed_all = group.gather(normed)
         projected = dot_nn(normed_all, projections[layer][:, : 2 * width]).astype(BF16)
         gnl, scanned, pre, side, states, squares = forward_mixer(
-            projected, normed_all, projections[layer], chan, state_taps, headp, q, width
-        )
-        square_sum = lax.psum(jnp.sum(squares, axis=-1), "tensor")
-        inv_gate = lax.rsqrt(square_sum / inner + EPSILON)[:, None]
-        mixed_raw = scatter_rows(dot_nt(gnl, outputs[layer]).astype(BF16)).astype(F32)
+            turn, projected, normed_all, projections[layer], chan, state_taps, headp, q, width
+        )
+        square_sum = group.total(jnp.sum(squares, axis=-1, keepdims=True))
+        inv_gate = lax.rsqrt(square_sum / inner + EPSILON)
+        mixed_raw = group.project(lambda rows: dot_nt(rows, outputs[layer]), gnl)
         saved.append(
             (hidden, inv_rows, normed_all, projected, gnl, scanned, pre, side, states, inv_gate, mixed_raw)
         )
-        hidden = keep_rows * (hidden + mixed_raw * own(inv_gate))
+        hidden = keep_rows * (hidden + mixed_raw * group.own(inv_gate))
     out_hidden = hidden
 
-    grad_flow = cotangent.astype(F32)
-    grads_projection, grads_output, small = [], [], []
+    grad_mix, mix_all = last_mix, last_mix_all
+    grads_projection, grads_output, sums = [], [], []
+    count = KCONV + 1
+    held = None
     for layer in reversed(range(LAYERS)):
         chan, state_taps, headp = tables[layer]
         (hidden, inv_rows, normed_all, projected, gnl, scanned, pre, side, states, inv_gate, mixed_raw) = saved[layer]
-        grad_mix = keep_rows * grad_flow
-        mix_low = grad_mix.astype(BF16)
-        mix_all = gather_rows(mix_low)
-        cross = gather_rows(jnp.sum(mix_low.astype(F32) * mixed_raw, axis=-1, keepdims=True))
+        dgn = dot_nn(mix_all, outputs[layer]).astype(BF16)
+        if layer == LAYERS - 1:
+            cross = group.total(jnp.sum(gnl.astype(F32) * dgn.astype(F32), axis=-1, keepdims=True))
+        else:
+            cross = group.gather(
+                jnp.sum(grad_mix.astype(BF16).astype(F32) * mixed_raw, axis=-1, keepdims=True)
+            )
+        scaled_mix = (mix_all.astype(F32) * inv_gate).astype(BF16)
+        grad_output = dot_tn(scaled_mix, gnl).astype(BF16)
+        grad_output = lax.psum_scatter(grad_output, "dp", scatter_dimension=0, tiled=True)
         rows_in = jnp.pad(
             jnp.concatenate([inv_gate, inv_gate * inv_gate * inv_gate * cross / inner], 1), ((0, 0), (0, 126))
         )
-        dgn = dot_nn(mix_all, outputs[layer]).astype(BF16)
-        scaled_mix = (mix_all.astype(F32) * inv_gate).astype(BF16)
-        grad_output = dot_tn(scaled_mix, gnl).astype(BF16)
-        grads_output.append(
-            lax.psum_scatter(grad_output, "dp", scatter_dimension=0, tiled=True).astype(F32)
-        )
         low, dchan, dstate, dhead = backward_mixer(
-            projected, pre, scanned, dgn, side, states, rows_in, chan, state_taps, headp, q, width
-        )
-        grad_normed = scatter_rows(dot_nt(low, projections[layer]).astype(BF16)).astype(F32)
+            turn, projected, pre, scanned, dgn, side, states, rows_in, chan, state_taps, headp, q, width
+        )
+        if held is not None:
+            low, held = lax.optimization_barrier((low, held))
+            grads_output.append(held[0])
+            grads_projection.append(held[1])
+            sums.append(held[2])
+        grad_normed = group.project(lambda rows: dot_nt(rows, projections[layer]), low)
         grad_projection = dot_tn(normed_all, low).astype(BF16)
-        grads_projection.append(
-            lax.psum_scatter(grad_projection, "dp", scatter_dimension=0, tiled=True).astype(F32)
-        )
+        grad_projection = lax.psum_scatter(grad_projection, "dp", scatter_dimension=0, tiled=True)
         unit_rows = hidden * inv_rows
         grad_pre = jnp.sum(grad_normed * unit_rows, axis=0)
         grad_unit = grad_normed * pre_gain[layer]
         grad_flow = grad_mix + inv_rows * (
             grad_unit - unit_rows * jnp.mean(grad_unit * unit_rows, axis=-1, keepdims=True)
         )
-        small.append((grad_pre, dchan, dstate, dhead))
-
-    count = KCONV + 1
-    pieces = []
-    for layer in range(LAYERS):
-        grad_pre, dchan, dstate, dhead = small[LAYERS - 1 - layer]
 
         def placed(values, total, start):
             full = jnp.zeros(values.shape[:-1] + (total,), F32)
@@ -522,46 +595,44 @@
 
         lanes = placed(dchan, inner, lane_start)
         skips = dchan[5].reshape(heads, HEAD).sum(axis=1)
-        per_head = placed(
-            jnp.stack([dhead[0, :heads], dhead[1, :heads], skips]),
-            lax.axis_size("tensor") * heads,
-            head_start,
-        )
-        pieces += [
-            grad_pre,
-            lanes[:count].reshape(-1),
-            lanes[6],
-            dstate[:count].reshape(-1),
-            per_head.reshape(-1),
-        ]
-    flat = jnp.concatenate(pieces)
-    flat = jnp.pad(flat, (0, -flat.shape[0] % 1024)).reshape(-1, 128)
-    flat = lax.psum(flat, ("dp", "tensor")).reshape(-1)
-    cut = [0]
-
-    def take(*shape):
-        size = 1
-        for extent in shape:
-            size *= extent
-        cut[0] += size
-        return flat[cut[0] - size : cut[0]].reshape(shape)
-
-    all_heads = lax.axis_size("tensor") * heads
-    sums = []
-    for layer in range(LAYERS):
-        g_pre, g_lanes, g_gain = take(hidden.shape[1]), take(count, inner), take(inner)
-        g_state, g_heads = take(count, 2 * N), take(3, all_heads)
-        sums.append((g_pre, jnp.concatenate([g_lanes, g_state], 1), g_heads[0], g_heads[1], g_heads[2], g_gain))
-    proj = jnp.stack(grads_projection[::-1])
-    grad_state = lax.psum(proj[:, :, 2 * width : 2 * width + 2 * N], "tensor")
+        per_head = placed(jnp.stack([dhead[0, :heads], dhead[1, :heads], skips]), all_heads, head_start)
+        flat = jnp.concatenate(
+            [
+                grad_pre,
+                lanes[:count].reshape(-1),
+                lanes[6],
+                dstate[:count].reshape(-1),
+                per_head.reshape(-1),
+            ]
+        )
+        flat = jnp.pad(flat, (0, -flat.shape[0] % 1024)).reshape(-1, 128)
+        held = (grad_output, grad_projection, sum_everywhere(flat))
+        if layer > 0:
+            grad_mix = keep_rows * grad_flow
+            mix_all = group.gather(grad_mix.astype(BF16))
+    grads_output.append(held[0])
+    grads_projection.append(held[1])
+    sums.append(held[2])
+
+    small = []
+    for flat in sums[::-1]:
+        flat = flat.reshape(-1)
+        cuts, start = [], 0
+        for size in (depth, count * inner, inner, count * 2 * N, all_heads, all_heads, all_heads):
+            cuts.append(flat[start : start + size])
+            start += size
+        taps = jnp.concatenate([cuts[1].reshape(count, inner), cuts[3].reshape(count, 2 * N)], 1)
+        small.append((cuts[0], taps, cuts[4], cuts[5], cuts[6], cuts[2]))
+    state_end = 2 * width + 2 * N
+    grads = [grad.astype(F32) for grad in grads_projection[::-1]]
     return (
         out_hidden,
         grad_flow,
-        jnp.stack([proj[:, :, :width], proj[:, :, width : 2 * width]], 1),
-        grad_state,
-        proj[:, :, 2 * width + 2 * N : 2 * width + 2 * N + heads],
-        jnp.stack(grads_output[::-1]).transpose(0, 2, 1),
-    ) + tuple(jnp.stack([layer_sums[i] for layer_sums in sums]) for i in range(6))
+        jnp.stack([jnp.stack([grad[:, :width], grad[:, width : 2 * width]]) for grad in grads]),
+        jnp.stack([group.sum_all(grad[:, 2 * width : state_end]) for grad in grads]),
+        jnp.stack([grad[:, state_end : state_end + heads] for grad in grads]),
+        jnp.stack([grad.astype(F32).T for grad in grads_output[::-1]]),
+    ) + tuple(jnp.stack([layer_sums[i] for layer_sums in small]) for i in range(6))
 
 
 def solution(mesh):

time: 1440 us -> 787 us (0.55)
  waiting for transfers between devices: 976 us -> 313 us
  starting transfers between devices: 1.42 us -> 25.5 us
  matrix products: 154 us -> 178 us
  blocking collectives: 19.2 us -> 0 us
    ppermute x0 -> x24, waiting for transfers between devices: none -> 264 us  [the longest x14 198 us: swap(): return lax.ppermute(values, 'tensor', [(0, 1), (1, 0)])]
    reduce_scatter x2, waiting for transfers between devices: 245 us -> 0.01 us  [per_device(): lax.psum_scatter(grad_projection, 'dp', scatter_dimension=0, tiled=True)]
    reduce_scatter x4 -> x0, waiting for transfers between devices: 161 us -> none  [scatter_rows(): return lax.psum_scatter(values, 'tensor', scatter_dimension=0, tiled=True)]
    all_gather x4 -> x0, waiting for transfers between devices: 158 us -> none  [gather_rows(): return lax.all_gather(values, 'tensor', axis=0, tiled=True)]
    reduce_scatter x2, waiting for transfers between devices: 149 us -> 0.01 us  [per_device(): lax.psum_scatter(grad_output, 'dp', scatter_dimension=0, tiled=True)]
    all_gather x2, waiting for transfers between devices: 176 us -> 46 us  [per_device(): projections.append(lax.all_gather(shard, 'dp', axis=0, tiled=True))]
    psum x2 -> x0, waiting for transfers between devices: 81.3 us -> none  [the longest x1 61.1 us: per_device(): flat = lax.psum(flat, ('dp', 'tensor')).reshape(-1)]
    ppermute x0 -> x24, starting transfers between devices: none -> 25.2 us  [the longest x14 19.4 us: swap(): return lax.ppermute(values, 'tensor', [(0, 1), (1, 0)])]
  transfers between devices with their start and end apart: 18 -> 32, of which waited for: 18 -> 18; matrix products, arithmetic and copies ran while one was open for 9% -> 28% of each run, Pallas kernels for 5% -> 24%
where the time goes in v2:
time: 787 us; the launch traced here: 778 us
  waiting for transfers between devices  313 us (40%)
  Pallas kernels  189 us (24%)
  matrix products  178 us (23%)
  other arithmetic  33.8 us (4%)
  starting transfers between devices  25.5 us (3%)
  local copies, waits for them, and re-layouts  22.2 us (3%)
  between operations  16.4 us (2%)
    ppermute x14, waiting for transfers between devices, swap(): return lax.ppermute(values, 'tensor', [(0, 1), (1, 0)])  198 us
    pallas_call x2, Pallas kernels, backward_mixer(): pl.pallas_call(backward_kernel, grid_spec=pltpu.PrefetchScalarGridSpec(nu...  118 us
    dot_general x8, matrix products, dot_nt(): lax.dot_general(a, b, (((1,), (1,)), ((), ())), preferred_element_type=F32)  75.3 us
    pallas_call x2, Pallas kernels, forward_mixer(): pl.pallas_call(forward_kernel, grid_spec=pltpu.PrefetchScalarGridSpec(num...  70.7 us
    dot_general x4, matrix products, dot_tn(): lax.dot_general(a, b, (((0,), (0,)), ((), ())), preferred_element_type=F32)  53.5 us
    dot_general x4, matrix products, dot_nn(): lax.dot_general(a, b, (((1,), (0,)), ((), ())), preferred_element_type=F32)  49.5 us
    all_gather x2, waiting for transfers between devices, per_device(): projections.append(lax.all_gather(shard, 'dp', axis=0, tiled=True))  46 us
    ppermute x2, waiting for transfers between devices, sum_everywhere(): values = values + lax.ppermute(values, 'tensor', [(0, 1), (1, 0)])  35.3 us
  transfers between devices with their start and end apart: 32, of which 18 were waited for; matrix products, arithmetic and copies ran while one was open for 28% of the time, Pallas kernels for 24%

profile of v2, /device:TPU:0, one launch (start us, length us, event | category | flops | bytes accessed | tf_op | source)
XLA Modules:
  0.0 778.1 jit_solution(10360042346738674275)
XLA Ops:
  19.3 33.6 %collective-permute-done = bf16[512,1536]{1,0:T(8,128)(2,1)S(1)} collective-permute-done((bf16[512,1536]{1,0:T(8,128)(2,1)}, bf16[512,1536]{1,0:T(8,128)(2,1)S(1)}, u32[]{:S(2)}, u32[]{:S(2)}) %collective-permute-start) | collective-permute-done | bytes 1572896 | tf_op jit(solution)/shard_map/ppermute | solution.py:400
  56.8 46.0 %all-gather.5.cloned.1.call-done.side_weight_ref = bf16[1536,3456]{1,0:T(8,128)(2,1)} async-done(((bf16[96,3456]{1,0:T(8,128)(2,1)}), bf16[1536,3456]{1,0:T(8,128)(2,1)}) %all-gather.5.cloned.1.call-update) | async-done | bytes 10616848 | tf_op jit(solution)/shard_map/all_gather | solution.py:505
  102.7 14.7 %fusion.4.gate_ref.value_ref = bf16[1024,3072]{1,0:T(8,128)(2,1)} fusion(bf16[1536,3456]{1,0:T(8,128)(2,1)} %all-gather.5.cloned.1.call-done.side_weight_ref, bf16[512,1536]{1,0:T(8,128)(2,1)S(1)} %collective-permute-done, bf16[512,1536]{1,0:T(8,128)(2,1)} %fusion.25), kind=kOutput, calls=%fused_computation.11 | convolution fusion | flops 9673113600 | bytes 18874368 | tf_op jit(solution)/shard_map/dot_general | solution.py:19
  117.4 35.4 %forward_mixer.2 = (bf16[1024,1536]{1,0:T(8,128)(2,1)}, bf16[1024,1536]{1,0:T(8,128)(2,1)}, bf16[1024,1536]{1,0:T(8,128)(2,1)}, f32[1024,640]{1,0:T(8,128)S(1)},...) custom-call(s32[1]{0:T(128)} %bitcast.1.turn_ref, bf16[1024,3072]{1,0:T(8,128)(2,1)} %fusion.4.gate_ref.value_ref, ...), custom_call_target="tpu_custom_call" | custom-call | flops 31457280000 | bytes 31457280 | tf_op jit(solution)/shard_map/forward_mixer/pallas_call | solution.py:302
  166.1 33.9 %collective-permute-done.2 = f32[1024,1]{0,1:T(1,128)S(1)} collective-permute-done((f32[1024,1]{0,1:T(1,128)S(1)}, f32[1024,1]{0,1:T(1,128)S(1)}, u32[]{:S(2)}, u32[]{:S(2)}) %collective-permute-start.2) | collective-permute-done | bytes 4128 | tf_op jit(solution)/shard_map/ppermute | solution.py:400
  212.2 34.6 %collective-permute-done.3 = bf16[512,1536]{1,0:T(8,128)(2,1)S(1)} collective-permute-done((bf16[512,1536]{1,0:T(8,128)(2,1)S(1)}, bf16[512,1536]{1,0:T(8,128)(2,1)S(1)}, u32[]{:S(2)}, u32[]{:S(2)}) %collective-permute-start.3) | collective-permute-done | bytes 1572896 | tf_op jit(solution)/shard_map/ppermute | solution.py:400
  249.8 15.7 %fusion.7.gate_ref.value_ref = bf16[1024,3072]{1,0:T(8,128)(2,1)} fusion(bf16[1536,3456]{1,0:T(8,128)(2,1)} %all-gather.9.cloned.1.call-done.side_weight_ref, bf16[512,1536]{1,0:T(8,128)(2,1)} %copy-done.20, bf16[512,1536]{1,0:T(8,128)(2,1)} %copy-done.14), kind=kOutput, calls=%fused_computation.12 | convolution fusion | flops 9673113600 | bytes 18874368 | tf_op jit(solution)/shard_map/dot_general | solution.py:19
  265.5 35.3 %forward_mixer.3 = (bf16[1024,1536]{1,0:T(8,128)(2,1)}, bf16[1024,1536]{1,0:T(8,128)(2,1)}, bf16[1024,1536]{1,0:T(8,128)(2,1)}, f32[1024,640]{1,0:T(8,128)S(1)},...) custom-call(s32[1]{0:T(128)} %bitcast.1.turn_ref, bf16[1024,3072]{1,0:T(8,128)(2,1)} %fusion.7.gate_ref.value_ref, ...), custom_call_target="tpu_custom_call" | custom-call | flops 31457280000 | bytes 31457280 | tf_op jit(solution)/shard_map/forward_mixer/pallas_call | solution.py:302
  305.2 9.8 %multiply_reduce_fusion = (f32[1024]{0:T(1024)S(1)}, bf16[1024,1536]{1,0:T(8,128)(2,1)}) fusion(bf16[1024,1536]{1,0:T(8,128)(2,1)} %get-tuple-element.38, bf16[1536,1536]{1,0:T(8,128)(2,1)} %all-gather.11.cloned.1.call-done, bf16[512,1536]{1,0:T(8,128)(2,1)} %collective-permute-done.6, bf16[512,1536]{1,0:T(8,128)(2,1)} %get-tuple-element.143), kind=kOutput, calls=%fused_computation.10 | convolution fusion | flops 4845992960 | bytes 14159872 | tf_op jit(solution)/shard_map/dot_general | solution.py:19
  329.0 59.2 %backward_mixer.2 = (bf16[1024,3456]{1,0:T(8,128)(2,1)}, f32[8,1536]{1,0:T(8,128)S(1)}, f32[8,256]{1,0:T(8,128)S(1)}, f32[8,128]{1,0:T(8,128)S(1)}) custom-call(s32[1]{0:T(128)} %bitcast.1.turn_ref, bf16[1024,3072]{1,0:T(8,128)(2,1)} %fusion.7.gate_ref.value_ref, bf16[1024,3072]{1,0:T(8,128)(2,1)} %fusion.7.gate_ref.value_ref, ...), custom_call_target="tpu_custom_call" | custom-call | flops 55050240000 | bytes 31457280 | tf_op jit(solution)/shard_map/backward_mixer/pallas_call | solution.py:350
  388.2 16.8 %convolution_convert_fusion.1 = bf16[1536,3456]{1,0:T(8,128)(2,1)} fusion(bf16[1024,3456]{1,0:T(8,128)(2,1)} %get-tuple-element.44, bf16[512,1536]{1,0:T(8,128)(2,1)S(1)} %copy-done.21, bf16[512,1536]{1,0:T(8,128)(2,1)S(1)} %copy-done.15), kind=kOutput, calls=%fused_computation.1 | convolution fusion | flops 10883235840 | bytes 20840448 | tf_op jit(solution)/shard_map/dot_general | solution.py:27
  405.1 10.8 %fusion.36 = bf16[512,1536]{1,0:T(8,128)(2,1)} fusion(bf16[1536,3456]{1,0:T(8,128)(2,1)} %all-gather.9.cloned.1.call-done.side_weight_ref, bf16[1024,3456]{1,0:T(8,128)(2,1)} %get-tuple-element.44), kind=kOutput, calls=%fused_computation.56 | convolution fusion | flops 5436604416 | bytes 15728640 | tf_op jit(solution)/shard_map/dot_general | solution.py:23
  418.1 30.8 %collective-permute-done.8 = bf16[512,1536]{1,0:T(8,128)(2,1)} collective-permute-done((bf16[512,1536]{1,0:T(8,128)(2,1)}, bf16[512,1536]{1,0:T(8,128)(2,1)}, u32[]{:S(2)}, u32[]{:S(2)}) %collective-permute-start.8) | collective-permute-done | bytes 1572896 | tf_op jit(solution)/shard_map/ppermute | solution.py:400
  448.9 11.3 %multiply_reduce_fusion.1 = (f32[1536]{0:T(1024)S(1)}, f32[512]{0:T(512)S(1)}, f32[512,1536]{1,0:T(8,128)S(1)}) fusion(f32[512,1536]{1,0:T(8,128)} %copy-done.12, f32[512]{0:T(512)S(1)} %copy-done.45, bf16[512,1536]{1,0:T(8,128)(2,1)} %collective-permute-done.8, f32[1536]{0:T(1024)S(1)} %copy-done.28, ...), kind=kOutput, calls=%fused_computation.44 | convolution fusion | flops 5442107392 | bytes 22036480 | tf_op jit(solution)/shard_map/dot_general | solution.py:23
  467.3 31.6 %collective-permute-done.11 = f32[168,128]{1,0:T(8,128)S(1)} collective-permute-done((f32[168,128]{1,0:T(8,128)S(1)}, f32[168,128]{1,0:T(8,128)S(1)}, u32[]{:S(2)}, u32[]{:S(2)}) %collective-permute-start.11) | collective-permute-done | bytes 86048 | tf_op jit(solution)/shard_map/ppermute | solution.py:453
  509.2 9.9 %collective-permute-done.14 = f32[168,128]{1,0:T(8,128)S(1)} collective-permute-done((f32[168,128]{1,0:T(8,128)S(1)}, f32[168,128]{1,0:T(8,128)S(1)}, u32[]{:S(2)}, u32[]{:S(2)}) %collective-permute-start.14) | collective-permute-done | bytes 86048 | tf_op jit(solution)/shard_map/ppermute | solution.py:456
  528.5 9.3 %convolution_convert_fusion.2 = bf16[1536,1536]{1,0:T(8,128)(2,1)} fusion(bf16[1024,1536]{1,0:T(8,128)(2,1)} %get-tuple-element.36, f32[1024]{0:T(1024)S(1)} %fusion.63, bf16[512,1536]{1,0:T(8,128)(2,1)} %collective-permute-done.9, bf16[512,1536]{1,0:T(8,128)(2,1)} %get-tuple-element.103), kind=kOutput, calls=%fused_computation.6 | convolution fusion | flops 4843634688 | bytes 11014144 | tf_op jit(solution)/shard_map/dot_general | solution.py:27
  537.9 9.4 %convolution_convert_fusion.4.dgn_ref = bf16[1024,1536]{1,0:T(8,128)(2,1)} fusion(bf16[1536,1536]{1,0:T(8,128)(2,1)} %all-gather.7.cloned.1.call-done, bf16[512,1536]{1,0:T(8,128)(2,1)} %collective-permute-done.9, bf16[512,1536]{1,0:T(8,128)(2,1)} %get-tuple-element.103), kind=kOutput, calls=%fused_computation.20 | convolution fusion | flops 4839702528 | bytes 11010048 | tf_op jit(solution)/shard_map/dot_general | solution.py:19
  547.3 58.9 %backward_mixer.3 = (bf16[1024,3456]{1,0:T(8,128)(2,1)}, f32[8,1536]{1,0:T(8,128)S(1)}, f32[8,256]{1,0:T(8,128)S(1)}, f32[8,128]{1,0:T(8,128)S(1)}) custom-call(s32[1]{0:T(128)} %bitcast.1.turn_ref, bf16[1024,3072]{1,0:T(8,128)(2,1)} %fusion.4.gate_ref.value_ref, bf16[1024,3072]{1,0:T(8,128)(2,1)} %fusion.4.gate_ref.value_ref, ...), custom_call_target="tpu_custom_call" | custom-call | flops 55050240000 | bytes 31457280 | tf_op jit(solution)/shard_map/backward_mixer/pallas_call | solution.py:350
  606.2 18.1 %convolution_convert_fusion = bf16[1536,3456]{1,0:T(8,128)(2,1)} fusion(bf16[1024,3456]{1,0:T(8,128)(2,1)} %get-tuple-element.53, bf16[512,1536]{1,0:T(8,128)(2,1)} %copy-done.19, bf16[512,1536]{1,0:T(8,128)(2,1)} %fusion.25), kind=kOutput, calls=%fused_computation | convolution fusion | flops 10883235840 | bytes 20840448 | tf_op jit(solution)/shard_map/dot_general | solution.py:27
  632.6 34.6 %collective-permute-done.4 = bf16[512,1536]{1,0:T(8,128)(2,1)S(1)} collective-permute-done((bf16[512,1536]{1,0:T(8,128)(2,1)}, bf16[512,1536]{1,0:T(8,128)(2,1)S(1)}, u32[]{:S(2)}, u32[]{:S(2)}) %collective-permute-start.4) | collective-permute-done | bytes 1572896 | tf_op jit(solution)/shard_map/ppermute | solution.py:400
  679.7 10.7 %fusion.39 = bf16[512,1536]{1,0:T(8,128)(2,1)} fusion(bf16[1536,3456]{1,0:T(8,128)(2,1)} %all-gather.5.cloned.1.call-done.side_weight_ref, bf16[1024,3456]{1,0:T(8,128)(2,1)} %get-tuple-element.53), kind=kOutput, calls=%fused_computation.57 | convolution fusion | flops 5436604416 | bytes 15728640 | tf_op jit(solution)/shard_map/dot_general | solution.py:23
  695.4 30.2 %collective-permute-done.16 = bf16[512,1536]{1,0:T(8,128)(2,1)} collective-permute-done((bf16[512,1536]{1,0:T(8,128)(2,1)}, bf16[512,1536]{1,0:T(8,128)(2,1)}, u32[]{:S(2)}, u32[]{:S(2)}) %collective-permute-start.16) | collective-permute-done | bytes 1572896 | tf_op jit(solution)/shard_map/ppermute | solution.py:400
  725.6 11.7 %fusion.30 = (f32[1536]{0:T(1024)S(1)}, f32[512]{0:T(512)S(1)}, f32[512,1536]{1,0:T(8,128)}) fusion(bf16[512,1536]{1,0:T(8,128)(2,1)S(1)} %copy-done.11, f32[512]{0:T(512)S(1)} %copy-done.43, f32[1536]{0:T(1024)S(1)} %copy-done.30, bf16[512,1536]{1,0:T(8,128)(2,1)} %collective-permute-done.16, ...), kind=kOutput, calls=%fused_computation.36 | convolution fusion | flops 5442893824 | bytes 20463616 | tf_op jit(solution)/shard_map/dot_general | solution.py:23
  (332 shorter events, 149.5 us)
Async XLA Ops:
  7.2 95.6 %all-gather.5.cloned.1.call-start = ((), (), s32[]{:S(2)}) async-start(), calls=%async_computation.4 | async-start | bytes 11280384 | tf_op jit(solution)/shard_map/all_gather | solution.py:505
  11.2 145.3 %all-gather.7.cloned.1.call-start = ((), (), s32[]{:S(2)}) async-start(), calls=%async_computation.5 | async-start | bytes 5013504 | tf_op jit(solution)/shard_map/all_gather | solution.py:506
  12.1 237.7 %all-gather.9.cloned.1.call-start = ((), (), s32[]{:S(2)}) async-start(), calls=%async_computation.6 | async-start | bytes 11280384 | tf_op jit(solution)/shard_map/all_gather | solution.py:505
  13.2 292.0 %all-gather.11.cloned.1.call-start = ((), (), s32[]{:S(2)}) async-start(), calls=%async_computation.7 | async-start | bytes 5013504 | tf_op jit(solution)/shard_map/all_gather | solution.py:506
  15.3 37.6 %collective-permute-start = (bf16[512,1536]{1,0:T(8,128)(2,1)}, bf16[512,1536]{1,0:T(8,128)(2,1)S(1)}, u32[]{:S(2)}, u32[]{:S(2)}) collective-permute-start(bf16[512,1536]{1,0:T(8,128)(2,1)} %fusion.25), channel_id=1, source_target_pairs={{0,1},{1,0},{2,3},{3,2},{4,5},{5,4},{6,7},{7,6},{8,9},{9,8},{10,11... | collective-permute-start | bytes 4718600 | tf_op jit(solution)/shard_map/ppermute | solution.py:400
  163.1 37.0 %collective-permute-start.1 = (bf16[512,1536]{1,0:T(8,128)(2,1)}, bf16[512,1536]{1,0:T(8,128)(2,1)}, u32[]{:S(2)}, u32[]{:S(2)}) collective-permute-start(bf16[512,1536]{1,0:T(8,128)(2,1)} %convolution_convert_fusion.7), channel_id=1, source_target_pairs={{0,1},{1,0},{2,3},{3,2},{4,5},{5,4},{6,7},{7,6},{8,9},{9,8},{10,11... | collective-permute-start | bytes 4718600 | tf_op jit(solution)/shard_map/ppermute | solution.py:400
  164.6 441.6 %reduce-scatter.5.cloned.1.call-start = ((), (), s32[]{:S(2)}) async-start(), calls=%async_computation.8 | async-start | bytes 5013504 | tf_op jit(solution)/shard_map/reduce_scatter | solution.py:570
  165.5 34.5 %collective-permute-start.2 = (f32[1024,1]{0,1:T(1,128)S(1)}, f32[1024,1]{0,1:T(1,128)S(1)}, u32[]{:S(2)}, u32[]{:S(2)}) collective-permute-start(f32[1024,1]{0,1:T(1,128)S(1)} %bitcast.154), channel_id=1, source_target_pairs={{0,1},{1,0},{2,3},{3,2},{4,5},{5,4},{6,7},{7,6},{8,9},{9,8},{10,11... | collective-permute-start | bytes 12296 | tf_op jit(solution)/shard_map/ppermute | solution.py:400
  209.4 37.4 %collective-permute-start.3 = (bf16[512,1536]{1,0:T(8,128)(2,1)S(1)}, bf16[512,1536]{1,0:T(8,128)(2,1)S(1)}, u32[]{:S(2)}, u32[]{:S(2)}) collective-permute-start(bf16[512,1536]{1,0:T(8,128)(2,1)S(1)} %multiply_convert_fusion.4), channel_id=1, source_target_pairs={{0,1},{1,0},{2,3},{3,2},{4,5},{5,4},{6,7},{7,6},{8,9},{9,8},{10,11... | collective-permute-start | bytes 4718600 | tf_op jit(solution)/shard_map/ppermute | solution.py:400
  211.0 94.2 %collective-permute-start.6 = (bf16[512,1536]{1,0:T(8,128)(2,1)}, bf16[512,1536]{1,0:T(8,128)(2,1)}, u32[]{:S(2)}, u32[]{:S(2)}) collective-permute-start(bf16[512,1536]{1,0:T(8,128)(2,1)} %get-tuple-element.143), channel_id=1, source_target_pairs={{0,1},{1,0},{2,3},{3,2},{4,5},{5,4},{6,7},{7,6},{8,9},{9,8},{10,11... | collective-permute-start | bytes 4718600 | tf_op jit(solution)/shard_map/ppermute | solution.py:400
  303.6 11.9 %collective-permute-start.5 = (f32[1024,1]{0,1:T(1,128)S(1)}, f32[1024,1]{0,1:T(1,128)S(1)}, u32[]{:S(2)}, u32[]{:S(2)}) collective-permute-start(f32[1024,1]{0,1:T(1,128)S(1)} %bitcast.156), channel_id=1, source_target_pairs={{0,1},{1,0},{2,3},{3,2},{4,5},{5,4},{6,7},{7,6},{8,9},{9,8},{10,11... | collective-permute-start | bytes 12296 | tf_op jit(solution)/shard_map/ppermute | solution.py:400
  315.1 9.8 %collective-permute-start.7 = (f32[1024,1]{0,1:T(1,128)S(1)}, f32[1024,1]{0,1:T(1,128)S(1)}, u32[]{:S(2)}, u32[]{:S(2)}) collective-permute-start(f32[1024,1]{0,1:T(1,128)S(1)} %bitcast.166), channel_id=1, source_target_pairs={{0,1},{1,0},{2,3},{3,2},{4,5},{5,4},{6,7},{7,6},{8,9},{9,8},{10,11... | collective-permute-start | bytes 12296 | tf_op jit(solution)/shard_map/ppermute | solution.py:400
  324.8 281.3 %reduce-scatter.7.cloned.1.call-start = ((), (), s32[]{:S(2)}) async-start(), calls=%async_computation.9 | async-start | bytes 11280384 | tf_op jit(solution)/shard_map/reduce_scatter | solution.py:584
  405.1 285.6 %reduce-scatter.11.cloned.1.call-start = ((), (), s32[]{:S(2)}) async-start(), calls=%async_computation.11 | async-start | bytes 5013504 | tf_op jit(solution)/shard_map/reduce_scatter | solution.py:570
  416.0 32.9 %collective-permute-start.8 = (bf16[512,1536]{1,0:T(8,128)(2,1)}, bf16[512,1536]{1,0:T(8,128)(2,1)}, u32[]{:S(2)}, u32[]{:S(2)}) collective-permute-start(bf16[512,1536]{1,0:T(8,128)(2,1)} %fusion.36), channel_id=1, source_target_pairs={{0,1},{1,0},{2,3},{3,2},{4,5},{5,4},{6,7},{7,6},{8,9},{9,8},{10,11... | collective-permute-start | bytes 4718600 | tf_op jit(solution)/shard_map/ppermute | solution.py:400
  465.1 63.4 %collective-permute-start.9 = (bf16[512,1536]{1,0:T(8,128)(2,1)}, bf16[512,1536]{1,0:T(8,128)(2,1)}, u32[]{:S(2)}, u32[]{:S(2)}) collective-permute-start(bf16[512,1536]{1,0:T(8,128)(2,1)} %get-tuple-element.103), channel_id=1, source_target_pairs={{0,1},{1,0},{2,3},{3,2},{4,5},{5,4},{6,7},{7,6},{8,9},{9,8},{10,11... | collective-permute-start | bytes 4718600 | tf_op jit(solution)/shard_map/ppermute | solution.py:400
  466.8 32.0 %collective-permute-start.11 = (f32[168,128]{1,0:T(8,128)S(1)}, f32[168,128]{1,0:T(8,128)S(1)}, u32[]{:S(2)}, u32[]{:S(2)}) collective-permute-start(f32[168,128]{1,0:T(8,128)S(1)} %pad_bitcast_fusion.1), channel_id=1, source_target_pairs={{0,1},{1,0},{2,3},{3,2},{4,5},{5,4},{6,7},{7,6},{8,9},{9,8},{10,11... | collective-permute-start | bytes 258056 | tf_op jit(solution)/shard_map/ppermute | solution.py:453
  498.9 10.3 %collective-permute-start.10 = (f32[512,1]{0,1:T(1,128)S(1)}, f32[512,1]{0,1:T(1,128)S(1)}, u32[]{:S(2)}, u32[]{:S(2)}) collective-permute-start(f32[512,1]{0,1:T(1,128)S(1)} %bitcast.164), channel_id=1, source_target_pairs={{0,1},{1,0},{2,3},{3,2},{4,5},{5,4},{6,7},{7,6},{8,9},{9,8},{10,11... | collective-permute-start | bytes 6152 | tf_op jit(solution)/shard_map/ppermute | solution.py:400
  507.7 11.4 %collective-permute-start.14 = (f32[168,128]{1,0:T(8,128)S(1)}, f32[168,128]{1,0:T(8,128)S(1)}, u32[]{:S(2)}, u32[]{:S(2)}) collective-permute-start(f32[168,128]{1,0:T(8,128)S(1)} %add.239), channel_id=1, source_target_pairs={{0,8},{2,10},{4,12},{6,14},{8,0},{10,2},{12,4},{14,6},{16,24},{18,... | collective-permute-start | bytes 258056 | tf_op jit(solution)/shard_map/ppermute | solution.py:456
  519.2 9.3 %collective-permute-start.15 = (f32[168,128]{1,0:T(8,128)S(1)}, f32[168,128]{1,0:T(8,128)S(1)}, u32[]{:S(2)}, u32[]{:S(2)}) collective-permute-start(f32[168,128]{1,0:T(8,128)S(1)} %add.240), channel_id=1, source_target_pairs={{0,16},{2,18},{4,20},{6,22},{8,24},{10,26},{12,28},{14,30},{16,0},... | collective-permute-start | bytes 258056 | tf_op jit(solution)/shard_map/ppermute | solution.py:456
  537.8 224.5 %reduce-scatter.9.cloned.1.call-start = ((), (), s32[]{:S(2)}) async-start(), calls=%async_computation.10 | async-start | bytes 11280384 | tf_op jit(solution)/shard_map/reduce_scatter | solution.py:584
  630.9 36.3 %collective-permute-start.4 = (bf16[512,1536]{1,0:T(8,128)(2,1)}, bf16[512,1536]{1,0:T(8,128)(2,1)S(1)}, u32[]{:S(2)}, u32[]{:S(2)}) collective-permute-start(bf16[512,1536]{1,0:T(8,128)(2,1)} %convolution_convert_fusion.6), channel_id=1, source_target_pairs={{0,1},{1,0},{2,3},{3,2},{4,5},{5,4},{6,7},{7,6},{8,9},{9,8},{10,11... | collective-permute-start | bytes 4718600 | tf_op jit(solution)/shard_map/ppermute | solution.py:400
  677.8 67.0 %collective-permute-start.18 = (f32[96,256]{1,0:T(8,128)S(1)}, f32[96,256]{1,0:T(8,128)S(1)}, u32[]{:S(2)}, u32[]{:S(2)}) collective-permute-start(f32[96,256]{1,0:T(8,128)S(1)} %slice.329), channel_id=1, source_target_pairs={{0,1},{1,0},{2,3},{3,2},{4,5},{5,4},{6,7},{7,6},{8,9},{9,8},{10,11... | collective-permute-start | bytes 294920 | tf_op jit(solution)/shard_map/ppermute | solution.py:400
  690.3 35.3 %collective-permute-start.16 = (bf16[512,1536]{1,0:T(8,128)(2,1)}, bf16[512,1536]{1,0:T(8,128)(2,1)}, u32[]{:S(2)}, u32[]{:S(2)}) collective-permute-start(bf16[512,1536]{1,0:T(8,128)(2,1)} %fusion.39), channel_id=1, source_target_pairs={{0,1},{1,0},{2,3},{3,2},{4,5},{5,4},{6,7},{7,6},{8,9},{9,8},{10,11... | collective-permute-start | bytes 4718600 | tf_op jit(solution)/shard_map/ppermute | solution.py:400
  (62 other events, 1469.0 us)
Sparse Core Ops, SparseCore 0:
  11.3 91.3 all-gather.4
  105.0 51.4 all-gather.6
  158.8 87.2 all-gather.8
  248.2 51.5 all-gather.10
  325.0 74.2 reduce-scatter.4
  405.2 123.4 reduce-scatter.6
  537.9 73.8 reduce-scatter.10
  624.4 118.5 reduce-scatter.8

commit v3 on v2

--- a/solution.py
+++ b/solution.py
@@ -3,6 +3,7 @@
 import jax.numpy as jnp
 from jax import lax
 from jax.experimental import pallas as pl
+from jax.experimental.layout import Layout, with_layout_constraint
 from jax.experimental.pallas import tpu as pltpu
 from jax.sharding import PartitionSpec as P
 
@@ -38,7 +39,7 @@
 
 
 def sigmoid(a):
-    return 1.0 / (1.0 + jnp.exp(-a))
+    return 0.5 * jnp.tanh(0.5 * a) + 0.5
 
 
 def iota(shape, dim):
@@ -97,16 +98,15 @@
     low_half = iota((1, PAIR), 1) < HEAD
 
     def one_pair(p, _):
-        lanes = pl.ds(pl.multiple_of(p * PAIR, PAIR), PAIR)
+        lanes = pl.ds(p * PAIR, PAIR)
         vbuf[8 : q + 8, lanes] = value_ref[:, lanes].astype(F32)
         pre = chan_ref[4:5, lanes] + chan_ref[3:4, lanes] * vbuf[8 : q + 8, lanes]
         for k in range(KCONV - 1):
             pre = pre + chan_ref[k : k + 1, lanes] * vbuf[5 + k : 5 + k + q, lanes]
         pre_ref[:, lanes] = pre.astype(BF16)
         x = pre * sigmoid(pre)
-        turn = lax.rem(128 - 2 * p, 128)
-        run_two = pltpu.roll(run_s[...], turn, 1)
-        step_two = pltpu.roll(step_s[...], turn, 1)
+        run_two = run_s[:, 2 * p : 2 * p + 2]
+        step_two = step_s[:, 2 * p : 2 * p + 2]
         run_a, run_b = run_two[:, 0:1], run_two[:, 1:2]
         run_pair = jnp.where(low_half, run_a, run_b)
         u = x * jnp.where(low_half, step_two[:, 0:1], step_two[:, 1:2])
@@ -130,7 +130,8 @@
         square_ref[...] += gated * gated
         return 0
 
-    lax.fori_loop(0, width // PAIR, one_pair, 0)
+    for p in range(width // PAIR):
+        one_pair(p, 0)
 
 
 def backward_kernel(
@@ -179,7 +180,7 @@
     head_lane = iota((1, 128), 1)
 
     def one_pair(p, _):
-        lanes = pl.ds(pl.multiple_of(p * PAIR, PAIR), PAIR)
+        lanes = pl.ds(p * PAIR, PAIR)
         inv = rows_ref[:, 0:1]
         pull = rows_ref[:, 1:2]
         gain = chan_ref[6:7, lanes]
@@ -191,7 +192,7 @@
         gated = scanned * silu_gate
         dgn = dgn_ref[:, lanes].astype(F32) * inv
         dgated = dgn * gain - gated * pull
-        dchan_ref[6:7, lanes] += jnp.sum(dgn * gated, 0, keepdims=True)
+        dchan_ref[5:6, lanes] += jnp.sum(dgn * gated, 0, keepdims=True)
         dy = dgated * silu_gate
         low_ref[:, lanes] = (
             dgated * scanned * (sig_gate + silu_gate * (1.0 - sig_gate))
@@ -199,10 +200,9 @@
         pre = pre_ref[:, lanes].astype(F32)
         sig_pre = sigmoid(pre)
         x = pre * sig_pre
-        dchan_ref[5:6, lanes] += jnp.sum(x * dy, 0, keepdims=True)
-        turn = lax.rem(128 - 2 * p, 128)
-        run_two = pltpu.roll(run_s[...], turn, 1)
-        step_two = pltpu.roll(step_s[...], turn, 1)
+        dchan_ref[6:7, lanes] += jnp.sum(x * dy, 0, keepdims=True)
+        run_two = run_s[:, 2 * p : 2 * p + 2]
+        step_two = step_s[:, 2 * p : 2 * p + 2]
         run_a, run_b = run_two[:, 0:1], run_two[:, 1:2]
         run_pair = jnp.where(low_half, run_a, run_b)
         step_pair = jnp.where(low_half, step_two[:, 0:1], step_two[:, 1:2])
@@ -254,10 +254,11 @@
             later = gbuf[3 - k : 3 - k + q, lanes]
             dv = dv + chan_ref[k : k + 1, lanes] * later
             dchan_ref[k : k + 1, lanes] += jnp.sum(value * later, 0, keepdims=True)
-        low_ref[:, pl.ds(pl.multiple_of(width + p * PAIR, PAIR), PAIR)] = dv.astype(BF16)
+        low_ref[:, pl.ds(width + p * PAIR, PAIR)] = dv.astype(BF16)
         return 0
 
-    lax.fori_loop(0, width // PAIR, one_pair, 0)
+    for p in range(width // PAIR):
+        one_pair(p, 0)
 
     dcbt_low = dcbt[...].astype(BF16)
     dconv = jnp.concatenate(
@@ -385,11 +386,463 @@
         cost_estimate=pl.CostEstimate(flops=rows * width * 35000, bytes_accessed=rows * width * 20, transcendentals=0),
         name="backward_mixer",
     )(turn, projected, projected, pre, scanned, dgn, side, states, rows_in, chan, state_taps, headp)
-
-
+CHUNK = 384
 LAYERS = 2
+
+
+def scatter_product_kernel(
+    first, chunks, left_ref, right_ref, out_left_ref, out_right_ref, layer_ref, out_layer_ref, small_ref, rows_ref,
+    wide_ref, side_ref, out_ref, total_ref, rows_come,
+    rows_ss, rows_rs, small_come, small_ss, small_rs,
+    keep0, keep1, keep2, send0, send1, send2, come0, come1, come2, ss0, rs0, ss1, rs1, ss2, rs2,
+):
+    k = pl.program_id(0)
+    me = lax.axis_index("dp")
+    tensor = lax.axis_index("tensor")
+    core, x_bit, z = lax.rem(me, 2), lax.rem(me // 2, 2), me // 4
+    rows = layer_ref.shape[0]
+    core_peer = me + 1 - 2 * core
+    x_peer = me + 2 - 4 * x_bit
+    z_peers = [lax.rem(me + 4 * (j + 1), 16) for j in range(3)]
+
+    def by_core(c):
+        return pltpu.make_async_remote_copy(
+            src_ref=send0.at[c], dst_ref=come0.at[c], send_sem=ss0.at[c], recv_sem=rs0.at[c],
+            device_id=(core_peer, tensor), device_id_type=pl.DeviceIdType.MESH,
+        )
+
+    def by_x(c):
+        return pltpu.make_async_remote_copy(
+            src_ref=send1.at[c], dst_ref=come1.at[c], send_sem=ss1.at[c], recv_sem=rs1.at[c],
+            device_id=(x_peer, tensor), device_id_type=pl.DeviceIdType.MESH,
+        )
+
+    def by_z(c, j):
+        return pltpu.make_async_remote_copy(
+            src_ref=send2.at[c, lax.rem(z + j + 1, 4)], dst_ref=come2.at[c, j],
+            send_sem=ss2.at[c, j], recv_sem=rs2.at[c, j],
+            device_id=(z_peers[j], tensor), device_id_type=pl.DeviceIdType.MESH,
+        )
+
+    small_peers = [(me, 1 - tensor), (core_peer, tensor), (x_peer, tensor)] + [
+        (lax.rem(me, 4) + 4 * (z + bit - 2 * bit * lax.rem(z // bit, 2)), tensor) for bit in (1, 2)
+    ]
+
+    def by_all(stage):
+        return pltpu.make_async_remote_copy(
+            src_ref=total_ref.at[stage], dst_ref=small_come.at[stage],
+            send_sem=small_ss.at[stage], recv_sem=small_rs.at[stage],
+            device_id=small_peers[stage], device_id_type=pl.DeviceIdType.MESH,
+        )
+
+    by_tensor = pltpu.make_async_remote_copy(
+        src_ref=rows_ref, dst_ref=rows_come, send_sem=rows_ss, recv_sem=rows_rs,
+        device_id=(me, 1 - tensor), device_id_type=pl.DeviceIdType.MESH,
+    )
+
+    @pl.when(k == 0)
+    def _():
+        total_ref[0] = small_ref[...]
+        barrier = pltpu.get_barrier_semaphore()
+        for peer in [(core_peer, tensor), (x_peer, tensor), (me, 1 - tensor)] + [(p, tensor) for p in z_peers]:
+            pl.semaphore_signal(barrier, inc=1, device_id=peer, device_id_type=pl.DeviceIdType.MESH)
+        pl.semaphore_wait(barrier, 6)
+        by_all(0).start()
+        by_tensor.start()
+
+    def multiply(left, right):
+        def tile(m, _):
+            part = dot_nn(left[pl.ds(m * 2 * rows, 2 * rows), :], right[...])
+            even, odd = part[:rows], part[rows:]
+            keep0[lax.rem(k, 2), m] = jnp.where(core == 0, even, odd)
+            send0[k, m] = jnp.where(core == 0, odd, even).astype(BF16)
+            return 0
+
+        lax.fori_loop(0, 8, tile, 0)
+        by_core(k).start()
+
+    @pl.when(k < first)
+    def _():
+        multiply(left_ref, right_ref)
+
+    @pl.when((k >= first) & (k < chunks))
+    def _():
+        multiply(out_left_ref, out_right_ref)
+
+    @pl.when((k >= 1) & (k < chunks + 1))
+    def _():
+        c = k - 1
+        by_core(c).wait_recv()
+
+        def tile(m, _):
+            keep1[lax.rem(c, 3), m] = keep0[lax.rem(c, 2), 2 * m + x_bit] + come0[c, 2 * m + x_bit].astype(F32)
+            send1[c, m] = (
+                keep0[lax.rem(c, 2), 2 * m + 1 - x_bit] + come0[c, 2 * m + 1 - x_bit].astype(F32)
+            ).astype(BF16)
+            return 0
+
+        lax.fori_loop(0, 4, tile, 0)
+        by_x(c).start()
+
+    @pl.when((k >= 3) & (k < chunks + 3))
+    def _():
+        c = k - 3
+        by_x(c).wait_recv()
+
+        def tile(m, _):
+            total = keep1[lax.rem(c, 3), m] + come1[c, m].astype(F32)
+            keep2[lax.rem(c, 3), m] = total
+            send2[c, m] = total.astype(BF16)
+            return 0
+
+        lax.fori_loop(0, 4, tile, 0)
+        for j in range(3):
+            by_z(c, j).start()
+
+    @pl.when(k >= 5)
+    def _():
+        c = k - 5
+        total = keep2[lax.rem(c, 3), z]
+        for j in range(3):
+            by_z(c, j).wait_recv()
+            total = total + come2[c, j].astype(F32)
+
+        @pl.when(c < first - 1)
+        def _():
+            wide_ref[0, 0] = total
+            wide_ref[1, 0] = layer_ref[...].astype(F32)
+
+        @pl.when(c == first - 1)
+        def _():
+            side_ref[0] = total
+            side_ref[1] = layer_ref[...].astype(F32)
+
+        @pl.when(c >= first)
+        def _():
+            out_ref[0] = total.T
+            out_ref[1] = out_layer_ref[...].astype(F32).T
+
+    for stage in range(5):
+
+        @pl.when(k == 2 * stage + 2)
+        def _():
+            by_all(stage).wait_recv()
+            total_ref[stage + 1] = total_ref[stage] + small_come[stage]
+            if stage < 4:
+                by_all(stage + 1).start()
+
+    @pl.when(k == chunks + 4)
+    def _():
+        by_tensor.wait()
+        for stage in range(5):
+            by_all(stage).wait_send()
+
+        def done(c, _):
+            by_core(c).wait_send()
+            by_x(c).wait_send()
+            for j in range(3):
+                by_z(c, j).wait_send()
+            return 0
+
+        lax.fori_loop(0, chunks, done, 0)
+
+
+def scatter_product(left, right, out_left, out_right, layer, out_layer, small, sent, collective):
+    depth, tokens = left.shape
+    width = out_right.shape[1]
+    first, second = right.shape[1] // CHUNK, width // CHUNK
+    chunks = first + second
+    rows = depth // 16
+    once = pl.Buffered(1)
+    anywhere = pl.BlockSpec(memory_space=pl.ANY)
+    done = lambda k, start, count: jnp.clip(k - start, 0, count - 1)
+    return pl.pallas_call(
+        functools.partial(scatter_product_kernel, first, chunks),
+        grid=(chunks + 5,),
+        in_specs=[
+            pl.BlockSpec((depth, tokens), lambda k: (0, 0), pipeline_mode=once),
+            pl.BlockSpec((tokens, CHUNK), lambda k: (0, done(k, 0, first))),
+            pl.BlockSpec((depth, tokens), lambda k: (0, 0), pipeline_mode=once),
+            pl.BlockSpec((tokens, CHUNK), lambda k: (0, done(k, first, second))),
+            pl.BlockSpec((rows, CHUNK), lambda k: (0, done(k, 5, first))),
+            pl.BlockSpec((rows, CHUNK), lambda k: (0, done(k, 5 + first, second))),
+            pl.BlockSpec(small.shape, lambda k: (0, 0), pipeline_mode=once),
+            anywhere,
+        ],
+        out_specs=[
+            pl.BlockSpec(
+                (LAYERS, 1, rows, CHUNK),
+                lambda k: (0, done(k, 5, first - 1) // second, 0, lax.rem(done(k, 5, first - 1), second)),
+            ),
+            pl.BlockSpec((LAYERS, rows, CHUNK), lambda k: (0, 0, 0)),
+            pl.BlockSpec((LAYERS, CHUNK, rows), lambda k: (0, done(k, 5 + first, second), 0)),
+            pl.BlockSpec((6,) + small.shape, lambda k: (0, 0, 0)),
+            anywhere,
+        ],
+        out_shape=[
+            jax.ShapeDtypeStruct((LAYERS, 2, rows, width), F32),
+            jax.ShapeDtypeStruct((LAYERS, rows, CHUNK), F32),
+            jax.ShapeDtypeStruct((LAYERS, width, rows), F32),
+            jax.ShapeDtypeStruct((6,) + small.shape, F32),
+            jax.ShapeDtypeStruct(sent.shape, sent.dtype),
+        ],
+        scratch_shapes=[
+            pltpu.SemaphoreType.DMA, pltpu.SemaphoreType.DMA,
+            pltpu.VMEM((5,) + small.shape, F32),
+            pltpu.SemaphoreType.DMA((5,)), pltpu.SemaphoreType.DMA((5,)),
+            pltpu.VMEM((2, 8, rows, CHUNK), F32),
+            pltpu.VMEM((3, 4, rows, CHUNK), F32),
+            pltpu.VMEM((3, 4, rows, CHUNK), F32),
+            pltpu.VMEM((chunks, 8, rows, CHUNK), BF16),
+            pltpu.VMEM((chunks, 4, rows, CHUNK), BF16),
+            pltpu.VMEM((chunks, 4, rows, CHUNK), BF16),
+            pltpu.VMEM((chunks, 8, rows, CHUNK), BF16),
+            pltpu.VMEM((chunks, 4, rows, CHUNK), BF16),
+            pltpu.VMEM((chunks, 3, rows, CHUNK), BF16),
+            pltpu.SemaphoreType.DMA((chunks,)), pltpu.SemaphoreType.DMA((chunks,)),
+            pltpu.SemaphoreType.DMA((chunks,)), pltpu.SemaphoreType.DMA((chunks,)),
+            pltpu.SemaphoreType.DMA((chunks, 3)), pltpu.SemaphoreType.DMA((chunks, 3)),
+        ],
+        compiler_params=pltpu.CompilerParams(
+            collective_id=collective, has_side_effects=True, vmem_limit_bytes=56 << 20
+        ),
+        cost_estimate=pl.CostEstimate(flops=90_000_000_000, bytes_accessed=20_000_000, transcendentals=0),
+        name="scatter_product",
+    )(left, right, out_left, out_right, layer, out_layer, small, sent)
+
+
+def last_sums_kernel(
+    pre_ref, total_ref, side_ref, pre_out, taps_out, decay_out, bias_out, skip_out, gain_out, state_out, step_out,
+    held, come, sent, side_come, ss, rs, side_ss, side_rs,
+):
+    me = lax.axis_index("dp")
+    tensor = lax.axis_index("tensor")
+    near = me // 4 * 4
+    peers = [(near + lax.rem(me + i, 4), lax.rem(tensor + j, 2)) for i in range(4) for j in range(2)][1:]
+    peers += [(lax.rem(me + 4 * j, 16), tensor) for j in (1, 2, 3)]
+    barrier = pltpu.get_barrier_semaphore()
+    for peer in peers:
+        pl.semaphore_signal(barrier, inc=1, device_id=peer, device_id_type=pl.DeviceIdType.MESH)
+    sent[...] = side_ref[:, :, : 2 * N]
+    held[0] = pre_ref[...]
+    pl.semaphore_wait(barrier, len(peers))
+    swap = pltpu.make_async_remote_copy(
+        src_ref=sent, dst_ref=side_come, send_sem=side_ss, recv_sem=side_rs,
+        device_id=(me, 1 - tensor), device_id_type=pl.DeviceIdType.MESH,
+    )
+    swap.start()
+    total = held[0]
+    for first, last, level in ((0, 7, 0), (7, 10, 1)):
+        copies = [
+            pltpu.make_async_remote_copy(
+                src_ref=held.at[level], dst_ref=come.at[i], send_sem=ss.at[i], recv_sem=rs.at[i],
+                device_id=peers[i], device_id_type=pl.DeviceIdType.MESH,
+            )
+            for i in range(first, last)
+        ]
+        for copy in copies:
+            copy.start()
+        if level == 0:
+            for layer in range(LAYERS):
+                rows = 8 * layer
+                taps_out[layer] = total_ref[rows : rows + taps_out.shape[1], :]
+                gain_out[layer : layer + 1, :] = total_ref[rows + 5 : rows + 6, 0 : gain_out.shape[1]]
+                pre_out[layer : layer + 1, :] = total_ref[rows + 6 : rows + 7, 0 : pre_out.shape[1]]
+                for i, out in enumerate((decay_out, bias_out, skip_out)):
+                    out[layer : layer + 1, :] = total_ref[rows + 7 : rows + 8, 128 * i : 128 * i + out.shape[1]]
+            step_out[...] = side_ref[:, :, 2 * N : 2 * N + step_out.shape[2]]
+        for copy in copies:
+            copy.wait()
+        for i in range(first, last):
+            total = total + come[i]
+        held[level + 1] = total
+    pre_out[0:1, :] = total[0:1, :]
+    swap.wait()
+    state_out[...] = sent[...] + side_come[...]
+
+
+def last_sums(pre, total, side, heads, all_heads, collective):
+    depth, inner = pre.shape[1], total.shape[1] - 2 * N
+    shapes = [(LAYERS, depth), (LAYERS, KCONV + 1, total.shape[1])] + [(LAYERS, all_heads)] * 3
+    shapes += [(LAYERS, inner), side.shape[:2] + (2 * N,), side.shape[:2] + (heads,)]
+    vmem = pl.BlockSpec(memory_space=pltpu.VMEM)
+    return pl.pallas_call(
+        last_sums_kernel,
+        in_specs=[vmem] * 3,
+        out_specs=[vmem] * len(shapes),
+        out_shape=[jax.ShapeDtypeStruct(shape, F32) for shape in shapes],
+        scratch_shapes=[
+            pltpu.VMEM((3,) + pre.shape, F32), pltpu.VMEM((10,) + pre.shape, F32),
+            pltpu.VMEM(shapes[-2], F32), pltpu.VMEM(shapes[-2], F32),
+            pltpu.SemaphoreType.DMA((10,)), pltpu.SemaphoreType.DMA((10,)),
+            pltpu.SemaphoreType.DMA, pltpu.SemaphoreType.DMA,
+        ],
+        compiler_params=pltpu.CompilerParams(collective_id=collective, has_side_effects=True),
+        name="last_sums",
+    )(pre, total, side)
+
+
+def gather_kernel(count, *refs):
+    shard_ref, swap_refs, full_ref, come_refs = refs[0], refs[1 : 1 + count], refs[1 + count], refs[2 + count : 2 + 2 * count]
+    local, zs, zr, xs, xr, cs, cr, ys, yr = refs[2 + 2 * count :]
+    me = lax.axis_index("dp")
+    tensor = lax.axis_index("tensor")
+    core, x_bit, z = lax.rem(me, 2), lax.rem(me // 2, 2), me // 4
+    rows = shard_ref.shape[0]
+    core_peer, x_peer = me + 1 - 2 * core, me + 2 - 4 * x_bit
+
+    def place(block_z, block_x):
+        return full_ref.at[pl.ds(pl.multiple_of(((block_z * 2 + block_x) * 2 + core) * rows, rows), rows), :]
+
+    def remote(source, target, send, receive, device):
+        return pltpu.make_async_remote_copy(
+            src_ref=source, dst_ref=target, send_sem=send, recv_sem=receive,
+            device_id=device, device_id_type=pl.DeviceIdType.MESH,
+        )
+
+    def along(block_z, up):
+        source = shard_ref if block_z is z else place(block_z, x_bit)
+        return remote(
+            source, place(block_z, x_bit), zs.at[up, block_z], zr.at[block_z], (me + 8 * up - 4, tensor)
+        )
+
+    def by_x(block_z):
+        source = shard_ref if block_z is z else place(block_z, x_bit)
+        return remote(source, place(block_z, x_bit), xs.at[block_z], xr.at[block_z], (x_peer, tensor))
+
+    def by_core(block_z, block_x):
+        source = shard_ref if block_z is z and block_x is x_bit else place(block_z, block_x)
+        return remote(
+            source, place(block_z, block_x), cs.at[block_z, block_x], cr.at[block_z, block_x], (core_peer, tensor)
+        )
+
+    barrier = pltpu.get_barrier_semaphore()
+    for peer in [(core_peer, tensor), (x_peer, tensor), (me, 1 - tensor)]:
+        pl.semaphore_signal(barrier, inc=1, device_id=peer, device_id_type=pl.DeviceIdType.MESH)
+    for up, there in ((1, z < 3), (0, z > 0)):
+
+        @pl.when(there)
+        def _():
+            pl.semaphore_signal(
+                barrier, inc=1, device_id=(me + 8 * up - 4, tensor), device_id_type=pl.DeviceIdType.MESH
+            )
+
+    pl.semaphore_wait(barrier, 3 + (z < 3).astype(jnp.int32) + (z > 0).astype(jnp.int32))
+
+    def each_way(action, step):
+        @pl.when(z >= step)
+        def _():
+            action(z - step, 1, z < 3)
+
+        @pl.when(z + step <= 3)
+        def _():
+            action(z + step, 0, z > 0)
+
+    @pl.when(z < 3)
+    def _():
+        along(z, 1).start()
+
+    @pl.when(z > 0)
+    def _():
+        along(z, 0).start()
+
+    by_x(z).start()
+    by_core(z, x_bit).start()
+    half = come_refs[0].shape[0] // 2
+    swaps = [
+        remote(
+            target.at[pl.ds(0, half), :], target.at[pl.ds(half, half), :], ys.at[i], yr.at[i], (me, 1 - tensor)
+        )
+        for i, target in enumerate(come_refs)
+    ]
+    for swap in swaps:
+        swap.start()
+    mine = pltpu.make_async_copy(shard_ref, place(z, x_bit), local)
+    mine.start()
+
+    def arrived(block_z, up, further):
+        along(block_z, up).wait_recv()
+
+        @pl.when(further)
+        def _():
+            along(block_z, up).start()
+
+        by_x(block_z).start()
+        by_core(block_z, x_bit).start()
+
+    def crossed(block_z, up, further):
+        by_x(block_z).wait_recv()
+        by_core(block_z, 1 - x_bit).start()
+
+    for step in (1, 2, 3):
+        each_way(arrived, step)
+        if step == 1:
+            crossed(z, 0, False)
+        else:
+            each_way(crossed, step - 1)
+    each_way(crossed, 3)
+
+    def finish(block_z, up, further):
+        by_x(block_z).wait_send()
+
+        @pl.when(further)
+        def _():
+            along(block_z, up).wait_send()
+
+    for step in (1, 2, 3):
+        each_way(finish, step)
+    by_x(z).wait_send()
+
+    @pl.when(z < 3)
+    def _():
+        along(z, 1).wait_send()
+
+    @pl.when(z > 0)
+    def _():
+        along(z, 0).wait_send()
+
+    for block_z in range(4):
+        for block_x in range(2):
+            by_core(block_z, block_x).wait()
+    mine.wait()
+    for swap in swaps:
+        swap.wait()
+
+
+def gather_all(shard, swapped, collective):
+    rows, columns = shard.shape
+    anywhere = pl.BlockSpec(memory_space=pl.ANY)
+    count = len(swapped)
+    return pl.pallas_call(
+        functools.partial(gather_kernel, count),
+        in_specs=[anywhere] * (1 + count),
+        out_specs=[anywhere] * (1 + count),
+        out_shape=[jax.ShapeDtypeStruct((16 * rows, columns), shard.dtype)]
+        + [jax.ShapeDtypeStruct(values.shape, values.dtype) for values in swapped],
+        scratch_shapes=[
+            pltpu.SemaphoreType.DMA,
+            pltpu.SemaphoreType.DMA((2, 4)), pltpu.SemaphoreType.DMA((4,)),
+            pltpu.SemaphoreType.DMA((4,)), pltpu.SemaphoreType.DMA((4,)),
+            pltpu.SemaphoreType.DMA((4, 2)), pltpu.SemaphoreType.DMA((4, 2)),
+            pltpu.SemaphoreType.DMA((count,)), pltpu.SemaphoreType.DMA((count,)),
+        ],
+        input_output_aliases={1 + i: 1 + i for i in range(count)},
+        compiler_params=pltpu.CompilerParams(collective_id=collective, has_side_effects=True),
+        cost_estimate=pl.CostEstimate(flops=60_000_000_000, bytes_accessed=20_000_000, transcendentals=0),
+        name="gather_all",
+    )(shard, *swapped)
+
+
 EPSILON = 1e-05
-BLOCK = 256
+BLOCK = 128
+
+
+def rowwise(values):
+    return with_layout_constraint(values, Layout(tuple(range(values.ndim))))
+
+
+def after(values, *others):
+    return lax.optimization_barrier((values,) + others)[0]
 
 
 class Pair:
@@ -412,9 +865,14 @@
         there = self.swap(values)
         return values + jnp.concatenate([there[self.rows :], there[: self.rows]], 0)
 
-    def project(self, function, values):
-        sent = self.swap(function(values[self.rows :]).astype(BF16))
-        return function(values[: self.rows]) + sent.astype(F32)
+    def project(self, function, values, exchange=None, *beside):
+        if not beside and exchange is None:
+            both = rowwise(function(values))
+            return rowwise(both[: self.rows] + self.swap(both[self.rows :].astype(BF16)).astype(F32))
+        sent = rowwise(function(values[self.rows :]).astype(BF16))
+        come = (exchange or self.swap)(sent)
+        mine = after(rowwise(function(values[: self.rows])), *beside)
+        return rowwise(mine + come.astype(F32))
 
     def sum_all(self, values):
         return values + self.swap(values)
@@ -437,7 +895,7 @@
     def total(self, values):
         return lax.psum(values, "tensor")
 
-    def project(self, function, values):
+    def project(self, function, values, exchange=None, *beside):
         return lax.psum_scatter(
             function(values).astype(BF16), "tensor", scatter_dimension=0, tiled=True
         ).astype(F32)
@@ -446,16 +904,12 @@
         return lax.psum(values, "tensor")
 
 
-def sum_everywhere(values):
-    size = lax.axis_size("dp")
-    if lax.axis_size("tensor") != 2 or size & (size - 1):
-        return lax.psum(values, ("dp", "tensor"))
-    values = values + lax.ppermute(values, "tensor", [(0, 1), (1, 0)])
-    bit = 1
-    while bit < size:
-        values = values + lax.ppermute(values, "dp", [(i, i ^ bit) for i in range(size)])
-        bit *= 2
-    return values
+def scatter_call(values):
+    return lax.psum_scatter(values, "dp", scatter_dimension=0, tiled=True)
+
+
+def after(values, *others):
+    return lax.optimization_barrier((values,) + others)[0]
 
 
 def per_device(
@@ -483,6 +937,7 @@
     head_start = tensor_index * heads
     lane_start = tensor_index * width
     q = min(BLOCK, local_rows * tensor_size)
+    fused = tensor_size == 2 and lax.axis_size("dp") == 16 and (2 * width + SIDE) % CHUNK == 0
     group = (Pair if tensor_size == 2 and local_rows % q == 0 else Group)(local_rows)
     turn = group.turn(q).astype(jnp.int32).reshape(1)
     position = tensor_index * local_rows + jnp.arange(local_rows)
@@ -491,9 +946,13 @@
     def part(table, start, size, axis=0):
         return lax.dynamic_slice_in_dim(table, start, size, axis)
 
-    projections, outputs = [], []
-    for layer in range(LAYERS):
-        shard = jnp.concatenate(
+    hidden = hidden_in.astype(F32)
+    inv_rows = lax.rsqrt(jnp.mean(hidden * hidden, axis=-1, keepdims=True) + EPSILON)
+    normed = rowwise((hidden * inv_rows * pre_gain[0]).astype(BF16))
+    last_mix = keep_rows * cotangent.astype(F32)
+    last_mix_low = rowwise(last_mix.astype(BF16))
+    shards = [
+        jnp.concatenate(
             [
                 gate_value_weight[layer, 0],
                 gate_value_weight[layer, 1],
@@ -502,8 +961,22 @@
             ],
             axis=1,
         )
-        projections.append(lax.all_gather(shard, "dp", axis=0, tiled=True))
-        outputs.append(lax.all_gather(out_weight[layer].T, "dp", axis=0, tiled=True))
+        for layer in range(LAYERS)
+    ]
+    projections, outputs = [], []
+    for layer in range(LAYERS):
+        if layer == 0 and fused:
+            full, first_normed_all, last_mix_all = gather_all(
+                shards[0], [jnp.pad(rows, ((0, local_rows), (0, 0))) for rows in (normed, last_mix_low)], 5
+            )
+        else:
+            shard = after(shards[layer], projections[0]) if layer > 0 else shards[layer]
+            full = lax.all_gather(shard, "dp", axis=0, tiled=True)
+        projections.append(full)
+        shard = after(out_weight[layer].T, projections[0])
+        outputs.append(lax.all_gather(shard, "dp", axis=0, tiled=True))
+    if not fused:
+        first_normed_all, last_mix_all = group.gather(normed), group.gather(last_mix_low)
 
     tables = []
     for layer in range(LAYERS):
@@ -529,32 +1002,63 @@
         )
         tables.append((chan, state_taps, headp))
 
-    last_mix = keep_rows * cotangent.astype(F32)
-    last_mix_all = group.gather(last_mix.astype(BF16))
-    hidden = hidden_in.astype(F32)
     saved = []
     for layer in range(LAYERS):
         chan, state_taps, headp = tables[layer]
-        inv_rows = lax.rsqrt(jnp.mean(hidden * hidden, axis=-1, keepdims=True) + EPSILON)
-        normed = (hidden * inv_rows * pre_gain[layer]).astype(BF16)
-        normed_all = group.gather(normed)
+        normed_all = first_normed_all
+        if layer > 0:
+            inv_rows = lax.rsqrt(jnp.mean(hidden * hidden, axis=-1, keepdims=True) + EPSILON)
+            normed = rowwise((hidden * inv_rows * pre_gain[layer]).astype(BF16))
+            normed_all = group.gather(normed)
         projected = dot_nn(normed_all, projections[layer][:, : 2 * width]).astype(BF16)
         gnl, scanned, pre, side, states, squares = forward_mixer(
             turn, projected, normed_all, projections[layer], chan, state_taps, headp, q, width
         )
+        if layer == 0 and fused:
+            normed_turned = normed_all.T
+            gnl = after(gnl, normed_turned)
         square_sum = group.total(jnp.sum(squares, axis=-1, keepdims=True))
         inv_gate = lax.rsqrt(square_sum / inner + EPSILON)
-        mixed_raw = group.project(lambda rows: dot_nt(rows, outputs[layer]), gnl)
+        mixed_raw = None
+        if layer < LAYERS - 1:
+            mixed_raw = group.project(lambda rows: dot_nt(rows, outputs[layer]), gnl)
         saved.append(
             (hidden, inv_rows, normed_all, projected, gnl, scanned, pre, side, states, inv_gate, mixed_raw)
         )
-        hidden = keep_rows * (hidden + mixed_raw * group.own(inv_gate))
-    out_hidden = hidden
+        if layer < LAYERS - 1:
+            hidden = rowwise(keep_rows * (hidden + mixed_raw * group.own(inv_gate)))
+
+    def last_hidden(low_gradient, gathered):
+        hidden, gnl, inv_gate = saved[-1][0], saved[-1][4], saved[-1][9]
+        swap = group.swap if tensor_size == 2 else None
+        mixed_raw = group.project(
+            lambda rows: dot_nt(rows, outputs[-1]),
+            after(gnl, low_gradient),
+            lambda sent: swap(after(sent, gathered)),
+        )
+        return keep_rows * (hidden + mixed_raw * group.own(inv_gate))
 
     grad_mix, mix_all = last_mix, last_mix_all
-    grads_projection, grads_output, sums = [], [], []
+    grads_projection, grads_output, small, pre_sums = [], [], [], []
     count = KCONV + 1
-    held = None
+    product = None
+
+    def small_of(dchan, dstate, dhead, grad_pre):
+        lanes = lax.dynamic_update_slice(jnp.zeros((6, inner), F32), dchan[:6], (0, lane_start))
+        skips = dchan[6].reshape(heads, HEAD).sum(axis=1)
+        per_head = lax.dynamic_update_slice(
+            jnp.zeros((3, 128), F32), jnp.stack([dhead[0, :heads], dhead[1, :heads], skips]), (0, head_start)
+        ).reshape(1, -1)
+        columns = inner + 2 * N
+        return jnp.concatenate(
+            [
+                jnp.concatenate([lanes, dstate[:6]], 1),
+                jnp.pad(grad_pre[None], ((0, 0), (0, columns - depth))),
+                jnp.pad(per_head, ((0, 0), (0, columns - 3 * 128))),
+            ],
+            0,
+        )
+
     for layer in reversed(range(LAYERS)):
         chan, state_taps, headp = tables[layer]
         (hidden, inv_rows, normed_all, projected, gnl, scanned, pre, side, states, inv_gate, mixed_raw) = saved[layer]
@@ -566,73 +1070,80 @@
                 jnp.sum(grad_mix.astype(BF16).astype(F32) * mixed_raw, axis=-1, keepdims=True)
             )
         scaled_mix = (mix_all.astype(F32) * inv_gate).astype(BF16)
-        grad_output = dot_tn(scaled_mix, gnl).astype(BF16)
-        grad_output = lax.psum_scatter(grad_output, "dp", scatter_dimension=0, tiled=True)
+        if layer > 0 or not fused:
+            product = dot_tn(scaled_mix, gnl).astype(BF16)
+            dgn = after(dgn, product)
+        else:
+            mix_turned = scaled_mix.T
+        if layer > 0 or not fused:
+            grads_output.append(scatter_call(product))
         rows_in = jnp.pad(
             jnp.concatenate([inv_gate, inv_gate * inv_gate * inv_gate * cross / inner], 1), ((0, 0), (0, 126))
         )
         low, dchan, dstate, dhead = backward_mixer(
             turn, projected, pre, scanned, dgn, side, states, rows_in, chan, state_taps, headp, q, width
         )
-        if held is not None:
-            low, held = lax.optimization_barrier((low, held))
-            grads_output.append(held[0])
-            grads_projection.append(held[1])
-            sums.append(held[2])
-        grad_normed = group.project(lambda rows: dot_nt(rows, projections[layer]), low)
-        grad_projection = dot_tn(normed_all, low).astype(BF16)
-        grad_projection = lax.psum_scatter(grad_projection, "dp", scatter_dimension=0, tiled=True)
+        project = lambda rows: dot_nt(rows, projections[layer])
+        if layer > 0 or not fused:
+            product = dot_tn(normed_all, low).astype(BF16)
+            grad_normed = group.project(project, low, None, product)
+            grads_projection.append(scatter_call(product))
+        else:
+
+            def exchange(sent):
+                small.append(small_of(dchan, dstate, dhead, jnp.zeros_like(pre_sums[0])))
+                found = scatter_product(
+                    normed_turned, low, mix_turned, gnl, grads_projection[0], grads_output[0],
+                    jnp.concatenate(small[::-1]), sent, 3,
+                )
+                small.extend(found[:4])
+                return found[4]
+
+            grad_normed = group.project(project, low, exchange)
         unit_rows = hidden * inv_rows
         grad_pre = jnp.sum(grad_normed * unit_rows, axis=0)
         grad_unit = grad_normed * pre_gain[layer]
         grad_flow = grad_mix + inv_rows * (
             grad_unit - unit_rows * jnp.mean(grad_unit * unit_rows, axis=-1, keepdims=True)
         )
-
-        def placed(values, total, start):
-            full = jnp.zeros(values.shape[:-1] + (total,), F32)
-            return lax.dynamic_update_slice_in_dim(full, values, start, values.ndim - 1)
-
-        lanes = placed(dchan, inner, lane_start)
-        skips = dchan[5].reshape(heads, HEAD).sum(axis=1)
-        per_head = placed(jnp.stack([dhead[0, :heads], dhead[1, :heads], skips]), all_heads, head_start)
-        flat = jnp.concatenate(
-            [
-                grad_pre,
-                lanes[:count].reshape(-1),
-                lanes[6],
-                dstate[:count].reshape(-1),
-                per_head.reshape(-1),
-            ]
-        )
-        flat = jnp.pad(flat, (0, -flat.shape[0] % 1024)).reshape(-1, 128)
-        held = (grad_output, grad_projection, sum_everywhere(flat))
+        pre_sums.append(grad_pre)
+        if layer > 0 or not fused:
+            small.append(small_of(dchan, dstate, dhead, grad_pre))
         if layer > 0:
-            grad_mix = keep_rows * grad_flow
-            mix_all = group.gather(grad_mix.astype(BF16))
-    grads_output.append(held[0])
-    grads_projection.append(held[1])
-    sums.append(held[2])
-
-    small = []
-    for flat in sums[::-1]:
-        flat = flat.reshape(-1)
-        cuts, start = [], 0
-        for size in (depth, count * inner, inner, count * 2 * N, all_heads, all_heads, all_heads):
-            cuts.append(flat[start : start + size])
-            start += size
-        taps = jnp.concatenate([cuts[1].reshape(count, inner), cuts[3].reshape(count, 2 * N)], 1)
-        small.append((cuts[0], taps, cuts[4], cuts[5], cuts[6], cuts[2]))
-    state_end = 2 * width + 2 * N
-    grads = [grad.astype(F32) for grad in grads_projection[::-1]]
+            grad_mix = rowwise(keep_rows * grad_flow)
+            mix_low = rowwise(grad_mix.astype(BF16))
+            mix_all = group.gather(mix_low)
+            if layer == LAYERS - 1:
+                out_hidden = last_hidden(mix_low, mix_all)
+    if fused:
+        grad_gate_value, side, grad_out, total = small[-4:]
+        pre, taps, decay, bias, skip, gain, grad_state, grad_step = last_sums(
+            grad_pre[None], total[5], side, heads, all_heads, 4
+        )
+    else:
+        total = lax.psum(jnp.stack(small[::-1]), ("dp", "tensor"))
+        pre, taps, gain = total[:, 6, :depth], total[:, :count], total[:, 5, :inner]
+        decay, bias, skip = (total[:, 7, 128 * i : 128 * i + all_heads] for i in range(3))
+        state_end = 2 * width + 2 * N
+        grads = jnp.stack(grads_projection[::-1]).astype(F32)
+        grad_gate_value = jnp.stack([grads[:, :, :width], grads[:, :, width : 2 * width]], 1)
+        grad_state = group.sum_all(grads[:, :, 2 * width : state_end])
+        grad_step = grads[:, :, state_end : state_end + heads]
+        grad_out = jnp.stack([grad.astype(F32).T for grad in grads_output[::-1]])
     return (
         out_hidden,
         grad_flow,
-        jnp.stack([jnp.stack([grad[:, :width], grad[:, width : 2 * width]]) for grad in grads]),
-        jnp.stack([group.sum_all(grad[:, 2 * width : state_end]) for grad in grads]),
-        jnp.stack([grad[:, state_end : state_end + heads] for grad in grads]),
-        jnp.stack([grad.astype(F32).T for grad in grads_output[::-1]]),
-    ) + tuple(jnp.stack([layer_sums[i] for layer_sums in small]) for i in range(6))
+        grad_gate_value,
+        grad_state,
+        grad_step,
+        grad_out,
+        pre,
+        taps,
+        decay,
+        bias,
+        skip,
+        gain,
+    )
 
 
 def solution(mesh):

time: 787 us -> 721 us (0.916)
  waiting for transfers between devices: 313 us -> 112 us
  Pallas kernels: 189 us -> 351 us
  matrix products: 178 us -> 139 us
  local copies, waits for them, and re-layouts: 22.2 us -> 45.1 us
  starting transfers between devices: 25.5 us -> 9.62 us
    pallas_call x0 -> x3, Pallas kernels: none -> 207 us  [the longest x1 119 us: scatter_product(): pl.pallas_call(functools.partial(scatter_product_kernel, first, chunks),...]
    ppermute x14 -> x9, waiting for transfers between devices: 198 us -> 98.6 us  [swap(): return lax.ppermute(values, 'tensor', [(0, 1), (1, 0)])]
    ppermute x10 -> x0, waiting for transfers between devices: 66.4 us -> none  [the longest x2 35.3 us: sum_everywhere(): values = values + lax.ppermute(values, 'tensor', [(0, 1), (1, 0)])]
    all_gather x4 -> x3, waiting for transfers between devices: 48.5 us -> 13.1 us  [the longest x2 13.1 us: per_device(): outputs.append(lax.all_gather(shard, 'dp', axis=0, tiled=True))]
    dot_general x4 -> x2, matrix products: 53.5 us -> 26.4 us  [dot_tn(): lax.dot_general(a, b, (((0,), (0,)), ((), ())), preferred_element_type=F32)]
    pallas_call x2, Pallas kernels: 118 us -> 94.6 us  [backward_mixer(): pl.pallas_call(backward_kernel, grid_spec=pltpu.PrefetchScalarGridSpec(nu...]
    pallas_call x2, Pallas kernels: 70.7 us -> 49.5 us  [forward_mixer(): pl.pallas_call(forward_kernel, grid_spec=pltpu.PrefetchScalarGridSpec(num...]
    dot_general x8 -> x7, matrix products: 75.3 us -> 62.3 us  [dot_nt(): lax.dot_general(a, b, (((1,), (1,)), ((), ())), preferred_element_type=F32)]
  transfers between devices with their start and end apart: 32 -> 14, of which waited for: 18 -> 8; matrix products, arithmetic and copies ran while one was open for 28% -> 23% of each run, Pallas kernels for 24% -> 20%
where the time goes in v3:
time: 721 us; the launch traced here: 713 us
  Pallas kernels  351 us (49%)
  matrix products  139 us (19%)
  waiting for transfers between devices  112 us (16%)
  local copies, waits for them, and re-layouts  45.1 us (6%)
  other arithmetic  40.7 us (6%)
  between operations  15.9 us (2%)
  starting transfers between devices  9.62 us (1%)
    pallas_call x1, Pallas kernels, scatter_product(): pl.pallas_call(functools.partial(scatter_product_kernel, first, chunks),...  119 us
    ppermute x9, waiting for transfers between devices, swap(): return lax.ppermute(values, 'tensor', [(0, 1), (1, 0)])  98.6 us
    pallas_call x2, Pallas kernels, backward_mixer(): pl.pallas_call(backward_kernel, grid_spec=pltpu.PrefetchScalarGridSpec(nu...  94.6 us
    pallas_call x1, Pallas kernels, gather_all(): pl.pallas_call(functools.partial(gather_kernel, count), in_specs=[anywher...  73 us
    dot_general x7, matrix products, dot_nt(): lax.dot_general(a, b, (((1,), (1,)), ((), ())), preferred_element_type=F32)  62.3 us
    dot_general x4, matrix products, dot_nn(): lax.dot_general(a, b, (((1,), (0,)), ((), ())), preferred_element_type=F32)  49.9 us
    pallas_call x2, Pallas kernels, forward_mixer(): pl.pallas_call(forward_kernel, grid_spec=pltpu.PrefetchScalarGridSpec(num...  49.5 us
    dot_general x2, matrix products, dot_tn(): lax.dot_general(a, b, (((0,), (0,)), ((), ())), preferred_element_type=F32)  26.4 us
  transfers between devices with their start and end apart: 14, of which 8 were waited for; matrix products, arithmetic and copies ran while one was open for 23% of the time, Pallas kernels for 20%

profile of v3, /device:TPU:0, one launch (start us, length us, event | category | flops | bytes accessed | tf_op | source)
XLA Modules:
  0.0 713.2 jit_solution(14717070197579687473)
XLA Ops:
  22.3 73.0 %gather_all.1 = (bf16[1536,3456]{1,0:T(8,128)(2,1)}, bf16[1024,1536]{1,0:T(8,128)(2,1)}, bf16[1024,1536]{1,0:T(8,128)(2,1)}) custom-call(bf16[96,3456]{1,0:T(8,128)(2,1)} %get-tuple-element.183.refs_0_, bf16[1024,1536]{1,0:T(8,128)(2,1)} %pad.50.refs_1_, bf16[1024,1536]{1,0:T(8,128)(2,1)} %pad.51.refs_2_), custom_call_target="tpu_custom_call", output_to_operand_aliasing={{1}: (1, {}), {2}: (2, {})} | custom-call | flops 60000002048 | bytes 20000000 | tf_op jit(solution)/shard_map/gather_all/pallas_call | solution.py:816
  101.7 15.4 %fusion.4.gate_ref.value_ref = bf16[1024,3072]{1,0:T(8,128)(2,1)} fusion(bf16[1024,1536]{1,0:T(8,128)(2,1)} %get-tuple-element.56.normed_ref, bf16[1536,3456]{1,0:T(8,128)(2,1)} %get-tuple-element.57.side_weight_ref), kind=kOutput, calls=%fused_computation.9 | convolution fusion | flops 9666822144 | bytes 18874368 | tf_op jit(solution)/shard_map/dot_general | solution.py:20
  117.2 24.8 %forward_mixer.2 = (bf16[1024,1536]{1,0:T(8,128)(2,1)}, bf16[1024,1536]{1,0:T(8,128)(2,1)}, bf16[1024,1536]{1,0:T(8,128)(2,1)}, f32[1024,640]{1,0:T(8,128)S(1)},...) custom-call(s32[1]{0:T(128)} %bitcast.1.turn_ref, bf16[1024,3072]{1,0:T(8,128)(2,1)} %fusion.4.gate_ref.value_ref, ...), custom_call_target="tpu_custom_call" | custom-call | flops 31457280000 | bytes 31457280 | tf_op jit(solution)/shard_map/forward_mixer/pallas_call | solution.py:303
  141.9 7.2 %all-gather.4.cloned.1.call-done = bf16[1536,1536]{1,0:T(8,128)(2,1)} async-done(((bf16[96,1536]{1,0:T(8,128)(2,1)}), bf16[1536,1536]{1,0:T(8,128)(2,1)}) %all-gather.4.cloned.1.call-update) | async-done | bytes 4718608 | tf_op jit(solution)/shard_map/all_gather | solution.py:977
  149.1 7.9 %fusion.75 = f32[1024,1536]{1,0:T(8,128)S(1)} fusion(bf16[1024,1536]{1,0:T(8,128)(2,1)} %get-tuple-element.59.out_right_ref, bf16[1536,1536]{1,0:T(8,128)(2,1)} %all-gather.4.cloned.1.call-done), kind=kOutput, calls=%fused_computation.147 | convolution fusion | flops 4831838208 | bytes 14155776 | tf_op jit(solution)/shard_map/dot_general | solution.py:24
  163.5 34.3 %collective-permute-done.1 = f32[1024,1]{0,1:T(1,128)S(1)} collective-permute-done((f32[1024,1]{0,1:T(1,128)S(1)}, f32[1024,1]{0,1:T(1,128)S(1)}, u32[]{:S(2)}, u32[]{:S(2)}) %collective-permute-start.1) | collective-permute-done | bytes 4128 | tf_op jit(solution)/shard_map/ppermute | solution.py:853
  207.2 33.9 %collective-permute-done.2 = bf16[512,1536]{1,0:T(8,128)(2,1)} collective-permute-done((bf16[512,1536]{1,0:T(8,128)(2,1)}, bf16[512,1536]{1,0:T(8,128)(2,1)}, u32[]{:S(2)}, u32[]{:S(2)}) %collective-permute-start.2) | collective-permute-done | bytes 1572896 | tf_op jit(solution)/shard_map/ppermute | solution.py:853
  244.8 15.4 %fusion.7.gate_ref.value_ref = bf16[1024,3072]{1,0:T(8,128)(2,1)} fusion(bf16[1536,3456]{1,0:T(8,128)(2,1)} %all-gather.6.cloned.1.call-done.side_weight_ref, bf16[512,1536]{1,0:T(8,128)(2,1)} %collective-permute-done.2, bf16[512,1536]{1,0:T(8,128)(2,1)} %multiply_convert_fusion.3), kind=kOutput, calls=%fused_computation.10 | convolution fusion | flops 9673113600 | bytes 18874368 | tf_op jit(solution)/shard_map/dot_general | solution.py:20
  260.3 24.8 %forward_mixer.3 = (bf16[1024,1536]{1,0:T(8,128)(2,1)}, bf16[1024,1536]{1,0:T(8,128)(2,1)}, bf16[1024,1536]{1,0:T(8,128)(2,1)}, f32[1024,640]{1,0:T(8,128)S(1)},...) custom-call(s32[1]{0:T(128)} %bitcast.1.turn_ref, bf16[1024,3072]{1,0:T(8,128)(2,1)} %fusion.7.gate_ref.value_ref, ...), custom_call_target="tpu_custom_call" | custom-call | flops 31457280000 | bytes 31457280 | tf_op jit(solution)/shard_map/forward_mixer/pallas_call | solution.py:303
  292.5 9.8 %multiply_reduce_fusion = (f32[1024]{0:T(1024)S(1)}, bf16[1024,1536]{1,0:T(8,128)(2,1)}) fusion(bf16[1024,1536]{1,0:T(8,128)(2,1)} %get-tuple-element.74, bf16[1024,1536]{1,0:T(8,128)(2,1)} %get-tuple-element.66, bf16[1536,1536]{1,0:T(8,128)(2,1)} %all-gather.8.cloned.1.call-done), kind=kOutput, calls=%fused_computation.7 | convolution fusion | flops 4839701504 | bytes 14159872 | tf_op jit(solution)/shard_map/dot_general | solution.py:20
  308.6 9.6 %convolution_convert_fusion.1 = bf16[1536,1536]{1,0:T(8,128)(2,1)} fusion(bf16[1024,1536]{1,0:T(8,128)(2,1)} %get-tuple-element.74, bf16[1024,1536]{1,0:T(8,128)(2,1)} %get-tuple-element.66, f32[1024]{0:T(1024)S(1)} %fusion.51), kind=kOutput, calls=%fused_computation.5 | convolution fusion | flops 4838916096 | bytes 11014144 | tf_op jit(solution)/shard_map/dot_general | solution.py:28
  320.4 47.2 %backward_mixer.2 = (bf16[1024,3456]{1,0:T(8,128)(2,1)}, f32[8,1536]{1,0:T(8,128)S(1)}, f32[8,256]{1,0:T(8,128)S(1)}, f32[8,128]{1,0:T(8,128)S(1)}) custom-call(s32[1]{0:T(128)} %bitcast.1.turn_ref, bf16[1024,3072]{1,0:T(8,128)(2,1)} %fusion.7.gate_ref.value_ref, bf16[1024,3072]{1,0:T(8,128)(2,1)} %fusion.7.gate_ref.value_ref, ...), custom_call_target="tpu_custom_call" | custom-call | flops 55050240000 | bytes 31457280 | tf_op jit(solution)/shard_map/backward_mixer/pallas_call | solution.py:351
  367.6 10.8 %fusion.33 = bf16[512,1536]{1,0:T(8,128)(2,1)} fusion(bf16[1536,3456]{1,0:T(8,128)(2,1)} %all-gather.6.cloned.1.call-done.side_weight_ref, bf16[1024,3456]{1,0:T(8,128)(2,1)} %get-tuple-element.72), kind=kOutput, calls=%fused_computation.53 | convolution fusion | flops 5436604416 | bytes 15728640 | tf_op jit(solution)/shard_map/dot_general | solution.py:24
  378.7 16.8 %convolution_convert_fusion = bf16[1536,3456]{1,0:T(8,128)(2,1)} fusion(bf16[1024,3456]{1,0:T(8,128)(2,1)S(1)} %copy-done.55, bf16[512,1536]{1,0:T(8,128)(2,1)} %collective-permute-done.2, bf16[512,1536]{1,0:T(8,128)(2,1)} %multiply_convert_fusion.3), kind=kOutput, calls=%fused_computation | convolution fusion | flops 10883235840 | bytes 20840448 | tf_op jit(solution)/shard_map/dot_general | solution.py:28
  395.5 11.1 %fusion.20 = f32[512,1536]{1,0:T(8,128)} fusion(bf16[1536,3456]{1,0:T(8,128)(2,1)} %all-gather.6.cloned.1.call-done.side_weight_ref, bf16[1024,3456]{1,0:T(8,128)(2,1)} %get-tuple-element.72), kind=kOutput, calls=%fused_computation.26 | convolution fusion | flops 5435817984 | bytes 17301504 | tf_op jit(solution)/shard_map/dot_general | solution.py:24
  429.5 6.8 convolution_convert_fusion.4
  437.0 7.5 %fusion.40 = f32[512,1536]{1,0:T(8,128)} fusion(bf16[1536,1536]{1,0:T(8,128)(2,1)} %all-gather.8.cloned.1.call-done, bf16[1024,1536]{1,0:T(8,128)(2,1)S(1)} %copy-done.54), kind=kOutput, calls=%fused_computation.57 | convolution fusion | flops 2415919104 | bytes 9437184 | tf_op jit(solution)/shard_map/dot_general | solution.py:24
  444.9 20.8 %collective-permute-done.6 = bf16[512,1536]{0,1:T(8,128)(2,1)} collective-permute-done((bf16[512,1536]{0,1:T(8,128)(2,1)}, bf16[512,1536]{0,1:T(8,128)(2,1)}, u32[]{:S(2)}, u32[]{:S(2)}) %collective-permute-start.6) | collective-permute-done | bytes 1572896 | tf_op jit(solution)/shard_map/ppermute | solution.py:853
  465.7 9.3 %convolution_convert_fusion.2.dgn_ref = bf16[1024,1536]{1,0:T(8,128)(2,1)} fusion(bf16[1536,1536]{1,0:T(8,128)(2,1)} %all-gather.4.cloned.1.call-done, bf16[512,1536]{0,1:T(8,128)(2,1)} %collective-permute-done.6, bf16[512,1536]{0,1:T(8,128)(2,1)} %copy.62), kind=kOutput, calls=%fused_computation.18 | convolution fusion | flops 4839702528 | bytes 11010048 | tf_op jit(solution)/shard_map/dot_general | solution.py:20
  475.1 47.4 %backward_mixer.3 = (bf16[1024,3456]{1,0:T(8,128)(2,1)}, f32[8,1536]{1,0:T(8,128)S(1)}, f32[8,256]{1,0:T(8,128)S(1)}, f32[8,128]{1,0:T(8,128)S(1)}) custom-call(s32[1]{0:T(128)} %bitcast.1.turn_ref, bf16[1024,3072]{1,0:T(8,128)(2,1)} %fusion.4.gate_ref.value_ref, bf16[1024,3072]{1,0:T(8,128)(2,1)} %fusion.4.gate_ref.value_ref, ...), custom_call_target="tpu_custom_call" | custom-call | flops 55050240000 | bytes 31457280 | tf_op jit(solution)/shard_map/backward_mixer/pallas_call | solution.py:351
  522.6 8.9 %fusion.16 = f32[512,1536]{1,0:T(8,128)} fusion(bf16[1536,3456]{1,0:T(8,128)(2,1)S(1)} %bitcast.106, bf16[1024,3456]{1,0:T(8,128)(2,1)} %get-tuple-element.80.right_ref), kind=kOutput, calls=%fused_computation.22 | convolution fusion | flops 5435817984 | bytes 17301504 | tf_op jit(solution)/shard_map/dot_general | solution.py:24
  541.5 9.5 %fusion.36.rows_ref = bf16[512,1536]{1,0:T(8,128)(2,1)} fusion(bf16[1536,3456]{1,0:T(8,128)(2,1)} %get-tuple-element.57.side_weight_ref, bf16[1024,3456]{1,0:T(8,128)(2,1)S(1)} %copy-done.56), kind=kOutput, calls=%fused_computation.54 | convolution fusion | flops 5436604416 | bytes 15728640 | tf_op jit(solution)/shard_map/dot_general | solution.py:24
  551.0 119.1 %scatter_product.1 = (f32[2,2,96,1536]{3,2,1,0:T(8,128)}, f32[2,96,384]{2,1,0:T(8,128)}, f32[2,1536,96]{2,1,0:T(8,128)}, f32[6,16,3328]{2,1,0:T(8,128)}, bf16[512,1536]{1,0:T(8,128)(2,1)}) custom-call(bf16[1536,1024]{1,0:T(8,128)(2,1)} %bitcast.82, bf16[1024,3456]{1,0:T(8,128)(2,1)} %get-tuple-element.80.right_ref, bf16[1536,1024]{1,0:T(8,128)(2,1)} %fusion.30.out_left_ref, ...), custom_call_target="tpu_custom_call" | custom-call | flops 89999998976 | bytes 20000000 | tf_op jit(solution)/shard_map/scatter_product/pallas_call | solution.py:559
  674.8 14.7 %last_sums.1 = (f32[2,1536]{1,0:T(2,128)}, f32[2,5,3328]{2,1,0:T(8,128)}, f32[2,48]{1,0:T(2,128)}, f32[2,48]{1,0:T(2,128)}, f32[2,48]{1,0:T(2,128)}, /*index=5*/...) custom-call(f32[1,1536]{1,0:T(1,128)} %broadcast_in_dim.11.pre_ref, ...), custom_call_target="tpu_custom_call" | custom-call | tf_op jit(solution)/shard_map/last_sums/pallas_call | solution.py:669
  (262 shorter events, 111.6 us)
Async XLA Ops:
  7.2 141.9 %all-gather.4.cloned.1.call-start = ((), (), s32[]{:S(2)}) async-start(), calls=%async_computation.2 | async-start | bytes 5013504 | tf_op jit(solution)/shard_map/all_gather | solution.py:977
  14.0 187.8 %copy-start.30 = (f32[1536]{0:T(1024)}, f32[1536]{0:T(1024)S(1)}, u32[]{:S(2)}) copy-start(f32[1536]{0:T(1024)S(1)} %get-tuple-element.140) | copy-start | bytes 18436
  22.3 73.9 %copy-start.48 = (f32[2,48]{1,0:T(2,128)S(1)}, f32[2,48]{1,0:T(2,128)}, u32[]{:S(2)}) copy-start(f32[2,48]{1,0:T(2,128)} %param.24) | copy-start | bytes 1156
  22.3 74.3 %copy-start.27 = (f32[2,5,3328]{2,0,1:T(2,128)S(1)}, f32[2,5,3328]{2,0,1:T(2,128)}, u32[]{:S(2)}) copy-start(f32[2,5,3328]{2,0,1:T(2,128)} %param.21) | copy-start | bytes 399364
  95.3 149.5 %all-gather.6.cloned.1.call-start = ((), (), s32[]{:S(2)}) async-start(), calls=%async_computation.3 | async-start | bytes 11280384 | tf_op jit(solution)/shard_map/all_gather | solution.py:974
  96.1 196.4 %all-gather.8.cloned.1.call-start = ((), (), s32[]{:S(2)}) async-start(), calls=%async_computation.4 | async-start | bytes 5013504 | tf_op jit(solution)/shard_map/all_gather | solution.py:977
  160.9 37.0 %collective-permute-start = (bf16[512,1536]{1,0:T(8,128)(2,1)}, bf16[512,1536]{1,0:T(8,128)(2,1)}, u32[]{:S(2)}, u32[]{:S(2)}) collective-permute-start(bf16[512,1536]{1,0:T(8,128)(2,1)} %slice.269), channel_id=1, source_target_pairs={{0,1},{1,0},{2,3},{3,2},{4,5},{5,4},{6,7},{7,6},{8,9},{9,8},{10,11... | collective-permute-start | bytes 4718600 | tf_op jit(solution)/shard_map/ppermute | solution.py:853
  162.4 388.6 %reduce-scatter.5.cloned.1.call-start = ((), (), s32[]{:S(2)}) async-start(), calls=%async_computation.6 | async-start | bytes 5013504 | tf_op jit(solution)/shard_map/reduce_scatter | solution.py:908
  162.9 34.9 %collective-permute-start.1 = (f32[1024,1]{0,1:T(1,128)S(1)}, f32[1024,1]{0,1:T(1,128)S(1)}, u32[]{:S(2)}, u32[]{:S(2)}) collective-permute-start(f32[1024,1]{0,1:T(1,128)S(1)} %bitcast.85), channel_id=1, source_target_pairs={{0,1},{1,0},{2,3},{3,2},{4,5},{5,4},{6,7},{7,6},{8,9},{9,8},{10,11... | collective-permute-start | bytes 12296 | tf_op jit(solution)/shard_map/ppermute | solution.py:853
  205.0 36.1 %collective-permute-start.2 = (bf16[512,1536]{1,0:T(8,128)(2,1)}, bf16[512,1536]{1,0:T(8,128)(2,1)}, u32[]{:S(2)}, u32[]{:S(2)}) collective-permute-start(bf16[512,1536]{1,0:T(8,128)(2,1)} %multiply_convert_fusion.3), channel_id=1, source_target_pairs={{0,1},{1,0},{2,3},{3,2},{4,5},{5,4},{6,7},{7,6},{8,9},{9,8},{10,11... | collective-permute-start | bytes 4718600 | tf_op jit(solution)/shard_map/ppermute | solution.py:853
  302.3 3.6 collective-permute-start.4
  304.6 3.7 collective-permute-start.3
  318.1 232.9 %reduce-scatter.3.cloned.1.call-start = ((), (), s32[]{:S(2)}) async-start(), calls=%async_computation.5 | async-start | bytes 11280384 | tf_op jit(solution)/shard_map/reduce_scatter | solution.py:908
  378.3 35.2 %collective-permute-start.5 = (bf16[512,1536]{1,0:T(8,128)(2,1)}, bf16[512,1536]{1,0:T(8,128)(2,1)}, u32[]{:S(2)}, u32[]{:S(2)}) collective-permute-start(bf16[512,1536]{1,0:T(8,128)(2,1)} %fusion.33), channel_id=1, source_target_pairs={{0,1},{1,0},{2,3},{3,2},{4,5},{5,4},{6,7},{7,6},{8,9},{9,8},{10,11... | collective-permute-start | bytes 4718600 | tf_op jit(solution)/shard_map/ppermute | solution.py:853
  427.5 17.0 %collective-permute-start.8 = (f32[512,1]{0,1:T(1,128)S(1)}, f32[512,1]{0,1:T(1,128)S(1)}, u32[]{:S(2)}, u32[]{:S(2)}) collective-permute-start(f32[512,1]{0,1:T(1,128)S(1)} %bitcast.97), channel_id=1, source_target_pairs={{0,1},{1,0},{2,3},{3,2},{4,5},{5,4},{6,7},{7,6},{8,9},{9,8},{10,11... | collective-permute-start | bytes 6152 | tf_op jit(solution)/shard_map/ppermute | solution.py:853
  428.1 37.6 %collective-permute-start.6 = (bf16[512,1536]{0,1:T(8,128)(2,1)}, bf16[512,1536]{0,1:T(8,128)(2,1)}, u32[]{:S(2)}, u32[]{:S(2)}) collective-permute-start(bf16[512,1536]{0,1:T(8,128)(2,1)} %copy.62), channel_id=1, source_target_pairs={{0,1},{1,0},{2,3},{3,2},{4,5},{5,4},{6,7},{7,6},{8,9},{9,8},{10,11... | collective-permute-start | bytes 4718600 | tf_op jit(solution)/shard_map/ppermute | solution.py:853
  436.3 101.1 %collective-permute-start.7 = (bf16[512,1536]{1,0:T(8,128)(2,1)}, bf16[512,1536]{1,0:T(8,128)(2,1)}, u32[]{:S(2)}, u32[]{:S(2)}) collective-permute-start(bf16[512,1536]{1,0:T(8,128)(2,1)} %convolution_convert_fusion.4), channel_id=1, source_target_pairs={{0,1},{1,0},{2,3},{3,2},{4,5},{5,4},{6,7},{7,6},{8,9},{9,8},{10,11... | collective-permute-start | bytes 4718600 | tf_op jit(solution)/shard_map/ppermute | solution.py:853
  465.7 56.8 %slice-start = ((s8[10616832]{0:T(1024)(128)(4,1)}), s8[4194304]{0:T(1024)(128)(4,1)S(1)}, s32[]{:S(2)}) async-start(s8[10616832]{0:T(1024)(128)(4,1)} %bitcast.105), calls=%async_computation.7 | async-start | bytes 8388608
  475.1 47.5 %slice-start.1 = ((s8[10616832]{0:T(1024)(128)(4,1)}), s8[4194304]{0:T(1024)(128)(4,1)S(1)}, s32[]{:S(2)}) async-start(s8[10616832]{0:T(1024)(128)(4,1)} %bitcast.105), calls=%async_computation.8 | async-start | bytes 8388608
  475.1 47.5 %slice-start.2 = ((s8[10616832]{0:T(1024)(128)(4,1)}), s8[2228224]{0:T(1024)(128)(4,1)S(1)}, s32[]{:S(2)}) async-start(s8[10616832]{0:T(1024)(128)(4,1)} %bitcast.105), calls=%async_computation.9 | async-start | bytes 4456448
  551.0 120.8 %copy-start.12 = (bf16[512,1536]{1,0:T(8,128)(2,1)S(1)}, bf16[512,1536]{1,0:T(8,128)(2,1)}, u32[]{:S(2)}) copy-start(bf16[512,1536]{1,0:T(8,128)(2,1)} %param.13) | copy-start | bytes 4718596
  551.0 120.8 %copy-start.29 = (f32[1536]{0:T(1024)S(1)}, f32[1536]{0:T(1024)}, u32[]{:S(2)}) copy-start(f32[1536]{0:T(1024)} %copy-done.28) | copy-start | bytes 18436
  551.0 120.8 %copy-start.41 = (f32[512]{0:T(512)S(1)}, f32[512]{0:T(512)}, u32[]{:S(2)}) copy-start(f32[512]{0:T(512)} %add_rsqrt_fusion.3) | copy-start | bytes 6148
  551.0 120.7 %copy-start.13 = (f32[512,1536]{1,0:T(8,128)S(1)}, f32[512,1536]{1,0:T(8,128)}, u32[]{:S(2)}) copy-start(f32[512,1536]{1,0:T(8,128)} %fusion.16) | copy-start | bytes 9437188
  (50 other events, 419.1 us)
Sparse Core Ops, SparseCore 0:
  95.5 53.5 all-gather.3
  151.4 87.2 all-gather.5
  240.9 51.5 all-gather.7
  318.3 73.1 reduce-scatter.4
  406.7 118.8 reduce-scatter.2

commit v4 on v3

--- a/solution.py
+++ b/solution.py
@@ -51,17 +51,29 @@
     return jnp.concatenate([jnp.where(low_half, values, zero), jnp.where(low_half, zero, values)], 0)
 
 
-def block_prep(side, headp_ref, q):
+def in_parts(values):
+    high = values.astype(BF16)
+    rest = values - high.astype(F32)
+    middle = rest.astype(BF16)
+    return high, middle, (rest - middle.astype(F32)).astype(BF16)
+
+
+def exact_ones(ones, *values):
+    parts = jnp.concatenate([jnp.concatenate(in_parts(one), 1) for one in values], 0)
+    size = values[0].shape[1]
+    total = dot_nn(ones, parts)
+    return total[:, :size] + total[:, size : 2 * size] + total[:, 2 * size :]
+
+
+def block_prep(side, headp_ref, lower):
     step = softplus(side + headp_ref[0:1, :])
-    lower = (iota((q, q), 0) >= iota((q, q), 1)).astype(F32)
-    running = exact_nn(lower, step * headp_ref[1:2, :])
-    return step, running
+    return step, exact_ones(lower, step * headp_ref[1:2, :])
 
 
 def forward_kernel(
     turn_ref, gate_ref, value_ref, normed_ref, side_weight_ref, chan_ref, state_taps_ref, headp_ref,
     gnl_ref, scanned_ref, pre_ref, side_ref, states_ref, square_ref,
-    state, vbuf, sbuf, step_s, run_s, runt_s, cb_s, bmat, bmat_t, cmat,
+    state, vbuf, sbuf, step_s, run_s, runt_s, cb_s, bmat, bmat_t, cmat, lower,
 ):
     q, width = gate_ref.shape
     step_index = pl.program_id(0)
@@ -69,12 +81,13 @@
     @pl.when(step_index == 0)
     def _():
         state[...] = jnp.zeros_like(state)
-        vbuf[0:8, :] = jnp.zeros((8, width), F32)
+        lower[...] = (iota((q, q), 0) >= iota((q, q), 1)).astype(BF16)
+        vbuf[:, 0:8, :] = jnp.zeros((width // PAIR, 8, PAIR), F32)
         sbuf[0:8, :] = jnp.zeros((8, 2 * N), F32)
 
     @pl.when(step_index > 0)
     def _():
-        vbuf[0:8, :] = vbuf[q : q + 8, :]
+        vbuf[:, 0:8, :] = vbuf[:, q : q + 8, :]
         sbuf[0:8, :] = sbuf[q : q + 8, :]
 
     side = dot_nn(normed_ref[...], side_weight_ref[...])
@@ -89,7 +102,7 @@
     cmat[...] = conv_state[:, N : 2 * N]
     bmat_t[...] = conv_state[:, 0:N].T
     cb_s[...] = dot_nt(conv_state[:, N : 2 * N], conv_state[:, 0:N])
-    step, running = block_prep(side[:, 2 * N :], headp_ref, q)
+    step, running = block_prep(side[:, 2 * N :], headp_ref, lower[...])
     step_s[...] = step
     run_s[...] = running
     runt_s[...] = running.T
@@ -99,10 +112,10 @@
 
     def one_pair(p, _):
         lanes = pl.ds(p * PAIR, PAIR)
-        vbuf[8 : q + 8, lanes] = value_ref[:, lanes].astype(F32)
-        pre = chan_ref[4:5, lanes] + chan_ref[3:4, lanes] * vbuf[8 : q + 8, lanes]
+        vbuf[p, 8 : q + 8, :] = value_ref[:, lanes].astype(F32)
+        pre = chan_ref[4:5, lanes] + chan_ref[3:4, lanes] * vbuf[p, 8 : q + 8, :]
         for k in range(KCONV - 1):
-            pre = pre + chan_ref[k : k + 1, lanes] * vbuf[5 + k : 5 + k + q, lanes]
+            pre = pre + chan_ref[k : k + 1, lanes] * vbuf[p, 5 + k : 5 + k + q, :]
         pre_ref[:, lanes] = pre.astype(BF16)
         x = pre * sigmoid(pre)
         run_two = run_s[:, 2 * p : 2 * p + 2]
@@ -139,7 +152,7 @@
     chan_ref, state_taps_ref, headp_ref,
     low_ref, dchan_ref, dstate_ref, dhead_ref,
     lam, gbuf, gsbuf, step_s, run_s, runt_s, cbt_s, bmat, cmat, cmat_t,
-    dcbt, db, dc, col_s, rowt_s, xdu_s, e_s, g_s, klan, spread,
+    dcbt, db, dc, col_s, rowt_s, per_head, spread, inv_s, pull_s, lower, later_s,
 ):
     q, width = gate_ref.shape
     step_index = pl.program_id(0)
@@ -147,7 +160,10 @@
     @pl.when(step_index == 0)
     def _():
         lam[...] = jnp.zeros_like(lam)
-        gbuf[q : q + 8, :] = jnp.zeros((8, width), F32)
+        lower[...] = (iota((q, q), 0) >= iota((q, q), 1)).astype(BF16)
+        later_s[:, 0:q] = (iota((q, q), 0) <= iota((q, q), 1)).astype(BF16)
+        later_s[:, q : 2 * q] = (iota((q, q), 0) > iota((q, q), 1)).astype(BF16)
+        gbuf[:, q : q + 8, :] = jnp.zeros((width // PAIR, 8, PAIR), F32)
         gsbuf[q : q + 8, :] = jnp.zeros((8, 2 * N), F32)
         dchan_ref[...] = jnp.zeros_like(dchan_ref)
         dstate_ref[...] = jnp.zeros_like(dstate_ref)
@@ -157,7 +173,7 @@
 
     @pl.when(step_index > 0)
     def _():
-        gbuf[q : q + 8, :] = gbuf[0:8, :]
+        gbuf[:, q : q + 8, :] = gbuf[:, 0:8, :]
         gsbuf[q : q + 8, :] = gsbuf[0:8, :]
 
     pre_state = side_ref[:, SIDE : SIDE + 2 * N]
@@ -167,7 +183,7 @@
     cmat[...] = conv_state[:, N : 2 * N]
     cmat_t[...] = conv_state[:, N : 2 * N].T
     cbt_s[...] = dot_nt(conv_state[:, 0:N], conv_state[:, N : 2 * N])
-    step, running = block_prep(side_ref[:, 2 * N : SIDE], headp_ref, q)
+    step, running = block_prep(side_ref[:, 2 * N : SIDE], headp_ref, lower[...])
     step_s[...] = step
     run_s[...] = running
     runt_s[...] = running.T
@@ -175,14 +191,17 @@
     db[...] = jnp.zeros_like(db)
     dc[...] = jnp.zeros_like(dc)
     col_s[...] = jnp.zeros_like(col_s)
+    inv_s[...] = jnp.broadcast_to(rows_ref[:, 0:1], (q, 128))
+    pull_s[...] = jnp.broadcast_to(rows_ref[:, 1:2], (q, 128))
     causal_t = iota((q, q), 1) >= iota((q, q), 0)
     low_half = iota((1, PAIR), 1) < HEAD
     head_lane = iota((1, 128), 1)
+    line = iota((16, PAIR), 0)
 
     def one_pair(p, _):
         lanes = pl.ds(p * PAIR, PAIR)
-        inv = rows_ref[:, 0:1]
-        pull = rows_ref[:, 1:2]
+        inv = inv_s[...]
+        pull = pull_s[...]
         gain = chan_ref[6:7, lanes]
         skip = chan_ref[5:6, lanes]
         gate = gate_ref[:, lanes].astype(F32)
@@ -234,24 +253,27 @@
         grow_last = jnp.exp(last)
         fade = jnp.exp(last - run_pair)
         from_state = dot_nn(cmat[...], start_low) * grow
-        e_s[:, lanes] = (dy * from_state).astype(BF16)
+        per_head[q : 2 * q, lanes] = (dy * from_state).astype(BF16)
         from_lam = dot_nn(bmat[...], lam_low) * fade
-        g_s[:, lanes] = (u * from_lam).astype(BF16)
+        per_head[2 * q : 3 * q, lanes] = (u * from_lam).astype(BF16)
         du = dot_nn(mixing, dy_stack) + from_lam
         dy_grow = (dy * grow).astype(BF16)
         dc[...] += dot_nt(dy_grow, start_low)
         db[...] += dot_nt((u * fade).astype(BF16), lam_low)
-        klan[:, lanes] = jnp.sum(lam_one * start_low.astype(F32), 0, keepdims=True) * grow_last
+        ends = in_parts(jnp.sum(lam_one * start_low.astype(F32), 0, keepdims=True) * grow_last)
+        per_head[3 * q : 3 * q + 16, lanes] = jnp.where(
+            line == 0, ends[0], jnp.where(line == 1, ends[1], jnp.where(line == 2, ends[2], jnp.zeros_like(ends[0])))
+        )
         lam[:, lanes] = lam_one * grow_last + dot_nn(cmat_t[...], dy_grow)
-        xdu_s[:, lanes] = (x * du).astype(BF16)
+        per_head[0:q, lanes] = (x * du).astype(BF16)
         gp = (du * step_pair + skip * dy) * (sig_pre * (1.0 + pre * (1.0 - sig_pre)))
-        gbuf[0:q, lanes] = gp
+        gbuf[p, 0:q, :] = gp
         value = value_ref[:, lanes].astype(F32)
         dv = chan_ref[3:4, lanes] * gp
         dchan_ref[3:4, lanes] += jnp.sum(value * gp, 0, keepdims=True)
         dchan_ref[4:5, lanes] += jnp.sum(gp, 0, keepdims=True)
         for k in range(KCONV - 1):
-            later = gbuf[3 - k : 3 - k + q, lanes]
+            later = gbuf[p, 3 - k : 3 - k + q, :]
             dv = dv + chan_ref[k : k + 1, lanes] * later
             dchan_ref[k : k + 1, lanes] += jnp.sum(value * later, 0, keepdims=True)
         low_ref[:, pl.ds(width + p * PAIR, PAIR)] = dv.astype(BF16)
@@ -276,16 +298,10 @@
         dstate_ref[k : k + 1, :] += jnp.sum(state_in * later, 0, keepdims=True)
     low_ref[:, 2 * width : 2 * width + 2 * N] = dstate.astype(BF16)
 
-    heads = spread[...]
-    direct = dot_nn(xdu_s[...], heads)
-    from_start = dot_nn(e_s[...], heads)
-    to_end = dot_nn(g_s[...], heads)
-    across = exact_nn(jnp.broadcast_to(klan[...], (8, width)), heads.astype(F32))[0:1, :]
-    upper = (iota((q, q), 0) <= iota((q, q), 1)).astype(F32)
-    strict = (iota((q, q), 0) > iota((q, q), 1)).astype(F32)
-    dlog = (
-        exact_nn(upper, rowt_s[...].T - col_s[...] + from_start) + exact_nn(strict, to_end) + across
-    )
+    sums = dot_nn(per_head[...], spread[...])
+    direct, from_start, to_end = sums[0:q], sums[q : 2 * q], sums[2 * q : 3 * q]
+    across = sums[3 * q : 3 * q + 1] + sums[3 * q + 1 : 3 * q + 2] + sums[3 * q + 2 : 3 * q + 3]
+    dlog = exact_ones(later_s[...], rowt_s[...].T - col_s[...] + from_start, to_end) + across
     rate = headp_ref[1:2, :]
     dstep = direct + rate * dlog
     dstep_in = dstep * sigmoid(side_ref[:, 2 * N : SIDE] + headp_ref[0:1, :])
@@ -318,11 +334,11 @@
                 pl.BlockSpec((q, 128), lambda i, turn: (place(i, turn), 0)),
             ],
             scratch_shapes=[
-                pltpu.VMEM((N, width), F32), pltpu.VMEM((q + 8, width), F32),
+                pltpu.VMEM((N, width), F32), pltpu.VMEM((width // PAIR, q + 8, PAIR), F32),
                 pltpu.VMEM((q + 8, 2 * N), F32),
                 pltpu.VMEM((q, 128), F32), pltpu.VMEM((q, 128), F32), pltpu.VMEM((128, q), F32),
                 pltpu.VMEM((q, q), F32), pltpu.VMEM((q, N), BF16), pltpu.VMEM((N, q), BF16),
-                pltpu.VMEM((q, N), BF16),
+                pltpu.VMEM((q, N), BF16), pltpu.VMEM((q, q), BF16),
             ],
         ),
         out_shape=[
@@ -365,15 +381,16 @@
                 fixed((8, width)), fixed((8, 2 * N)), fixed((8, 128)),
             ],
             scratch_shapes=[
-                pltpu.VMEM((N, width), F32), pltpu.VMEM((q + 8, width), F32),
+                pltpu.VMEM((N, width), F32), pltpu.VMEM((width // PAIR, q + 8, PAIR), F32),
                 pltpu.VMEM((q + 8, 2 * N), F32),
                 pltpu.VMEM((q, 128), F32), pltpu.VMEM((q, 128), F32), pltpu.VMEM((128, q), F32),
                 pltpu.VMEM((q, q), F32), pltpu.VMEM((q, N), BF16), pltpu.VMEM((q, N), BF16),
                 pltpu.VMEM((N, q), BF16),
                 pltpu.VMEM((q, q), F32), pltpu.VMEM((q, N), F32), pltpu.VMEM((q, N), F32),
                 pltpu.VMEM((q, 128), F32), pltpu.VMEM((128, q), F32),
-                pltpu.VMEM((q, width), BF16), pltpu.VMEM((q, width), BF16), pltpu.VMEM((q, width), BF16),
-                pltpu.VMEM((1, width), F32), pltpu.VMEM((width, 128), BF16),
+                pltpu.VMEM((3 * q + 16, width), BF16), pltpu.VMEM((width, 128), BF16),
+                pltpu.VMEM((q, 128), F32), pltpu.VMEM((q, 128), F32),
+                pltpu.VMEM((q, q), BF16), pltpu.VMEM((q, 2 * q), BF16),
             ],
         ),
         out_shape=[
@@ -388,232 +405,549 @@
     )(turn, projected, projected, pre, scanned, dgn, side, states, rows_in, chan, state_taps, headp)
 CHUNK = 384
 LAYERS = 2
-
-
-def scatter_product_kernel(
-    first, chunks, left_ref, right_ref, out_left_ref, out_right_ref, layer_ref, out_layer_ref, small_ref, rows_ref,
-    wide_ref, side_ref, out_ref, total_ref, rows_come,
-    rows_ss, rows_rs, small_come, small_ss, small_rs,
+ROW_TILE = 256
+SPAN = 768
+X_LAG = 3
+Z_LAG = 6
+
+
+def last_backward_kernel(
+    groups, blocks,
+    gate_ref, value_ref, pre_ref, scanned_ref, dgn_ref, side_ref, states_ref, rows_ref,
+    chan_ref, state_taps_ref, headp_ref, small_ref,
+    own_left_ref, other_left_ref, normed_left_ref, gnl_ref, weight_ref,
+    wide_ref, side_out_ref, out_ref, total_ref, own_ref,
+    lam, gbuf, gsbuf, step_s, run_s, runt_s, cbt_s, bmat, cmat, cmat_t,
+    dcbt, db, dc, col_s, rowt_s, per_head, head_s, spread, inv_s, pull_s, lower, later_s,
+    sums, state_sums, head_sums, low, left, tiles,
     keep0, keep1, keep2, send0, send1, send2, come0, come1, come2, ss0, rs0, ss1, rs1, ss2, rs2,
+    rows_send, rows_come, rows_ss, rows_rs, small_s, small_come, small_ss, small_rs, local,
 ):
     k = pl.program_id(0)
     me = lax.axis_index("dp")
     tensor = lax.axis_index("tensor")
     core, x_bit, z = lax.rem(me, 2), lax.rem(me // 2, 2), me // 4
-    rows = layer_ref.shape[0]
+    q, width = gate_ref.shape
+    inner = groups * width
+    depth = left.shape[0]
+    half = rows_send.shape[1]
+    heads = width // HEAD
+    mixing_steps = groups * blocks
+    halves = width // CHUNK
+    first = inner // CHUNK
+    chunks = 3 * first + 1
+    rows = depth // 16
+    tile_count = depth // ROW_TILE
     core_peer = me + 1 - 2 * core
     x_peer = me + 2 - 4 * x_bit
     z_peers = [lax.rem(me + 4 * (j + 1), 16) for j in range(3)]
+    small_peers = [core_peer, x_peer] + [
+        lax.rem(me, 4) + 4 * (z + bit - 2 * bit * lax.rem(z // bit, 2)) for bit in (1, 2)
+    ]
+
+    def remote(source, target, send, receive, dp, tp):
+        return pltpu.make_async_remote_copy(
+            src_ref=source, dst_ref=target, send_sem=send, recv_sem=receive,
+            device_id=(dp, tp), device_id_type=pl.DeviceIdType.MESH,
+        )
 
     def by_core(c):
-        return pltpu.make_async_remote_copy(
-            src_ref=send0.at[c], dst_ref=come0.at[c], send_sem=ss0.at[c], recv_sem=rs0.at[c],
-            device_id=(core_peer, tensor), device_id_type=pl.DeviceIdType.MESH,
-        )
+        return remote(send0.at[lax.rem(c, 3)], come0.at[lax.rem(c, 3)], ss0.at[c], rs0.at[c], core_peer, tensor)
 
     def by_x(c):
-        return pltpu.make_async_remote_copy(
-            src_ref=send1.at[c], dst_ref=come1.at[c], send_sem=ss1.at[c], recv_sem=rs1.at[c],
-            device_id=(x_peer, tensor), device_id_type=pl.DeviceIdType.MESH,
-        )
+        return remote(send1.at[lax.rem(c, 4)], come1.at[lax.rem(c, 6)], ss1.at[c], rs1.at[c], x_peer, tensor)
 
     def by_z(c, j):
-        return pltpu.make_async_remote_copy(
-            src_ref=send2.at[c, lax.rem(z + j + 1, 4)], dst_ref=come2.at[c, j],
-            send_sem=ss2.at[c, j], recv_sem=rs2.at[c, j],
-            device_id=(z_peers[j], tensor), device_id_type=pl.DeviceIdType.MESH,
-        )
-
-    small_peers = [(me, 1 - tensor), (core_peer, tensor), (x_peer, tensor)] + [
-        (lax.rem(me, 4) + 4 * (z + bit - 2 * bit * lax.rem(z // bit, 2)), tensor) for bit in (1, 2)
+        return remote(
+            send2.at[lax.rem(c, 4), pl.ds(pl.multiple_of(lax.rem(z + j + 1, 4) * rows, rows), rows), :], come2.at[c, j], ss2.at[c, j], rs2.at[c, j], z_peers[j], tensor
+        )
+
+    def by_tensor(t):
+        return remote(rows_send.at[t], rows_come.at[t], rows_ss.at[t], rows_rs.at[t], me, 1 - tensor)
+
+    def by_all(stage):
+        return remote(
+            small_s.at[stage], small_come.at[stage], small_ss.at[stage], small_rs.at[stage], small_peers[stage], tensor
+        )
+
+    def tile_copy(t):
+        return pltpu.make_async_copy(
+            weight_ref.at[pl.ds(t * ROW_TILE, ROW_TILE), :], tiles.at[t % 2], local.at[3 + t % 2]
+        )
+
+    mix_copies = [
+        pltpu.make_async_copy(ref, left.at[:, pl.ds(i * half, half)], local.at[6 * i])
+        for i, ref in enumerate((own_left_ref, other_left_ref))
     ]
-
-    def by_all(stage):
-        return pltpu.make_async_remote_copy(
-            src_ref=total_ref.at[stage], dst_ref=small_come.at[stage],
-            send_sem=small_ss.at[stage], recv_sem=small_rs.at[stage],
-            device_id=small_peers[stage], device_id_type=pl.DeviceIdType.MESH,
-        )
-
-    by_tensor = pltpu.make_async_remote_copy(
-        src_ref=rows_ref, dst_ref=rows_come, send_sem=rows_ss, recv_sem=rows_rs,
-        device_id=(me, 1 - tensor), device_id_type=pl.DeviceIdType.MESH,
-    )
+    gnl_copies = [
+        pltpu.make_async_copy(
+            gnl_ref.at[:, pl.ds(i * width, width)], low.at[:, pl.ds(i * inner + width, width)], local.at[1 + 4 * i]
+        )
+        for i in range(2)
+    ]
+    normed_copy = pltpu.make_async_copy(normed_left_ref, left, local.at[2])
+
+    def at(offset, action):
+        s = k - offset
+        there = (
+            ((s >= 0) & (s < blocks - 1) & (lax.rem(s, 2) == 0))
+            | ((s >= blocks - 1) & (s < mixing_steps - 1) & (lax.rem(s, 2) == 1))
+            | ((s >= mixing_steps - 1) & (s < mixing_steps + 4))
+        )
+
+        @pl.when(there)
+        def _():
+            action(chunk_at(s, blocks))
 
     @pl.when(k == 0)
     def _():
-        total_ref[0] = small_ref[...]
+        for copy in mix_copies + gnl_copies:
+            copy.start()
         barrier = pltpu.get_barrier_semaphore()
         for peer in [(core_peer, tensor), (x_peer, tensor), (me, 1 - tensor)] + [(p, tensor) for p in z_peers]:
             pl.semaphore_signal(barrier, inc=1, device_id=peer, device_id_type=pl.DeviceIdType.MESH)
         pl.semaphore_wait(barrier, 6)
+        sums[...] = jnp.zeros_like(sums)
+        state_sums[...] = jnp.zeros_like(state_sums)
+        head_sums[...] = jnp.zeros_like(head_sums)
+        rowt_s[...] = jnp.zeros_like(rowt_s)
+        col_s[...] = jnp.zeros_like(col_s)
+        head_s[...] = jnp.zeros_like(head_s)
+        dcbt[...] = jnp.zeros_like(dcbt)
+        db[...] = jnp.zeros_like(db)
+        dc[...] = jnp.zeros_like(dc)
+        gsbuf[...] = jnp.zeros_like(gsbuf)
+        for g in range(groups):
+            spread[g] = ((iota((width, 128), 0) // HEAD + g * heads) == iota((width, 128), 1)).astype(BF16)
+        lower[...] = (iota((q, q), 0) >= iota((q, q), 1)).astype(BF16)
+        later_s[:, 0:q] = (iota((q, q), 0) <= iota((q, q), 1)).astype(BF16)
+        later_s[:, q : 2 * q] = (iota((q, q), 0) > iota((q, q), 1)).astype(BF16)
+
+        def prepare(b, _):
+            here = pl.ds(pl.multiple_of(lax.rem(b + tensor * (blocks // 2), blocks) * q, q), q)
+            pre_state = side_ref[here, SIDE : SIDE + 2 * N]
+            conv_state = (pre_state * sigmoid(pre_state)).astype(BF16)
+            bmat[b] = conv_state[:, 0:N]
+            cmat[b] = conv_state[:, N : 2 * N]
+            cmat_t[b] = conv_state[:, N : 2 * N].T
+            cbt_s[b] = dot_nt(conv_state[:, 0:N], conv_state[:, N : 2 * N])
+            step, running = block_prep(side_ref[here, 2 * N : SIDE], headp_ref, lower[...])
+            step_s[b] = step
+            run_s[b] = running
+            runt_s[b] = running.T
+            return 0
+
+        lax.fori_loop(0, blocks, prepare, 0, unroll=4)
+
+    def mix(g):
+        b = blocks - 1 - lax.rem(k, blocks)
+        place = lax.rem(b + tensor * (blocks // 2), blocks)
+        here = pl.ds(pl.multiple_of(place * q, q), q)
+
+        @pl.when(lax.rem(k, blocks) == 0)
+        def _():
+            lam[...] = jnp.zeros_like(lam)
+            gbuf[:, q : q + 8, :] = jnp.zeros((width // PAIR, 8, PAIR), F32)
+
+        @pl.when(lax.rem(k, blocks) > 0)
+        def _():
+            gbuf[:, q : q + 8, :] = gbuf[:, 0:8, :]
+
+        inv_s[...] = jnp.broadcast_to(rows_ref[:, 0:1], (q, 128))
+        pull_s[...] = jnp.broadcast_to(rows_ref[:, 1:2], (q, 128))
+        causal_t = iota((q, q), 1) >= iota((q, q), 0)
+        low_half = iota((1, PAIR), 1) < HEAD
+        head_lane = iota((1, 128), 1)
+        line = iota((16, PAIR), 0)
+
+        def column(kind, p):
+            return slice(kind * inner + g * width + p * PAIR, kind * inner + g * width + (p + 1) * PAIR)
+
+        for p in range(width // PAIR):
+            lanes = slice(p * PAIR, (p + 1) * PAIR)
+            inv = inv_s[...]
+            pull = pull_s[...]
+            gain = chan_ref[6:7, lanes]
+            skip = chan_ref[5:6, lanes]
+            gate = gate_ref[:, lanes].astype(F32)
+            sig_gate = sigmoid(gate)
+            silu_gate = gate * sig_gate
+            scanned = scanned_ref[:, lanes].astype(F32)
+            gated = scanned * silu_gate
+            dgn = dgn_ref[:, lanes].astype(F32) * inv
+            dgated = dgn * gain - gated * pull
+            sums[g, 5:6, lanes] += jnp.sum(dgn * gated, 0, keepdims=True)
+            dy = dgated * silu_gate
+            low[here, column(0, p)] = (dgated * scanned * (sig_gate + silu_gate * (1.0 - sig_gate))).astype(BF16)
+            pre = pre_ref[:, lanes].astype(F32)
+            sig_pre = sigmoid(pre)
+            x = pre * sig_pre
+            sums[g, 6:7, lanes] += jnp.sum(x * dy, 0, keepdims=True)
+            h = g * heads + 2 * p
+            run_two = run_s[b, :, h : h + 2]
+            step_two = step_s[b, :, h : h + 2]
+            run_a, run_b = run_two[:, 0:1], run_two[:, 1:2]
+            run_pair = jnp.where(low_half, run_a, run_b)
+            step_pair = jnp.where(low_half, step_two[:, 0:1], step_two[:, 1:2])
+            u = x * step_pair
+            u_low = u.astype(BF16)
+            dy_stack = stacked(dy.astype(BF16), low_half)
+            products = dot_nt(u_low, dy_stack)
+            cbt = cbt_s[b]
+            table_a = jnp.where(causal_t, jnp.exp(runt_s[b, h : h + 1, :] - run_a), 0.0)
+            table_b = jnp.where(causal_t, jnp.exp(runt_s[b, h + 1 : h + 2, :] - run_b), 0.0)
+            mix_a = table_a * cbt
+            mix_b = table_b * cbt
+            mixing = jnp.concatenate([mix_a.astype(BF16), mix_b.astype(BF16)], 1)
+            prod_a = products[:, 0:q]
+            prod_b = products[:, q : 2 * q]
+            dcbt[b] += prod_a * table_a + prod_b * table_b
+            flow_a = prod_a * mix_a
+            flow_b = prod_b * mix_b
+            rowt_s[b, h : h + 1, :] = jnp.sum(flow_a, 0, keepdims=True)
+            rowt_s[b, h + 1 : h + 2, :] = jnp.sum(flow_b, 0, keepdims=True)
+            col_s[b] += jnp.where(
+                head_lane == h, jnp.sum(flow_a, 1, keepdims=True), 0.0
+            ) + jnp.where(head_lane == h + 1, jnp.sum(flow_b, 1, keepdims=True), 0.0)
+            start_low = states_ref[0, :, lanes]
+            lam_one = lam[:, lanes]
+            lam_low = lam_one.astype(BF16)
+            grow = jnp.exp(run_pair)
+            last = run_pair[q - 1 : q, :]
+            grow_last = jnp.exp(last)
+            fade = jnp.exp(last - run_pair)
+            from_state = dot_nn(cmat[b], start_low) * grow
+            per_head[q : 2 * q, lanes] = (dy * from_state).astype(BF16)
+            from_lam = dot_nn(bmat[b], lam_low) * fade
+            per_head[2 * q : 3 * q, lanes] = (u * from_lam).astype(BF16)
+            du = dot_nn(mixing, dy_stack) + from_lam
+            dy_grow = (dy * grow).astype(BF16)
+            dc[b] += dot_nt(dy_grow, start_low)
+            db[b] += dot_nt((u * fade).astype(BF16), lam_low)
+            ends = in_parts(jnp.sum(lam_one * start_low.astype(F32), 0, keepdims=True) * grow_last)
+            per_head[3 * q : 3 * q + 16, lanes] = jnp.where(
+                line == 0,
+                ends[0],
+                jnp.where(line == 1, ends[1], jnp.where(line == 2, ends[2], jnp.zeros_like(ends[0]))),
+            )
+            lam[:, lanes] = lam_one * grow_last + dot_nn(cmat_t[b], dy_grow)
+            per_head[0:q, lanes] = (x * du).astype(BF16)
+            gp = (du * step_pair + skip * dy) * (sig_pre * (1.0 + pre * (1.0 - sig_pre)))
+            gbuf[p, 0:q, :] = gp
+            value = value_ref[:, lanes].astype(F32)
+            dv = chan_ref[3:4, lanes] * gp
+            sums[g, 3:4, lanes] += jnp.sum(value * gp, 0, keepdims=True)
+            sums[g, 4:5, lanes] += jnp.sum(gp, 0, keepdims=True)
+            for tap in range(KCONV - 1):
+                later = gbuf[p, 3 - tap : 3 - tap + q, :]
+                dv = dv + chan_ref[tap : tap + 1, lanes] * later
+                sums[g, tap : tap + 1, lanes] += jnp.sum(value * later, 0, keepdims=True)
+            low[here, column(1, p)] = dv.astype(BF16)
+
+        head_s[b] += dot_nn(per_head[...], spread[g])
+        if g < groups - 1:
+            return
+        found = head_s[b]
+        direct, from_start, to_end = found[0:q], found[q : 2 * q], found[2 * q : 3 * q]
+        ends = found[3 * q : 3 * q + 1] + found[3 * q + 1 : 3 * q + 2] + found[3 * q + 2 : 3 * q + 3]
+        dlog = exact_ones(later_s[...], rowt_s[b].T - col_s[b] + from_start, to_end) + ends
+        rate = headp_ref[1:2, :]
+        dstep = direct + rate * dlog
+        dstep_in = dstep * sigmoid(side_ref[here, 2 * N : SIDE] + headp_ref[0:1, :])
+        head_sums[0:1, :] += jnp.sum(step_s[b] * dlog, 0, keepdims=True) * rate
+        head_sums[1:2, :] += jnp.sum(dstep_in, 0, keepdims=True)
+        low[here, 2 * inner + 2 * N : 2 * inner + SIDE] = dstep_in.astype(BF16)
+
+        gsbuf[q : q + 8, :] = gsbuf[0:8, :]
+        dcbt_low = dcbt[b].astype(BF16)
+        dconv = jnp.concatenate([db[b] + dot_nn(dcbt_low, cmat[b]), dc[b] + dot_tn(dcbt_low, bmat[b])], 1)
+        pre_state = side_ref[here, SIDE : SIDE + 2 * N]
+        sig_state = sigmoid(pre_state)
+        gp_state = dconv * (sig_state * (1.0 + pre_state * (1.0 - sig_state)))
+        gsbuf[0:q, :] = gp_state
+        state_in = side_ref[here, 0 : 2 * N]
+        dstate = state_taps_ref[3:4, :] * gp_state
+        state_sums[3:4, :] += jnp.sum(state_in * gp_state, 0, keepdims=True)
+        state_sums[4:5, :] += jnp.sum(gp_state, 0, keepdims=True)
+        for tap in range(KCONV - 1):
+            later = gsbuf[3 - tap : 3 - tap + q, :]
+            dstate = dstate + state_taps_ref[tap : tap + 1, :] * later
+            state_sums[tap : tap + 1, :] += jnp.sum(state_in * later, 0, keepdims=True)
+        low[here, 2 * inner : 2 * inner + 2 * N] = dstate.astype(BF16)
+
+    for g in range(groups):
+
+        @pl.when((k >= g * blocks) & (k < (g + 1) * blocks))
+        def _():
+            mix(g)
+
+    @pl.when(k == mixing_steps - 3)
+    def _():
+        tile_copy(0).start()
+        tile_copy(1).start()
+
+    @pl.when(k == mixing_steps)
+    def _():
+        for g in range(groups):
+            small_s[0, 0:8, g * width : (g + 1) * width] = sums[g]
+        small_s[0, 0:8, inner:] = state_sums[...]
+        small_s[0, 5:7, inner : inner + 128] = head_sums[0:2, :]
+        small_s[0, 8:16, :] = small_ref[...]
         by_all(0).start()
-        by_tensor.start()
-
-    def multiply(left, right):
-        def tile(m, _):
-            part = dot_nn(left[pl.ds(m * 2 * rows, 2 * rows), :], right[...])
-            even, odd = part[:rows], part[rows:]
-            keep0[lax.rem(k, 2), m] = jnp.where(core == 0, even, odd)
-            send0[k, m] = jnp.where(core == 0, odd, even).astype(BF16)
-            return 0
-
-        lax.fori_loop(0, 8, tile, 0)
-        by_core(k).start()
-
-    @pl.when(k < first)
-    def _():
-        multiply(left_ref, right_ref)
-
-    @pl.when((k >= first) & (k < chunks))
-    def _():
-        multiply(out_left_ref, out_right_ref)
-
-    @pl.when((k >= 1) & (k < chunks + 1))
-    def _():
-        c = k - 1
+
+    for stage in range(4):
+
+        @pl.when(k == mixing_steps + 1 + 2 * stage)
+        def _():
+            by_all(stage).wait_recv()
+            if stage < 3:
+                small_s[stage + 1] = small_s[stage] + small_come[stage]
+                by_all(stage + 1).start()
+            else:
+                total_ref[...] = small_s[stage] + small_come[stage]
+
+    for t in range(tile_count):
+
+        @pl.when(k == mixing_steps + t)
+        def _():
+            tile_copy(t).wait()
+
+            rows_send[t] = dot_nt(low[half:, :], tiles[t % 2]).astype(BF16)
+            by_tensor(t).start()
+            own_ref[:, t * ROW_TILE : (t + 1) * ROW_TILE] = dot_nt(low[:half, :], tiles[t % 2])
+            if t + 2 < tile_count:
+                tile_copy(t + 2).start()
+
+    def part(index, size):
+        return pl.ds(pl.multiple_of(index * size, size), size)
+
+    def receive_core(c):
         by_core(c).wait_recv()
 
-        def tile(m, _):
-            keep1[lax.rem(c, 3), m] = keep0[lax.rem(c, 2), 2 * m + x_bit] + come0[c, 2 * m + x_bit].astype(F32)
-            send1[c, m] = (
-                keep0[lax.rem(c, 2), 2 * m + 1 - x_bit] + come0[c, 2 * m + 1 - x_bit].astype(F32)
-            ).astype(BF16)
-            return 0
-
-        lax.fori_loop(0, 4, tile, 0)
+        @pl.when(c >= 4)
+        def _():
+            by_x(c - 4).wait_send()
+
+        mine, other = part(x_bit, 4 * rows), part(1 - x_bit, 4 * rows)
+        send1[lax.rem(c, 4)] = (keep0[lax.rem(c, 2), other, :] + come0[lax.rem(c, 3), other, :].astype(F32)).astype(BF16)
         by_x(c).start()
-
-    @pl.when((k >= 3) & (k < chunks + 3))
-    def _():
-        c = k - 3
+        keep1[lax.rem(c, 4)] = keep0[lax.rem(c, 2), mine, :] + come0[lax.rem(c, 3), mine, :].astype(F32)
+
+    def receive_x(c):
         by_x(c).wait_recv()
 
-        def tile(m, _):
-            total = keep1[lax.rem(c, 3), m] + come1[c, m].astype(F32)
-            keep2[lax.rem(c, 3), m] = total
-            send2[c, m] = total.astype(BF16)
-            return 0
-
-        lax.fori_loop(0, 4, tile, 0)
+        @pl.when(c >= 4)
+        def _():
+            for j in range(3):
+                by_z(c - 4, j).wait_send()
+
+        total = keep1[lax.rem(c, 4)] + come1[lax.rem(c, 6)].astype(F32)
+        keep2[lax.rem(c, 4)] = total
+        send2[lax.rem(c, 4)] = total.astype(BF16)
         for j in range(3):
             by_z(c, j).start()
 
-    @pl.when(k >= 5)
-    def _():
-        c = k - 5
-        total = keep2[lax.rem(c, 3), z]
+    def receive_z(c):
+        total = keep2[lax.rem(c, 4), part(z, rows), :]
         for j in range(3):
             by_z(c, j).wait_recv()
             total = total + come2[c, j].astype(F32)
 
-        @pl.when(c < first - 1)
-        def _():
-            wide_ref[0, 0] = total
-            wide_ref[1, 0] = layer_ref[...].astype(F32)
+        @pl.when(c < first)
+        def _():
+            out_ref[...] = total.T
+
+        @pl.when((c >= first) & (c < chunks - 1))
+        def _():
+            wide_ref[0] = total
+
+        @pl.when(c == chunks - 1)
+        def _():
+            side_out_ref[...] = total
+
+    def multiply(c):
+        @pl.when(c == 0)
+        def _():
+            for copy in mix_copies + gnl_copies:
+                copy.wait()
+
+        @pl.when(c == first)
+        def _():
+            normed_copy.wait()
+
+        @pl.when(c >= 3)
+        def _():
+            by_core(c - 3).wait_send()
+
+        def product(start):
+            columns = pl.ds(pl.multiple_of(start, 128), CHUNK)
+            send0[lax.rem(c, 3)] = dot_nn(left[part(1 - core, 8 * rows), :], low[:, columns]).astype(BF16)
+            by_core(c).start()
+            keep0[lax.rem(c, 2)] = dot_nn(left[part(core, 8 * rows), :], low[:, columns])
+
+        @pl.when(c < first)
+        def _():
+            product(width + c // halves * inner + lax.rem(c, halves) * CHUNK)
+
+        @pl.when((c >= first) & (c < chunks - 1))
+        def _():
+            kind, j = chunk_place(c - first, halves)
+            product(kind * inner + j * CHUNK)
+
+        @pl.when(c == chunks - 1)
+        def _():
+            product(2 * inner)
 
         @pl.when(c == first - 1)
         def _():
-            side_ref[0] = total
-            side_ref[1] = layer_ref[...].astype(F32)
-
-        @pl.when(c >= first)
-        def _():
-            out_ref[0] = total.T
-            out_ref[1] = out_layer_ref[...].astype(F32).T
-
-    for stage in range(5):
-
-        @pl.when(k == 2 * stage + 2)
-        def _():
-            by_all(stage).wait_recv()
-            total_ref[stage + 1] = total_ref[stage] + small_come[stage]
-            if stage < 4:
-                by_all(stage + 1).start()
-
-    @pl.when(k == chunks + 4)
+            normed_copy.start()
+
+    at(Z_LAG, receive_z)
+    at(X_LAG, receive_x)
+    at(1, receive_core)
+    at(0, multiply)
+
+    @pl.when(k == mixing_steps + 3 + Z_LAG)
     def _():
-        by_tensor.wait()
-        for stage in range(5):
+        for t in range(tile_count):
+            by_tensor(t).wait()
+            columns = slice(t * ROW_TILE, (t + 1) * ROW_TILE)
+            own_ref[:, columns] = own_ref[:, columns] + rows_come[t].astype(F32)
+        for stage in range(4):
             by_all(stage).wait_send()
-
-        def done(c, _):
+        for c in range(chunks - 3, chunks):
             by_core(c).wait_send()
+        for c in range(chunks - 4, chunks):
             by_x(c).wait_send()
             for j in range(3):
                 by_z(c, j).wait_send()
-            return 0
-
-        lax.fori_loop(0, chunks, done, 0)
-
-
-def scatter_product(left, right, out_left, out_right, layer, out_layer, small, sent, collective):
-    depth, tokens = left.shape
-    width = out_right.shape[1]
-    first, second = right.shape[1] // CHUNK, width // CHUNK
-    chunks = first + second
+
+
+def chunk_at(step, blocks):
+    return (
+        (jnp.clip(step, 0, blocks - 1) + 1) // 2
+        + jnp.clip(step - blocks + 1, 0, blocks) // 2
+        + jnp.clip(step - 2 * blocks + 1, 0, 4)
+    )
+
+
+def chunk_place(a, halves):
+    return lax.rem(a // halves, 2), a // (2 * halves) * halves + lax.rem(a, halves)
+
+
+def last_backward(
+    projected, pre, scanned, dgn, side, states, rows_in, chan, state_taps, headp,
+    small, own_left, other_left, normed_left, gnl, weight, q, collective,
+):
+    tokens, inner = pre.shape
+    depth = normed_left.shape[0]
+    blocks = tokens // q
+    groups = inner // SPAN
+    first = inner // CHUNK
+    halves = SPAN // CHUNK
+    mixing_steps = groups * blocks
+    chunks = 3 * first + 1
     rows = depth // 16
+    half = tokens // 2
+    tile_count = depth // ROW_TILE
+    last = mixing_steps - 1
+
+    def group(k):
+        return jnp.minimum(k, last) // blocks
+
+    def block(k):
+        return blocks - 1 - lax.rem(jnp.minimum(k, last), blocks)
+
+    def place(k):
+        return lax.rem(block(k) + lax.axis_index("tensor") * (blocks // 2), blocks)
+
+    def done(k):
+        return chunk_at(k - Z_LAG, blocks)
+
+    def wide_of(k):
+        return chunk_place(jnp.clip(done(k) - first, 0, 2 * first - 1), halves)
+
+    def out_of(k):
+        return jnp.minimum(done(k), first - 1)
+
     once = pl.Buffered(1)
     anywhere = pl.BlockSpec(memory_space=pl.ANY)
-    done = lambda k, start, count: jnp.clip(k - start, 0, count - 1)
+    columns = lambda start: pl.BlockSpec((q, SPAN), lambda k: (place(k), start + group(k)))
+    scratch = [
+        pltpu.VMEM((N, SPAN), F32), pltpu.VMEM((SPAN // PAIR, q + 8, PAIR), F32), pltpu.VMEM((q + 8, 2 * N), F32),
+        pltpu.VMEM((blocks, q, 128), F32), pltpu.VMEM((blocks, q, 128), F32), pltpu.VMEM((blocks, 128, q), F32),
+        pltpu.VMEM((blocks, q, q), F32),
+        pltpu.VMEM((blocks, q, N), BF16), pltpu.VMEM((blocks, q, N), BF16), pltpu.VMEM((blocks, N, q), BF16),
+        pltpu.VMEM((blocks, q, q), F32), pltpu.VMEM((blocks, q, N), F32), pltpu.VMEM((blocks, q, N), F32),
+        pltpu.VMEM((blocks, q, 128), F32), pltpu.VMEM((blocks, 128, q), F32),
+        pltpu.VMEM((3 * q + 16, SPAN), BF16), pltpu.VMEM((blocks, 3 * q + 16, 128), F32),
+        pltpu.VMEM((groups, SPAN, 128), BF16),
+        pltpu.VMEM((q, 128), F32), pltpu.VMEM((q, 128), F32),
+        pltpu.VMEM((q, q), BF16), pltpu.VMEM((q, 2 * q), BF16),
+        pltpu.VMEM((groups, 8, SPAN), F32), pltpu.VMEM((8, 2 * N), F32), pltpu.VMEM((8, 128), F32),
+        pltpu.VMEM((tokens, 2 * inner + SIDE), BF16), pltpu.VMEM((depth, tokens), BF16),
+        pltpu.VMEM((2, ROW_TILE, 2 * inner + SIDE), BF16),
+        pltpu.VMEM((2, 8 * rows, CHUNK), F32),
+        pltpu.VMEM((4, 4 * rows, CHUNK), F32),
+        pltpu.VMEM((4, 4 * rows, CHUNK), F32),
+        pltpu.VMEM((3, 8 * rows, CHUNK), BF16),
+        pltpu.VMEM((4, 4 * rows, CHUNK), BF16),
+        pltpu.VMEM((4, 4 * rows, CHUNK), BF16),
+        pltpu.VMEM((3, 8 * rows, CHUNK), BF16),
+        pltpu.VMEM((6, 4 * rows, CHUNK), BF16),
+        pltpu.VMEM((chunks, 3, rows, CHUNK), BF16),
+        pltpu.SemaphoreType.DMA((chunks,)), pltpu.SemaphoreType.DMA((chunks,)),
+        pltpu.SemaphoreType.DMA((chunks,)), pltpu.SemaphoreType.DMA((chunks,)),
+        pltpu.SemaphoreType.DMA((chunks, 3)), pltpu.SemaphoreType.DMA((chunks, 3)),
+        pltpu.VMEM((tile_count, half, ROW_TILE), BF16), pltpu.VMEM((tile_count, half, ROW_TILE), BF16),
+        pltpu.SemaphoreType.DMA((tile_count,)), pltpu.SemaphoreType.DMA((tile_count,)),
+        pltpu.VMEM((4, 16, inner + 2 * N), F32), pltpu.VMEM((4, 16, inner + 2 * N), F32),
+        pltpu.SemaphoreType.DMA((4,)), pltpu.SemaphoreType.DMA((4,)),
+        pltpu.SemaphoreType.DMA((7,)),
+    ]
     return pl.pallas_call(
-        functools.partial(scatter_product_kernel, first, chunks),
-        grid=(chunks + 5,),
+        functools.partial(last_backward_kernel, groups, blocks),
+        grid=(mixing_steps + 4 + Z_LAG,),
         in_specs=[
-            pl.BlockSpec((depth, tokens), lambda k: (0, 0), pipeline_mode=once),
-            pl.BlockSpec((tokens, CHUNK), lambda k: (0, done(k, 0, first))),
-            pl.BlockSpec((depth, tokens), lambda k: (0, 0), pipeline_mode=once),
-            pl.BlockSpec((tokens, CHUNK), lambda k: (0, done(k, first, second))),
-            pl.BlockSpec((rows, CHUNK), lambda k: (0, done(k, 5, first))),
-            pl.BlockSpec((rows, CHUNK), lambda k: (0, done(k, 5 + first, second))),
+            columns(0), columns(groups), columns(0), columns(0), columns(0),
+            pl.BlockSpec((tokens, SIDE + 2 * N), lambda k: (0, 0), pipeline_mode=once),
+            pl.BlockSpec((1, N, SPAN), lambda k: (block(k), 0, group(k))),
+            pl.BlockSpec((q, 128), lambda k: (place(k), 0)),
+            pl.BlockSpec((8, SPAN), lambda k: (0, group(k))),
+            pl.BlockSpec((8, 2 * N), lambda k: (0, 0)),
+            pl.BlockSpec((8, 128), lambda k: (0, 0)),
             pl.BlockSpec(small.shape, lambda k: (0, 0), pipeline_mode=once),
-            anywhere,
+            anywhere, anywhere, anywhere, anywhere, anywhere,
         ],
         out_specs=[
-            pl.BlockSpec(
-                (LAYERS, 1, rows, CHUNK),
-                lambda k: (0, done(k, 5, first - 1) // second, 0, lax.rem(done(k, 5, first - 1), second)),
-            ),
-            pl.BlockSpec((LAYERS, rows, CHUNK), lambda k: (0, 0, 0)),
-            pl.BlockSpec((LAYERS, CHUNK, rows), lambda k: (0, done(k, 5 + first, second), 0)),
-            pl.BlockSpec((6,) + small.shape, lambda k: (0, 0, 0)),
-            anywhere,
+            pl.BlockSpec((1, rows, CHUNK), lambda k: (wide_of(k)[0], 0, wide_of(k)[1])),
+            pl.BlockSpec((rows, CHUNK), lambda k: (0, 0)),
+            pl.BlockSpec((CHUNK, rows), lambda k: (out_of(k), 0)),
+            pl.BlockSpec((16, inner + 2 * N), lambda k: (0, 0)),
+            pl.BlockSpec((half, depth), lambda k: (0, 0)),
         ],
         out_shape=[
-            jax.ShapeDtypeStruct((LAYERS, 2, rows, width), F32),
-            jax.ShapeDtypeStruct((LAYERS, rows, CHUNK), F32),
-            jax.ShapeDtypeStruct((LAYERS, width, rows), F32),
-            jax.ShapeDtypeStruct((6,) + small.shape, F32),
-            jax.ShapeDtypeStruct(sent.shape, sent.dtype),
+            jax.ShapeDtypeStruct((2, rows, inner), F32),
+            jax.ShapeDtypeStruct((rows, CHUNK), F32),
+            jax.ShapeDtypeStruct((inner, rows), F32),
+            jax.ShapeDtypeStruct((16, inner + 2 * N), F32),
+            jax.ShapeDtypeStruct((half, depth), F32),
         ],
-        scratch_shapes=[
-            pltpu.SemaphoreType.DMA, pltpu.SemaphoreType.DMA,
-            pltpu.VMEM((5,) + small.shape, F32),
-            pltpu.SemaphoreType.DMA((5,)), pltpu.SemaphoreType.DMA((5,)),
-            pltpu.VMEM((2, 8, rows, CHUNK), F32),
-            pltpu.VMEM((3, 4, rows, CHUNK), F32),
-            pltpu.VMEM((3, 4, rows, CHUNK), F32),
-            pltpu.VMEM((chunks, 8, rows, CHUNK), BF16),
-            pltpu.VMEM((chunks, 4, rows, CHUNK), BF16),
-            pltpu.VMEM((chunks, 4, rows, CHUNK), BF16),
-            pltpu.VMEM((chunks, 8, rows, CHUNK), BF16),
-            pltpu.VMEM((chunks, 4, rows, CHUNK), BF16),
-            pltpu.VMEM((chunks, 3, rows, CHUNK), BF16),
-            pltpu.SemaphoreType.DMA((chunks,)), pltpu.SemaphoreType.DMA((chunks,)),
-            pltpu.SemaphoreType.DMA((chunks,)), pltpu.SemaphoreType.DMA((chunks,)),
-            pltpu.SemaphoreType.DMA((chunks, 3)), pltpu.SemaphoreType.DMA((chunks, 3)),
-        ],
+        scratch_shapes=scratch,
         compiler_params=pltpu.CompilerParams(
-            collective_id=collective, has_side_effects=True, vmem_limit_bytes=56 << 20
+            collective_id=collective, has_side_effects=True, vmem_limit_bytes=60 << 20
         ),
-        cost_estimate=pl.CostEstimate(flops=90_000_000_000, bytes_accessed=20_000_000, transcendentals=0),
-        name="scatter_product",
-    )(left, right, out_left, out_right, layer, out_layer, small, sent)
+        cost_estimate=pl.CostEstimate(flops=130_000_000_000, bytes_accessed=60_000_000, transcendentals=0),
+        name="last_backward",
+    )(
+        projected, projected, pre, scanned, dgn, side, states, rows_in, chan, state_taps, headp,
+        small, own_left, other_left, normed_left, gnl, weight,
+    )
 
 
 def last_sums_kernel(
     pre_ref, total_ref, side_ref, pre_out, taps_out, decay_out, bias_out, skip_out, gain_out, state_out, step_out,
-    held, come, sent, side_come, ss, rs, side_ss, side_rs,
+    held, come, sent, side_come, total_come, ss, rs, side_ss, side_rs,
 ):
     me = lax.axis_index("dp")
     tensor = lax.axis_index("tensor")
@@ -626,45 +960,69 @@
     sent[...] = side_ref[:, :, : 2 * N]
     held[0] = pre_ref[...]
     pl.semaphore_wait(barrier, len(peers))
-    swap = pltpu.make_async_remote_copy(
-        src_ref=sent, dst_ref=side_come, send_sem=side_ss, recv_sem=side_rs,
-        device_id=(me, 1 - tensor), device_id_type=pl.DeviceIdType.MESH,
-    )
-    swap.start()
+
+    def remote(source, target, send, receive, peer):
+        return pltpu.make_async_remote_copy(
+            src_ref=source, dst_ref=target, send_sem=send, recv_sem=receive,
+            device_id=peer, device_id_type=pl.DeviceIdType.MESH,
+        )
+
+    swaps = [
+        remote(sent, side_come, side_ss.at[0], side_rs.at[0], (me, 1 - tensor)),
+        remote(total_ref, total_come, side_ss.at[1], side_rs.at[1], (me, 1 - tensor)),
+    ]
     total = held[0]
     for first, last, level in ((0, 7, 0), (7, 10, 1)):
         copies = [
-            pltpu.make_async_remote_copy(
-                src_ref=held.at[level], dst_ref=come.at[i], send_sem=ss.at[i], recv_sem=rs.at[i],
-                device_id=peers[i], device_id_type=pl.DeviceIdType.MESH,
-            )
-            for i in range(first, last)
+            remote(held.at[level], come.at[i], ss.at[i], rs.at[i], peers[i]) for i in range(first, last)
         ]
         for copy in copies:
             copy.start()
         if level == 0:
-            for layer in range(LAYERS):
-                rows = 8 * layer
-                taps_out[layer] = total_ref[rows : rows + taps_out.shape[1], :]
-                gain_out[layer : layer + 1, :] = total_ref[rows + 5 : rows + 6, 0 : gain_out.shape[1]]
-                pre_out[layer : layer + 1, :] = total_ref[rows + 6 : rows + 7, 0 : pre_out.shape[1]]
-                for i, out in enumerate((decay_out, bias_out, skip_out)):
-                    out[layer : layer + 1, :] = total_ref[rows + 7 : rows + 8, 128 * i : 128 * i + out.shape[1]]
-            step_out[...] = side_ref[:, :, 2 * N : 2 * N + step_out.shape[2]]
+            for swap in swaps:
+                swap.start()
         for copy in copies:
             copy.wait()
         for i in range(first, last):
             total = total + come[i]
         held[level + 1] = total
-    pre_out[0:1, :] = total[0:1, :]
-    swap.wait()
+    pre_out[0:1, :] = total
+    step_out[...] = side_ref[:, :, 2 * N : 2 * N + step_out.shape[2]]
+    for swap in swaps:
+        swap.wait()
     state_out[...] = sent[...] + side_come[...]
-
-
-def last_sums(pre, total, side, heads, all_heads, collective):
-    depth, inner = pre.shape[1], total.shape[1] - 2 * N
-    shapes = [(LAYERS, depth), (LAYERS, KCONV + 1, total.shape[1])] + [(LAYERS, all_heads)] * 3
-    shapes += [(LAYERS, inner), side.shape[:2] + (2 * N,), side.shape[:2] + (heads,)]
+    width = total_ref.shape[1] - 2 * N
+    count = taps_out.shape[1]
+    heads = step_out.shape[2]
+    to_heads = ((iota((width, 128), 0) // HEAD) == iota((width, 128), 1)).astype(F32)
+    both = total_ref[...] + total_come[...]
+    for layer in range(LAYERS):
+        at = 8 * layer
+        if layer > 0:
+            pre_out[layer : layer + 1, :] = both[at + 7 : at + 8, 0 : pre_out.shape[1]]
+        taps_out[layer, :, 2 * width :] = both[at : at + count, width:]
+    for here in range(2):
+
+        @pl.when(tensor == here)
+        def _():
+            for place, ref in ((here, total_ref), (1 - here, total_come)):
+                lanes = slice(place * width, (place + 1) * width)
+                skips = exact_nn(ref[:, 0:width], to_heads)
+                for layer in range(LAYERS):
+                    at = 8 * layer
+                    row = slice(layer, layer + 1)
+                    taps_out[layer, :, lanes] = ref[at : at + count, 0:width]
+                    gain_out[row, lanes] = ref[at + 5 : at + 6, 0:width]
+                    some = slice(place * heads, (place + 1) * heads)
+                    decay_out[row, some] = ref[at + 5 : at + 6, width : width + heads]
+                    bias_out[row, some] = ref[at + 6 : at + 7, width : width + heads]
+                    skip_out[row, some] = skips[at + 6 : at + 7, 0:heads]
+
+
+def last_sums(pre, total, side, heads, collective):
+    depth, width = pre.shape[1], total.shape[1] - 2 * N
+    shapes = [(LAYERS, depth), (LAYERS, KCONV + 1, 2 * width + 2 * N)] + [(LAYERS, 2 * heads)] * 3
+    shapes += [(LAYERS, 2 * width), side.shape[:2] + (2 * N,), side.shape[:2] + (heads,)]
     vmem = pl.BlockSpec(memory_space=pltpu.VMEM)
     return pl.pallas_call(
         last_sums_kernel,
@@ -673,9 +1031,9 @@
         out_shape=[jax.ShapeDtypeStruct(shape, F32) for shape in shapes],
         scratch_shapes=[
             pltpu.VMEM((3,) + pre.shape, F32), pltpu.VMEM((10,) + pre.shape, F32),
-            pltpu.VMEM(shapes[-2], F32), pltpu.VMEM(shapes[-2], F32),
+            pltpu.VMEM(shapes[-2], F32), pltpu.VMEM(shapes[-2], F32), pltpu.VMEM(total.shape, F32),
             pltpu.SemaphoreType.DMA((10,)), pltpu.SemaphoreType.DMA((10,)),
-            pltpu.SemaphoreType.DMA, pltpu.SemaphoreType.DMA,
+            pltpu.SemaphoreType.DMA((2,)), pltpu.SemaphoreType.DMA((2,)),
         ],
         compiler_params=pltpu.CompilerParams(collective_id=collective, has_side_effects=True),
         name="last_sums",
@@ -841,8 +1199,13 @@
     return with_layout_constraint(values, Layout(tuple(range(values.ndim))))
 
 
-def after(values, *others):
-    return lax.optimization_barrier((values,) + others)[0]
+def together(*values):
+    return lax.optimization_barrier(values)
+
+
+def by_peers(values):
+    tokens, depth = values.shape
+    return values.T.reshape(4, 2, 2, depth // 16, tokens).transpose(2, 1, 0, 3, 4).reshape(depth, tokens)
 
 
 class Pair:
@@ -865,14 +1228,12 @@
         there = self.swap(values)
         return values + jnp.concatenate([there[self.rows :], there[: self.rows]], 0)
 
-    def project(self, function, values, exchange=None, *beside):
-        if not beside and exchange is None:
-            both = rowwise(function(values))
-            return rowwise(both[: self.rows] + self.swap(both[self.rows :].astype(BF16)).astype(F32))
+    def project(self, function, values, *beside):
         sent = rowwise(function(values[self.rows :]).astype(BF16))
-        come = (exchange or self.swap)(sent)
-        mine = after(rowwise(function(values[: self.rows])), *beside)
-        return rowwise(mine + come.astype(F32))
+        come = self.swap(sent)
+        mine = rowwise(function(values[: self.rows]))
+        mine, come, *beside = together(mine, come, *beside)
+        return [rowwise(mine + come.astype(F32))] + beside
 
     def sum_all(self, values):
         return values + self.swap(values)
@@ -895,10 +1256,11 @@
     def total(self, values):
         return lax.psum(values, "tensor")
 
-    def project(self, function, values, exchange=None, *beside):
-        return lax.psum_scatter(
+    def project(self, function, values, *beside):
+        total = lax.psum_scatter(
             function(values).astype(BF16), "tensor", scatter_dimension=0, tiled=True
         ).astype(F32)
+        return [total] + list(beside)
 
     def sum_all(self, values):
         return lax.psum(values, "tensor")
@@ -906,10 +1268,6 @@
 
 def scatter_call(values):
     return lax.psum_scatter(values, "dp", scatter_dimension=0, tiled=True)
-
-
-def after(values, *others):
-    return lax.optimization_barrier((values,) + others)[0]
 
 
 def per_device(
@@ -937,7 +1295,17 @@
     head_start = tensor_index * heads
     lane_start = tensor_index * width
     q = min(BLOCK, local_rows * tensor_size)
-    fused = tensor_size == 2 and lax.axis_size("dp") == 16 and (2 * width + SIDE) % CHUNK == 0
+    fused = (
+        tensor_size == 2
+        and lax.axis_size("dp") == 16
+        and width == 2 * SPAN
+        and heads <= 32
+        and SIDE == CHUNK
+        and depth <= width
+        and depth % ROW_TILE == 0
+        and local_rows % ROW_TILE == 0
+        and local_rows * 2 // q == 8
+    )
     group = (Pair if tensor_size == 2 and local_rows % q == 0 else Group)(local_rows)
     turn = group.turn(q).astype(jnp.int32).reshape(1)
     position = tensor_index * local_rows + jnp.arange(local_rows)
@@ -970,10 +1338,12 @@
                 shards[0], [jnp.pad(rows, ((0, local_rows), (0, 0))) for rows in (normed, last_mix_low)], 5
             )
         else:
-            shard = after(shards[layer], projections[0]) if layer > 0 else shards[layer]
+            shard = shards[layer]
+            if layer > 0:
+                shard, projections[0] = together(shard, projections[0])
             full = lax.all_gather(shard, "dp", axis=0, tiled=True)
         projections.append(full)
-        shard = after(out_weight[layer].T, projections[0])
+        shard, projections[0] = together(out_weight[layer].T, projections[0])
         outputs.append(lax.all_gather(shard, "dp", axis=0, tiled=True))
     if not fused:
         first_normed_all, last_mix_all = group.gather(normed), group.gather(last_mix_low)
@@ -1001,7 +1371,6 @@
             ((0, 6), (0, 128 - heads)),
         )
         tables.append((chan, state_taps, headp))
-
     saved = []
     for layer in range(LAYERS):
         chan, state_taps, headp = tables[layer]
@@ -1010,33 +1379,26 @@
             inv_rows = lax.rsqrt(jnp.mean(hidden * hidden, axis=-1, keepdims=True) + EPSILON)
             normed = rowwise((hidden * inv_rows * pre_gain[layer]).astype(BF16))
             normed_all = group.gather(normed)
+            if fused:
+                gate_norm = (saved[0][4].astype(F32) * saved[0][9]).astype(BF16)
         projected = dot_nn(normed_all, projections[layer][:, : 2 * width]).astype(BF16)
         gnl, scanned, pre, side, states, squares = forward_mixer(
             turn, projected, normed_all, projections[layer], chan, state_taps, headp, q, width
         )
         if layer == 0 and fused:
-            normed_turned = normed_all.T
-            gnl = after(gnl, normed_turned)
+            normed_turned = by_peers(normed_all)
         square_sum = group.total(jnp.sum(squares, axis=-1, keepdims=True))
         inv_gate = lax.rsqrt(square_sum / inner + EPSILON)
         mixed_raw = None
         if layer < LAYERS - 1:
-            mixed_raw = group.project(lambda rows: dot_nt(rows, outputs[layer]), gnl)
+            beside = [normed_turned] if fused else []
+            mixed_raw, *beside = group.project(lambda rows: dot_nt(rows, outputs[layer]), gnl, *beside)
+            normed_turned = beside[0] if fused else None
         saved.append(
             (hidden, inv_rows, normed_all, projected, gnl, scanned, pre, side, states, inv_gate, mixed_raw)
         )
         if layer < LAYERS - 1:
             hidden = rowwise(keep_rows * (hidden + mixed_raw * group.own(inv_gate)))
-
-    def last_hidden(low_gradient, gathered):
-        hidden, gnl, inv_gate = saved[-1][0], saved[-1][4], saved[-1][9]
-        swap = group.swap if tensor_size == 2 else None
-        mixed_raw = group.project(
-            lambda rows: dot_nt(rows, outputs[-1]),
-            after(gnl, low_gradient),
-            lambda sent: swap(after(sent, gathered)),
-        )
-        return keep_rows * (hidden + mixed_raw * group.own(inv_gate))
 
     grad_mix, mix_all = last_mix, last_mix_all
     grads_projection, grads_output, small, pre_sums = [], [], [], []
@@ -1059,47 +1421,55 @@
             0,
         )
 
+    def small_local(dchan, dstate, dhead, grad_pre):
+        lanes = jnp.concatenate([dchan[:7], jnp.pad(grad_pre[None], ((0, 0), (0, width - depth)))], 0)
+        beside = jnp.concatenate([dstate[:5], jnp.pad(dhead[:2], ((0, 0), (0, 2 * N - 128))), dstate[7:8]], 0)
+        return jnp.concatenate([lanes, beside], 1)
+
     for layer in reversed(range(LAYERS)):
         chan, state_taps, headp = tables[layer]
         (hidden, inv_rows, normed_all, projected, gnl, scanned, pre, side, states, inv_gate, mixed_raw) = saved[layer]
+        if layer > 0 or not fused:
+            scaled_mix = (mix_all.astype(F32) * inv_gate).astype(BF16)
+            product = dot_tn(scaled_mix, gnl).astype(BF16)
+            mix_all, product = together(mix_all, product)
+            grads_output.append(scatter_call(product))
         dgn = dot_nn(mix_all, outputs[layer]).astype(BF16)
         if layer == LAYERS - 1:
             cross = group.total(jnp.sum(gnl.astype(F32) * dgn.astype(F32), axis=-1, keepdims=True))
+            gnl, cross = together(gnl, cross)
+            if fused:
+                sent = rowwise(dot_nt(gnl[local_rows:], outputs[layer]).astype(BF16))
+                dgn, sent = together(dgn, sent)
+                come = group.swap(sent)
+            else:
+                mixed_raw = group.project(lambda rows: dot_nt(rows, outputs[layer]), gnl)[0]
+                out_hidden = keep_rows * (hidden + mixed_raw * group.own(inv_gate))
         else:
             cross = group.gather(
                 jnp.sum(grad_mix.astype(BF16).astype(F32) * mixed_raw, axis=-1, keepdims=True)
             )
-        scaled_mix = (mix_all.astype(F32) * inv_gate).astype(BF16)
-        if layer > 0 or not fused:
-            product = dot_tn(scaled_mix, gnl).astype(BF16)
-            dgn = after(dgn, product)
-        else:
-            mix_turned = scaled_mix.T
-        if layer > 0 or not fused:
-            grads_output.append(scatter_call(product))
         rows_in = jnp.pad(
             jnp.concatenate([inv_gate, inv_gate * inv_gate * inv_gate * cross / inner], 1), ((0, 0), (0, 126))
         )
-        low, dchan, dstate, dhead = backward_mixer(
-            turn, projected, pre, scanned, dgn, side, states, rows_in, chan, state_taps, headp, q, width
-        )
+        if layer == 0 and fused:
+            wide_sums, side_sums, out_sums, total, grad_normed = last_backward(
+                projected, pre, scanned, dgn, side, states, rows_in, chan, state_taps, headp,
+                small[0], *mix_turned, normed_turned, gate_norm, projections[0], q, 3,
+            )
+        else:
+            low, dchan, dstate, dhead = backward_mixer(
+                turn, projected, pre, scanned, dgn, side, states, rows_in, chan, state_taps, headp, q, width
+            )
+            if layer == LAYERS - 1 and fused:
+                low, come = together(low, come)
+                mixed_raw = rowwise(dot_nt(gnl[:local_rows], outputs[layer])) + come.astype(F32)
+                out_hidden = keep_rows * (hidden + mixed_raw * group.own(inv_gate))
         project = lambda rows: dot_nt(rows, projections[layer])
         if layer > 0 or not fused:
             product = dot_tn(normed_all, low).astype(BF16)
-            grad_normed = group.project(project, low, None, product)
+            grad_normed, product = group.project(project, low, product)
             grads_projection.append(scatter_call(product))
-        else:
-
-            def exchange(sent):
-                small.append(small_of(dchan, dstate, dhead, jnp.zeros_like(pre_sums[0])))
-                found = scatter_product(
-                    normed_turned, low, mix_turned, gnl, grads_projection[0], grads_output[0],
-                    jnp.concatenate(small[::-1]), sent, 3,
-                )
-                small.extend(found[:4])
-                return found[4]
-
-            grad_normed = group.project(project, low, exchange)
         unit_rows = hidden * inv_rows
         grad_pre = jnp.sum(grad_normed * unit_rows, axis=0)
         grad_unit = grad_normed * pre_gain[layer]
@@ -1108,18 +1478,24 @@
         )
         pre_sums.append(grad_pre)
         if layer > 0 or not fused:
-            small.append(small_of(dchan, dstate, dhead, grad_pre))
+            small.append((small_local if fused else small_of)(dchan, dstate, dhead, grad_pre))
         if layer > 0:
             grad_mix = rowwise(keep_rows * grad_flow)
             mix_low = rowwise(grad_mix.astype(BF16))
             mix_all = group.gather(mix_low)
-            if layer == LAYERS - 1:
-                out_hidden = last_hidden(mix_low, mix_all)
+            if fused:
+                own_turned = by_peers(mix_low)
+                mix_all, own_turned = together(mix_all, own_turned)
+                mix_turned = (own_turned, by_peers(mix_all[local_rows:]))
     if fused:
-        grad_gate_value, side, grad_out, total = small[-4:]
+        layer_sums = grads_projection[0].astype(F32)
         pre, taps, decay, bias, skip, gain, grad_state, grad_step = last_sums(
-            grad_pre[None], total[5], side, heads, all_heads, 4
-        )
+            grad_pre[None], total, jnp.stack([side_sums, layer_sums[:, 2 * width :]]), heads, 4
+        )
+        grad_gate_value = jnp.stack(
+            [wide_sums, jnp.stack([layer_sums[:, :width], layer_sums[:, width : 2 * width]])]
+        )
+        grad_out = jnp.stack([out_sums, grads_output[0].astype(F32).T])
     else:
         total = lax.psum(jnp.stack(small[::-1]), ("dp", "tensor"))
         pre, taps, gain = total[:, 6, :depth], total[:, :count], total[:, 5, :inner]

time: 721 us -> 672 us (0.932)
  matrix products: 139 us -> 115 us
  Pallas kernels: 351 us -> 331 us
  other arithmetic: 40.7 us -> 32.7 us
    pallas_call x2 -> x1, Pallas kernels: 94.6 us -> 38.3 us  [backward_mixer(): pl.pallas_call(backward_kernel, grid_spec=pltpu.PrefetchScalarGridSpec(nu...]
    pallas_call x1, Pallas kernels: 119 us -> 159 us  [last_backward(): pl.pallas_call(functools.partial(last_backward_kernel, groups, blocks), g...]
    dot_general x7 -> x6, matrix products: 62.3 us -> 42.9 us  [dot_nt(): lax.dot_general(a, b, (((1,), (1,)), ((), ())), preferred_element_type=F32)]
    transpose x1 -> x8, local copies, waits for them, and re-layouts: 0.85 us -> 19.4 us  [the longest x7 17.5 us: by_peers(): values.T.reshape(4, 2, 2, depth // 16, tokens).transpose(2, 1, 0, 3, 4)]
    unnamed x134 -> x132, local copies, waits for them, and re-layouts: 21.2 us -> 14.3 us
  transfers between devices with their start and end apart: 14 -> 14, of which waited for: 8 -> 8; matrix products, arithmetic and copies ran while one was open for 23% -> 23% of each run, Pallas kernels for 20% -> 37%
where the time goes in v4:
time: 672 us; the launch traced here: 663 us
  Pallas kernels  331 us (49%)
  matrix products  115 us (17%)
  waiting for transfers between devices  114 us (17%)
  local copies, waits for them, and re-layouts  43.9 us (7%)
  other arithmetic  32.7 us (5%)
  between operations  15.7 us (2%)
  starting transfers between devices  11.3 us (2%)
    pallas_call x1, Pallas kernels, last_backward(): pl.pallas_call(functools.partial(last_backward_kernel, groups, blocks), g...  159 us
    ppermute x9, waiting for transfers between devices, swap(): return lax.ppermute(values, 'tensor', [(0, 1), (1, 0)])  101 us
    pallas_call x1, Pallas kernels, gather_all(): pl.pallas_call(functools.partial(gather_kernel, count), in_specs=[anywher...  73.1 us
    dot_general x4, matrix products, dot_nn(): lax.dot_general(a, b, (((1,), (0,)), ((), ())), preferred_element_type=F32)  48.3 us
    pallas_call x2, Pallas kernels, forward_mixer(): pl.pallas_call(forward_kernel, grid_spec=pltpu.PrefetchScalarGridSpec(num...  47.5 us
    dot_general x6, matrix products, dot_nt(): lax.dot_general(a, b, (((1,), (1,)), ((), ())), preferred_element_type=F32)  42.9 us
    pallas_call x1, Pallas kernels, backward_mixer(): pl.pallas_call(backward_kernel, grid_spec=pltpu.PrefetchScalarGridSpec(nu...  38.3 us
    dot_general x2, matrix products, dot_tn(): lax.dot_general(a, b, (((0,), (0,)), ((), ())), preferred_element_type=F32)  24 us
  transfers between devices with their start and end apart: 14, of which 8 were waited for; matrix products, arithmetic and copies ran while one was open for 23% of the time, Pallas kernels for 37%

profile of v4, /device:TPU:0, one launch (start us, length us, event | category | flops | bytes accessed | tf_op | source)
XLA Modules:
  0.0 663.5 jit_solution(4527953471390511901)
XLA Ops:
  21.5 73.1 %gather_all.1 = (bf16[1536,3456]{1,0:T(8,128)(2,1)}, bf16[1024,1536]{1,0:T(8,128)(2,1)}, bf16[1024,1536]{1,0:T(8,128)(2,1)}) custom-call(bf16[96,3456]{1,0:T(8,128)(2,1)} %get-tuple-element.206.refs_0_, bf16[1024,1536]{1,0:T(8,128)(2,1)} %pad.40.refs_1_, bf16[1024,1536]{1,0:T(8,128)(2,1)} %pad.41.refs_2_), custom_call_target="tpu_custom_call", output_to_operand_aliasing={{1}: (1, {}), {2}: (2, {})} | custom-call | flops 60000002048 | bytes 20000000 | tf_op jit(solution)/shard_map/gather_all/pallas_call | solution.py:1174
  96.4 15.2 %fusion.4.gate_ref.value_ref = bf16[1024,3072]{1,0:T(8,128)(2,1)} fusion(bf16[1024,1536]{1,0:T(8,128)(2,1)} %get-tuple-element.66.normed_ref, bf16[1536,3456]{1,0:T(8,128)(2,1)} %get-tuple-element.70.side_weight_ref.weight_ref), kind=kOutput, calls=%fused_computation.9 | convolution fusion | flops 9666822144 | bytes 18874368 | tf_op jit(solution)/shard_map/dot_general | solution.py:20
  111.6 23.9 %forward_mixer.2 = (bf16[1024,1536]{1,0:T(8,128)(2,1)}, bf16[1024,1536]{1,0:T(8,128)(2,1)}, bf16[1024,1536]{1,0:T(8,128)(2,1)}, f32[1024,640]{1,0:T(8,128)S(1)},...) custom-call(s32[1]{0:T(128)} %bitcast.1.turn_ref, bf16[1024,3072]{1,0:T(8,128)(2,1)} %fusion.4.gate_ref.value_ref, ...), custom_call_target="tpu_custom_call" | custom-call | flops 31457280000 | bytes 31457280 | tf_op jit(solution)/shard_map/forward_mixer/pallas_call | solution.py:319
  136.9 11.4 %all-gather.4.cloned.1.call-done = bf16[1536,1536]{1,0:T(8,128)(2,1)} async-done(((bf16[96,1536]{1,0:T(8,128)(2,1)}), bf16[1536,1536]{1,0:T(8,128)(2,1)}) %all-gather.4.cloned.1.call-update) | async-done | bytes 4718608 | tf_op jit(solution)/shard_map/all_gather | solution.py:1347
  148.3 6.6 convolution_convert_fusion.5
  157.5 4.7 copy.63
  166.4 25.5 %collective-permute-done.1 = f32[1024,1]{0,1:T(1,128)S(1)} collective-permute-done((f32[1024,1]{0,1:T(1,128)S(1)}, f32[1024,1]{0,1:T(1,128)S(1)}, u32[]{:S(2)}, u32[]{:S(2)}) %collective-permute-start.1) | collective-permute-done | bytes 4128 | tf_op jit(solution)/shard_map/ppermute | solution.py:1216
  191.9 4.6 fusion.35
  202.1 34.2 %collective-permute-done.2 = bf16[512,1536]{1,0:T(8,128)(2,1)S(1)} collective-permute-done((bf16[512,1536]{1,0:T(8,128)(2,1)S(1)}, bf16[512,1536]{1,0:T(8,128)(2,1)S(1)}, u32[]{:S(2)}, u32[]{:S(2)}) %collective-permute-start.2) | collective-permute-done | bytes 1572896 | tf_op jit(solution)/shard_map/ppermute | solution.py:1216
  239.4 14.6 %fusion.7.gate_ref.value_ref = bf16[1024,3072]{1,0:T(8,128)(2,1)} fusion(bf16[1536,3456]{1,0:T(8,128)(2,1)} %all-gather.6.cloned.1.call-done.side_weight_ref, bf16[512,1536]{1,0:T(8,128)(2,1)} %copy-done.22, bf16[512,1536]{1,0:T(8,128)(2,1)S(1)} %multiply_convert_fusion.3), kind=kOutput, calls=%fused_computation.10 | convolution fusion | flops 9673113600 | bytes 18874368 | tf_op jit(solution)/shard_map/dot_general | solution.py:20
  254.0 23.7 %forward_mixer.3 = (bf16[1024,1536]{1,0:T(8,128)(2,1)}, bf16[1024,1536]{1,0:T(8,128)(2,1)}, bf16[1024,1536]{1,0:T(8,128)(2,1)}, f32[1024,640]{1,0:T(8,128)S(1)},...) custom-call(s32[1]{0:T(128)} %bitcast.1.turn_ref, bf16[1024,3072]{1,0:T(8,128)(2,1)} %fusion.7.gate_ref.value_ref, ...), custom_call_target="tpu_custom_call" | custom-call | flops 31457280000 | bytes 31457280 | tf_op jit(solution)/shard_map/forward_mixer/pallas_call | solution.py:319
  281.6 9.7 %convolution_convert_fusion.1 = bf16[1536,1536]{1,0:T(8,128)(2,1)} fusion(bf16[1024,1536]{1,0:T(8,128)(2,1)} %get-tuple-element.82, bf16[1024,1536]{1,0:T(8,128)(2,1)} %get-tuple-element.80, f32[1024]{0:T(1024)S(1)} %fusion.50), kind=kOutput, calls=%fused_computation.5 | convolution fusion | flops 4838916096 | bytes 11014144 | tf_op jit(solution)/shard_map/dot_general | solution.py:28
  291.6 9.8 %multiply_reduce_fusion = (f32[1024]{0:T(1024)S(1)}, bf16[1024,1536]{1,0:T(8,128)(2,1)}) fusion(bf16[1024,1536]{1,0:T(8,128)(2,1)} %get-tuple-element.82, bf16[1024,1536]{1,0:T(8,128)(2,1)} %get-tuple-element.80, bf16[1536,1536]{1,0:T(8,128)(2,1)} %all-gather.8.cloned.1.call-done), kind=kOutput, calls=%fused_computation.7 | convolution fusion | flops 4839701504 | bytes 14159872 | tf_op jit(solution)/shard_map/dot_general | solution.py:20
  305.3 5.8 convolution_convert_fusion.4
  312.8 38.3 %backward_mixer.1 = (bf16[1024,3456]{1,0:T(8,128)(2,1)}, f32[8,1536]{1,0:T(8,128)S(1)}, f32[8,256]{1,0:T(8,128)S(1)}, f32[8,128]{1,0:T(8,128)S(1)}) custom-call(s32[1]{0:T(128)} %bitcast.1.turn_ref, bf16[1024,3072]{1,0:T(8,128)(2,1)} %fusion.7.gate_ref.value_ref, bf16[1024,3072]{1,0:T(8,128)(2,1)} %fusion.7.gate_ref.value_ref, ...), custom_call_target="tpu_custom_call" | custom-call | flops 55050240000 | bytes 31457280 | tf_op jit(solution)/shard_map/backward_mixer/pallas_call | solution.py:367
  355.4 11.3 %fusion.28 = bf16[512,1536]{1,0:T(8,128)(2,1)} fusion(bf16[1536,3456]{1,0:T(8,128)(2,1)} %all-gather.6.cloned.1.call-done.side_weight_ref, bf16[1024,3456]{1,0:T(8,128)(2,1)} %get-tuple-element.92), kind=kOutput, calls=%fused_computation.46 | convolution fusion | flops 5436604416 | bytes 15728640 | tf_op jit(solution)/shard_map/dot_general | solution.py:24
  367.3 14.3 %convolution_convert_fusion = bf16[1536,3456]{1,0:T(8,128)(2,1)} fusion(bf16[1024,3456]{1,0:T(8,128)(2,1)S(1)} %copy-done.57, bf16[512,1536]{1,0:T(8,128)(2,1)S(1)} %copy-done.23, bf16[512,1536]{1,0:T(8,128)(2,1)S(1)} %copy-done.16), kind=kOutput, calls=%fused_computation | convolution fusion | flops 10883235840 | bytes 20840448 | tf_op jit(solution)/shard_map/dot_general | solution.py:28
  381.5 10.3 %fusion.16 = f32[512,1536]{1,0:T(8,128)S(1)} fusion(bf16[1536,3456]{1,0:T(8,128)(2,1)} %all-gather.6.cloned.1.call-done.side_weight_ref, bf16[1024,3456]{1,0:T(8,128)(2,1)} %get-tuple-element.92), kind=kOutput, calls=%fused_computation.22 | convolution fusion | flops 5435817984 | bytes 17301504 | tf_op jit(solution)/shard_map/dot_general | solution.py:24
  391.9 10.0 %collective-permute-done.6 = bf16[512,1536]{1,0:T(8,128)(2,1)S(1)} collective-permute-done((bf16[512,1536]{1,0:T(8,128)(2,1)}, bf16[512,1536]{1,0:T(8,128)(2,1)S(1)}, u32[]{:S(2)}, u32[]{:S(2)}) %collective-permute-start.6) | collective-permute-done | bytes 1572896 | tf_op jit(solution)/shard_map/ppermute | solution.py:1216
  403.1 5.6 multiply_reduce_fusion.2
  415.7 27.2 %collective-permute-done.8 = f32[512,1]{0,1:T(1,128)S(1)} collective-permute-done((f32[512,1]{0,1:T(1,128)S(1)}, f32[512,1]{0,1:T(1,128)S(1)}, u32[]{:S(2)}, u32[]{:S(2)}) %collective-permute-start.8) | collective-permute-done | bytes 2080 | tf_op jit(solution)/shard_map/ppermute | solution.py:1216
  454.2 8.7 %convolution_convert_fusion.2.dgn_ref = bf16[1024,1536]{1,0:T(8,128)(2,1)} fusion(bf16[1024,1536]{1,0:T(8,128)(2,1)S(1)} %copy-done.12, bf16[1536,1536]{1,0:T(8,128)(2,1)} %all-gather.4.cloned.1.call-done), kind=kOutput, calls=%fused_computation.18 | convolution fusion | flops 4833411072 | bytes 11010048 | tf_op jit(solution)/shard_map/dot_general | solution.py:20
  463.0 158.6 %last_backward.1 = (f32[2,96,1536]{2,1,0:T(8,128)}, f32[96,384]{1,0:T(8,128)}, f32[1536,96]{1,0:T(8,128)}, f32[16,1792]{1,0:T(8,128)}, f32[512,1536]{1,0:T(8,128)}) custom-call(bf16[1024,3072]{1,0:T(8,128)(2,1)} %fusion.4.gate_ref.value_ref, bf16[1024,3072]{1,0:T(8,128)(2,1)} %fusion.4.gate_ref.value_ref, bf16[1024,1536]{1,0:T(8,128)(2,1)} %get-tuple-element.95.pre_ref, ...), custom_call_target="tpu_custom_call" | custom-call | flops 130000003072 | bytes 60000000 | tf_op jit(solution)/shard_map/last_backward/pallas_call | solution.py:908
  634.5 13.7 %last_sums.1 = (f32[2,1536]{1,0:T(2,128)}, f32[2,5,3328]{2,1,0:T(8,128)}, f32[2,48]{1,0:T(2,128)}, f32[2,48]{1,0:T(2,128)}, f32[2,48]{1,0:T(2,128)}, /*index=5*/...) custom-call(f32[1,1536]{1,0:T(1,128)} %broadcast_in_dim.11.pre_ref, f32[16,1792]{1,0:T(8,128)} %get-tuple-element.108.total_ref, ...), custom_call_target="tpu_custom_call" | custom-call | tf_op jit(solution)/shard_map/last_sums/pallas_call | solution.py:1027
  (248 shorter events, 87.2 us)
Async XLA Ops:
  7.2 141.1 %all-gather.4.cloned.1.call-start = ((), (), s32[]{:S(2)}) async-start(), calls=%async_computation.2 | async-start | bytes 5013504 | tf_op jit(solution)/shard_map/all_gather | solution.py:1347
  11.3 188.8 %copy-start.29 = (f32[1536]{0:T(1024)}, f32[1536]{0:T(1024)S(1)}, u32[]{:S(2)}) copy-start(f32[1536]{0:T(1024)S(1)} %get-tuple-element.160) | copy-start | bytes 18436
  15.7 180.9 %copy-start.41 = (f32[512]{0:T(512)}, f32[512]{0:T(512)S(1)}, u32[]{:S(2)}) copy-start(f32[512]{0:T(512)S(1)} %fusion.57) | copy-start | bytes 6148
  21.4 74.0 %copy-start.50 = (f32[2,48]{1,0:T(2,128)S(1)}, f32[2,48]{1,0:T(2,128)}, u32[]{:S(2)}) copy-start(f32[2,48]{1,0:T(2,128)} %param.24) | copy-start | bytes 1156
  21.4 74.4 %copy-start.28 = (f32[2,5,3328]{2,0,1:T(2,128)S(1)}, f32[2,5,3328]{2,0,1:T(2,128)}, u32[]{:S(2)}) copy-start(f32[2,5,3328]{2,0,1:T(2,128)} %param.21) | copy-start | bytes 399364
  21.4 74.7 %copy-start.51 = (f32[2,48]{1,0:T(2,128)S(1)}, f32[2,48]{1,0:T(2,128)}, u32[]{:S(2)}) copy-start(f32[2,48]{1,0:T(2,128)} %param.22) | copy-start | bytes 1156
  21.4 74.7 %copy-start.52 = (f32[2,48]{1,0:T(2,128)S(1)}, f32[2,48]{1,0:T(2,128)}, u32[]{:S(2)}) copy-start(f32[2,48]{1,0:T(2,128)} %param.23) | copy-start | bytes 1156
  21.4 74.8 %copy-start.43 = (f32[2,3072]{1,0:T(2,128)S(1)}, f32[2,3072]{1,0:T(2,128)}, u32[]{:S(2)}) copy-start(f32[2,3072]{1,0:T(2,128)} %param.25) | copy-start | bytes 73732
  94.6 144.8 %all-gather.6.cloned.1.call-start = ((), (), s32[]{:S(2)}) async-start(), calls=%async_computation.3 | async-start | bytes 11280384 | tf_op jit(solution)/shard_map/all_gather | solution.py:1344
  95.4 196.2 %all-gather.8.cloned.1.call-start = ((), (), s32[]{:S(2)}) async-start(), calls=%async_computation.4 | async-start | bytes 5013504 | tf_op jit(solution)/shard_map/all_gather | solution.py:1347
  154.9 41.6 %collective-permute-start = (bf16[512,1536]{1,0:T(8,128)(2,1)}, bf16[512,1536]{1,0:T(8,128)(2,1)}, u32[]{:S(2)}, u32[]{:S(2)}) collective-permute-start(bf16[512,1536]{1,0:T(8,128)(2,1)} %convolution_convert_fusion.5), channel_id=1, source_target_pairs={{0,1},{1,0},{2,3},{3,2},{4,5},{5,4},{6,7},{7,6},{8,9},{9,8},{10,11... | collective-permute-start | bytes 4718600 | tf_op jit(solution)/shard_map/ppermute | solution.py:1216
  156.6 35.2 %collective-permute-start.1 = (f32[1024,1]{0,1:T(1,128)S(1)}, f32[1024,1]{0,1:T(1,128)S(1)}, u32[]{:S(2)}, u32[]{:S(2)}) collective-permute-start(f32[1024,1]{0,1:T(1,128)S(1)} %bitcast.110), channel_id=1, source_target_pairs={{0,1},{1,0},{2,3},{3,2},{4,5},{5,4},{6,7},{7,6},{8,9},{9,8},{10,11... | collective-permute-start | bytes 12296 | tf_op jit(solution)/shard_map/ppermute | solution.py:1216
  157.3 472.3 %reduce-scatter.7.cloned.1.call-start = ((), (), s32[]{:S(2)}) async-start(), calls=%async_computation.6 | async-start | bytes 5013504
  200.5 35.9 %collective-permute-start.2 = (bf16[512,1536]{1,0:T(8,128)(2,1)S(1)}, bf16[512,1536]{1,0:T(8,128)(2,1)S(1)}, u32[]{:S(2)}, u32[]{:S(2)}) collective-permute-start(bf16[512,1536]{1,0:T(8,128)(2,1)S(1)} %multiply_convert_fusion.3), channel_id=1, source_target_pairs={{0,1},{1,0},{2,3},{3,2},{4,5},{5,4},{6,7},{7,6},{8,9},{9,8},{10,11... | collective-permute-start | bytes 4718600 | tf_op jit(solution)/shard_map/ppermute | solution.py:1216
  277.9 3.7 collective-permute-start.3
  301.4 3.6 collective-permute-start.4
  302.9 329.6 %reduce-scatter.5.cloned.1.call-start = ((), (), s32[]{:S(2)}) async-start(), calls=%async_computation.5 | async-start | bytes 11280384 | tf_op jit(solution)/shard_map/reduce_scatter | solution.py:1270
  311.1 44.3 %collective-permute-start.5 = (bf16[512,1536]{1,0:T(8,128)(2,1)S(1)}, bf16[512,1536]{1,0:T(8,128)(2,1)S(1)}, u32[]{:S(2)}, u32[]{:S(2)}) collective-permute-start(bf16[512,1536]{1,0:T(8,128)(2,1)S(1)} %convolution_convert_fusion.4), channel_id=1, source_target_pairs={{0,1},{1,0},{2,3},{3,2},{4,5},{5,4},{6,7},{7,6},{8,9},{9,8},{10,11... | collective-permute-start | bytes 4718600 | tf_op jit(solution)/shard_map/ppermute | solution.py:1216
  366.7 35.2 %collective-permute-start.6 = (bf16[512,1536]{1,0:T(8,128)(2,1)}, bf16[512,1536]{1,0:T(8,128)(2,1)S(1)}, u32[]{:S(2)}, u32[]{:S(2)}) collective-permute-start(bf16[512,1536]{1,0:T(8,128)(2,1)} %fusion.28), channel_id=1, source_target_pairs={{0,1},{1,0},{2,3},{3,2},{4,5},{5,4},{6,7},{7,6},{8,9},{9,8},{10,11... | collective-permute-start | bytes 4718600 | tf_op jit(solution)/shard_map/ppermute | solution.py:1216
  408.7 35.3 %collective-permute-start.7 = (bf16[512,1536]{1,0:T(8,128)(2,1)S(1)}, bf16[512,1536]{1,0:T(8,128)(2,1)}, u32[]{:S(2)}, u32[]{:S(2)}) collective-permute-start(bf16[512,1536]{1,0:T(8,128)(2,1)S(1)} %get-tuple-element.163), channel_id=1, source_target_pairs={{0,1},{1,0},{2,3},{3,2},{4,5},{5,4},{6,7},{7,6},{8,9},{9,8},{10,11... | collective-permute-start | bytes 4718600 | tf_op jit(solution)/shard_map/ppermute | solution.py:1216
  411.6 31.3 %collective-permute-start.8 = (f32[512,1]{0,1:T(1,128)S(1)}, f32[512,1]{0,1:T(1,128)S(1)}, u32[]{:S(2)}, u32[]{:S(2)}) collective-permute-start(f32[512,1]{0,1:T(1,128)S(1)} %bitcast.120), channel_id=1, source_target_pairs={{0,1},{1,0},{2,3},{3,2},{4,5},{5,4},{6,7},{7,6},{8,9},{9,8},{10,11... | collective-permute-start | bytes 6152 | tf_op jit(solution)/shard_map/ppermute | solution.py:1216
  462.9 158.7 %copy-start.7 = (bf16[512,1536]{1,0:T(8,128)(2,1)S(1)}, bf16[512,1536]{1,0:T(8,128)(2,1)}, u32[]{:S(2)}) copy-start(bf16[512,1536]{1,0:T(8,128)(2,1)} %param.13) | copy-start | bytes 4718596
  462.9 158.7 %copy-start.32 = (f32[1536]{0:T(1024)S(1)}, f32[1536]{0:T(1024)}, u32[]{:S(2)}) copy-start(f32[1536]{0:T(1024)} %copy-done.31) | copy-start | bytes 18436
  462.9 158.7 %copy-start.40 = (f32[512]{0:T(512)S(1)}, f32[512]{0:T(512)}, u32[]{:S(2)}) copy-start(f32[512]{0:T(512)} %copy-done.39) | copy-start | bytes 6148
  (50 other events, 602.3 us)
Sparse Core Ops, SparseCore 0:
  94.7 53.5 all-gather.3
  150.6 87.2 all-gather.5
  240.2 51.3 all-gather.7
  303.0 73.1 reduce-scatter.6
  413.3 152.8 reduce-scatter.4

commit v5 on v4

--- a/solution.py
+++ b/solution.py
@@ -350,7 +350,7 @@
             jax.ShapeDtypeStruct((rows, 128), F32),
         ],
         compiler_params=pltpu.CompilerParams(vmem_limit_bytes=48 << 20),
-        cost_estimate=pl.CostEstimate(flops=rows * width * 20000, bytes_accessed=rows * width * 20, transcendentals=0),
+        cost_estimate=pl.CostEstimate(flops=2_000_000_000, bytes_accessed=1_000_000, transcendentals=0),
         name="forward_mixer",
     )(turn, projected, projected, normed, packed, chan, state_taps, headp)
 
@@ -400,7 +400,7 @@
             jax.ShapeDtypeStruct((8, 128), F32),
         ],
         compiler_params=pltpu.CompilerParams(vmem_limit_bytes=48 << 20),
-        cost_estimate=pl.CostEstimate(flops=rows * width * 35000, bytes_accessed=rows * width * 20, transcendentals=0),
+        cost_estimate=pl.CostEstimate(flops=2_000_000_000, bytes_accessed=1_000_000, transcendentals=0),
         name="backward_mixer",
     )(turn, projected, projected, pre, scanned, dgn, side, states, rows_in, chan, state_taps, headp)
 CHUNK = 384
@@ -415,7 +415,7 @@
     groups, blocks,
     gate_ref, value_ref, pre_ref, scanned_ref, dgn_ref, side_ref, states_ref, rows_ref,
     chan_ref, state_taps_ref, headp_ref, small_ref,
-    own_left_ref, other_left_ref, normed_left_ref, gnl_ref, weight_ref,
+    own_left_ref, other_left_ref, normed_left_ref, gnl_ref, weight_ref, before_ref,
     wide_ref, side_out_ref, out_ref, total_ref, own_ref,
     lam, gbuf, gsbuf, step_s, run_s, runt_s, cbt_s, bmat, cmat, cmat_t,
     dcbt, db, dc, col_s, rowt_s, per_head, head_s, spread, inv_s, pull_s, lower, later_s,
@@ -837,7 +837,7 @@
 
 def last_backward(
     projected, pre, scanned, dgn, side, states, rows_in, chan, state_taps, headp,
-    small, own_left, other_left, normed_left, gnl, weight, q, collective,
+    small, own_left, other_left, normed_left, gnl, weight, before, q, collective,
 ):
     tokens, inner = pre.shape
     depth = normed_left.shape[0]
@@ -917,7 +917,7 @@
             pl.BlockSpec((8, 2 * N), lambda k: (0, 0)),
             pl.BlockSpec((8, 128), lambda k: (0, 0)),
             pl.BlockSpec(small.shape, lambda k: (0, 0), pipeline_mode=once),
-            anywhere, anywhere, anywhere, anywhere, anywhere,
+            anywhere, anywhere, anywhere, anywhere, anywhere, anywhere,
         ],
         out_specs=[
             pl.BlockSpec((1, rows, CHUNK), lambda k: (wide_of(k)[0], 0, wide_of(k)[1])),
@@ -937,11 +937,11 @@
         compiler_params=pltpu.CompilerParams(
             collective_id=collective, has_side_effects=True, vmem_limit_bytes=60 << 20
         ),
-        cost_estimate=pl.CostEstimate(flops=130_000_000_000, bytes_accessed=60_000_000, transcendentals=0),
+        cost_estimate=pl.CostEstimate(flops=2_000_000_000, bytes_accessed=1_000_000, transcendentals=0),
         name="last_backward",
     )(
         projected, projected, pre, scanned, dgn, side, states, rows_in, chan, state_taps, headp,
-        small, own_left, other_left, normed_left, gnl, weight,
+        small, own_left, other_left, normed_left, gnl, weight, before,
     )
 
 
@@ -1038,11 +1038,14 @@
         compiler_params=pltpu.CompilerParams(collective_id=collective, has_side_effects=True),
         name="last_sums",
     )(pre, total, side)
-
-
-def gather_kernel(count, *refs):
-    shard_ref, swap_refs, full_ref, come_refs = refs[0], refs[1 : 1 + count], refs[1 + count], refs[2 + count : 2 + 2 * count]
-    local, zs, zr, xs, xr, cs, cr, ys, yr = refs[2 + 2 * count :]
+EPSILON = 1e-05
+
+
+def gather_kernel(
+    hidden_ref, cotangent_ref, keep_ref, gain_ref, gate_value_ref, state_ref, step_ref,
+    full_ref, normed_ref, mix_ref,
+    shard_ref, normed_s, mix_s, local, zs, zr, xs, xr, cs, cr, ys, yr,
+):
     me = lax.axis_index("dp")
     tensor = lax.axis_index("tensor")
     core, x_bit, z = lax.rem(me, 2), lax.rem(me // 2, 2), me // 4
@@ -1074,6 +1077,12 @@
             source, place(block_z, block_x), cs.at[block_z, block_x], cr.at[block_z, block_x], (core_peer, tensor)
         )
 
+    width = gate_value_ref.shape[3]
+    shard_ref[:, 0:width] = gate_value_ref[0, 0]
+    shard_ref[:, width : 2 * width] = gate_value_ref[0, 1]
+    shard_ref[:, 2 * width : 2 * width + 2 * N] = state_ref[0]
+    shard_ref[:, 2 * width + 2 * N :] = jnp.zeros((rows, 128), BF16)
+    shard_ref[:, 2 * width + 2 * N : 2 * width + 2 * N + step_ref.shape[2]] = step_ref[0]
     barrier = pltpu.get_barrier_semaphore()
     for peer in [(core_peer, tensor), (x_peer, tensor), (me, 1 - tensor)]:
         pl.semaphore_signal(barrier, inc=1, device_id=peer, device_id_type=pl.DeviceIdType.MESH)
@@ -1106,17 +1115,37 @@
 
     by_x(z).start()
     by_core(z, x_bit).start()
-    half = come_refs[0].shape[0] // 2
+    mine = pltpu.make_async_copy(shard_ref, place(z, x_bit), local.at[0])
+    mine.start()
+    half = hidden_ref.shape[0]
     swaps = [
-        remote(
-            target.at[pl.ds(0, half), :], target.at[pl.ds(half, half), :], ys.at[i], yr.at[i], (me, 1 - tensor)
-        )
-        for i, target in enumerate(come_refs)
+        remote(source, target.at[pl.ds(half, half), :], ys.at[i], yr.at[i], (me, 1 - tensor))
+        for i, (source, target) in enumerate(((normed_s, normed_ref), (mix_s, mix_ref)))
     ]
-    for swap in swaps:
-        swap.start()
-    mine = pltpu.make_async_copy(shard_ref, place(z, x_bit), local)
-    mine.start()
+    kept = [
+        pltpu.make_async_copy(source, target.at[pl.ds(0, half), :], local.at[1 + i])
+        for i, (source, target) in enumerate(((normed_s, normed_ref), (mix_s, mix_ref)))
+    ]
+
+    def normalize(i, _):
+        here = pl.ds(pl.multiple_of(i * 64, 64), 64)
+        hidden = hidden_ref[here, :].astype(F32)
+        inv = lax.rsqrt(jnp.mean(hidden * hidden, axis=-1, keepdims=True) + EPSILON)
+        normed_s[here, :] = (hidden * inv * gain_ref[0:1, :]).astype(BF16)
+        return 0
+
+    lax.fori_loop(0, half // 64, normalize, 0)
+    swaps[0].start()
+    kept[0].start()
+
+    def mask(i, _):
+        here = pl.ds(pl.multiple_of(i * 64, 64), 64)
+        mix_s[here, :] = (cotangent_ref[here, :].astype(F32) * keep_ref[here, :]).astype(BF16)
+        return 0
+
+    lax.fori_loop(0, half // 64, mask, 0)
+    swaps[1].start()
+    kept[1].start()
 
     def arrived(block_z, up, further):
         along(block_z, up).wait_recv()
@@ -1163,35 +1192,45 @@
         for block_x in range(2):
             by_core(block_z, block_x).wait()
     mine.wait()
-    for swap in swaps:
+    for swap in swaps + kept:
         swap.wait()
 
 
-def gather_all(shard, swapped, collective):
-    rows, columns = shard.shape
+def gather_all(hidden, cotangent, keep, gain, gate_value, state, step, collective):
+    half, depth = hidden.shape
+    rows, width = gate_value.shape[2:]
+    columns = 2 * width + SIDE
     anywhere = pl.BlockSpec(memory_space=pl.ANY)
-    count = len(swapped)
+    first = lambda shape: pl.BlockSpec(shape, lambda i: (0,) * len(shape))
     return pl.pallas_call(
-        functools.partial(gather_kernel, count),
-        in_specs=[anywhere] * (1 + count),
-        out_specs=[anywhere] * (1 + count),
-        out_shape=[jax.ShapeDtypeStruct((16 * rows, columns), shard.dtype)]
-        + [jax.ShapeDtypeStruct(values.shape, values.dtype) for values in swapped],
+        gather_kernel,
+        grid=(1,),
+        in_specs=[
+            first((half, depth)), first((half, depth)), first((half, 1)), first((1, depth)),
+            first((1, 2, rows, width)), first((1, rows, 2 * N)), first((1, rows, step.shape[2])),
+        ],
+        out_specs=[anywhere] * 3,
+        out_shape=[
+            jax.ShapeDtypeStruct((16 * rows, columns), BF16),
+            jax.ShapeDtypeStruct((2 * half, depth), BF16),
+            jax.ShapeDtypeStruct((2 * half, depth), BF16),
+        ],
         scratch_shapes=[
-            pltpu.SemaphoreType.DMA,
+            pltpu.VMEM((rows, columns), BF16), pltpu.VMEM((half, depth), BF16), pltpu.VMEM((half, depth), BF16),
+            pltpu.SemaphoreType.DMA((3,)),
             pltpu.SemaphoreType.DMA((2, 4)), pltpu.SemaphoreType.DMA((4,)),
             pltpu.SemaphoreType.DMA((4,)), pltpu.SemaphoreType.DMA((4,)),
             pltpu.SemaphoreType.DMA((4, 2)), pltpu.SemaphoreType.DMA((4, 2)),
-            pltpu.SemaphoreType.DMA((count,)), pltpu.SemaphoreType.DMA((count,)),
+            pltpu.SemaphoreType.DMA((2,)), pltpu.SemaphoreType.DMA((2,)),
         ],
-        input_output_aliases={1 + i: 1 + i for i in range(count)},
-        compiler_params=pltpu.CompilerParams(collective_id=collective, has_side_effects=True),
-        cost_estimate=pl.CostEstimate(flops=60_000_000_000, bytes_accessed=20_000_000, transcendentals=0),
+        compiler_params=pltpu.CompilerParams(
+            collective_id=collective, has_side_effects=True, vmem_limit_bytes=60 << 20
+        ),
+        cost_estimate=pl.CostEstimate(flops=2_000_000_000, bytes_accessed=1_000_000, transcendentals=0),
         name="gather_all",
-    )(shard, *swapped)
-
-
-EPSILON = 1e-05
+    )(hidden, cotangent, keep, gain, gate_value, state, step)
+
+
 BLOCK = 128
 
 
@@ -1335,7 +1374,7 @@
     for layer in range(LAYERS):
         if layer == 0 and fused:
             full, first_normed_all, last_mix_all = gather_all(
-                shards[0], [jnp.pad(rows, ((0, local_rows), (0, 0))) for rows in (normed, last_mix_low)], 5
+                hidden_in, cotangent, keep_rows, pre_gain[:1], gate_value_weight, state_weight, step_weight, 5
             )
         else:
             shard = shards[layer]
@@ -1385,15 +1424,17 @@
         gnl, scanned, pre, side, states, squares = forward_mixer(
             turn, projected, normed_all, projections[layer], chan, state_taps, headp, q, width
         )
-        if layer == 0 and fused:
-            normed_turned = by_peers(normed_all)
         square_sum = group.total(jnp.sum(squares, axis=-1, keepdims=True))
         inv_gate = lax.rsqrt(square_sum / inner + EPSILON)
         mixed_raw = None
         if layer < LAYERS - 1:
-            beside = [normed_turned] if fused else []
-            mixed_raw, *beside = group.project(lambda rows: dot_nt(rows, outputs[layer]), gnl, *beside)
-            normed_turned = beside[0] if fused else None
+            if fused:
+                normed_turned = by_peers(normed_all)
+                mixed_raw, normed_turned = group.project(
+                    lambda rows: dot_nt(rows, outputs[layer]), gnl, normed_turned
+                )
+            else:
+                mixed_raw = group.project(lambda rows: dot_nt(rows, outputs[layer]), gnl)[0]
         saved.append(
             (hidden, inv_rows, normed_all, projected, gnl, scanned, pre, side, states, inv_gate, mixed_raw)
         )
@@ -1455,7 +1496,7 @@
         if layer == 0 and fused:
             wide_sums, side_sums, out_sums, total, grad_normed = last_backward(
                 projected, pre, scanned, dgn, side, states, rows_in, chan, state_taps, headp,
-                small[0], *mix_turned, normed_turned, gate_norm, projections[0], q, 3,
+                small[0], *mix_turned, normed_turned, gate_norm, projections[0], product[:16, :128], q, 3,
             )
         else:
             low, dchan, dstate, dhead = backward_mixer(
@@ -1467,9 +1508,18 @@
                 out_hidden = keep_rows * (hidden + mixed_raw * group.own(inv_gate))
         project = lambda rows: dot_nt(rows, projections[layer])
         if layer > 0 or not fused:
-            product = dot_tn(normed_all, low).astype(BF16)
-            grad_normed, product = group.project(project, low, product)
-            grads_projection.append(scatter_call(product))
+            if fused:
+                sent = rowwise(project(low[local_rows:]).astype(BF16))
+                low, sent = together(low, sent)
+                come = group.swap(sent)
+                product = dot_tn(normed_all, low).astype(BF16)
+                grads_projection.append(scatter_call(product))
+                mine = rowwise(project(low[:local_rows]))
+                mine, come, product = together(mine, come, product)
+                grad_normed = rowwise(mine + come.astype(F32))
+            else:
+                grads_projection.append(scatter_call(dot_tn(normed_all, low).astype(BF16)))
+                grad_normed = group.project(project, low)[0]
         unit_rows = hidden * inv_rows
         grad_pre = jnp.sum(grad_normed * unit_rows, axis=0)
         grad_unit = grad_normed * pre_gain[layer]

time: 672 us -> 650 us (0.967)
  Pallas kernels: 331 us -> 308 us
  waiting for transfers between devices: 114 us -> 124 us
    pallas_call x1, Pallas kernels: 159 us -> 131 us  [last_backward(): pl.pallas_call(functools.partial(last_backward_kernel, groups, blocks), g...]
    ppermute x9, waiting for transfers between devices: 101 us -> 112 us  [swap(): return lax.ppermute(values, 'tensor', [(0, 1), (1, 0)])]
    unnamed x132 -> x93, local copies, waits for them, and re-layouts: 14.3 us -> 15.1 us
  transfers between devices with their start and end apart: 14 -> 14, of which waited for: 8 -> 8; matrix products, arithmetic and copies ran while one was open for 23% -> 25% of each run, Pallas kernels for 37% -> 34%
where the time goes in v5:
time: 650 us; the launch traced here: 641 us
  Pallas kernels  308 us (47%)
  waiting for transfers between devices  124 us (19%)
  matrix products  113 us (17%)
  local copies, waits for them, and re-layouts  38.5 us (6%)
  other arithmetic  30.9 us (5%)
  between operations  15.7 us (2%)
  starting transfers between devices  11 us (2%)
    pallas_call x1, Pallas kernels, last_backward(): pl.pallas_call(functools.partial(last_backward_kernel, groups, blocks), g...  131 us
    ppermute x9, waiting for transfers between devices, swap(): return lax.ppermute(values, 'tensor', [(0, 1), (1, 0)])  112 us
    pallas_call x1, Pallas kernels, gather_all(): pl.pallas_call(gather_kernel, grid=(1,), in_specs=[first((half, depth)),...  76.2 us
    dot_general x4, matrix products, dot_nn(): lax.dot_general(a, b, (((1,), (0,)), ((), ())), preferred_element_type=F32)  48.1 us
    pallas_call x2, Pallas kernels, forward_mixer(): pl.pallas_call(forward_kernel, grid_spec=pltpu.PrefetchScalarGridSpec(num...  47.6 us
    dot_general x6, matrix products, dot_nt(): lax.dot_general(a, b, (((1,), (1,)), ((), ())), preferred_element_type=F32)  41 us
    pallas_call x1, Pallas kernels, backward_mixer(): pl.pallas_call(backward_kernel, grid_spec=pltpu.PrefetchScalarGridSpec(nu...  38 us
    dot_general x2, matrix products, dot_tn(): lax.dot_general(a, b, (((0,), (0,)), ((), ())), preferred_element_type=F32)  24 us
  transfers between devices with their start and end apart: 14, of which 8 were waited for; matrix products, arithmetic and copies ran while one was open for 25% of the time, Pallas kernels for 34%

profile of v5, /device:TPU:0, one launch (start us, length us, event | category | flops | bytes accessed | tf_op | source)
XLA Modules:
  0.0 640.8 jit_solution(14704492392726440568)
XLA Ops:
  13.9 76.2 %gather_all.1 = (bf16[1536,3456]{1,0:T(8,128)(2,1)}, bf16[1024,1536]{1,0:T(8,128)(2,1)}, bf16[1024,1536]{1,0:T(8,128)(2,1)}) custom-call(bf16[512,1536]{1,0:T(8,128)(2,1)} %hidden_ref.1, bf16[512,1536]{1,0:T(8,128)(2,1)} %cotangent_ref.1, f32[512,1]{1,0:T(8,128)} %fusion.36.keep_ref, f32[1,1536]{1,0:T(1,128)} %get-tuple-element.201.gain_ref, ...), custom_call_target="tpu_custom_call" | custom-call | flops 2000000000 | bytes 1000000 | tf_op jit(solution)/shard_map/gather_all/pallas_call | solution.py:1205
  94.2 14.1 %fusion.4.gate_ref.value_ref = bf16[1024,3072]{1,0:T(8,128)(2,1)} fusion(bf16[1024,1536]{1,0:T(8,128)(2,1)S(1)} %copy-done.11, bf16[1536,3456]{1,0:T(8,128)(2,1)} %get-tuple-element.72.side_weight_ref.weight_ref), kind=kOutput, calls=%fused_computation.9 | convolution fusion | flops 9666822144 | bytes 18874368 | tf_op jit(solution)/shard_map/dot_general | solution.py:20
  108.4 23.8 %forward_mixer.2 = (bf16[1024,1536]{1,0:T(8,128)(2,1)}, bf16[1024,1536]{1,0:T(8,128)(2,1)}, bf16[1024,1536]{1,0:T(8,128)(2,1)}, f32[1024,640]{1,0:T(8,128)S(1)},...) custom-call(s32[1]{0:T(128)} %bitcast.1.turn_ref, bf16[1024,3072]{1,0:T(8,128)(2,1)} %fusion.4.gate_ref.value_ref, ...), custom_call_target="tpu_custom_call" | custom-call | flops 2000000000 | bytes 1000000 | tf_op jit(solution)/shard_map/forward_mixer/pallas_call | solution.py:319
  134.4 9.4 %all-gather.4.cloned.1.call-done = bf16[1536,1536]{1,0:T(8,128)(2,1)} async-done(((bf16[96,1536]{1,0:T(8,128)(2,1)}), bf16[1536,1536]{1,0:T(8,128)(2,1)}) %all-gather.4.cloned.1.call-update) | async-done | bytes 4718608 | tf_op jit(solution)/shard_map/all_gather | solution.py:1386
  143.8 6.6 %convolution_convert_fusion.5 = bf16[512,1536]{1,0:T(8,128)(2,1)} fusion(bf16[1536,1536]{1,0:T(8,128)(2,1)} %all-gather.4.cloned.1.call-done, bf16[1024,1536]{1,0:T(8,128)(2,1)} %get-tuple-element.73), kind=kOutput, calls=%fused_computation.44 | convolution fusion | flops 2416705536 | bytes 7864320 | tf_op jit(solution)/shard_map/dot_general | solution.py:24
  158.1 29.2 %collective-permute-done.1 = f32[1024,1]{0,1:T(1,128)S(1)} collective-permute-done((f32[1024,1]{0,1:T(1,128)S(1)}, f32[1024,1]{0,1:T(1,128)S(1)}, u32[]{:S(2)}, u32[]{:S(2)}) %collective-permute-start.1) | collective-permute-done | bytes 4128 | tf_op jit(solution)/shard_map/ppermute | solution.py:1255
  187.4 4.7 fusion.32
  197.9 34.2 %collective-permute-done.2 = bf16[512,1536]{1,0:T(8,128)(2,1)S(1)} collective-permute-done((bf16[512,1536]{1,0:T(8,128)(2,1)S(1)}, bf16[512,1536]{1,0:T(8,128)(2,1)S(1)}, u32[]{:S(2)}, u32[]{:S(2)}) %collective-permute-start.2) | collective-permute-done | bytes 1572896 | tf_op jit(solution)/shard_map/ppermute | solution.py:1255
  234.4 14.3 %fusion.7.gate_ref.value_ref = bf16[1024,3072]{1,0:T(8,128)(2,1)} fusion(bf16[1536,3456]{1,0:T(8,128)(2,1)} %all-gather.6.cloned.1.call-done.side_weight_ref, bf16[512,1536]{1,0:T(8,128)(2,1)S(1)} %collective-permute-done.2, bf16[512,1536]{1,0:T(8,128)(2,1)S(1)} %multiply_convert_fusion.3), kind=kOutput, calls=%fused_computation.10 | convolution fusion | flops 9673113600 | bytes 18874368 | tf_op jit(solution)/shard_map/dot_general | solution.py:20
  248.7 23.8 %forward_mixer.3 = (bf16[1024,1536]{1,0:T(8,128)(2,1)}, bf16[1024,1536]{1,0:T(8,128)(2,1)}, bf16[1024,1536]{1,0:T(8,128)(2,1)}, f32[1024,640]{1,0:T(8,128)S(1)},...) custom-call(s32[1]{0:T(128)} %bitcast.1.turn_ref, bf16[1024,3072]{1,0:T(8,128)(2,1)} %fusion.7.gate_ref.value_ref, ...), custom_call_target="tpu_custom_call" | custom-call | flops 2000000000 | bytes 1000000 | tf_op jit(solution)/shard_map/forward_mixer/pallas_call | solution.py:319
  276.4 9.9 %convolution_convert_fusion.1 = bf16[1536,1536]{1,0:T(8,128)(2,1)} fusion(bf16[1024,1536]{1,0:T(8,128)(2,1)} %get-tuple-element.84, bf16[1024,1536]{1,0:T(8,128)(2,1)} %get-tuple-element.82, f32[1024]{0:T(1024)S(1)} %fusion.46), kind=kOutput, calls=%fused_computation.5 | convolution fusion | flops 4838916096 | bytes 11014144 | tf_op jit(solution)/shard_map/dot_general | solution.py:28
  287.8 10.9 %multiply_reduce_fusion = (f32[1024]{0:T(1024)S(1)}, bf16[1024,1536]{1,0:T(8,128)(2,1)}) fusion(bf16[1024,1536]{1,0:T(8,128)(2,1)} %get-tuple-element.84, bf16[1024,1536]{1,0:T(8,128)(2,1)} %get-tuple-element.82, bf16[1536,1536]{1,0:T(8,128)(2,1)} %all-gather.8.cloned.1.call-done), kind=kOutput, calls=%fused_computation.7 | convolution fusion | flops 4839701504 | bytes 14159872 | tf_op jit(solution)/shard_map/dot_general | solution.py:20
  307.9 38.0 %backward_mixer.1 = (bf16[1024,3456]{1,0:T(8,128)(2,1)}, f32[8,1536]{1,0:T(8,128)S(1)}, f32[8,256]{1,0:T(8,128)S(1)}, f32[8,128]{1,0:T(8,128)S(1)}) custom-call(s32[1]{0:T(128)} %bitcast.1.turn_ref, bf16[1024,3072]{1,0:T(8,128)(2,1)} %fusion.7.gate_ref.value_ref, bf16[1024,3072]{1,0:T(8,128)(2,1)} %fusion.7.gate_ref.value_ref, ...), custom_call_target="tpu_custom_call" | custom-call | flops 2000000000 | bytes 1000000 | tf_op jit(solution)/shard_map/backward_mixer/pallas_call | solution.py:367
  345.9 9.9 %fusion.25 = bf16[512,1536]{1,0:T(8,128)(2,1)S(1)} fusion(bf16[1536,3456]{1,0:T(8,128)(2,1)} %all-gather.6.cloned.1.call-done.side_weight_ref, bf16[1024,3456]{1,0:T(8,128)(2,1)} %get-tuple-element.95), kind=kOutput, calls=%fused_computation.42 | convolution fusion | flops 5436604416 | bytes 15728640 | tf_op jit(solution)/shard_map/dot_general | solution.py:24
  355.8 14.1 %convolution_convert_fusion = bf16[1536,3456]{1,0:T(8,128)(2,1)} fusion(bf16[1024,3456]{1,0:T(8,128)(2,1)S(1)} %copy-done.38, bf16[512,1536]{1,0:T(8,128)(2,1)S(1)} %copy-done.20, bf16[512,1536]{1,0:T(8,128)(2,1)S(1)} %copy-done.15), kind=kOutput, calls=%fused_computation | convolution fusion | flops 10883235840 | bytes 20840448 | tf_op jit(solution)/shard_map/dot_general | solution.py:28
  370.5 5.0 fusion.29
  375.5 11.2 %fusion.13 = f32[512,1536]{1,0:T(8,128)S(1)} fusion(bf16[1536,3456]{1,0:T(8,128)(2,1)} %all-gather.6.cloned.1.call-done.side_weight_ref, bf16[1024,3456]{1,0:T(8,128)(2,1)} %get-tuple-element.95), kind=kOutput, calls=%fused_computation.19 | convolution fusion | flops 5435817984 | bytes 17301504 | tf_op jit(solution)/shard_map/dot_general | solution.py:24
  386.7 18.4 %collective-permute-done.6 = bf16[512,1536]{1,0:T(8,128)(2,1)S(1)} collective-permute-done((bf16[512,1536]{1,0:T(8,128)(2,1)S(1)}, bf16[512,1536]{1,0:T(8,128)(2,1)S(1)}, u32[]{:S(2)}, u32[]{:S(2)}) %collective-permute-start.6) | collective-permute-done | bytes 1572896 | tf_op jit(solution)/shard_map/ppermute | solution.py:1255
  406.1 5.9 multiply_reduce_fusion.2
  420.3 26.0 %collective-permute-done.8 = f32[512,1]{0,1:T(1,128)S(1)} collective-permute-done((f32[512,1]{0,1:T(1,128)S(1)}, f32[512,1]{0,1:T(1,128)S(1)}, u32[]{:S(2)}, u32[]{:S(2)}) %collective-permute-start.8) | collective-permute-done | bytes 2080 | tf_op jit(solution)/shard_map/ppermute | solution.py:1255
  457.5 8.8 %convolution_convert_fusion.2.dgn_ref = bf16[1024,1536]{1,0:T(8,128)(2,1)} fusion(bf16[1024,1536]{1,0:T(8,128)(2,1)S(1)} %copy-done.13, bf16[1536,1536]{1,0:T(8,128)(2,1)} %all-gather.4.cloned.1.call-done), kind=kOutput, calls=%fused_computation.17 | convolution fusion | flops 4833411072 | bytes 11010048 | tf_op jit(solution)/shard_map/dot_general | solution.py:20
  466.3 131.1 %last_backward.1 = (f32[2,96,1536]{2,1,0:T(8,128)}, f32[96,384]{1,0:T(8,128)}, f32[1536,96]{1,0:T(8,128)}, f32[16,1792]{1,0:T(8,128)}, f32[512,1536]{1,0:T(8,128)}) custom-call(bf16[1024,3072]{1,0:T(8,128)(2,1)} %fusion.4.gate_ref.value_ref, bf16[1024,3072]{1,0:T(8,128)(2,1)} %fusion.4.gate_ref.value_ref, bf16[1024,1536]{1,0:T(8,128)(2,1)} %get-tuple-element.99.pre_ref, ...), custom_call_target="tpu_custom_call" | custom-call | flops 2000000000 | bytes 1000000 | tf_op jit(solution)/shard_map/last_backward/pallas_call | solution.py:908
  601.0 4.4 fusion.20
  610.4 15.0 %last_sums.1 = (f32[2,1536]{1,0:T(2,128)}, f32[2,5,3328]{2,1,0:T(8,128)}, f32[2,48]{1,0:T(2,128)}, f32[2,48]{1,0:T(2,128)}, f32[2,48]{1,0:T(2,128)}, /*index=5*/...) custom-call(f32[1,1536]{1,0:T(1,128)} %broadcast_in_dim.11.pre_ref, f32[16,1792]{1,0:T(8,128)} %get-tuple-element.112.total_ref, ...), custom_call_target="tpu_custom_call" | custom-call | tf_op jit(solution)/shard_map/last_sums/pallas_call | solution.py:1027
  (205 shorter events, 80.3 us)
Async XLA Ops:
  7.2 136.6 %all-gather.4.cloned.1.call-start = ((), (), s32[]{:S(2)}) async-start(), calls=%async_computation.2 | async-start | bytes 5013504 | tf_op jit(solution)/shard_map/all_gather | solution.py:1386
  13.9 76.4 %copy-start.26 = (bf16[2,96,24]{2,1,0:T(8,128)(2,1)S(1)}, bf16[2,96,24]{2,1,0:T(8,128)(2,1)}, u32[]{:S(2)}) copy-start(bf16[2,96,24]{2,1,0:T(8,128)(2,1)} %copy.75.step_ref) | copy-start | bytes 27652
  13.9 76.4 %copy-start.28 = (bf16[2,96,256]{2,1,0:T(8,128)(2,1)S(1)}, bf16[2,96,256]{2,1,0:T(8,128)(2,1)}, u32[]{:S(2)}) copy-start(bf16[2,96,256]{2,1,0:T(8,128)(2,1)} %state_ref.1) | copy-start | bytes 294916
  90.2 143.9 %all-gather.6.cloned.1.call-start = ((), (), s32[]{:S(2)}) async-start(), calls=%async_computation.3 | async-start | bytes 11280384 | tf_op jit(solution)/shard_map/all_gather | solution.py:1383
  92.5 195.3 %all-gather.8.cloned.1.call-start = ((), (), s32[]{:S(2)}) async-start(), calls=%async_computation.4 | async-start | bytes 5013504 | tf_op jit(solution)/shard_map/all_gather | solution.py:1386
  93.2 512.2 %reduce-scatter.7.cloned.1.call-start = ((), (), s32[]{:S(2)}) async-start(), calls=%async_computation.6 | async-start | bytes 5013504
  150.4 41.7 %collective-permute-start = (bf16[512,1536]{1,0:T(8,128)(2,1)}, bf16[512,1536]{1,0:T(8,128)(2,1)}, u32[]{:S(2)}, u32[]{:S(2)}) collective-permute-start(bf16[512,1536]{1,0:T(8,128)(2,1)} %convolution_convert_fusion.5), channel_id=1, source_target_pairs={{0,1},{1,0},{2,3},{3,2},{4,5},{5,4},{6,7},{7,6},{8,9},{9,8},{10,11... | collective-permute-start | bytes 4718600 | tf_op jit(solution)/shard_map/ppermute | solution.py:1255
  152.1 35.2 %collective-permute-start.1 = (f32[1024,1]{0,1:T(1,128)S(1)}, f32[1024,1]{0,1:T(1,128)S(1)}, u32[]{:S(2)}, u32[]{:S(2)}) collective-permute-start(f32[1024,1]{0,1:T(1,128)S(1)} %bitcast.103), channel_id=1, source_target_pairs={{0,1},{1,0},{2,3},{3,2},{4,5},{5,4},{6,7},{7,6},{8,9},{9,8},{10,11... | collective-permute-start | bytes 12296 | tf_op jit(solution)/shard_map/ppermute | solution.py:1255
  156.0 31.4 %copy-start.16 = (bf16[1024,1536]{1,0:T(8,128)(2,1)S(1)}, bf16[1024,1536]{1,0:T(8,128)(2,1)}, u32[]{:S(2)}) copy-start(bf16[1024,1536]{1,0:T(8,128)(2,1)} %get-tuple-element.73) | copy-start | bytes 9437188
  196.2 37.9 %copy-start.14 = (bf16[512,1536]{1,0:T(8,128)(2,1)}, bf16[512,1536]{1,0:T(8,128)(2,1)S(1)}, u32[]{:S(2)}) copy-start(bf16[512,1536]{1,0:T(8,128)(2,1)S(1)} %multiply_convert_fusion.3) | copy-start | bytes 4718596
  196.2 35.8 %collective-permute-start.2 = (bf16[512,1536]{1,0:T(8,128)(2,1)S(1)}, bf16[512,1536]{1,0:T(8,128)(2,1)S(1)}, u32[]{:S(2)}, u32[]{:S(2)}) collective-permute-start(bf16[512,1536]{1,0:T(8,128)(2,1)S(1)} %multiply_convert_fusion.3), channel_id=1, source_target_pairs={{0,1},{1,0},{2,3},{3,2},{4,5},{5,4},{6,7},{7,6},{8,9},{9,8},{10,11... | collective-permute-start | bytes 4718600 | tf_op jit(solution)/shard_map/ppermute | solution.py:1255
  272.7 3.7 collective-permute-start.3
  286.3 322.0 %reduce-scatter.5.cloned.1.call-start = ((), (), s32[]{:S(2)}) async-start(), calls=%async_computation.5 | async-start | bytes 11280384 | tf_op jit(solution)/shard_map/reduce_scatter | solution.py:1309
  298.7 3.6 collective-permute-start.4
  306.1 39.8 %collective-permute-start.5 = (bf16[512,1536]{1,0:T(8,128)(2,1)}, bf16[512,1536]{1,0:T(8,128)(2,1)}, u32[]{:S(2)}, u32[]{:S(2)}) collective-permute-start(bf16[512,1536]{1,0:T(8,128)(2,1)} %convolution_convert_fusion.4), channel_id=1, source_target_pairs={{0,1},{1,0},{2,3},{3,2},{4,5},{5,4},{6,7},{7,6},{8,9},{9,8},{10,11... | collective-permute-start | bytes 4718600 | tf_op jit(solution)/shard_map/ppermute | solution.py:1255
  369.9 35.2 %collective-permute-start.6 = (bf16[512,1536]{1,0:T(8,128)(2,1)S(1)}, bf16[512,1536]{1,0:T(8,128)(2,1)S(1)}, u32[]{:S(2)}, u32[]{:S(2)}) collective-permute-start(bf16[512,1536]{1,0:T(8,128)(2,1)S(1)} %fusion.25), channel_id=1, source_target_pairs={{0,1},{1,0},{2,3},{3,2},{4,5},{5,4},{6,7},{7,6},{8,9},{9,8},{10,11... | collective-permute-start | bytes 4718600 | tf_op jit(solution)/shard_map/ppermute | solution.py:1255
  375.5 29.6 %copy-start.5 = (f32[512,1536]{1,0:T(8,128)S(1)}, f32[512,1536]{1,0:T(8,128)}, u32[]{:S(2)}) copy-start(f32[512,1536]{1,0:T(8,128)} %copy-done.4) | copy-start | bytes 9437188
  386.7 19.4 %copy-start.9 = (f32[512,1536]{1,0:T(8,128)S(1)}, f32[512,1536]{1,0:T(8,128)}, u32[]{:S(2)}) copy-start(f32[512,1536]{1,0:T(8,128)} %copy-done.8) | copy-start | bytes 9437188
  386.7 19.4 %copy-start.18 = (bf16[512,1536]{1,0:T(8,128)(2,1)S(1)}, bf16[512,1536]{1,0:T(8,128)(2,1)}, u32[]{:S(2)}) copy-start(bf16[512,1536]{1,0:T(8,128)(2,1)} %cotangent_ref.1) | copy-start | bytes 4718596
  412.0 35.4 %collective-permute-start.7 = (bf16[512,1536]{1,0:T(8,128)(2,1)S(1)}, bf16[512,1536]{1,0:T(8,128)(2,1)}, u32[]{:S(2)}, u32[]{:S(2)}) collective-permute-start(bf16[512,1536]{1,0:T(8,128)(2,1)S(1)} %get-tuple-element.179), channel_id=1, source_target_pairs={{0,1},{1,0},{2,3},{3,2},{4,5},{5,4},{6,7},{7,6},{8,9},{9,8},{10,11... | collective-permute-start | bytes 4718600 | tf_op jit(solution)/shard_map/ppermute | solution.py:1255
  414.9 31.5 %collective-permute-start.8 = (f32[512,1]{0,1:T(1,128)S(1)}, f32[512,1]{0,1:T(1,128)S(1)}, u32[]{:S(2)}, u32[]{:S(2)}) collective-permute-start(f32[512,1]{0,1:T(1,128)S(1)} %bitcast.112), channel_id=1, source_target_pairs={{0,1},{1,0},{2,3},{3,2},{4,5},{5,4},{6,7},{7,6},{8,9},{9,8},{10,11... | collective-permute-start | bytes 6152 | tf_op jit(solution)/shard_map/ppermute | solution.py:1255
  466.3 131.2 %copy-start.7 = (bf16[512,1536]{1,0:T(8,128)(2,1)S(1)}, bf16[512,1536]{1,0:T(8,128)(2,1)}, u32[]{:S(2)}) copy-start(bf16[512,1536]{1,0:T(8,128)(2,1)} %hidden_ref.1) | copy-start | bytes 4718596
  466.3 131.2 %copy-start.27 = (f32[1536]{0:T(1024)S(1)}, f32[1536]{0:T(1024)}, u32[]{:S(2)}) copy-start(f32[1536]{0:T(1024)} %get-tuple-element.176) | copy-start | bytes 18436
  609.5 19.2 %copy-start.21 = (f32[2,96,1536]{2,1,0:T(8,128)S(1)}, f32[2,96,1536]{2,1,0:T(8,128)}, u32[]{:S(2)}) copy-start(f32[2,96,1536]{2,1,0:T(8,128)} %get-tuple-element.111) | copy-start | bytes 3538948
  (31 other events, 167.6 us)
Sparse Core Ops, SparseCore 0:
  90.4 53.3 all-gather.3
  146.6 87.2 all-gather.5
  236.2 51.5 all-gather.7
  291.5 74.0 reduce-scatter.6
  370.1 119.4 reduce-scatter.4

commit v6 on v5

--- a/solution.py
+++ b/solution.py
@@ -413,7 +413,7 @@
 
 def last_backward_kernel(
     groups, blocks,
-    gate_ref, value_ref, pre_ref, scanned_ref, dgn_ref, side_ref, states_ref, rows_ref,
+    gate_ref, value_ref, pre_ref, scanned_ref, own_dgn_ref, other_dgn_ref, side_ref, states_ref, rows_ref,
     chan_ref, state_taps_ref, headp_ref, small_ref,
     own_left_ref, other_left_ref, normed_left_ref, gnl_ref, weight_ref, before_ref,
     wide_ref, side_out_ref, out_ref, total_ref, own_ref,
@@ -421,7 +421,7 @@
     dcbt, db, dc, col_s, rowt_s, per_head, head_s, spread, inv_s, pull_s, lower, later_s,
     sums, state_sums, head_sums, low, left, tiles,
     keep0, keep1, keep2, send0, send1, send2, come0, come1, come2, ss0, rs0, ss1, rs1, ss2, rs2,
-    rows_send, rows_come, rows_ss, rows_rs, small_s, small_come, small_ss, small_rs, local,
+    rows_send, rows_come, rows_ss, rows_rs, small_s, small_come, small_ss, small_rs, local, turns,
 ):
     k = pl.program_id(0)
     me = lax.axis_index("dp")
@@ -475,17 +475,26 @@
             weight_ref.at[pl.ds(t * ROW_TILE, ROW_TILE), :], tiles.at[t % 2], local.at[3 + t % 2]
         )
 
-    mix_copies = [
-        pltpu.make_async_copy(ref, left.at[:, pl.ds(i * half, half)], local.at[6 * i])
-        for i, ref in enumerate((own_left_ref, other_left_ref))
-    ]
+    def ordered(ref, first, size, semaphore):
+        return [
+            pltpu.make_async_copy(
+                ref.at[pl.ds(((i * 2 + j) * 2 + c) * rows, rows), :],
+                left.at[pl.ds(((c * 2 + j) * 4 + i) * rows, rows), pl.ds(first, size)],
+                turns.at[semaphore, (i * 2 + j) * 2 + c],
+            )
+            for i in range(4)
+            for j in range(2)
+            for c in range(2)
+        ]
+
+    mix_copies = ordered(own_left_ref, 0, half, 0) + ordered(other_left_ref, half, half, 1)
+    normed_copies = ordered(normed_left_ref, 0, 2 * half, 2)
     gnl_copies = [
         pltpu.make_async_copy(
             gnl_ref.at[:, pl.ds(i * width, width)], low.at[:, pl.ds(i * inner + width, width)], local.at[1 + 4 * i]
         )
         for i in range(2)
     ]
-    normed_copy = pltpu.make_async_copy(normed_left_ref, left, local.at[2])
 
     def at(offset, action):
         s = k - offset
@@ -574,7 +583,7 @@
             silu_gate = gate * sig_gate
             scanned = scanned_ref[:, lanes].astype(F32)
             gated = scanned * silu_gate
-            dgn = dgn_ref[:, lanes].astype(F32) * inv
+            dgn = jnp.where(place < blocks // 2, own_dgn_ref[:, lanes], other_dgn_ref[:, lanes]).astype(F32) * inv
             dgated = dgn * gain - gated * pull
             sums[g, 5:6, lanes] += jnp.sum(dgn * gated, 0, keepdims=True)
             dy = dgated * silu_gate
@@ -712,9 +721,10 @@
         def _():
             tile_copy(t).wait()
 
-            rows_send[t] = dot_nt(low[half:, :], tiles[t % 2]).astype(BF16)
+            product = dot_nt(low[...], tiles[t % 2])
+            rows_send[t] = product[half:].astype(BF16)
             by_tensor(t).start()
-            own_ref[:, t * ROW_TILE : (t + 1) * ROW_TILE] = dot_nt(low[:half, :], tiles[t % 2])
+            own_ref[:, t * ROW_TILE : (t + 1) * ROW_TILE] = product[:half]
             if t + 2 < tile_count:
                 tile_copy(t + 2).start()
 
@@ -773,7 +783,8 @@
 
         @pl.when(c == first)
         def _():
-            normed_copy.wait()
+            for copy in normed_copies:
+                copy.wait()
 
         @pl.when(c >= 3)
         def _():
@@ -800,7 +811,8 @@
 
         @pl.when(c == first - 1)
         def _():
-            normed_copy.start()
+            for copy in normed_copies:
+                copy.start()
 
     at(Z_LAG, receive_z)
     at(X_LAG, receive_x)
@@ -836,7 +848,7 @@
 
 
 def last_backward(
-    projected, pre, scanned, dgn, side, states, rows_in, chan, state_taps, headp,
+    projected, pre, scanned, own_dgn, other_dgn, side, states, rows_in, chan, state_taps, headp,
     small, own_left, other_left, normed_left, gnl, weight, before, q, collective,
 ):
     tokens, inner = pre.shape
@@ -903,13 +915,15 @@
         pltpu.SemaphoreType.DMA((tile_count,)), pltpu.SemaphoreType.DMA((tile_count,)),
         pltpu.VMEM((4, 16, inner + 2 * N), F32), pltpu.VMEM((4, 16, inner + 2 * N), F32),
         pltpu.SemaphoreType.DMA((4,)), pltpu.SemaphoreType.DMA((4,)),
-        pltpu.SemaphoreType.DMA((7,)),
+        pltpu.SemaphoreType.DMA((6,)), pltpu.SemaphoreType.DMA((3, 16)),
     ]
     return pl.pallas_call(
         functools.partial(last_backward_kernel, groups, blocks),
         grid=(mixing_steps + 4 + Z_LAG,),
         in_specs=[
-            columns(0), columns(groups), columns(0), columns(0), columns(0),
+            columns(0), columns(groups), columns(0), columns(0),
+            pl.BlockSpec((q, SPAN), lambda k: (jnp.minimum(place(k), blocks // 2 - 1), group(k))),
+            pl.BlockSpec((q, SPAN), lambda k: (jnp.maximum(place(k) - blocks // 2, 0), group(k))),
             pl.BlockSpec((tokens, SIDE + 2 * N), lambda k: (0, 0), pipeline_mode=once),
             pl.BlockSpec((1, N, SPAN), lambda k: (block(k), 0, group(k))),
             pl.BlockSpec((q, 128), lambda k: (place(k), 0)),
@@ -940,7 +954,7 @@
         cost_estimate=pl.CostEstimate(flops=2_000_000_000, bytes_accessed=1_000_000, transcendentals=0),
         name="last_backward",
     )(
-        projected, projected, pre, scanned, dgn, side, states, rows_in, chan, state_taps, headp,
+        projected, projected, pre, scanned, own_dgn, other_dgn, side, states, rows_in, chan, state_taps, headp,
         small, own_left, other_left, normed_left, gnl, weight, before,
     )
 
@@ -1240,11 +1254,6 @@
 
 def together(*values):
     return lax.optimization_barrier(values)
-
-
-def by_peers(values):
-    tokens, depth = values.shape
-    return values.T.reshape(4, 2, 2, depth // 16, tokens).transpose(2, 1, 0, 3, 4).reshape(depth, tokens)
 
 
 class Pair:
@@ -1429,7 +1438,7 @@
         mixed_raw = None
         if layer < LAYERS - 1:
             if fused:
-                normed_turned = by_peers(normed_all)
+                normed_turned = normed_all.T
                 mixed_raw, normed_turned = group.project(
                     lambda rows: dot_nt(rows, outputs[layer]), gnl, normed_turned
                 )
@@ -1475,7 +1484,8 @@
             product = dot_tn(scaled_mix, gnl).astype(BF16)
             mix_all, product = together(mix_all, product)
             grads_output.append(scatter_call(product))
-        dgn = dot_nn(mix_all, outputs[layer]).astype(BF16)
+        if layer > 0 or not fused:
+            dgn = dot_nn(mix_all, outputs[layer]).astype(BF16)
         if layer == LAYERS - 1:
             cross = group.total(jnp.sum(gnl.astype(F32) * dgn.astype(F32), axis=-1, keepdims=True))
             gnl, cross = together(gnl, cross)
@@ -1495,8 +1505,8 @@
         )
         if layer == 0 and fused:
             wide_sums, side_sums, out_sums, total, grad_normed = last_backward(
-                projected, pre, scanned, dgn, side, states, rows_in, chan, state_taps, headp,
-                small[0], *mix_turned, normed_turned, gate_norm, projections[0], product[:16, :128], q, 3,
+                projected, pre, scanned, *dgn_parts, side, states, rows_in, chan, state_taps, headp,
+                small[0], *mix_turned, normed_turned, gate_norm, projections[0], small[0], q, 3,
             )
         else:
             low, dchan, dstate, dhead = backward_mixer(
@@ -1532,11 +1542,15 @@
         if layer > 0:
             grad_mix = rowwise(keep_rows * grad_flow)
             mix_low = rowwise(grad_mix.astype(BF16))
-            mix_all = group.gather(mix_low)
             if fused:
-                own_turned = by_peers(mix_low)
-                mix_all, own_turned = together(mix_all, own_turned)
-                mix_turned = (own_turned, by_peers(mix_all[local_rows:]))
+                come = group.swap(mix_low)
+                own_turned = mix_low.T
+                own_dgn = dot_nn(mix_low, outputs[layer - 1]).astype(BF16)
+                come, own_turned, own_dgn = together(come, own_turned, own_dgn)
+                mix_turned = (own_turned, come.T)
+                dgn_parts = (own_dgn, dot_nn(come, outputs[layer - 1]).astype(BF16))
+            else:
+                mix_all = group.gather(mix_low)
     if fused:
         layer_sums = grads_projection[0].astype(F32)
         pre, taps, decay, bias, skip, gain, grad_state, grad_step = last_sums(

time: 650 us -> 645 us (level)
  local copies, waits for them, and re-layouts: 38.5 us -> 27.9 us
    transpose x7 -> x0, local copies, waits for them, and re-layouts: 14.2 us -> none  [by_peers(): values.T.reshape(4, 2, 2, depth // 16, tokens).transpose(2, 1, 0, 3, 4)]
    dot_general x4 -> x5, matrix products: 48.1 us -> 51.3 us  [dot_nn(): lax.dot_general(a, b, (((1,), (0,)), ((), ())), preferred_element_type=F32)]
    unnamed x93 -> x97, local copies, waits for them, and re-layouts: 15.1 us -> 13.5 us
  transfers between devices with their start and end apart: 14 -> 14, of which waited for: 8 -> 9; matrix products, arithmetic and copies ran while one was open for 25% -> 24% of each run, Pallas kernels for 34% -> 35%
where the time goes in v6:
time: 645 us; the launch traced here: 634 us
  Pallas kernels  313 us (49%)
  waiting for transfers between devices  123 us (19%)
  matrix products  115 us (18%)
  other arithmetic  28.9 us (4%)
  local copies, waits for them, and re-layouts  27.9 us (4%)
  between operations  15.8 us (2%)
  starting transfers between devices  10.7 us (2%)
    pallas_call x1, Pallas kernels, last_backward(): pl.pallas_call(functools.partial(last_backward_kernel, groups, blocks), g...  136 us
    ppermute x9, waiting for transfers between devices, swap(): return lax.ppermute(values, 'tensor', [(0, 1), (1, 0)])  109 us
    pallas_call x1, Pallas kernels, gather_all(): pl.pallas_call(gather_kernel, grid=(1,), in_specs=[first((half, depth)),...  76.2 us
    dot_general x5, matrix products, dot_nn(): lax.dot_general(a, b, (((1,), (0,)), ((), ())), preferred_element_type=F32)  51.3 us
    pallas_call x2, Pallas kernels, forward_mixer(): pl.pallas_call(forward_kernel, grid_spec=pltpu.PrefetchScalarGridSpec(num...  47.5 us
    dot_general x6, matrix products, dot_nt(): lax.dot_general(a, b, (((1,), (1,)), ((), ())), preferred_element_type=F32)  40.2 us
    pallas_call x1, Pallas kernels, backward_mixer(): pl.pallas_call(backward_kernel, grid_spec=pltpu.PrefetchScalarGridSpec(nu...  37.9 us
    dot_general x2, matrix products, dot_tn(): lax.dot_general(a, b, (((0,), (0,)), ((), ())), preferred_element_type=F32)  23.8 us
  transfers between devices with their start and end apart: 14, of which 9 were waited for; matrix products, arithmetic and copies ran while one was open for 24% of the time, Pallas kernels for 35%

profile of v6, /device:TPU:0, one launch (start us, length us, event | category | flops | bytes accessed | tf_op | source)
XLA Modules:
  0.0 634.4 jit_solution(4572919505200008646)
XLA Ops:
  13.9 76.2 %gather_all.1 = (bf16[1536,3456]{1,0:T(8,128)(2,1)}, bf16[1024,1536]{1,0:T(8,128)(2,1)}, bf16[1024,1536]{1,0:T(8,128)(2,1)}) custom-call(bf16[512,1536]{1,0:T(8,128)(2,1)} %hidden_ref.1, bf16[512,1536]{1,0:T(8,128)(2,1)} %cotangent_ref.1, f32[512,1]{1,0:T(8,128)} %fusion.36.keep_ref, f32[1,1536]{1,0:T(1,128)} %get-tuple-element.201.gain_ref, ...), custom_call_target="tpu_custom_call" | custom-call | flops 2000000000 | bytes 1000000 | tf_op jit(solution)/shard_map/gather_all/pallas_call | solution.py:1219
  94.2 14.1 %fusion.4.gate_ref.value_ref = bf16[1024,3072]{1,0:T(8,128)(2,1)} fusion(bf16[1024,1536]{1,0:T(8,128)(2,1)S(1)} %copy-done.11, bf16[1536,3456]{1,0:T(8,128)(2,1)} %get-tuple-element.72.side_weight_ref.weight_ref), kind=kOutput, calls=%fused_computation.9 | convolution fusion | flops 9666822144 | bytes 18874368 | tf_op jit(solution)/shard_map/dot_general | solution.py:20
  108.4 23.7 %forward_mixer.2 = (bf16[1024,1536]{1,0:T(8,128)(2,1)}, bf16[1024,1536]{1,0:T(8,128)(2,1)}, bf16[1024,1536]{1,0:T(8,128)(2,1)}, f32[1024,640]{1,0:T(8,128)S(1)},...) custom-call(s32[1]{0:T(128)} %bitcast.1.turn_ref, bf16[1024,3072]{1,0:T(8,128)(2,1)} %fusion.4.gate_ref.value_ref, ...), custom_call_target="tpu_custom_call" | custom-call | flops 2000000000 | bytes 1000000 | tf_op jit(solution)/shard_map/forward_mixer/pallas_call | solution.py:319
  133.7 10.1 %all-gather.4.cloned.1.call-done = bf16[1536,1536]{1,0:T(8,128)(2,1)} async-done(((bf16[96,1536]{1,0:T(8,128)(2,1)}), bf16[1536,1536]{1,0:T(8,128)(2,1)}) %all-gather.4.cloned.1.call-update) | async-done | bytes 4718608 | tf_op jit(solution)/shard_map/all_gather | solution.py:1395
  143.8 6.6 %convolution_convert_fusion.6 = bf16[512,1536]{1,0:T(8,128)(2,1)} fusion(bf16[1536,1536]{1,0:T(8,128)(2,1)} %all-gather.4.cloned.1.call-done, bf16[1024,1536]{1,0:T(8,128)(2,1)} %get-tuple-element.73), kind=kOutput, calls=%fused_computation.44 | convolution fusion | flops 2416705536 | bytes 7864320 | tf_op jit(solution)/shard_map/dot_general | solution.py:24
  157.4 29.8 %collective-permute-done.1 = f32[1024,1]{0,1:T(1,128)S(1)} collective-permute-done((f32[1024,1]{0,1:T(1,128)S(1)}, f32[1024,1]{0,1:T(1,128)S(1)}, u32[]{:S(2)}, u32[]{:S(2)}) %collective-permute-start.1) | collective-permute-done | bytes 4128 | tf_op jit(solution)/shard_map/ppermute | solution.py:1264
  187.3 5.1 fusion.32
  196.6 34.3 %collective-permute-done.2 = bf16[512,1536]{1,0:T(8,128)(2,1)S(1)} collective-permute-done((bf16[512,1536]{1,0:T(8,128)(2,1)S(1)}, bf16[512,1536]{1,0:T(8,128)(2,1)S(1)}, u32[]{:S(2)}, u32[]{:S(2)}) %collective-permute-start.2) | collective-permute-done | bytes 1572896 | tf_op jit(solution)/shard_map/ppermute | solution.py:1264
  233.9 14.5 %fusion.7.gate_ref.value_ref = bf16[1024,3072]{1,0:T(8,128)(2,1)} fusion(bf16[1536,3456]{1,0:T(8,128)(2,1)} %all-gather.6.cloned.1.call-done.side_weight_ref, bf16[512,1536]{1,0:T(8,128)(2,1)S(1)} %collective-permute-done.2, bf16[512,1536]{1,0:T(8,128)(2,1)S(1)} %multiply_convert_fusion.3), kind=kOutput, calls=%fused_computation.10 | convolution fusion | flops 9673113600 | bytes 18874368 | tf_op jit(solution)/shard_map/dot_general | solution.py:20
  248.4 23.8 %forward_mixer.3 = (bf16[1024,1536]{1,0:T(8,128)(2,1)}, bf16[1024,1536]{1,0:T(8,128)(2,1)}, bf16[1024,1536]{1,0:T(8,128)(2,1)}, f32[1024,640]{1,0:T(8,128)S(1)},...) custom-call(s32[1]{0:T(128)} %bitcast.1.turn_ref, bf16[1024,3072]{1,0:T(8,128)(2,1)} %fusion.7.gate_ref.value_ref, ...), custom_call_target="tpu_custom_call" | custom-call | flops 2000000000 | bytes 1000000 | tf_op jit(solution)/shard_map/forward_mixer/pallas_call | solution.py:319
  276.2 9.7 %convolution_convert_fusion.1 = bf16[1536,1536]{1,0:T(8,128)(2,1)} fusion(bf16[1024,1536]{1,0:T(8,128)(2,1)} %get-tuple-element.84, bf16[1024,1536]{1,0:T(8,128)(2,1)} %get-tuple-element.82, f32[1024]{0:T(1024)S(1)} %fusion.46), kind=kOutput, calls=%fused_computation.5 | convolution fusion | flops 4838916096 | bytes 11014144 | tf_op jit(solution)/shard_map/dot_general | solution.py:28
  287.7 9.9 %multiply_reduce_fusion = (f32[1024]{0:T(1024)S(1)}, bf16[1024,1536]{1,0:T(8,128)(2,1)}) fusion(bf16[1024,1536]{1,0:T(8,128)(2,1)} %get-tuple-element.84, bf16[1024,1536]{1,0:T(8,128)(2,1)} %get-tuple-element.82, bf16[1536,1536]{1,0:T(8,128)(2,1)} %all-gather.8.cloned.1.call-done), kind=kOutput, calls=%fused_computation.7 | convolution fusion | flops 4839701504 | bytes 14159872 | tf_op jit(solution)/shard_map/dot_general | solution.py:20
  306.8 37.9 %backward_mixer.1 = (bf16[1024,3456]{1,0:T(8,128)(2,1)}, f32[8,1536]{1,0:T(8,128)S(1)}, f32[8,256]{1,0:T(8,128)S(1)}, f32[8,128]{1,0:T(8,128)S(1)}) custom-call(s32[1]{0:T(128)} %bitcast.1.turn_ref, bf16[1024,3072]{1,0:T(8,128)(2,1)} %fusion.7.gate_ref.value_ref, bf16[1024,3072]{1,0:T(8,128)(2,1)} %fusion.7.gate_ref.value_ref, ...), custom_call_target="tpu_custom_call" | custom-call | flops 2000000000 | bytes 1000000 | tf_op jit(solution)/shard_map/backward_mixer/pallas_call | solution.py:367
  344.8 9.9 %fusion.25 = bf16[512,1536]{1,0:T(8,128)(2,1)S(1)} fusion(bf16[1536,3456]{1,0:T(8,128)(2,1)} %all-gather.6.cloned.1.call-done.side_weight_ref, bf16[1024,3456]{1,0:T(8,128)(2,1)} %get-tuple-element.95), kind=kOutput, calls=%fused_computation.40 | convolution fusion | flops 5436604416 | bytes 15728640 | tf_op jit(solution)/shard_map/dot_general | solution.py:24
  354.7 14.1 %convolution_convert_fusion = bf16[1536,3456]{1,0:T(8,128)(2,1)} fusion(bf16[1024,3456]{1,0:T(8,128)(2,1)S(1)} %copy-done.38, bf16[512,1536]{1,0:T(8,128)(2,1)S(1)} %copy-done.20, bf16[512,1536]{1,0:T(8,128)(2,1)S(1)} %copy-done.17), kind=kOutput, calls=%fused_computation | convolution fusion | flops 10883235840 | bytes 20840448 | tf_op jit(solution)/shard_map/dot_general | solution.py:28
  369.5 5.3 fusion.29
  374.8 9.5 %fusion.13 = f32[512,1536]{1,0:T(8,128)S(1)} fusion(bf16[1536,3456]{1,0:T(8,128)(2,1)} %all-gather.6.cloned.1.call-done.side_weight_ref, bf16[1024,3456]{1,0:T(8,128)(2,1)S(1)} %bitcast.101), kind=kOutput, calls=%fused_computation.18 | convolution fusion | flops 5435817984 | bytes 17301504 | tf_op jit(solution)/shard_map/dot_general | solution.py:24
  384.4 19.7 %collective-permute-done.6 = bf16[512,1536]{1,0:T(8,128)(2,1)S(1)} collective-permute-done((bf16[512,1536]{1,0:T(8,128)(2,1)S(1)}, bf16[512,1536]{1,0:T(8,128)(2,1)S(1)}, u32[]{:S(2)}, u32[]{:S(2)}) %collective-permute-start.6) | collective-permute-done | bytes 1572896 | tf_op jit(solution)/shard_map/ppermute | solution.py:1264
  405.0 5.7 multiply_reduce_fusion.2
  418.8 6.0 convolution_convert_fusion.4.own_dgn_ref
  425.5 21.4 %collective-permute-done.8 = f32[512,1]{0,1:T(1,128)S(1)} collective-permute-done((f32[512,1]{0,1:T(1,128)S(1)}, f32[512,1]{0,1:T(1,128)S(1)}, u32[]{:S(2)}, u32[]{:S(2)}) %collective-permute-start.8) | collective-permute-done | bytes 2080 | tf_op jit(solution)/shard_map/ppermute | solution.py:1264
  448.0 6.8 %convolution_convert_fusion.3.other_dgn_ref = bf16[512,1536]{1,0:T(8,128)(2,1)} fusion(bf16[512,1536]{0,1:T(8,128)(2,1)} %collective-permute-done.7, bf16[1536,1536]{1,0:T(8,128)(2,1)} %all-gather.4.cloned.1.call-done), kind=kOutput, calls=%fused_computation.41 | convolution fusion | flops 2416705536 | bytes 7864320 | tf_op jit(solution)/shard_map/dot_general | solution.py:20
  454.8 135.5 %last_backward.1 = (f32[2,96,1536]{2,1,0:T(8,128)}, f32[96,384]{1,0:T(8,128)}, f32[1536,96]{1,0:T(8,128)}, f32[16,1792]{1,0:T(8,128)}, f32[512,1536]{1,0:T(8,128)}) custom-call(bf16[1024,3072]{1,0:T(8,128)(2,1)} %fusion.4.gate_ref.value_ref, bf16[1024,3072]{1,0:T(8,128)(2,1)} %fusion.4.gate_ref.value_ref, bf16[1024,1536]{1,0:T(8,128)(2,1)} %get-tuple-element.99.pre_ref, ...), custom_call_target="tpu_custom_call" | custom-call | flops 2000000000 | bytes 1000000 | tf_op jit(solution)/shard_map/last_backward/pallas_call | solution.py:920
  603.2 15.6 %last_sums.1 = (f32[2,1536]{1,0:T(2,128)}, f32[2,5,3328]{2,1,0:T(8,128)}, f32[2,48]{1,0:T(2,128)}, f32[2,48]{1,0:T(2,128)}, f32[2,48]{1,0:T(2,128)}, /*index=5*/...) custom-call(f32[1,1536]{1,0:T(1,128)} %broadcast_in_dim.11.pre_ref, f32[16,1792]{1,0:T(8,128)} %get-tuple-element.112.total_ref, ...), custom_call_target="tpu_custom_call" | custom-call | tf_op jit(solution)/shard_map/last_sums/pallas_call | solution.py:1041
  (204 shorter events, 73.3 us)
Async XLA Ops:
  7.2 136.6 %all-gather.4.cloned.1.call-start = ((), (), s32[]{:S(2)}) async-start(), calls=%async_computation.2 | async-start | bytes 5013504 | tf_op jit(solution)/shard_map/all_gather | solution.py:1395
  13.9 76.4 %copy-start.26 = (bf16[2,96,24]{2,1,0:T(8,128)(2,1)S(1)}, bf16[2,96,24]{2,1,0:T(8,128)(2,1)}, u32[]{:S(2)}) copy-start(bf16[2,96,24]{2,1,0:T(8,128)(2,1)} %copy.69.step_ref) | copy-start | bytes 27652
  13.9 76.4 %copy-start.28 = (bf16[2,96,256]{2,1,0:T(8,128)(2,1)S(1)}, bf16[2,96,256]{2,1,0:T(8,128)(2,1)}, u32[]{:S(2)}) copy-start(bf16[2,96,256]{2,1,0:T(8,128)(2,1)} %state_ref.1) | copy-start | bytes 294916
  90.2 143.7 %all-gather.6.cloned.1.call-start = ((), (), s32[]{:S(2)}) async-start(), calls=%async_computation.3 | async-start | bytes 11280384 | tf_op jit(solution)/shard_map/all_gather | solution.py:1392
  92.5 195.2 %all-gather.8.cloned.1.call-start = ((), (), s32[]{:S(2)}) async-start(), calls=%async_computation.4 | async-start | bytes 5013504 | tf_op jit(solution)/shard_map/all_gather | solution.py:1395
  93.2 505.1 %reduce-scatter.7.cloned.1.call-start = ((), (), s32[]{:S(2)}) async-start(), calls=%async_computation.6 | async-start | bytes 5013504
  108.4 23.7 %copy-start.1 = (f32[8,1536]{1,0:T(8,128)}, f32[8,1536]{1,0:T(8,128)S(1)}, u32[]{:S(2)}) copy-start(f32[8,1536]{1,0:T(8,128)S(1)} %get-tuple-element.215.chan_ref) | copy-start | bytes 147460
  150.4 42.0 %collective-permute-start = (bf16[512,1536]{1,0:T(8,128)(2,1)}, bf16[512,1536]{1,0:T(8,128)(2,1)S(1)}, u32[]{:S(2)}, u32[]{:S(2)}) collective-permute-start(bf16[512,1536]{1,0:T(8,128)(2,1)} %convolution_convert_fusion.6), channel_id=1, source_target_pairs={{0,1},{1,0},{2,3},{3,2},{4,5},{5,4},{6,7},{7,6},{8,9},{9,8},{10,11... | collective-permute-start | bytes 4718600 | tf_op jit(solution)/shard_map/ppermute | solution.py:1264
  152.1 35.2 %collective-permute-start.1 = (f32[1024,1]{0,1:T(1,128)S(1)}, f32[1024,1]{0,1:T(1,128)S(1)}, u32[]{:S(2)}, u32[]{:S(2)}) collective-permute-start(f32[1024,1]{0,1:T(1,128)S(1)} %bitcast.86), channel_id=1, source_target_pairs={{0,1},{1,0},{2,3},{3,2},{4,5},{5,4},{6,7},{7,6},{8,9},{9,8},{10,11... | collective-permute-start | bytes 12296 | tf_op jit(solution)/shard_map/ppermute | solution.py:1264
  194.9 39.0 %copy-start.16 = (bf16[512,1536]{1,0:T(8,128)(2,1)}, bf16[512,1536]{1,0:T(8,128)(2,1)S(1)}, u32[]{:S(2)}) copy-start(bf16[512,1536]{1,0:T(8,128)(2,1)S(1)} %multiply_convert_fusion.3) | copy-start | bytes 4718596
  194.9 35.9 %collective-permute-start.2 = (bf16[512,1536]{1,0:T(8,128)(2,1)S(1)}, bf16[512,1536]{1,0:T(8,128)(2,1)S(1)}, u32[]{:S(2)}, u32[]{:S(2)}) collective-permute-start(bf16[512,1536]{1,0:T(8,128)(2,1)S(1)} %multiply_convert_fusion.3), channel_id=1, source_target_pairs={{0,1},{1,0},{2,3},{3,2},{4,5},{5,4},{6,7},{7,6},{8,9},{9,8},{10,11... | collective-permute-start | bytes 4718600 | tf_op jit(solution)/shard_map/ppermute | solution.py:1264
  272.5 3.7 collective-permute-start.3
  285.9 315.2 %reduce-scatter.5.cloned.1.call-start = ((), (), s32[]{:S(2)}) async-start(), calls=%async_computation.5 | async-start | bytes 11280384 | tf_op jit(solution)/shard_map/reduce_scatter | solution.py:1318
  297.5 3.6 collective-permute-start.4
  305.0 39.8 %collective-permute-start.5 = (bf16[512,1536]{1,0:T(8,128)(2,1)}, bf16[512,1536]{1,0:T(8,128)(2,1)}, u32[]{:S(2)}, u32[]{:S(2)}) collective-permute-start(bf16[512,1536]{1,0:T(8,128)(2,1)} %convolution_convert_fusion.5), channel_id=1, source_target_pairs={{0,1},{1,0},{2,3},{3,2},{4,5},{5,4},{6,7},{7,6},{8,9},{9,8},{10,11... | collective-permute-start | bytes 4718600 | tf_op jit(solution)/shard_map/ppermute | solution.py:1264
  368.9 35.2 %collective-permute-start.6 = (bf16[512,1536]{1,0:T(8,128)(2,1)S(1)}, bf16[512,1536]{1,0:T(8,128)(2,1)S(1)}, u32[]{:S(2)}, u32[]{:S(2)}) collective-permute-start(bf16[512,1536]{1,0:T(8,128)(2,1)S(1)} %fusion.25), channel_id=1, source_target_pairs={{0,1},{1,0},{2,3},{3,2},{4,5},{5,4},{6,7},{7,6},{8,9},{9,8},{10,11... | collective-permute-start | bytes 4718600 | tf_op jit(solution)/shard_map/ppermute | solution.py:1264
  374.8 29.2 %copy-start.5 = (f32[512,1536]{1,0:T(8,128)S(1)}, f32[512,1536]{1,0:T(8,128)}, u32[]{:S(2)}) copy-start(f32[512,1536]{1,0:T(8,128)} %copy-done.4) | copy-start | bytes 9437188
  384.3 20.7 %copy-start.9 = (f32[512,1536]{1,0:T(8,128)S(1)}, f32[512,1536]{1,0:T(8,128)}, u32[]{:S(2)}) copy-start(f32[512,1536]{1,0:T(8,128)} %copy-done.8) | copy-start | bytes 9437188
  384.3 20.7 %copy-start.15 = (bf16[512,1536]{1,0:T(8,128)(2,1)S(1)}, bf16[512,1536]{1,0:T(8,128)(2,1)}, u32[]{:S(2)}) copy-start(bf16[512,1536]{1,0:T(8,128)(2,1)} %copy-done.14) | copy-start | bytes 4718596
  384.3 20.7 %copy-start.18 = (bf16[512,1536]{1,0:T(8,128)(2,1)S(1)}, bf16[512,1536]{1,0:T(8,128)(2,1)}, u32[]{:S(2)}) copy-start(bf16[512,1536]{1,0:T(8,128)(2,1)} %cotangent_ref.1) | copy-start | bytes 4718596
  412.5 35.5 %collective-permute-start.7 = (bf16[512,1536]{0,1:T(8,128)(2,1)S(1)}, bf16[512,1536]{0,1:T(8,128)(2,1)}, u32[]{:S(2)}, u32[]{:S(2)}) collective-permute-start(bf16[512,1536]{0,1:T(8,128)(2,1)S(1)} %copy.75), channel_id=1, source_target_pairs={{0,1},{1,0},{2,3},{3,2},{4,5},{5,4},{6,7},{7,6},{8,9},{9,8},{10,11... | collective-permute-start | bytes 4718600 | tf_op jit(solution)/shard_map/ppermute | solution.py:1264
  417.7 29.1 %collective-permute-start.8 = (f32[512,1]{0,1:T(1,128)S(1)}, f32[512,1]{0,1:T(1,128)S(1)}, u32[]{:S(2)}, u32[]{:S(2)}) collective-permute-start(f32[512,1]{0,1:T(1,128)S(1)} %bitcast.95), channel_id=1, source_target_pairs={{0,1},{1,0},{2,3},{3,2},{4,5},{5,4},{6,7},{7,6},{8,9},{9,8},{10,11... | collective-permute-start | bytes 6152 | tf_op jit(solution)/shard_map/ppermute | solution.py:1264
  454.8 135.5 %copy-start.7 = (bf16[512,1536]{1,0:T(8,128)(2,1)S(1)}, bf16[512,1536]{1,0:T(8,128)(2,1)}, u32[]{:S(2)}) copy-start(bf16[512,1536]{1,0:T(8,128)(2,1)} %hidden_ref.1) | copy-start | bytes 4718596
  454.8 135.6 %copy-start.27 = (f32[1536]{0:T(1024)S(1)}, f32[1536]{0:T(1024)}, u32[]{:S(2)}) copy-start(f32[1536]{0:T(1024)} %get-tuple-element.176) | copy-start | bytes 18436
  (33 other events, 196.1 us)
Sparse Core Ops, SparseCore 0:
  90.4 53.3 all-gather.3
  146.6 87.2 all-gather.5
  236.2 51.3 all-gather.7
  291.4 74.0 reduce-scatter.6
  370.0 133.4 reduce-scatter.4

commit v7 on v6

--- a/solution.py
+++ b/solution.py
@@ -1057,7 +1057,7 @@
 
 def gather_kernel(
     hidden_ref, cotangent_ref, keep_ref, gain_ref, gate_value_ref, state_ref, step_ref,
-    full_ref, normed_ref, mix_ref,
+    full_ref, normed_ref, mix_ref, inv_ref, next_ref,
     shard_ref, normed_s, mix_s, local, zs, zr, xs, xr, cs, cr, ys, yr,
 ):
     me = lax.axis_index("dp")
@@ -1092,11 +1092,15 @@
         )
 
     width = gate_value_ref.shape[3]
-    shard_ref[:, 0:width] = gate_value_ref[0, 0]
-    shard_ref[:, width : 2 * width] = gate_value_ref[0, 1]
-    shard_ref[:, 2 * width : 2 * width + 2 * N] = state_ref[0]
-    shard_ref[:, 2 * width + 2 * N :] = jnp.zeros((rows, 128), BF16)
-    shard_ref[:, 2 * width + 2 * N : 2 * width + 2 * N + step_ref.shape[2]] = step_ref[0]
+
+    def pack(target, layer):
+        target[:, 0:width] = gate_value_ref[layer, 0]
+        target[:, width : 2 * width] = gate_value_ref[layer, 1]
+        target[:, 2 * width : 2 * width + 2 * N] = state_ref[layer]
+        target[:, 2 * width + 2 * N :] = jnp.zeros((rows, 128), BF16)
+        target[:, 2 * width + 2 * N : 2 * width + 2 * N + step_ref.shape[2]] = step_ref[layer]
+
+    pack(shard_ref, 0)
     barrier = pltpu.get_barrier_semaphore()
     for peer in [(core_peer, tensor), (x_peer, tensor), (me, 1 - tensor)]:
         pl.semaphore_signal(barrier, inc=1, device_id=peer, device_id_type=pl.DeviceIdType.MESH)
@@ -1145,6 +1149,7 @@
         here = pl.ds(pl.multiple_of(i * 64, 64), 64)
         hidden = hidden_ref[here, :].astype(F32)
         inv = lax.rsqrt(jnp.mean(hidden * hidden, axis=-1, keepdims=True) + EPSILON)
+        inv_ref[here, :] = inv
         normed_s[here, :] = (hidden * inv * gain_ref[0:1, :]).astype(BF16)
         return 0
 
@@ -1160,6 +1165,7 @@
     lax.fori_loop(0, half // 64, mask, 0)
     swaps[1].start()
     kept[1].start()
+    pack(next_ref, 1)
 
     def arrived(block_z, up, further):
         along(block_z, up).wait_recv()
@@ -1221,13 +1227,15 @@
         grid=(1,),
         in_specs=[
             first((half, depth)), first((half, depth)), first((half, 1)), first((1, depth)),
-            first((1, 2, rows, width)), first((1, rows, 2 * N)), first((1, rows, step.shape[2])),
+            first((LAYERS, 2, rows, width)), first((LAYERS, rows, 2 * N)), first((LAYERS, rows, step.shape[2])),
         ],
-        out_specs=[anywhere] * 3,
+        out_specs=[anywhere] * 3 + [first((half, 1)), first((rows, columns))],
         out_shape=[
             jax.ShapeDtypeStruct((16 * rows, columns), BF16),
             jax.ShapeDtypeStruct((2 * half, depth), BF16),
             jax.ShapeDtypeStruct((2 * half, depth), BF16),
+            jax.ShapeDtypeStruct((half, 1), F32),
+            jax.ShapeDtypeStruct((rows, columns), BF16),
         ],
         scratch_shapes=[
             pltpu.VMEM((rows, columns), BF16), pltpu.VMEM((half, depth), BF16), pltpu.VMEM((half, depth), BF16),
@@ -1382,7 +1390,7 @@
     projections, outputs = [], []
     for layer in range(LAYERS):
         if layer == 0 and fused:
-            full, first_normed_all, last_mix_all = gather_all(
+            full, first_normed_all, last_mix_all, inv_rows, shards[1] = gather_all(
                 hidden_in, cotangent, keep_rows, pre_gain[:1], gate_value_weight, state_weight, step_weight, 5
             )
         else:

time: 645 us -> 645 us (level)
    unnamed x97 -> x93, local copies, waits for them, and re-layouts: 13.5 us -> 14.6 us
where the time goes in v7:
time: 645 us; the launch traced here: 635 us
  Pallas kernels  313 us (49%)
  waiting for transfers between devices  124 us (19%)
  matrix products  116 us (18%)
  other arithmetic  27.9 us (4%)
  local copies, waits for them, and re-layouts  27.7 us (4%)
  between operations  15.7 us (2%)
  starting transfers between devices  10.7 us (2%)
    pallas_call x1, Pallas kernels, last_backward(): pl.pallas_call(functools.partial(last_backward_kernel, groups, blocks), g...  135 us
    ppermute x9, waiting for transfers between devices, swap(): return lax.ppermute(values, 'tensor', [(0, 1), (1, 0)])  109 us
    pallas_call x1, Pallas kernels, gather_all(): pl.pallas_call(gather_kernel, grid=(1,), in_specs=[first((half, depth)),...  77.5 us
    dot_general x5, matrix products, dot_nn(): lax.dot_general(a, b, (((1,), (0,)), ((), ())), preferred_element_type=F32)  52.1 us
    pallas_call x2, Pallas kernels, forward_mixer(): pl.pallas_call(forward_kernel, grid_spec=pltpu.PrefetchScalarGridSpec(num...  47.8 us
    dot_general x6, matrix products, dot_nt(): lax.dot_general(a, b, (((1,), (1,)), ((), ())), preferred_element_type=F32)  40.4 us
    pallas_call x1, Pallas kernels, backward_mixer(): pl.pallas_call(backward_kernel, grid_spec=pltpu.PrefetchScalarGridSpec(nu...  38 us
    dot_general x2, matrix products, dot_tn(): lax.dot_general(a, b, (((0,), (0,)), ((), ())), preferred_element_type=F32)  23.8 us
  transfers between devices with their start and end apart: 14, of which 9 were waited for; matrix products, arithmetic and copies ran while one was open for 24% of the time, Pallas kernels for 35%

profile of v7, /device:TPU:0, one launch (start us, length us, event | category | flops | bytes accessed | tf_op | source)
XLA Modules:
  0.0 634.9 jit_solution(12308487327246931557)
XLA Ops:
  14.0 77.5 %gather_all.1 = (bf16[1536,3456]{1,0:T(8,128)(2,1)}, bf16[1024,1536]{1,0:T(8,128)(2,1)}, bf16[1024,1536]{1,0:T(8,128)(2,1)}, f32[512,1]{1,0:T(8,128)}, bf16[96,3456]{1,0:T(8,128)(2,1)}) custom-call(bf16[512,1536]{1,0:T(8,128)(2,1)} %hidden_ref.1, bf16[512,1536]{1,0:T(8,128)(2,1)} %cotangent_ref.1, f32[512,1]{1,0:T(8,128)} %fusion.33.keep_ref, ...), custom_call_target="tpu_custom_call" | custom-call | flops 2000000000 | bytes 1000000 | tf_op jit(solution)/shard_map/gather_all/pallas_call | solution.py:1225
  93.9 15.2 %fusion.4.gate_ref.value_ref = bf16[1024,3072]{1,0:T(8,128)(2,1)} fusion(bf16[1024,1536]{1,0:T(8,128)(2,1)} %get-tuple-element.70.normed_ref, bf16[1536,3456]{1,0:T(8,128)(2,1)} %get-tuple-element.75.side_weight_ref.weight_ref), kind=kOutput, calls=%fused_computation.9 | convolution fusion | flops 9666822144 | bytes 18874368 | tf_op jit(solution)/shard_map/dot_general | solution.py:20
  109.1 23.7 %forward_mixer.2 = (bf16[1024,1536]{1,0:T(8,128)(2,1)}, bf16[1024,1536]{1,0:T(8,128)(2,1)}, bf16[1024,1536]{1,0:T(8,128)(2,1)}, f32[1024,640]{1,0:T(8,128)S(1)},...) custom-call(s32[1]{0:T(128)} %bitcast.1.turn_ref, bf16[1024,3072]{1,0:T(8,128)(2,1)} %fusion.4.gate_ref.value_ref, ...), custom_call_target="tpu_custom_call" | custom-call | flops 2000000000 | bytes 1000000 | tf_op jit(solution)/shard_map/forward_mixer/pallas_call | solution.py:319
  134.4 10.6 %all-gather.4.cloned.1.call-done = bf16[1536,1536]{1,0:T(8,128)(2,1)} async-done(((bf16[96,1536]{1,0:T(8,128)(2,1)}), bf16[1536,1536]{1,0:T(8,128)(2,1)}) %all-gather.4.cloned.1.call-update) | async-done | bytes 4718608 | tf_op jit(solution)/shard_map/all_gather | solution.py:1403
  145.0 6.6 %convolution_convert_fusion.6 = bf16[512,1536]{1,0:T(8,128)(2,1)} fusion(bf16[1536,1536]{1,0:T(8,128)(2,1)} %all-gather.4.cloned.1.call-done, bf16[1024,1536]{1,0:T(8,128)(2,1)} %get-tuple-element.76), kind=kOutput, calls=%fused_computation.42 | convolution fusion | flops 2416705536 | bytes 7864320 | tf_op jit(solution)/shard_map/dot_general | solution.py:24
  158.6 29.9 %collective-permute-done.1 = f32[1024,1]{0,1:T(1,128)S(1)} collective-permute-done((f32[1024,1]{0,1:T(1,128)S(1)}, f32[1024,1]{0,1:T(1,128)S(1)}, u32[]{:S(2)}, u32[]{:S(2)}) %collective-permute-start.1) | collective-permute-done | bytes 4128 | tf_op jit(solution)/shard_map/ppermute | solution.py:1272
  188.5 5.1 fusion.31
  197.8 34.3 %collective-permute-done.2 = bf16[512,1536]{1,0:T(8,128)(2,1)S(1)} collective-permute-done((bf16[512,1536]{1,0:T(8,128)(2,1)S(1)}, bf16[512,1536]{1,0:T(8,128)(2,1)S(1)}, u32[]{:S(2)}, u32[]{:S(2)}) %collective-permute-start.2) | collective-permute-done | bytes 1572896 | tf_op jit(solution)/shard_map/ppermute | solution.py:1272
  234.5 14.2 %fusion.7.gate_ref.value_ref = bf16[1024,3072]{1,0:T(8,128)(2,1)} fusion(bf16[1536,3456]{1,0:T(8,128)(2,1)} %all-gather.6.cloned.1.call-done.side_weight_ref, bf16[512,1536]{1,0:T(8,128)(2,1)S(1)} %collective-permute-done.2, bf16[512,1536]{1,0:T(8,128)(2,1)S(1)} %multiply_convert_fusion.3), kind=kOutput, calls=%fused_computation.10 | convolution fusion | flops 9673113600 | bytes 18874368 | tf_op jit(solution)/shard_map/dot_general | solution.py:20
  248.7 24.1 %forward_mixer.3 = (bf16[1024,1536]{1,0:T(8,128)(2,1)}, bf16[1024,1536]{1,0:T(8,128)(2,1)}, bf16[1024,1536]{1,0:T(8,128)(2,1)}, f32[1024,640]{1,0:T(8,128)S(1)},...) custom-call(s32[1]{0:T(128)} %bitcast.1.turn_ref, bf16[1024,3072]{1,0:T(8,128)(2,1)} %fusion.7.gate_ref.value_ref, ...), custom_call_target="tpu_custom_call" | custom-call | flops 2000000000 | bytes 1000000 | tf_op jit(solution)/shard_map/forward_mixer/pallas_call | solution.py:319
  276.8 9.7 %convolution_convert_fusion.1 = bf16[1536,1536]{1,0:T(8,128)(2,1)} fusion(bf16[1024,1536]{1,0:T(8,128)(2,1)} %get-tuple-element.87, bf16[1024,1536]{1,0:T(8,128)(2,1)} %get-tuple-element.85, f32[1024]{0:T(1024)S(1)} %fusion.43), kind=kOutput, calls=%fused_computation.5 | convolution fusion | flops 4838916096 | bytes 11014144 | tf_op jit(solution)/shard_map/dot_general | solution.py:28
  288.4 9.9 %multiply_reduce_fusion = (f32[1024]{0:T(1024)S(1)}, bf16[1024,1536]{1,0:T(8,128)(2,1)}) fusion(bf16[1024,1536]{1,0:T(8,128)(2,1)} %get-tuple-element.87, bf16[1024,1536]{1,0:T(8,128)(2,1)} %get-tuple-element.85, bf16[1536,1536]{1,0:T(8,128)(2,1)} %all-gather.8.cloned.1.call-done), kind=kOutput, calls=%fused_computation.7 | convolution fusion | flops 4839701504 | bytes 14159872 | tf_op jit(solution)/shard_map/dot_general | solution.py:20
  307.6 38.0 %backward_mixer.1 = (bf16[1024,3456]{1,0:T(8,128)(2,1)}, f32[8,1536]{1,0:T(8,128)S(1)}, f32[8,256]{1,0:T(8,128)S(1)}, f32[8,128]{1,0:T(8,128)S(1)}) custom-call(s32[1]{0:T(128)} %bitcast.1.turn_ref, bf16[1024,3072]{1,0:T(8,128)(2,1)} %fusion.7.gate_ref.value_ref, bf16[1024,3072]{1,0:T(8,128)(2,1)} %fusion.7.gate_ref.value_ref, ...), custom_call_target="tpu_custom_call" | custom-call | flops 2000000000 | bytes 1000000 | tf_op jit(solution)/shard_map/backward_mixer/pallas_call | solution.py:367
  345.5 9.9 %fusion.24 = bf16[512,1536]{1,0:T(8,128)(2,1)S(1)} fusion(bf16[1536,3456]{1,0:T(8,128)(2,1)} %all-gather.6.cloned.1.call-done.side_weight_ref, bf16[1024,3456]{1,0:T(8,128)(2,1)} %get-tuple-element.98), kind=kOutput, calls=%fused_computation.38 | convolution fusion | flops 5436604416 | bytes 15728640 | tf_op jit(solution)/shard_map/dot_general | solution.py:24
  355.5 14.1 %convolution_convert_fusion = bf16[1536,3456]{1,0:T(8,128)(2,1)} fusion(bf16[1024,3456]{1,0:T(8,128)(2,1)S(1)} %copy-done.36, bf16[512,1536]{1,0:T(8,128)(2,1)S(1)} %copy-done.19, bf16[512,1536]{1,0:T(8,128)(2,1)S(1)} %copy-done.16), kind=kOutput, calls=%fused_computation | convolution fusion | flops 10883235840 | bytes 20840448 | tf_op jit(solution)/shard_map/dot_general | solution.py:28
  371.3 5.3 fusion.28
  376.6 9.7 %fusion.13 = f32[512,1536]{1,0:T(8,128)S(1)} fusion(bf16[1536,3456]{1,0:T(8,128)(2,1)} %all-gather.6.cloned.1.call-done.side_weight_ref, bf16[1024,3456]{1,0:T(8,128)(2,1)S(1)} %bitcast.93), kind=kOutput, calls=%fused_computation.17 | convolution fusion | flops 5435817984 | bytes 17301504 | tf_op jit(solution)/shard_map/dot_general | solution.py:24
  386.4 19.5 %collective-permute-done.6 = bf16[512,1536]{1,0:T(8,128)(2,1)S(1)} collective-permute-done((bf16[512,1536]{1,0:T(8,128)(2,1)S(1)}, bf16[512,1536]{1,0:T(8,128)(2,1)S(1)}, u32[]{:S(2)}, u32[]{:S(2)}) %collective-permute-start.6) | collective-permute-done | bytes 1572896 | tf_op jit(solution)/shard_map/ppermute | solution.py:1272
  406.9 5.7 multiply_reduce_fusion.2
  420.7 6.1 convolution_convert_fusion.4.own_dgn_ref
  427.4 21.4 %collective-permute-done.8 = f32[512,1]{0,1:T(1,128)S(1)} collective-permute-done((f32[512,1]{0,1:T(1,128)S(1)}, f32[512,1]{0,1:T(1,128)S(1)}, u32[]{:S(2)}, u32[]{:S(2)}) %collective-permute-start.8) | collective-permute-done | bytes 2080 | tf_op jit(solution)/shard_map/ppermute | solution.py:1272
  449.8 6.8 %convolution_convert_fusion.3.other_dgn_ref = bf16[512,1536]{1,0:T(8,128)(2,1)} fusion(bf16[512,1536]{0,1:T(8,128)(2,1)} %collective-permute-done.7, bf16[1536,1536]{1,0:T(8,128)(2,1)} %all-gather.4.cloned.1.call-done), kind=kOutput, calls=%fused_computation.39 | convolution fusion | flops 2416705536 | bytes 7864320 | tf_op jit(solution)/shard_map/dot_general | solution.py:20
  456.6 134.9 %last_backward.1 = (f32[2,96,1536]{2,1,0:T(8,128)}, f32[96,384]{1,0:T(8,128)}, f32[1536,96]{1,0:T(8,128)}, f32[16,1792]{1,0:T(8,128)}, f32[512,1536]{1,0:T(8,128)}) custom-call(bf16[1024,3072]{1,0:T(8,128)(2,1)} %fusion.4.gate_ref.value_ref, bf16[1024,3072]{1,0:T(8,128)(2,1)} %fusion.4.gate_ref.value_ref, bf16[1024,1536]{1,0:T(8,128)(2,1)} %get-tuple-element.103.pre_ref, ...), custom_call_target="tpu_custom_call" | custom-call | flops 2000000000 | bytes 1000000 | tf_op jit(solution)/shard_map/last_backward/pallas_call | solution.py:920
  604.4 14.9 %last_sums.1 = (f32[2,1536]{1,0:T(2,128)}, f32[2,5,3328]{2,1,0:T(8,128)}, f32[2,48]{1,0:T(2,128)}, f32[2,48]{1,0:T(2,128)}, f32[2,48]{1,0:T(2,128)}, /*index=5*/...) custom-call(f32[1,1536]{1,0:T(1,128)} %broadcast_in_dim.11.pre_ref, f32[16,1792]{1,0:T(8,128)} %get-tuple-element.116.total_ref, ...), custom_call_target="tpu_custom_call" | custom-call | tf_op jit(solution)/shard_map/last_sums/pallas_call | solution.py:1041
  (196 shorter events, 72.4 us)
Async XLA Ops:
  7.2 137.8 %all-gather.4.cloned.1.call-start = ((), (), s32[]{:S(2)}) async-start(), calls=%async_computation.2 | async-start | bytes 5013504 | tf_op jit(solution)/shard_map/all_gather | solution.py:1403
  13.9 79.1 %copy-start.30 = (f32[2,48]{1,0:T(2,128)S(1)}, f32[2,48]{1,0:T(2,128)}, u32[]{:S(2)}) copy-start(f32[2,48]{1,0:T(2,128)} %param.22) | copy-start | bytes 1156
  13.9 79.1 %copy-start.31 = (f32[2,48]{1,0:T(2,128)S(1)}, f32[2,48]{1,0:T(2,128)}, u32[]{:S(2)}) copy-start(f32[2,48]{1,0:T(2,128)} %param.23) | copy-start | bytes 1156
  13.9 79.1 %copy-start.32 = (f32[2,48]{1,0:T(2,128)S(1)}, f32[2,48]{1,0:T(2,128)}, u32[]{:S(2)}) copy-start(f32[2,48]{1,0:T(2,128)} %param.24) | copy-start | bytes 1156
  13.9 79.5 %copy-start.27 = (f32[2,3072]{1,0:T(2,128)S(1)}, f32[2,3072]{1,0:T(2,128)}, u32[]{:S(2)}) copy-start(f32[2,3072]{1,0:T(2,128)} %param.25) | copy-start | bytes 73732
  13.9 79.5 %copy-start.25 = (f32[2,5,3328]{2,0,1:T(2,128)S(1)}, f32[2,5,3328]{2,0,1:T(2,128)}, u32[]{:S(2)}) copy-start(f32[2,5,3328]{2,0,1:T(2,128)} %param.21) | copy-start | bytes 399364
  91.4 143.1 %all-gather.6.cloned.1.call-start = ((), (), s32[]{:S(2)}) async-start(), calls=%async_computation.3 | async-start | bytes 11280384 | tf_op jit(solution)/shard_map/all_gather | solution.py:1400
  92.2 196.2 %all-gather.8.cloned.1.call-start = ((), (), s32[]{:S(2)}) async-start(), calls=%async_computation.4 | async-start | bytes 5013504 | tf_op jit(solution)/shard_map/all_gather | solution.py:1403
  92.9 506.5 %reduce-scatter.7.cloned.1.call-start = ((), (), s32[]{:S(2)}) async-start(), calls=%async_computation.6 | async-start | bytes 5013504
  109.1 23.7 %copy-start.1 = (f32[8,1536]{1,0:T(8,128)}, f32[8,1536]{1,0:T(8,128)S(1)}, u32[]{:S(2)}) copy-start(f32[8,1536]{1,0:T(8,128)S(1)} %get-tuple-element.216.chan_ref) | copy-start | bytes 147460
  151.6 42.1 %collective-permute-start = (bf16[512,1536]{1,0:T(8,128)(2,1)}, bf16[512,1536]{1,0:T(8,128)(2,1)S(1)}, u32[]{:S(2)}, u32[]{:S(2)}) collective-permute-start(bf16[512,1536]{1,0:T(8,128)(2,1)} %convolution_convert_fusion.6), channel_id=1, source_target_pairs={{0,1},{1,0},{2,3},{3,2},{4,5},{5,4},{6,7},{7,6},{8,9},{9,8},{10,11... | collective-permute-start | bytes 4718600 | tf_op jit(solution)/shard_map/ppermute | solution.py:1272
  153.3 35.2 %collective-permute-start.1 = (f32[1024,1]{0,1:T(1,128)S(1)}, f32[1024,1]{0,1:T(1,128)S(1)}, u32[]{:S(2)}, u32[]{:S(2)}) collective-permute-start(f32[1024,1]{0,1:T(1,128)S(1)} %bitcast.78), channel_id=1, source_target_pairs={{0,1},{1,0},{2,3},{3,2},{4,5},{5,4},{6,7},{7,6},{8,9},{9,8},{10,11... | collective-permute-start | bytes 12296 | tf_op jit(solution)/shard_map/ppermute | solution.py:1272
  196.2 38.4 %copy-start.15 = (bf16[512,1536]{1,0:T(8,128)(2,1)}, bf16[512,1536]{1,0:T(8,128)(2,1)S(1)}, u32[]{:S(2)}) copy-start(bf16[512,1536]{1,0:T(8,128)(2,1)S(1)} %multiply_convert_fusion.3) | copy-start | bytes 4718596
  196.2 35.9 %collective-permute-start.2 = (bf16[512,1536]{1,0:T(8,128)(2,1)S(1)}, bf16[512,1536]{1,0:T(8,128)(2,1)S(1)}, u32[]{:S(2)}, u32[]{:S(2)}) collective-permute-start(bf16[512,1536]{1,0:T(8,128)(2,1)S(1)} %multiply_convert_fusion.3), channel_id=1, source_target_pairs={{0,1},{1,0},{2,3},{3,2},{4,5},{5,4},{6,7},{7,6},{8,9},{9,8},{10,11... | collective-permute-start | bytes 4718600 | tf_op jit(solution)/shard_map/ppermute | solution.py:1272
  273.1 3.7 collective-permute-start.3
  286.5 315.8 %reduce-scatter.5.cloned.1.call-start = ((), (), s32[]{:S(2)}) async-start(), calls=%async_computation.5 | async-start | bytes 11280384 | tf_op jit(solution)/shard_map/reduce_scatter | solution.py:1326
  298.3 3.6 collective-permute-start.4
  305.8 39.8 %collective-permute-start.5 = (bf16[512,1536]{1,0:T(8,128)(2,1)}, bf16[512,1536]{1,0:T(8,128)(2,1)}, u32[]{:S(2)}, u32[]{:S(2)}) collective-permute-start(bf16[512,1536]{1,0:T(8,128)(2,1)} %convolution_convert_fusion.5), channel_id=1, source_target_pairs={{0,1},{1,0},{2,3},{3,2},{4,5},{5,4},{6,7},{7,6},{8,9},{9,8},{10,11... | collective-permute-start | bytes 4718600 | tf_op jit(solution)/shard_map/ppermute | solution.py:1272
  370.7 35.2 %collective-permute-start.6 = (bf16[512,1536]{1,0:T(8,128)(2,1)S(1)}, bf16[512,1536]{1,0:T(8,128)(2,1)S(1)}, u32[]{:S(2)}, u32[]{:S(2)}) collective-permute-start(bf16[512,1536]{1,0:T(8,128)(2,1)S(1)} %fusion.24), channel_id=1, source_target_pairs={{0,1},{1,0},{2,3},{3,2},{4,5},{5,4},{6,7},{7,6},{8,9},{9,8},{10,11... | collective-permute-start | bytes 4718600 | tf_op jit(solution)/shard_map/ppermute | solution.py:1272
  376.6 29.2 %copy-start.5 = (f32[512,1536]{1,0:T(8,128)S(1)}, f32[512,1536]{1,0:T(8,128)}, u32[]{:S(2)}) copy-start(f32[512,1536]{1,0:T(8,128)} %copy-done.4) | copy-start | bytes 9437188
  414.3 35.5 %collective-permute-start.7 = (bf16[512,1536]{0,1:T(8,128)(2,1)S(1)}, bf16[512,1536]{0,1:T(8,128)(2,1)}, u32[]{:S(2)}, u32[]{:S(2)}) collective-permute-start(bf16[512,1536]{0,1:T(8,128)(2,1)S(1)} %copy.71), channel_id=1, source_target_pairs={{0,1},{1,0},{2,3},{3,2},{4,5},{5,4},{6,7},{7,6},{8,9},{9,8},{10,11... | collective-permute-start | bytes 4718600 | tf_op jit(solution)/shard_map/ppermute | solution.py:1272
  419.5 29.2 %collective-permute-start.8 = (f32[512,1]{0,1:T(1,128)S(1)}, f32[512,1]{0,1:T(1,128)S(1)}, u32[]{:S(2)}, u32[]{:S(2)}) collective-permute-start(f32[512,1]{0,1:T(1,128)S(1)} %bitcast.88), channel_id=1, source_target_pairs={{0,1},{1,0},{2,3},{3,2},{4,5},{5,4},{6,7},{7,6},{8,9},{9,8},{10,11... | collective-permute-start | bytes 6152 | tf_op jit(solution)/shard_map/ppermute | solution.py:1272
  456.6 134.9 %copy-start.7 = (bf16[512,1536]{1,0:T(8,128)(2,1)S(1)}, bf16[512,1536]{1,0:T(8,128)(2,1)}, u32[]{:S(2)}) copy-start(bf16[512,1536]{1,0:T(8,128)(2,1)} %hidden_ref.1) | copy-start | bytes 4718596
  456.6 134.9 %copy-start.26 = (f32[1536]{0:T(1024)S(1)}, f32[1536]{0:T(1024)}, u32[]{:S(2)}) copy-start(f32[1536]{0:T(1024)} %get-tuple-element.180) | copy-start | bytes 18436
  (31 other events, 238.5 us)
Sparse Core Ops, SparseCore 0:
  91.6 53.3 all-gather.3
  147.3 87.2 all-gather.5
  236.8 51.5 all-gather.7
  292.1 74.0 reduce-scatter.6
  370.7 131.4 reduce-scatter.4

commit v8 on v6

--- a/solution.py
+++ b/solution.py
@@ -1049,7 +1049,7 @@
             pltpu.SemaphoreType.DMA((10,)), pltpu.SemaphoreType.DMA((10,)),
             pltpu.SemaphoreType.DMA((2,)), pltpu.SemaphoreType.DMA((2,)),
         ],
-        compiler_params=pltpu.CompilerParams(collective_id=collective, has_side_effects=True),
+        compiler_params=pltpu.CompilerParams(collective_id=collective, has_side_effects=True, vmem_limit_bytes=60 << 20),
         name="last_sums",
     )(pre, total, side)
 EPSILON = 1e-05

time: 645 us -> 645 us (level)
  no operation moved by 1% of the time
where the time goes in v8:
time: 645 us; the launch traced here: 634 us
  Pallas kernels  313 us (49%)
  waiting for transfers between devices  123 us (19%)
  matrix products  115 us (18%)
  other arithmetic  28.9 us (4%)
  local copies, waits for them, and re-layouts  27.9 us (4%)
  between operations  15.8 us (2%)
  starting transfers between devices  10.7 us (2%)
    pallas_call x1, Pallas kernels, last_backward(): pl.pallas_call(functools.partial(last_backward_kernel, groups, blocks), g...  136 us
    ppermute x9, waiting for transfers between devices, swap(): return lax.ppermute(values, 'tensor', [(0, 1), (1, 0)])  109 us
    pallas_call x1, Pallas kernels, gather_all(): pl.pallas_call(gather_kernel, grid=(1,), in_specs=[first((half, depth)),...  76.2 us
    dot_general x5, matrix products, dot_nn(): lax.dot_general(a, b, (((1,), (0,)), ((), ())), preferred_element_type=F32)  51.3 us
    pallas_call x2, Pallas kernels, forward_mixer(): pl.pallas_call(forward_kernel, grid_spec=pltpu.PrefetchScalarGridSpec(num...  47.5 us
    dot_general x6, matrix products, dot_nt(): lax.dot_general(a, b, (((1,), (1,)), ((), ())), preferred_element_type=F32)  40.2 us
    pallas_call x1, Pallas kernels, backward_mixer(): pl.pallas_call(backward_kernel, grid_spec=pltpu.PrefetchScalarGridSpec(nu...  37.9 us
    dot_general x2, matrix products, dot_tn(): lax.dot_general(a, b, (((0,), (0,)), ((), ())), preferred_element_type=F32)  23.8 us
  transfers between devices with their start and end apart: 14, of which 9 were waited for; matrix products, arithmetic and copies ran while one was open for 24% of the time, Pallas kernels for 35%

profile of v8, /device:TPU:0, one launch (start us, length us, event | category | flops | bytes accessed | tf_op | source)
XLA Modules:
  0.0 634.4 jit_solution(4572919505200008646)
XLA Ops:
  13.9 76.2 %gather_all.1 = (bf16[1536,3456]{1,0:T(8,128)(2,1)}, bf16[1024,1536]{1,0:T(8,128)(2,1)}, bf16[1024,1536]{1,0:T(8,128)(2,1)}) custom-call(bf16[512,1536]{1,0:T(8,128)(2,1)} %hidden_ref.1, bf16[512,1536]{1,0:T(8,128)(2,1)} %cotangent_ref.1, f32[512,1]{1,0:T(8,128)} %fusion.36.keep_ref, f32[1,1536]{1,0:T(1,128)} %get-tuple-element.201.gain_ref, ...), custom_call_target="tpu_custom_call" | custom-call | flops 2000000000 | bytes 1000000 | tf_op jit(solution)/shard_map/gather_all/pallas_call | solution.py:1219
  94.2 14.1 %fusion.4.gate_ref.value_ref = bf16[1024,3072]{1,0:T(8,128)(2,1)} fusion(bf16[1024,1536]{1,0:T(8,128)(2,1)S(1)} %copy-done.11, bf16[1536,3456]{1,0:T(8,128)(2,1)} %get-tuple-element.72.side_weight_ref.weight_ref), kind=kOutput, calls=%fused_computation.9 | convolution fusion | flops 9666822144 | bytes 18874368 | tf_op jit(solution)/shard_map/dot_general | solution.py:20
  108.4 23.7 %forward_mixer.2 = (bf16[1024,1536]{1,0:T(8,128)(2,1)}, bf16[1024,1536]{1,0:T(8,128)(2,1)}, bf16[1024,1536]{1,0:T(8,128)(2,1)}, f32[1024,640]{1,0:T(8,128)S(1)},...) custom-call(s32[1]{0:T(128)} %bitcast.1.turn_ref, bf16[1024,3072]{1,0:T(8,128)(2,1)} %fusion.4.gate_ref.value_ref, ...), custom_call_target="tpu_custom_call" | custom-call | flops 2000000000 | bytes 1000000 | tf_op jit(solution)/shard_map/forward_mixer/pallas_call | solution.py:319
  133.7 10.1 %all-gather.4.cloned.1.call-done = bf16[1536,1536]{1,0:T(8,128)(2,1)} async-done(((bf16[96,1536]{1,0:T(8,128)(2,1)}), bf16[1536,1536]{1,0:T(8,128)(2,1)}) %all-gather.4.cloned.1.call-update) | async-done | bytes 4718608 | tf_op jit(solution)/shard_map/all_gather | solution.py:1395
  143.8 6.6 %convolution_convert_fusion.6 = bf16[512,1536]{1,0:T(8,128)(2,1)} fusion(bf16[1536,1536]{1,0:T(8,128)(2,1)} %all-gather.4.cloned.1.call-done, bf16[1024,1536]{1,0:T(8,128)(2,1)} %get-tuple-element.73), kind=kOutput, calls=%fused_computation.44 | convolution fusion | flops 2416705536 | bytes 7864320 | tf_op jit(solution)/shard_map/dot_general | solution.py:24
  157.4 29.8 %collective-permute-done.1 = f32[1024,1]{0,1:T(1,128)S(1)} collective-permute-done((f32[1024,1]{0,1:T(1,128)S(1)}, f32[1024,1]{0,1:T(1,128)S(1)}, u32[]{:S(2)}, u32[]{:S(2)}) %collective-permute-start.1) | collective-permute-done | bytes 4128 | tf_op jit(solution)/shard_map/ppermute | solution.py:1264
  187.3 5.1 fusion.32
  196.6 34.3 %collective-permute-done.2 = bf16[512,1536]{1,0:T(8,128)(2,1)S(1)} collective-permute-done((bf16[512,1536]{1,0:T(8,128)(2,1)S(1)}, bf16[512,1536]{1,0:T(8,128)(2,1)S(1)}, u32[]{:S(2)}, u32[]{:S(2)}) %collective-permute-start.2) | collective-permute-done | bytes 1572896 | tf_op jit(solution)/shard_map/ppermute | solution.py:1264
  233.9 14.5 %fusion.7.gate_ref.value_ref = bf16[1024,3072]{1,0:T(8,128)(2,1)} fusion(bf16[1536,3456]{1,0:T(8,128)(2,1)} %all-gather.6.cloned.1.call-done.side_weight_ref, bf16[512,1536]{1,0:T(8,128)(2,1)S(1)} %collective-permute-done.2, bf16[512,1536]{1,0:T(8,128)(2,1)S(1)} %multiply_convert_fusion.3), kind=kOutput, calls=%fused_computation.10 | convolution fusion | flops 9673113600 | bytes 18874368 | tf_op jit(solution)/shard_map/dot_general | solution.py:20
  248.4 23.8 %forward_mixer.3 = (bf16[1024,1536]{1,0:T(8,128)(2,1)}, bf16[1024,1536]{1,0:T(8,128)(2,1)}, bf16[1024,1536]{1,0:T(8,128)(2,1)}, f32[1024,640]{1,0:T(8,128)S(1)},...) custom-call(s32[1]{0:T(128)} %bitcast.1.turn_ref, bf16[1024,3072]{1,0:T(8,128)(2,1)} %fusion.7.gate_ref.value_ref, ...), custom_call_target="tpu_custom_call" | custom-call | flops 2000000000 | bytes 1000000 | tf_op jit(solution)/shard_map/forward_mixer/pallas_call | solution.py:319
  276.2 9.7 %convolution_convert_fusion.1 = bf16[1536,1536]{1,0:T(8,128)(2,1)} fusion(bf16[1024,1536]{1,0:T(8,128)(2,1)} %get-tuple-element.84, bf16[1024,1536]{1,0:T(8,128)(2,1)} %get-tuple-element.82, f32[1024]{0:T(1024)S(1)} %fusion.46), kind=kOutput, calls=%fused_computation.5 | convolution fusion | flops 4838916096 | bytes 11014144 | tf_op jit(solution)/shard_map/dot_general | solution.py:28
  287.7 9.9 %multiply_reduce_fusion = (f32[1024]{0:T(1024)S(1)}, bf16[1024,1536]{1,0:T(8,128)(2,1)}) fusion(bf16[1024,1536]{1,0:T(8,128)(2,1)} %get-tuple-element.84, bf16[1024,1536]{1,0:T(8,128)(2,1)} %get-tuple-element.82, bf16[1536,1536]{1,0:T(8,128)(2,1)} %all-gather.8.cloned.1.call-done), kind=kOutput, calls=%fused_computation.7 | convolution fusion | flops 4839701504 | bytes 14159872 | tf_op jit(solution)/shard_map/dot_general | solution.py:20
  306.8 37.9 %backward_mixer.1 = (bf16[1024,3456]{1,0:T(8,128)(2,1)}, f32[8,1536]{1,0:T(8,128)S(1)}, f32[8,256]{1,0:T(8,128)S(1)}, f32[8,128]{1,0:T(8,128)S(1)}) custom-call(s32[1]{0:T(128)} %bitcast.1.turn_ref, bf16[1024,3072]{1,0:T(8,128)(2,1)} %fusion.7.gate_ref.value_ref, bf16[1024,3072]{1,0:T(8,128)(2,1)} %fusion.7.gate_ref.value_ref, ...), custom_call_target="tpu_custom_call" | custom-call | flops 2000000000 | bytes 1000000 | tf_op jit(solution)/shard_map/backward_mixer/pallas_call | solution.py:367
  344.8 9.9 %fusion.25 = bf16[512,1536]{1,0:T(8,128)(2,1)S(1)} fusion(bf16[1536,3456]{1,0:T(8,128)(2,1)} %all-gather.6.cloned.1.call-done.side_weight_ref, bf16[1024,3456]{1,0:T(8,128)(2,1)} %get-tuple-element.95), kind=kOutput, calls=%fused_computation.40 | convolution fusion | flops 5436604416 | bytes 15728640 | tf_op jit(solution)/shard_map/dot_general | solution.py:24
  354.7 14.1 %convolution_convert_fusion = bf16[1536,3456]{1,0:T(8,128)(2,1)} fusion(bf16[1024,3456]{1,0:T(8,128)(2,1)S(1)} %copy-done.38, bf16[512,1536]{1,0:T(8,128)(2,1)S(1)} %copy-done.20, bf16[512,1536]{1,0:T(8,128)(2,1)S(1)} %copy-done.17), kind=kOutput, calls=%fused_computation | convolution fusion | flops 10883235840 | bytes 20840448 | tf_op jit(solution)/shard_map/dot_general | solution.py:28
  369.5 5.3 fusion.29
  374.8 9.5 %fusion.13 = f32[512,1536]{1,0:T(8,128)S(1)} fusion(bf16[1536,3456]{1,0:T(8,128)(2,1)} %all-gather.6.cloned.1.call-done.side_weight_ref, bf16[1024,3456]{1,0:T(8,128)(2,1)S(1)} %bitcast.101), kind=kOutput, calls=%fused_computation.18 | convolution fusion | flops 5435817984 | bytes 17301504 | tf_op jit(solution)/shard_map/dot_general | solution.py:24
  384.4 19.7 %collective-permute-done.6 = bf16[512,1536]{1,0:T(8,128)(2,1)S(1)} collective-permute-done((bf16[512,1536]{1,0:T(8,128)(2,1)S(1)}, bf16[512,1536]{1,0:T(8,128)(2,1)S(1)}, u32[]{:S(2)}, u32[]{:S(2)}) %collective-permute-start.6) | collective-permute-done | bytes 1572896 | tf_op jit(solution)/shard_map/ppermute | solution.py:1264
  405.0 5.7 multiply_reduce_fusion.2
  418.8 6.0 convolution_convert_fusion.4.own_dgn_ref
  425.5 21.4 %collective-permute-done.8 = f32[512,1]{0,1:T(1,128)S(1)} collective-permute-done((f32[512,1]{0,1:T(1,128)S(1)}, f32[512,1]{0,1:T(1,128)S(1)}, u32[]{:S(2)}, u32[]{:S(2)}) %collective-permute-start.8) | collective-permute-done | bytes 2080 | tf_op jit(solution)/shard_map/ppermute | solution.py:1264
  448.0 6.8 %convolution_convert_fusion.3.other_dgn_ref = bf16[512,1536]{1,0:T(8,128)(2,1)} fusion(bf16[512,1536]{0,1:T(8,128)(2,1)} %collective-permute-done.7, bf16[1536,1536]{1,0:T(8,128)(2,1)} %all-gather.4.cloned.1.call-done), kind=kOutput, calls=%fused_computation.41 | convolution fusion | flops 2416705536 | bytes 7864320 | tf_op jit(solution)/shard_map/dot_general | solution.py:20
  454.8 135.5 %last_backward.1 = (f32[2,96,1536]{2,1,0:T(8,128)}, f32[96,384]{1,0:T(8,128)}, f32[1536,96]{1,0:T(8,128)}, f32[16,1792]{1,0:T(8,128)}, f32[512,1536]{1,0:T(8,128)}) custom-call(bf16[1024,3072]{1,0:T(8,128)(2,1)} %fusion.4.gate_ref.value_ref, bf16[1024,3072]{1,0:T(8,128)(2,1)} %fusion.4.gate_ref.value_ref, bf16[1024,1536]{1,0:T(8,128)(2,1)} %get-tuple-element.99.pre_ref, ...), custom_call_target="tpu_custom_call" | custom-call | flops 2000000000 | bytes 1000000 | tf_op jit(solution)/shard_map/last_backward/pallas_call | solution.py:920
  603.2 15.6 %last_sums.1 = (f32[2,1536]{1,0:T(2,128)}, f32[2,5,3328]{2,1,0:T(8,128)}, f32[2,48]{1,0:T(2,128)}, f32[2,48]{1,0:T(2,128)}, f32[2,48]{1,0:T(2,128)}, /*index=5*/...) custom-call(f32[1,1536]{1,0:T(1,128)} %broadcast_in_dim.11.pre_ref, f32[16,1792]{1,0:T(8,128)} %get-tuple-element.112.total_ref, ...), custom_call_target="tpu_custom_call" | custom-call | tf_op jit(solution)/shard_map/last_sums/pallas_call | solution.py:1041
  (204 shorter events, 73.3 us)
Async XLA Ops:
  7.2 136.6 %all-gather.4.cloned.1.call-start = ((), (), s32[]{:S(2)}) async-start(), calls=%async_computation.2 | async-start | bytes 5013504 | tf_op jit(solution)/shard_map/all_gather | solution.py:1395
  13.9 76.4 %copy-start.26 = (bf16[2,96,24]{2,1,0:T(8,128)(2,1)S(1)}, bf16[2,96,24]{2,1,0:T(8,128)(2,1)}, u32[]{:S(2)}) copy-start(bf16[2,96,24]{2,1,0:T(8,128)(2,1)} %copy.69.step_ref) | copy-start | bytes 27652
  13.9 76.4 %copy-start.28 = (bf16[2,96,256]{2,1,0:T(8,128)(2,1)S(1)}, bf16[2,96,256]{2,1,0:T(8,128)(2,1)}, u32[]{:S(2)}) copy-start(bf16[2,96,256]{2,1,0:T(8,128)(2,1)} %state_ref.1) | copy-start | bytes 294916
  90.2 143.7 %all-gather.6.cloned.1.call-start = ((), (), s32[]{:S(2)}) async-start(), calls=%async_computation.3 | async-start | bytes 11280384 | tf_op jit(solution)/shard_map/all_gather | solution.py:1392
  92.5 195.2 %all-gather.8.cloned.1.call-start = ((), (), s32[]{:S(2)}) async-start(), calls=%async_computation.4 | async-start | bytes 5013504 | tf_op jit(solution)/shard_map/all_gather | solution.py:1395
  93.2 505.1 %reduce-scatter.7.cloned.1.call-start = ((), (), s32[]{:S(2)}) async-start(), calls=%async_computation.6 | async-start | bytes 5013504
  108.4 23.7 %copy-start.1 = (f32[8,1536]{1,0:T(8,128)}, f32[8,1536]{1,0:T(8,128)S(1)}, u32[]{:S(2)}) copy-start(f32[8,1536]{1,0:T(8,128)S(1)} %get-tuple-element.215.chan_ref) | copy-start | bytes 147460
  150.4 42.0 %collective-permute-start = (bf16[512,1536]{1,0:T(8,128)(2,1)}, bf16[512,1536]{1,0:T(8,128)(2,1)S(1)}, u32[]{:S(2)}, u32[]{:S(2)}) collective-permute-start(bf16[512,1536]{1,0:T(8,128)(2,1)} %convolution_convert_fusion.6), channel_id=1, source_target_pairs={{0,1},{1,0},{2,3},{3,2},{4,5},{5,4},{6,7},{7,6},{8,9},{9,8},{10,11... | collective-permute-start | bytes 4718600 | tf_op jit(solution)/shard_map/ppermute | solution.py:1264
  152.1 35.2 %collective-permute-start.1 = (f32[1024,1]{0,1:T(1,128)S(1)}, f32[1024,1]{0,1:T(1,128)S(1)}, u32[]{:S(2)}, u32[]{:S(2)}) collective-permute-start(f32[1024,1]{0,1:T(1,128)S(1)} %bitcast.86), channel_id=1, source_target_pairs={{0,1},{1,0},{2,3},{3,2},{4,5},{5,4},{6,7},{7,6},{8,9},{9,8},{10,11... | collective-permute-start | bytes 12296 | tf_op jit(solution)/shard_map/ppermute | solution.py:1264
  194.9 39.0 %copy-start.16 = (bf16[512,1536]{1,0:T(8,128)(2,1)}, bf16[512,1536]{1,0:T(8,128)(2,1)S(1)}, u32[]{:S(2)}) copy-start(bf16[512,1536]{1,0:T(8,128)(2,1)S(1)} %multiply_convert_fusion.3) | copy-start | bytes 4718596
  194.9 35.9 %collective-permute-start.2 = (bf16[512,1536]{1,0:T(8,128)(2,1)S(1)}, bf16[512,1536]{1,0:T(8,128)(2,1)S(1)}, u32[]{:S(2)}, u32[]{:S(2)}) collective-permute-start(bf16[512,1536]{1,0:T(8,128)(2,1)S(1)} %multiply_convert_fusion.3), channel_id=1, source_target_pairs={{0,1},{1,0},{2,3},{3,2},{4,5},{5,4},{6,7},{7,6},{8,9},{9,8},{10,11... | collective-permute-start | bytes 4718600 | tf_op jit(solution)/shard_map/ppermute | solution.py:1264
  272.5 3.7 collective-permute-start.3
  285.9 315.2 %reduce-scatter.5.cloned.1.call-start = ((), (), s32[]{:S(2)}) async-start(), calls=%async_computation.5 | async-start | bytes 11280384 | tf_op jit(solution)/shard_map/reduce_scatter | solution.py:1318
  297.5 3.6 collective-permute-start.4
  305.0 39.8 %collective-permute-start.5 = (bf16[512,1536]{1,0:T(8,128)(2,1)}, bf16[512,1536]{1,0:T(8,128)(2,1)}, u32[]{:S(2)}, u32[]{:S(2)}) collective-permute-start(bf16[512,1536]{1,0:T(8,128)(2,1)} %convolution_convert_fusion.5), channel_id=1, source_target_pairs={{0,1},{1,0},{2,3},{3,2},{4,5},{5,4},{6,7},{7,6},{8,9},{9,8},{10,11... | collective-permute-start | bytes 4718600 | tf_op jit(solution)/shard_map/ppermute | solution.py:1264
  368.9 35.2 %collective-permute-start.6 = (bf16[512,1536]{1,0:T(8,128)(2,1)S(1)}, bf16[512,1536]{1,0:T(8,128)(2,1)S(1)}, u32[]{:S(2)}, u32[]{:S(2)}) collective-permute-start(bf16[512,1536]{1,0:T(8,128)(2,1)S(1)} %fusion.25), channel_id=1, source_target_pairs={{0,1},{1,0},{2,3},{3,2},{4,5},{5,4},{6,7},{7,6},{8,9},{9,8},{10,11... | collective-permute-start | bytes 4718600 | tf_op jit(solution)/shard_map/ppermute | solution.py:1264
  374.8 29.2 %copy-start.5 = (f32[512,1536]{1,0:T(8,128)S(1)}, f32[512,1536]{1,0:T(8,128)}, u32[]{:S(2)}) copy-start(f32[512,1536]{1,0:T(8,128)} %copy-done.4) | copy-start | bytes 9437188
  384.3 20.7 %copy-start.9 = (f32[512,1536]{1,0:T(8,128)S(1)}, f32[512,1536]{1,0:T(8,128)}, u32[]{:S(2)}) copy-start(f32[512,1536]{1,0:T(8,128)} %copy-done.8) | copy-start | bytes 9437188
  384.3 20.7 %copy-start.15 = (bf16[512,1536]{1,0:T(8,128)(2,1)S(1)}, bf16[512,1536]{1,0:T(8,128)(2,1)}, u32[]{:S(2)}) copy-start(bf16[512,1536]{1,0:T(8,128)(2,1)} %copy-done.14) | copy-start | bytes 4718596
  384.3 20.7 %copy-start.18 = (bf16[512,1536]{1,0:T(8,128)(2,1)S(1)}, bf16[512,1536]{1,0:T(8,128)(2,1)}, u32[]{:S(2)}) copy-start(bf16[512,1536]{1,0:T(8,128)(2,1)} %cotangent_ref.1) | copy-start | bytes 4718596
  412.5 35.5 %collective-permute-start.7 = (bf16[512,1536]{0,1:T(8,128)(2,1)S(1)}, bf16[512,1536]{0,1:T(8,128)(2,1)}, u32[]{:S(2)}, u32[]{:S(2)}) collective-permute-start(bf16[512,1536]{0,1:T(8,128)(2,1)S(1)} %copy.75), channel_id=1, source_target_pairs={{0,1},{1,0},{2,3},{3,2},{4,5},{5,4},{6,7},{7,6},{8,9},{9,8},{10,11... | collective-permute-start | bytes 4718600 | tf_op jit(solution)/shard_map/ppermute | solution.py:1264
  417.7 29.1 %collective-permute-start.8 = (f32[512,1]{0,1:T(1,128)S(1)}, f32[512,1]{0,1:T(1,128)S(1)}, u32[]{:S(2)}, u32[]{:S(2)}) collective-permute-start(f32[512,1]{0,1:T(1,128)S(1)} %bitcast.95), channel_id=1, source_target_pairs={{0,1},{1,0},{2,3},{3,2},{4,5},{5,4},{6,7},{7,6},{8,9},{9,8},{10,11... | collective-permute-start | bytes 6152 | tf_op jit(solution)/shard_map/ppermute | solution.py:1264
  454.8 135.5 %copy-start.7 = (bf16[512,1536]{1,0:T(8,128)(2,1)S(1)}, bf16[512,1536]{1,0:T(8,128)(2,1)}, u32[]{:S(2)}) copy-start(bf16[512,1536]{1,0:T(8,128)(2,1)} %hidden_ref.1) | copy-start | bytes 4718596
  454.8 135.6 %copy-start.27 = (f32[1536]{0:T(1024)S(1)}, f32[1536]{0:T(1024)}, u32[]{:S(2)}) copy-start(f32[1536]{0:T(1024)} %get-tuple-element.176) | copy-start | bytes 18436
  (33 other events, 196.1 us)
Sparse Core Ops, SparseCore 0:
  90.4 53.3 all-gather.3
  146.6 87.2 all-gather.5
  236.2 51.3 all-gather.7
  291.4 74.0 reduce-scatter.6
  370.0 133.4 reduce-scatter.4
